TPU v7x, 32 devices: a whole 2x2x4 slice. The times are simulated.
32 devices in a mesh: band: 32 (over z, y, x, core).
Axes of the slice: x: 2, y: 2, z: 4, core: 2. Of those that a mesh axis runs over, the one named last changes fastest.
Arguments:
- orbitals: bfloat16 [64, 884736], P('band'), may hold values from -24 to 24
Outputs:
- exchange: float32 [64, 884736], P('band')
- gram: float32 [64, 2], P('band')
- energy: float32 [], replicated
All inputs are finite; a program needn't handle non-finite values.
Results may differ from a plain program's by a relative error of at most 0.0055.
The roundings to bfloat16 on the way count: a program that leaves them out, or rounds other values in their place, can miss the bound.
Values may be sent and summed in bfloat16 or wider, within the bound.
No kernel may reach another device: no remote copies, remote signals or barrier semaphores. Data moves between devices by JAX's collectives and lax.ppermute only.
A program may use at most 256 MiB of HBM per device.

v0:
```python
import jax
import jax.numpy as jnp
import ml_dtypes
import numpy as np
from jax import lax
from jax.experimental import pallas as pl
from jax.experimental.pallas import tpu as pltpu
from jax.sharding import PartitionSpec as P

G = 96
HALF = G // 2 + 1
NGRID = G * G * G
LANES = 128
ROWS = NGRID // LANES
PLANE = G * G // LANES
QUADS = G // 4
Y_PITCH = 104
WAVE_UNIT = 0.05
SCREEN_SQ = 0.0121
BF16 = jnp.bfloat16
F32 = jnp.float32


def dft_tables():
    n = np.arange(G)
    phases = (n[:, None] * n[None, :]) % G
    angles = phases.astype(np.float32) * np.float32(2.0 * np.pi / G)
    rounded = [f(angles).astype(ml_dtypes.bfloat16).astype(np.float32) for f in (np.cos, np.sin)]
    return rounded[0], rounded[1]


def section_tables():
    c, s = dft_tables()
    h = HALF
    t1 = np.zeros((Y_PITCH, G), np.float32)
    t1[:h] = c[:h]
    t1[h : 2 * h] = -s[:h]
    t2 = np.block([[c, s], [-s, c]])
    t3 = np.zeros((2, 2, LANES, 4, 2, 64), np.float32)
    back = (G - np.arange(h)) % G
    for p in range(2):
        t3[0, p, :G, 0, p, :h] = c[:h].T
        t3[1, p, :G, 0, p, :h] = s[:h].T
        t3[0, p, :G, 1, p, :h] = -s[:h].T
        t3[1, p, :G, 1, p, :h] = c[:h].T
        t3[0, p, :G, 2, p, :h] = c[back].T
        t3[1, p, :G, 2, p, :h] = s[back].T
        t3[0, p, :G, 3, p, :h] = s[back].T
        t3[1, p, :G, 3, p, :h] = -c[back].T
    t3 = t3.reshape(4 * LANES, 4 * LANES)
    order = np.concatenate([np.arange(G // 2), G - 1 - np.arange(G // 2)])
    a1 = np.block([[c[:, order], -s[:, order]], [s[:, order], c[:, order]]])
    rows = np.arange(G).reshape(QUADS, 4).T.reshape(-1)
    a2 = np.block([[c[rows], -s[rows]], [s[rows], c[rows]]])
    weight = np.full((h, 1), 2.0, np.float32)
    weight[0] = weight[h - 1] = 1.0
    a3 = np.zeros((3, 2, 2, 2, 64, 2, LANES), np.float32)
    for third in range(3):
        for lane in range(LANES):
            r, x3 = divmod(third * LANES + lane, G)
            for p in range(2):
                a3[third, r - third, 0, p, :h, p, lane] = weight[:, 0] * c[x3, :h]
                a3[third, r - third, 1, p, :h, p, lane] = -weight[:, 0] * s[x3, :h]
    a3 = a3.reshape(3, 4 * LANES, 2 * LANES)
    sel = np.zeros((2, 2 * LANES, 2 * LANES), np.float32)
    for r in range(4):
        for x in range(G):
            sel[r // 2, r * G + x - (r // 2) * LANES, (r % 2) * LANES + x] = 1.0
    return [t.astype(ml_dtypes.bfloat16) for t in (t1, t2, t3, a1, a2, a3, sel)]


def screening():
    n = np.arange(G)
    m = np.where(n <= G // 2, n, n - G).astype(np.float64)
    sq = m * m
    q2 = WAVE_UNIT * (sq[:HALF, None, None] + sq[None, :, None] + sq[None, None, :HALF])
    safe = np.where(q2 > 0, q2, 1.0)
    kern = 4.0 * np.pi * (1.0 - np.exp(-q2 / (4.0 * SCREEN_SQ))) / safe
    kern = np.where(q2 > 0, kern, np.pi / SCREEN_SQ)
    out = np.zeros((HALF, G, 2, 64), np.float32)
    out[:, :, :, :HALF] = kern[:, :, None, :]
    return out.reshape(HALF * G, LANES)


def dot(a, b):
    return jnp.dot(a, b, preferred_element_type=F32)


def lanes(*parts):
    return jnp.concatenate(parts, axis=1)


def stack(*parts):
    return jnp.concatenate(parts, axis=0)


def widen(src, dst, chunk):
    @pl.loop(0, src.shape[0] // chunk)
    def _(i):
        at = pl.ds(i * chunk, chunk)
        dst[at, :] = src[at, :].astype(F32)


def split_rows(rows, sel_ref):
    first = dot(lanes(rows[0], rows[1]), sel_ref[0])
    second = dot(lanes(rows[1], rows[2]), sel_ref[1])
    return [first[:, :LANES], first[:, LANES:], second[:, :LANES], second[:, LANES:]]


def pairs_kernel(
    own_ref, par_ref, t1, t2, t3, a1, a2, a3, sel, kern,
    own_out, par_out, energy_out,
    own_f, par_f, own_u, yw, z, x34, staged,
):
    widen(own_ref, own_f, 576)
    widen(par_ref, par_f, 576)

    @pl.loop(0, QUADS)
    def _(q):
        for p in range(2):
            rows = [
                own_f[pl.ds(2 * (3 * q + s) + p, G, stride=2 * PLANE), :].astype(BF16)
                for s in range(3)
            ]
            for r, part in enumerate(split_rows(rows, sel)):
                own_u[p, 4 * q + r] = part.astype(BF16)

    half_y = G * Y_PITCH

    @pl.loop(0, QUADS)
    def _(q):
        rows = [par_f[pl.ds(3 * q + s, G, stride=PLANE), :].astype(BF16) for s in range(3)]
        for r, part in enumerate(split_rows(rows, sel)):
            b = 4 * q + r
            density = [(own_u[p, b].astype(F32) * part).astype(BF16) for p in range(2)]
            y = dot(t1[...], lanes(*density))
            for p in range(2):
                at = pl.multiple_of(p * half_y + b * Y_PITCH, 8)
                yw[pl.ds(at, Y_PITCH), :] = y[:, p * LANES : (p + 1) * LANES]

    @pl.loop(0, HALF)
    def _(k1):
        def line(p, part):
            return yw[pl.ds(p * half_y + part * HALF + k1, G, stride=Y_PITCH), :].astype(BF16)

        out = dot(t2[...], stack(lanes(line(0, 0), line(1, 0)), lanes(line(0, 1), line(1, 1))))
        at = pl.ds(pl.multiple_of(k1 * G, 16), G)
        x34[at, : 2 * LANES] = out[:G].astype(BF16)
        x34[at, 2 * LANES :] = out[G:].astype(BF16)

    chunk = 336

    @pl.loop(0, HALF * G // chunk)
    def _(m):
        at = pl.ds(pl.multiple_of(m * chunk, 16), chunk)
        field = x34[at, :]
        factor = kern[at, :]
        for h in range(2):
            out = dot(field, t3[:, 2 * h * LANES : 2 * (h + 1) * LANES])
            for e in range(2):
                spectrum = out[:, e * LANES : (e + 1) * LANES].astype(BF16).astype(F32)
                z[2 * h + e, at, :] = spectrum * factor

    @pl.loop(0, G // 2)
    def _(pair):
        parts = []
        for e in range(2):
            k2 = 2 * pair + e
            mirror = G + jnp.where(k2 == 0, 0, G - k2)
            parts.append(
                stack(
                    z[0, pl.ds(k2, G // 2, stride=G), :].astype(BF16),
                    z[2, pl.ds(mirror, G // 2, stride=G), :].astype(BF16),
                    z[1, pl.ds(k2, G // 2, stride=G), :].astype(BF16),
                    z[3, pl.ds(mirror, G // 2, stride=G), :].astype(BF16),
                )
            )
        out = dot(a1[...], lanes(*parts))
        for e in range(2):
            at = pl.multiple_of((2 * pair + e) * 2 * G, 8)
            yw[pl.ds(at, 2 * G), :] = out[:, e * LANES : (e + 1) * LANES]

    @pl.loop(0, G // 2)
    def _(pair):
        parts = []
        for e in range(2):
            x1 = 2 * pair + e
            parts.append(
                stack(
                    yw[pl.ds(x1, G, stride=2 * G), :].astype(BF16),
                    yw[pl.ds(G + x1, G, stride=2 * G), :].astype(BF16),
                )
            )
        out = dot(a2[...], lanes(*parts))
        for r in range(4):
            block = [
                lanes(
                    out[r * QUADS : (r + 1) * QUADS, e * LANES : (e + 1) * LANES],
                    out[G + r * QUADS : G + (r + 1) * QUADS, e * LANES : (e + 1) * LANES],
                )
                for e in range(2)
            ]
            at = pl.multiple_of((r // 2) * G * QUADS + pair * 2 * QUADS, 16)
            left = (r % 2) * 2 * LANES
            x34[pl.ds(at, 2 * QUADS), left : left + 2 * LANES] = stack(*block).astype(BF16)

    energy_out[...] = jnp.zeros_like(energy_out)
    planes = 8
    block_rows = planes * QUADS
    scale = F32(1.0 / NGRID)

    @pl.loop(0, G // planes)
    def _(ch):
        at = pl.multiple_of(ch * block_rows, 16)
        low = x34[pl.ds(at, block_rows), :]
        high = x34[pl.ds(G * QUADS + at, block_rows), :]
        fields = [low, lanes(low[:, 2 * LANES :], high[:, : 2 * LANES]), high]
        total = jnp.zeros((QUADS, LANES), F32)
        for third in range(3):
            out = dot(fields[third], a3[third]) * scale
            for i in range(planes):
                row = (ch * planes + i) * PLANE + third
                partner = par_f[pl.ds(row, QUADS, stride=3), :]
                sent = jnp.zeros((QUADS, LANES), F32)
                for p in range(2):
                    potential = out[i * QUADS : (i + 1) * QUADS, p * LANES : (p + 1) * LANES]
                    own_at = pl.ds(2 * row + p, QUADS, stride=6)
                    own_out[own_at, :] = potential * partner
                    sent = sent + potential * own_f[own_at, :]
                total = total + sent * partner
                staged[pl.ds(i * PLANE + third, QUADS, stride=3), :] = sent
        energy_out[...] += total
        at = pl.multiple_of(ch * planes * PLANE, 16)
        par_out[pl.ds(at, planes * PLANE), :] = staged[...].astype(BF16)


def pair_terms(own, partner, tables, kern, interpret=False):
    vmem = pl.BlockSpec(memory_space=pltpu.VMEM)
    return pl.pallas_call(
        pairs_kernel,
        out_shape=(
            jax.ShapeDtypeStruct((2 * ROWS, LANES), F32),
            jax.ShapeDtypeStruct((ROWS, LANES), BF16),
            jax.ShapeDtypeStruct((QUADS, LANES), F32),
        ),
        in_specs=[vmem] * 10,
        out_specs=(vmem, vmem, vmem),
        scratch_shapes=[
            pltpu.VMEM((2 * ROWS, LANES), F32),
            pltpu.VMEM((ROWS, LANES), F32),
            pltpu.VMEM((2, G, G, LANES), BF16),
            pltpu.VMEM((2 * G * Y_PITCH, LANES), F32),
            pltpu.VMEM((4, HALF * G, LANES), F32),
            pltpu.VMEM((HALF * G, 4 * LANES), BF16),
            pltpu.VMEM((8 * PLANE, LANES), F32),
        ],
        compiler_params=pltpu.CompilerParams(vmem_limit_bytes=62 * 1024 * 1024),
        cost_estimate=pl.CostEstimate(
            flops=20_000_000_000, bytes_accessed=20_000_000, transcendentals=0
        ),
        interpret=interpret,
        name="pair_terms",
    )(own, partner, *tables, kern)


BLOCK = 576


def sum_kernel(own_ref, first_ref, second_ref, back0_ref, back1_ref, out_ref, gram_ref, orb, exch):
    orb[...] = own_ref[...].astype(F32)
    exch[...] = first_ref[...] + second_ref[...]
    total = []
    for p, back in enumerate((back0_ref, back1_ref)):
        at = pl.ds(p, BLOCK, stride=2)
        value = exch[at, :] + back[...].astype(F32)
        exch[at, :] = value
        total.append(value)
    out_ref[...] = exch[...]

    @pl.when(pl.program_id(0) == 0)
    def _():
        gram_ref[...] = jnp.zeros_like(gram_ref)

    for i in range(2):
        bands = orb[pl.ds(i, BLOCK, stride=2), :]
        for p in range(2):
            gram_ref[2 * i + p] += jnp.sum((bands * total[p]).reshape(-1, 8, LANES), axis=0)


def add_returned(own, first, second, back0, back1, interpret=False):
    wide = pl.BlockSpec((2 * BLOCK, LANES), lambda i: (i, 0))
    flat = pl.BlockSpec((BLOCK, LANES), lambda i: (i, 0))
    return pl.pallas_call(
        sum_kernel,
        grid=(ROWS // BLOCK,),
        out_shape=(
            jax.ShapeDtypeStruct((2 * ROWS, LANES), F32),
            jax.ShapeDtypeStruct((4, 8, LANES), F32),
        ),
        in_specs=[wide, wide, wide, flat, flat],
        out_specs=(wide, pl.BlockSpec((4, 8, LANES), lambda i: (0, 0, 0))),
        scratch_shapes=[pltpu.VMEM((2 * BLOCK, LANES), F32)] * 2,
        interpret=interpret,
        name="add_returned",
    )(own, first, second, back0, back1)


def from_behind(block, axis, distance):
    size = lax.axis_size(axis)
    return lax.ppermute(block, axis, [((i - distance) % size, i) for i in range(size)])


def sum_over(value, axis):
    size = lax.axis_size(axis)
    if size & (size - 1):
        return lax.psum(value, axis)
    step = 1
    while step < size:
        value = value + lax.ppermute(value, axis, [(i ^ step, i) for i in range(size)])
        step *= 2
    return value


def per_device(orbitals):
    tables = section_tables()
    kern = screening()
    bands = orbitals.reshape(2, ROWS, LANES)
    own = bands.transpose(1, 0, 2).reshape(2 * ROWS, LANES)
    previous = [from_behind(bands[j], "band", 1) for j in range(2)]
    first, sent0, energy0 = pair_terms(own, previous[0], tables, kern)
    back0 = from_behind(sent0, "band", -1)
    second, sent1, energy1 = pair_terms(own, previous[1], tables, kern)
    back1 = from_behind(sent1, "band", -1)
    pair_energy = jnp.sum(energy0 + energy1).reshape(1, 1)
    total = sum_over(jnp.broadcast_to(pair_energy, (8, LANES)), "band")[0, 0]
    energy = -2.0 * total / F32(NGRID) / F32(2 * lax.axis_size("band") * orbitals.shape[0])
    exchange, gram = add_returned(own, first, second, back0, back1)
    gram = jnp.sum(gram, axis=(1, 2)).reshape(2, 2) / F32(NGRID)
    exchange = exchange.reshape(ROWS, 2, LANES).transpose(1, 0, 2).reshape(2, NGRID)
    return exchange, gram, energy


def solution(mesh):
    return jax.shard_map(
        per_device,
        mesh=mesh,
        in_specs=(P("band", None),),
        out_specs=(P("band", None), P("band", None), P()),
        check_vma=False,
    )
```

profile of v0, /device:TPU:0, one launch (start us, length us, event | category | flops | bytes accessed | tf_op | source)
XLA Modules:
  0.0 259.2 jit_solution(9360038188110190745)
XLA Ops:
  0.6 40.0 %slice_reduce_fusion = (bf16[884736]{0:T(1024)(128)(2,1)S(1)}, bf16[884736]{0:T(1024)(128)(2,1)}) fusion(bf16[2,884736]{1,0:T(2,128)(2,1)} %param.9), kind=kLoop, calls=%fused_computation | loop fusion | bytes 7077888 | tf_op jit(solution)/shard_map/slice | solution.py:329
  40.6 0.5 collective-permute-start.1
  41.0 2.6 %collective-permute-start = (bf16[6912,128]{1,0:T(8,128)(2,1)}, bf16[6912,128]{1,0:T(8,128)(2,1)}, u32[]{:S(2)}, u32[]{:S(2)}) collective-permute-start(bf16[6912,128]{1,0:T(8,128)(2,1)} %bitcast.11), channel_id=1, source_target_pairs={{31,0},{0,1},{1,2},{2,3},{3,4},{4,5},{5,6},{6,7},{7,8},{8,9},{9,10... | collective-permute-start | bytes 5308424 | tf_op jit(solution)/shard_map/ppermute | solution.py:310
  43.6 23.5 %collective-permute-done.1.par_ref = bf16[6912,128]{1,0:T(8,128)(2,1)S(1)} collective-permute-done((bf16[6912,128]{1,0:T(8,128)(2,1)S(1)}, bf16[6912,128]{1,0:T(8,128)(2,1)S(1)}, u32[]{:S(2)}, u32[]{:S(2)}) %collective-permute-start.1) | collective-permute-done | bytes 1769504 | tf_op jit(solution)/shard_map/ppermute | solution.py:310
  67.2 0.0 copy-start.2
  67.2 1.3 copy-done.2
  68.5 68.4 %pair_terms.3 = (f32[13824,128]{1,0:T(8,128)}, bf16[6912,128]{1,0:T(8,128)(2,1)}, f32[24,128]{1,0:T(8,128)}) custom-call(bf16[13824,128]{1,0:T(8,128)(2,1)} %bitcast.13, bf16[6912,128]{1,0:T(8,128)(2,1)} %copy-done.2, bf16[104,96]{1,0:T(8,128)(2,1)} %constant.30.clone.t1, bf16[192,192]{1,0:T(8,128)(2,1)} %constant.31.clone.t2, ...), custom_call_target="tpu_custom_call" | custom-call | flops 20000000000 | bytes 20000000 | tf_op jit(solution)/shard_map/pair_terms/pallas_call | solution.py:239
  136.8 0.0 copy-start.1
  136.8 0.0 collective-permute-start.3
  136.8 0.0 collective-permute-done.par_ref
  136.9 68.5 %pair_terms.2 = (f32[13824,128]{1,0:T(8,128)}, bf16[6912,128]{1,0:T(8,128)(2,1)}, f32[24,128]{1,0:T(8,128)}) custom-call(bf16[13824,128]{1,0:T(8,128)(2,1)} %bitcast.14, bf16[6912,128]{1,0:T(8,128)(2,1)} %collective-permute-done.par_ref, bf16[104,96]{1,0:T(8,128)(2,1)} %constant.30.clone.t1, bf16[192,192]{1,0:T(8,128)(2,1)} %constant.31.clone.t2, ...), custom_call_target="tpu_custom_call" | custom-call | flops 20000000000 | bytes 20000000 | tf_op jit(solution)/shard_map/pair_terms/pallas_call | solution.py:239
  205.4 2.4 collective-permute-start.2
  207.8 0.0 copy-done.1
  207.8 1.3 add_reduce_fusion
  209.1 0.6 broadcast_in_dim.2
  209.8 0.1 collective-permute-start.4
  209.8 1.2 collective-permute-done.4
  211.0 0.6 broadcast_add_fusion
  211.6 0.1 collective-permute-start.5
  211.7 16.6 %collective-permute-done.5 = f32[8,128]{1,0:T(8,128)S(1)} collective-permute-done((f32[8,128]{1,0:T(8,128)S(1)}, f32[8,128]{1,0:T(8,128)S(1)}, u32[]{:S(2)}, u32[]{:S(2)}) %collective-permute-start.5) | collective-permute-done | bytes 4128 | tf_op jit(solution)/shard_map/ppermute | solution.py:319
  228.3 0.6 fusion
  229.0 0.1 collective-permute-start.6
  229.0 3.6 %collective-permute-done.6 = f32[8,128]{1,0:T(8,128)S(1)} collective-permute-done((f32[8,128]{1,0:T(8,128)S(1)}, f32[8,128]{1,0:T(8,128)S(1)}, u32[]{:S(2)}, u32[]{:S(2)}) %collective-permute-start.6) | collective-permute-done | bytes 4128 | tf_op jit(solution)/shard_map/ppermute | solution.py:319
  232.6 0.2 collective-permute-start.7
  232.8 3.4 %collective-permute-done.7 = f32[8,128]{1,0:T(8,128)S(1)} collective-permute-done((f32[8,128]{1,0:T(8,128)S(1)}, f32[8,128]{1,0:T(8,128)S(1)}, u32[]{:S(2)}, u32[]{:S(2)}) %collective-permute-start.7) | collective-permute-done | bytes 4128 | tf_op jit(solution)/shard_map/ppermute | solution.py:319
  236.3 1.2 collective-permute-start.8
  237.5 3.3 %collective-permute-done.8 = f32[8,128]{1,0:T(8,128)S(1)} collective-permute-done((f32[8,128]{1,0:T(8,128)S(1)}, f32[8,128]{1,0:T(8,128)S(1)}, u32[]{:S(2)}, u32[]{:S(2)}) %collective-permute-start.8) | collective-permute-done | bytes 4128 | tf_op jit(solution)/shard_map/ppermute | solution.py:319
  240.8 0.5 slice.13
  241.9 0.0 collective-permute-done.3.back1_ref
  241.9 0.0 copy-start
  241.9 0.0 collective-permute-done.2.back0_ref
  242.0 1.2 copy-done
  243.1 13.5 %add_returned.1 = (f32[13824,128]{1,0:T(8,128)}, f32[4,8,128]{2,1,0:T(8,128)}) custom-call(bf16[13824,128]{1,0:T(8,128)(2,1)} %bitcast.15, f32[13824,128]{1,0:T(8,128)} %get-tuple-element.11.first_ref, f32[13824,128]{1,0:T(8,128)} %get-tuple-element.12.second_ref, bf16[6912,128]{1,0:T(8,128)(2,1)} %collective-permute-done.2.back0_ref, bf16[6912,128]{1,0:T(8,128)(2,1)} %copy-done), custom_call_target="tpu_custom_call" | custom-call | tf_op jit(solution)/shard_map/add_returned/pallas_call | solution.py:293
  256.6 0.8 reduce_sum.18
  257.5 0.6 div.12
  (4 shorter events, 0.0 us)
Async XLA Ops:
  40.6 26.6 %collective-permute-start.1 = (bf16[6912,128]{1,0:T(8,128)(2,1)S(1)}, bf16[6912,128]{1,0:T(8,128)(2,1)S(1)}, u32[]{:S(2)}, u32[]{:S(2)}) collective-permute-start(bf16[6912,128]{1,0:T(8,128)(2,1)S(1)} %bitcast.16), channel_id=1, source_target_pairs={{31,0},{0,1},{1,2},{2,3},{3,4},{4,5},{5,6},{6,7},{7,8},{8,9},{9,10... | collective-permute-start | bytes 5308424 | tf_op jit(solution)/shard_map/ppermute | solution.py:310
  41.0 95.8 %collective-permute-start = (bf16[6912,128]{1,0:T(8,128)(2,1)}, bf16[6912,128]{1,0:T(8,128)(2,1)}, u32[]{:S(2)}, u32[]{:S(2)}) collective-permute-start(bf16[6912,128]{1,0:T(8,128)(2,1)} %bitcast.11), channel_id=1, source_target_pairs={{31,0},{0,1},{1,2},{2,3},{3,4},{4,5},{5,6},{6,7},{7,8},{8,9},{9,10... | collective-permute-start | bytes 5308424 | tf_op jit(solution)/shard_map/ppermute | solution.py:310
  67.2 1.3 copy-start.2
  136.8 70.9 %copy-start.1 = (f32[24,128]{1,0:T(8,128)S(1)}, f32[24,128]{1,0:T(8,128)}, u32[]{:S(2)}) copy-start(f32[24,128]{1,0:T(8,128)} %get-tuple-element.18) | copy-start | bytes 36868
  136.8 105.1 %collective-permute-start.3 = (bf16[6912,128]{1,0:T(8,128)(2,1)}, bf16[6912,128]{1,0:T(8,128)(2,1)S(1)}, u32[]{:S(2)}, u32[]{:S(2)}) collective-permute-start(bf16[6912,128]{1,0:T(8,128)(2,1)} %get-tuple-element.14), channel_id=1, source_target_pairs={{1,0},{2,1},{3,2},{4,3},{5,4},{6,5},{7,6},{8,7},{9,8},{10,9},{11,1... | collective-permute-start | bytes 5308424 | tf_op jit(solution)/shard_map/ppermute | solution.py:310
  205.4 36.6 %collective-permute-start.2 = (bf16[6912,128]{1,0:T(8,128)(2,1)}, bf16[6912,128]{1,0:T(8,128)(2,1)}, u32[]{:S(2)}, u32[]{:S(2)}) collective-permute-start(bf16[6912,128]{1,0:T(8,128)(2,1)} %get-tuple-element.13), channel_id=1, source_target_pairs={{1,0},{2,1},{3,2},{4,3},{5,4},{6,5},{7,6},{8,7},{9,8},{10,9},{11,1... | collective-permute-start | bytes 5308424 | tf_op jit(solution)/shard_map/ppermute | solution.py:310
  209.8 1.2 collective-permute-start.4
  211.6 16.7 %collective-permute-start.5 = (f32[8,128]{1,0:T(8,128)S(1)}, f32[8,128]{1,0:T(8,128)S(1)}, u32[]{:S(2)}, u32[]{:S(2)}) collective-permute-start(f32[8,128]{1,0:T(8,128)S(1)} %broadcast_add_fusion), channel_id=1, source_target_pairs={{2,0},{3,1},{0,2},{1,3},{6,4},{7,5},{4,6},{5,7},{10,8},{11,9},{8,1... | collective-permute-start | bytes 12296 | tf_op jit(solution)/shard_map/ppermute | solution.py:319
  229.0 3.7 %collective-permute-start.6 = (f32[8,128]{1,0:T(8,128)S(1)}, f32[8,128]{1,0:T(8,128)S(1)}, u32[]{:S(2)}, u32[]{:S(2)}) collective-permute-start(f32[8,128]{1,0:T(8,128)S(1)} %fusion), channel_id=1, source_target_pairs={{4,0},{5,1},{6,2},{7,3},{0,4},{1,5},{2,6},{3,7},{12,8},{13,9},{14,... | collective-permute-start | bytes 12296 | tf_op jit(solution)/shard_map/ppermute | solution.py:319
  232.6 3.6 %collective-permute-start.7 = (f32[8,128]{1,0:T(8,128)S(1)}, f32[8,128]{1,0:T(8,128)S(1)}, u32[]{:S(2)}, u32[]{:S(2)}) collective-permute-start(f32[8,128]{1,0:T(8,128)S(1)} %add.21), channel_id=1, source_target_pairs={{8,0},{9,1},{10,2},{11,3},{12,4},{13,5},{14,6},{15,7},{0,8},{1,9},... | collective-permute-start | bytes 12296 | tf_op jit(solution)/shard_map/ppermute | solution.py:319
  236.3 4.5 %collective-permute-start.8 = (f32[8,128]{1,0:T(8,128)S(1)}, f32[8,128]{1,0:T(8,128)S(1)}, u32[]{:S(2)}, u32[]{:S(2)}) collective-permute-start(f32[8,128]{1,0:T(8,128)S(1)} %add.22), channel_id=1, source_target_pairs={{16,0},{17,1},{18,2},{19,3},{20,4},{21,5},{22,6},{23,7},{24,8},{25... | collective-permute-start | bytes 12296 | tf_op jit(solution)/shard_map/ppermute | solution.py:319
  241.9 1.2 copy-start
where the time goes:
time: 260 us; the launch traced here: 259 us
  Pallas kernels  150 us (58%)
  waiting for transfers between devices  51.6 us (20%)
  local copies, waits for them, and re-layouts  44.2 us (17%)
  starting transfers between devices  7.08 us (3%)
  other arithmetic  3.45 us (1%)
    pallas_call x2, Pallas kernels, pair_terms(): pl.pallas_call(pairs_kernel, out_shape=(jax.ShapeDtypeStruct((2 * ROWS, L...  137 us
    slice x1, local copies, waits for them, and re-layouts, per_device(): previous = [from_behind(bands[j], 'band', 1) for j in range(2)]  40 us
    ppermute x5, waiting for transfers between devices, sum_over(): lax.ppermute(value, axis, [(i ^ step, i) for i in range(size)])  28 us
    ppermute x4, waiting for transfers between devices, from_behind(): lax.ppermute(block, axis, [((i - distance) % size, i) for i in range(size)])  23.5 us
    pallas_call x1, Pallas kernels, add_returned(): pl.pallas_call(sum_kernel, grid=(ROWS // BLOCK,), out_shape=(jax.ShapeDty...  13.5 us
    ppermute x4, starting transfers between devices, from_behind(): lax.ppermute(block, axis, [((i - distance) % size, i) for i in range(size)])  5.46 us
  transfers between devices with their start and end apart: 9, of which 6 were waited for; matrix products, arithmetic and copies ran while one was open for 1% of the time, Pallas kernels for 53%

commit v1 on v0

v1 whole, which is shorter than its diff:
```python
import jax
import jax.numpy as jnp
import ml_dtypes
import numpy as np
from jax import lax
from jax.experimental import pallas as pl
from jax.experimental.pallas import tpu as pltpu
from jax.sharding import PartitionSpec as P

G = 96
HALF = G // 2 + 1
NGRID = G * G * G
LANES = 128
ROWS = NGRID // LANES
PLANE = G * G // LANES
QUADS = G // 4
KPAD = HALF + 1
Y_ROWS = 104
Y_PITCH = Y_ROWS + 1
Z_PITCH = G + 1
W_PITCH = 2 * G + 1
F_PITCH = PLANE + 1
WAVE_UNIT = 0.05
SCREEN_SQ = 0.0121
BF16 = jnp.bfloat16
F32 = jnp.float32


def dft_tables():
    n = np.arange(G)
    phases = (n[:, None] * n[None, :]) % G
    angles = phases.astype(np.float32) * np.float32(2.0 * np.pi / G)
    rounded = [f(angles).astype(ml_dtypes.bfloat16).astype(np.float32) for f in (np.cos, np.sin)]
    return rounded[0], rounded[1]


def section_tables():
    c, s = dft_tables()
    h = HALF
    t1 = np.zeros((Y_ROWS, G), np.float32)
    t1[:h] = c[:h]
    t1[h : 2 * h] = -s[:h]
    t2 = np.block([[c, s], [-s, c]])
    t3 = np.zeros((2, 2, LANES, 4, 2, 64), np.float32)
    back = (G - np.arange(h)) % G
    for p in range(2):
        t3[0, p, :G, 0, p, :h] = c[:h].T
        t3[1, p, :G, 0, p, :h] = s[:h].T
        t3[0, p, :G, 1, p, :h] = -s[:h].T
        t3[1, p, :G, 1, p, :h] = c[:h].T
        t3[0, p, :G, 2, p, :h] = c[back].T
        t3[1, p, :G, 2, p, :h] = s[back].T
        t3[0, p, :G, 3, p, :h] = s[back].T
        t3[1, p, :G, 3, p, :h] = -c[back].T
    t3 = t3.reshape(4 * LANES, 4 * LANES)
    order = np.concatenate([np.arange(G // 2), G - 1 - np.arange(G // 2)])
    a1 = np.block([[c[:, order], -s[:, order]], [s[:, order], c[:, order]]])
    rows = np.arange(G).reshape(QUADS, 4).T.reshape(-1)
    a2 = np.block([[c[rows], -s[rows]], [s[rows], c[rows]]])
    weight = np.full((h, 1), 2.0, np.float32)
    weight[0] = weight[h - 1] = 1.0
    a3 = np.zeros((3, 2, 2, 2, 64, 2, LANES), np.float32)
    for third in range(3):
        for lane in range(LANES):
            r, x3 = divmod(third * LANES + lane, G)
            for p in range(2):
                a3[third, r - third, 0, p, :h, p, lane] = weight[:, 0] * c[x3, :h]
                a3[third, r - third, 1, p, :h, p, lane] = -weight[:, 0] * s[x3, :h]
    a3 = a3.reshape(3, 4 * LANES, 2 * LANES)
    sel = np.zeros((2, 2 * LANES, 2 * LANES), np.float32)
    for r in range(4):
        for x in range(G):
            sel[r // 2, r * G + x - (r // 2) * LANES, (r % 2) * LANES + x] = 1.0
    return [t.astype(ml_dtypes.bfloat16) for t in (t1, t2, t3, a1, a2, a3, sel)]


def screening():
    n = np.arange(G)
    m = np.where(n <= G // 2, n, n - G).astype(np.float64)
    sq = m * m
    q2 = WAVE_UNIT * (sq[:HALF, None, None] + sq[None, :, None] + sq[None, None, :HALF])
    safe = np.where(q2 > 0, q2, 1.0)
    kern = 4.0 * np.pi * (1.0 - np.exp(-q2 / (4.0 * SCREEN_SQ))) / safe
    kern = np.where(q2 > 0, kern, np.pi / SCREEN_SQ)
    out = np.zeros((KPAD, G, 2, 64), np.float32)
    out[:HALF, :, :, :HALF] = kern[:, :, None, :]
    return out.reshape(KPAD * G, LANES)


def dot(a, b):
    return jnp.dot(a, b, preferred_element_type=F32)


def lanes(*parts):
    return jnp.concatenate(parts, axis=1)


def stack(*parts):
    return jnp.concatenate(parts, axis=0)


def split_rows(rows, sel_ref):
    first = dot(lanes(rows[0], rows[1]), sel_ref[0])
    second = dot(lanes(rows[1], rows[2]), sel_ref[1])
    return [first[:, :LANES], first[:, LANES:], second[:, :LANES], second[:, LANES:]]


def widen_planes(src, dst):
    @pl.loop(0, G // 2)
    def _(i):
        value = src[pl.ds(pl.multiple_of(i * 2 * PLANE, 16), 2 * PLANE), :].astype(F32)
        dst[pl.ds(2 * i * F_PITCH, PLANE), :] = value[:PLANE]
        dst[pl.ds((2 * i + 1) * F_PITCH, PLANE), :] = value[PLANE:]


def split_kernel(raw_ref, out0, out1, wide):
    wide[...] = raw_ref[...].astype(F32)
    for p, out in enumerate((out0, out1)):
        out[...] = wide[pl.ds(p, out.shape[0], stride=2), :].astype(BF16)


def split_bands(raw, interpret=False):
    rows = 1152
    flat = pl.BlockSpec((rows, LANES), lambda i: (i, 0))
    return pl.pallas_call(
        split_kernel,
        grid=(ROWS // rows,),
        out_shape=(jax.ShapeDtypeStruct((ROWS, LANES), BF16),) * 2,
        in_specs=[pl.BlockSpec((2 * rows, LANES), lambda i: (i, 0))],
        out_specs=(flat, flat),
        scratch_shapes=[pltpu.VMEM((2 * rows, LANES), F32)],
        interpret=interpret,
        name="split_bands",
    )(raw)


def rows_kernel(own0, own1, sel, out, wide):
    for p, own in enumerate((own0, own1)):
        widen_planes(own, wide)

        @pl.loop(0, QUADS)
        def _(q):
            rows = [wide[pl.ds(3 * q + s, G, stride=F_PITCH), :].astype(BF16) for s in range(3)]
            for r, part in enumerate(split_rows(rows, sel)):
                out[p, 4 * q + r] = part.astype(BF16)


def padded_rows(own0, own1, sel, interpret=False):
    vmem = pl.BlockSpec(memory_space=pltpu.VMEM)
    return pl.pallas_call(
        rows_kernel,
        out_shape=jax.ShapeDtypeStruct((2, G, G, LANES), BF16),
        in_specs=[vmem] * 3,
        out_specs=vmem,
        scratch_shapes=[pltpu.VMEM((G * F_PITCH, LANES), F32)],
        compiler_params=pltpu.CompilerParams(vmem_limit_bytes=32 * 1024 * 1024),
        interpret=interpret,
        name="padded_rows",
    )(own0, own1, sel)


def pairs_kernel(
    own0, own1, own_u, par_ref, t1, t2, t3, a1, a2, a3, sel, kern,
    own_out, par_out, energy_out,
    par_f, yw, z, x34, own_f, staged,
):
    widen_planes(par_ref, par_f)
    half_y = G * Y_PITCH

    @pl.loop(0, QUADS)
    def _(q):
        rows = [par_f[pl.ds(3 * q + s, G, stride=F_PITCH), :].astype(BF16) for s in range(3)]
        for r, part in enumerate(split_rows(rows, sel)):
            b = 4 * q + r
            density = [(own_u[p, b].astype(F32) * part).astype(BF16) for p in range(2)]
            y = dot(t1[...], lanes(*density))
            for p in range(2):
                yw[pl.ds(p * half_y + b * Y_PITCH, Y_ROWS), :] = y[:, p * LANES : (p + 1) * LANES]

    @pl.loop(0, HALF, unroll=7)
    def _(k1):
        def line(p, part):
            return yw[pl.ds(p * half_y + part * HALF + k1, G, stride=Y_PITCH), :].astype(BF16)

        out = dot(t2[...], stack(lanes(line(0, 0), line(1, 0)), lanes(line(0, 1), line(1, 1))))
        at = pl.ds(pl.multiple_of(k1 * G, 16), G)
        x34[at, : 2 * LANES] = out[:G].astype(BF16)
        x34[at, 2 * LANES :] = out[G:].astype(BF16)

    @pl.loop(0, KPAD // 2)
    def _(m):
        at = pl.ds(pl.multiple_of(m * 2 * G, 16), 2 * G)
        field = x34[at, :]
        factor = kern[at, :]
        for h in range(2):
            out = dot(field, t3[:, 2 * h * LANES : 2 * (h + 1) * LANES])
            for e in range(2):
                spectrum = out[:, e * LANES : (e + 1) * LANES].astype(BF16).astype(F32)
                value = spectrum * factor
                for i in range(2):
                    row = (2 * m + i) * Z_PITCH
                    z[2 * h + e, pl.ds(row, G), :] = value[i * G : (i + 1) * G]

    @pl.loop(0, G // 2, unroll=2)
    def _(pair):
        parts = []
        for e in range(2):
            k2 = 2 * pair + e
            mirror = Z_PITCH + jnp.where(k2 == 0, 0, G - k2)
            parts.append(
                stack(
                    z[0, pl.ds(k2, G // 2, stride=Z_PITCH), :].astype(BF16),
                    z[2, pl.ds(mirror, G // 2, stride=Z_PITCH), :].astype(BF16),
                    z[1, pl.ds(k2, G // 2, stride=Z_PITCH), :].astype(BF16),
                    z[3, pl.ds(mirror, G // 2, stride=Z_PITCH), :].astype(BF16),
                )
            )
        out = dot(a1[...], lanes(*parts))
        for e in range(2):
            at = (2 * pair + e) * W_PITCH
            yw[pl.ds(at, 2 * G), :] = out[:, e * LANES : (e + 1) * LANES]

    @pl.loop(0, G // 2, unroll=2)
    def _(pair):
        parts = []
        for e in range(2):
            x1 = 2 * pair + e
            parts.append(
                stack(
                    yw[pl.ds(x1, G, stride=W_PITCH), :].astype(BF16),
                    yw[pl.ds(G + x1, G, stride=W_PITCH), :].astype(BF16),
                )
            )
        out = dot(a2[...], lanes(*parts))
        for r in range(4):
            block = [
                lanes(
                    out[r * QUADS : (r + 1) * QUADS, e * LANES : (e + 1) * LANES],
                    out[G + r * QUADS : G + (r + 1) * QUADS, e * LANES : (e + 1) * LANES],
                )
                for e in range(2)
            ]
            at = pl.multiple_of((r // 2) * G * QUADS + pair * 2 * QUADS, 16)
            left = (r % 2) * 2 * LANES
            x34[pl.ds(at, 2 * QUADS), left : left + 2 * LANES] = stack(*block).astype(BF16)

    energy_out[...] = jnp.zeros_like(energy_out)
    planes = 8
    block_rows = planes * QUADS
    scale = F32(1.0 / NGRID)

    @pl.loop(0, G // planes)
    def _(ch):
        at = pl.multiple_of(ch * block_rows, 16)
        low = x34[pl.ds(at, block_rows), :]
        high = x34[pl.ds(G * QUADS + at, block_rows), :]
        fields = [low, lanes(low[:, 2 * LANES :], high[:, : 2 * LANES]), high]
        flat = pl.ds(pl.multiple_of(ch * planes * PLANE, 16), planes * PLANE)
        own_f[0] = own0[flat, :].astype(F32)
        own_f[1] = own1[flat, :].astype(F32)
        total = jnp.zeros((QUADS, LANES), F32)
        for third in range(3):
            out = dot(fields[third], a3[third]) * scale
            for i in range(planes):
                plane = ch * planes + i
                partner = par_f[pl.ds(plane * F_PITCH + third, QUADS, stride=3), :]
                here = pl.ds(i * PLANE + third, QUADS, stride=3)
                there = pl.ds(plane * PLANE + third, QUADS, stride=3)
                sent = jnp.zeros((QUADS, LANES), F32)
                for p in range(2):
                    potential = out[i * QUADS : (i + 1) * QUADS, p * LANES : (p + 1) * LANES]
                    own_out[p, there, :] = potential * partner
                    sent = sent + potential * own_f[p, here, :]
                total = total + sent * partner
                staged[here, :] = sent
        energy_out[...] += total
        par_out[flat, :] = staged[...].astype(BF16)


def pair_terms(own0, own1, own_u, partner, tables, kern, interpret=False):
    vmem = pl.BlockSpec(memory_space=pltpu.VMEM)
    return pl.pallas_call(
        pairs_kernel,
        out_shape=(
            jax.ShapeDtypeStruct((2, ROWS, LANES), F32),
            jax.ShapeDtypeStruct((ROWS, LANES), BF16),
            jax.ShapeDtypeStruct((QUADS, LANES), F32),
        ),
        in_specs=[vmem] * 12,
        out_specs=(vmem, vmem, vmem),
        scratch_shapes=[
            pltpu.VMEM((G * F_PITCH, LANES), F32),
            pltpu.VMEM((2 * G * Y_PITCH, LANES), F32),
            pltpu.VMEM((4, KPAD * Z_PITCH, LANES), F32),
            pltpu.VMEM((KPAD * G, 4 * LANES), BF16),
            pltpu.VMEM((2, 8 * PLANE, LANES), F32),
            pltpu.VMEM((8 * PLANE, LANES), F32),
        ],
        compiler_params=pltpu.CompilerParams(vmem_limit_bytes=62 * 1024 * 1024),
        cost_estimate=pl.CostEstimate(
            flops=20_000_000_000, bytes_accessed=20_000_000, transcendentals=0
        ),
        interpret=interpret,
        name="pair_terms",
    )(own0, own1, own_u, partner, *tables, kern)


BLOCK = 1152


def first_sum_kernel(own0, own1, first, second, back0, exch0, part1, gram_ref):
    @pl.when(pl.program_id(0) == 0)
    def _():
        gram_ref[...] = jnp.zeros_like(gram_ref)

    exchange = first[0] + second[0] + back0[...].astype(F32)
    exch0[...] = exchange
    part1[...] = first[1] + second[1]
    for i, own in enumerate((own0, own1)):
        gram_ref[i] += jnp.sum((own[...].astype(F32) * exchange).reshape(-1, 8, LANES), axis=0)


def first_sum(own, first, second, back0, interpret=False):
    flat = pl.BlockSpec((BLOCK, LANES), lambda i: (i, 0))
    both = pl.BlockSpec((2, BLOCK, LANES), lambda i: (0, i, 0))
    return pl.pallas_call(
        first_sum_kernel,
        grid=(ROWS // BLOCK,),
        out_shape=(
            jax.ShapeDtypeStruct((ROWS, LANES), F32),
            jax.ShapeDtypeStruct((ROWS, LANES), F32),
            jax.ShapeDtypeStruct((2, 8, LANES), F32),
        ),
        in_specs=[flat, flat, both, both, flat],
        out_specs=(flat, flat, pl.BlockSpec((2, 8, LANES), lambda i: (0, 0, 0))),
        compiler_params=pltpu.CompilerParams(vmem_limit_bytes=32 * 1024 * 1024),
        interpret=interpret,
        name="first_sum",
    )(*own, first, second, back0)


def last_sum_kernel(own0, own1, exch0, part1, back1, out_ref, gram_ref):
    @pl.when(pl.program_id(0) == 0)
    def _():
        gram_ref[...] = jnp.zeros_like(gram_ref)

    exchange = part1[...] + back1[...].astype(F32)
    out_ref[pl.ds(0, BLOCK, stride=2), :] = exch0[...]
    out_ref[pl.ds(1, BLOCK, stride=2), :] = exchange
    for i, own in enumerate((own0, own1)):
        gram_ref[i] += jnp.sum((own[...].astype(F32) * exchange).reshape(-1, 8, LANES), axis=0)


def last_sum(own, exch0, part1, back1, interpret=False):
    flat = pl.BlockSpec((BLOCK, LANES), lambda i: (i, 0))
    return pl.pallas_call(
        last_sum_kernel,
        grid=(ROWS // BLOCK,),
        out_shape=(
            jax.ShapeDtypeStruct((2 * ROWS, LANES), F32),
            jax.ShapeDtypeStruct((2, 8, LANES), F32),
        ),
        in_specs=[flat] * 5,
        out_specs=(
            pl.BlockSpec((2 * BLOCK, LANES), lambda i: (i, 0)),
            pl.BlockSpec((2, 8, LANES), lambda i: (0, 0, 0)),
        ),
        compiler_params=pltpu.CompilerParams(vmem_limit_bytes=32 * 1024 * 1024),
        interpret=interpret,
        name="last_sum",
    )(*own, exch0, part1, back1)


def from_behind(block, axis, distance):
    size = lax.axis_size(axis)
    return lax.ppermute(block, axis, [((i - distance) % size, i) for i in range(size)])


def sum_over(value, axis):
    size = lax.axis_size(axis)
    if size & (size - 1):
        return lax.psum(value, axis)
    steps = [1 << bit for bit in range(size.bit_length() - 1)]
    for step in [s for s in steps if s != 2] + [s for s in steps if s == 2]:
        value = value + lax.ppermute(value, axis, [(i ^ step, i) for i in range(size)])
    return value


def per_device(orbitals):
    tables = section_tables()
    kern = screening()
    raw = orbitals.reshape(2, ROWS, LANES).transpose(1, 0, 2).reshape(2 * ROWS, LANES)
    own = split_bands(raw)
    previous = [from_behind(own[j], "band", 1) for j in range(2)]
    own_u = padded_rows(*own, tables[-1])
    first, sent0, energy0 = pair_terms(*own, own_u, previous[0], tables, kern)
    back0 = from_behind(sent0, "band", -1)
    second, sent1, energy1 = pair_terms(*own, own_u, previous[1], tables, kern)
    back1 = from_behind(sent1, "band", -1)
    pair_energy = jnp.sum(energy0 + energy1).reshape(1, 1)
    total = sum_over(jnp.broadcast_to(pair_energy, (8, LANES)), "band")[0, 0]
    energy = -2.0 * total / F32(NGRID) / F32(2 * lax.axis_size("band") * orbitals.shape[0])
    exch0, part1, gram0 = first_sum(own, first, second, back0)
    exchange, gram1 = last_sum(own, exch0, part1, back1)
    gram = jnp.stack([jnp.sum(g, axis=(1, 2)) for g in (gram0, gram1)], axis=1) / F32(NGRID)
    exchange = exchange.reshape(ROWS, 2, LANES).transpose(1, 0, 2).reshape(2, NGRID)
    return exchange, gram, energy


def solution(mesh):
    return jax.shard_map(
        per_device,
        mesh=mesh,
        in_specs=(P("band", None),),
        out_specs=(P("band", None), P("band", None), P()),
        check_vma=False,
    )
```

time: 260 us -> 166 us (0.64)
  Pallas kernels: 150 us -> 109 us
  local copies, waits for them, and re-layouts: 44.2 us -> 11.4 us
  waiting for transfers between devices: 51.6 us -> 32.7 us
    pallas_call x3 -> x6, Pallas kernels: 150 us -> 109 us  [the longest x2 84.4 us: pair_terms(): pl.pallas_call(pairs_kernel, out_shape=(jax.ShapeDtypeStruct((2, ROWS, LA...]
    slice x1 -> x0, local copies, waits for them, and re-layouts: 40 us -> none  [per_device(): previous = [from_behind(bands[j], 'band', 1) for j in range(2)]]
    ppermute x4, waiting for transfers between devices: 23.5 us -> 9.09 us  [from_behind(): lax.ppermute(block, axis, [((i - distance) % size, i) for i in range(size)])]
    unnamed x6 -> x17, local copies, waits for them, and re-layouts: 2.48 us -> 10.3 us
    ppermute x5, waiting for transfers between devices: 28 us -> 23.6 us  [sum_over(): lax.ppermute(value, axis, [(i ^ step, i) for i in range(size)])]
  transfers between devices with their start and end apart: 9 -> 9, of which waited for: 6 -> 6; matrix products, arithmetic and copies ran while one was open for 1% -> 2% of each run, Pallas kernels for 53% -> 60%
where the time goes in v1:
time: 166 us
  Pallas kernels  109 us (66%)
  waiting for transfers between devices  32.7 us (20%)
  local copies, waits for them, and re-layouts  11.4 us (7%)
  starting transfers between devices  7.03 us (4%)
  other arithmetic  2.83 us (2%)
  between operations  2.56 us (2%)
    pallas_call x2, Pallas kernels, pair_terms(): pl.pallas_call(pairs_kernel, out_shape=(jax.ShapeDtypeStruct((2, ROWS, LA...  84.4 us
    ppermute x5, waiting for transfers between devices, sum_over(): lax.ppermute(value, axis, [(i ^ step, i) for i in range(size)])  23.6 us
    unnamed x17, local copies, waits for them, and re-layouts  10.3 us
    pallas_call x1, Pallas kernels, padded_rows(): pl.pallas_call(rows_kernel, out_shape=jax.ShapeDtypeStruct((2, G, G, LANE...  9.6 us
    ppermute x4, waiting for transfers between devices, from_behind(): lax.ppermute(block, axis, [((i - distance) % size, i) for i in range(size)])  9.09 us
    pallas_call x1, Pallas kernels, split_bands(): pl.pallas_call(split_kernel, grid=(ROWS // rows,), out_shape=(jax.ShapeDt...  5.82 us
    pallas_call x1, Pallas kernels, first_sum(): pl.pallas_call(first_sum_kernel, grid=(ROWS // BLOCK,), out_shape=(jax.Sh...  5.58 us
    ppermute x4, starting transfers between devices, from_behind(): lax.ppermute(block, axis, [((i - distance) % size, i) for i in range(size)])  5.34 us
  transfers between devices with their start and end apart: 9, of which 6 were waited for; matrix products, arithmetic and copies ran while one was open for 2% of the time, Pallas kernels for 60%

profile of v1, /device:TPU:0, one launch (start us, length us, event | category | flops | bytes accessed | tf_op | source)
XLA Modules:
  0.0 165.9 jit_solution(17418269116725063344)
XLA Ops:
  0.6 0.0 copy-start.6
  0.6 5.8 %split_bands.1 = (bf16[6912,128]{1,0:T(8,128)(2,1)}, bf16[6912,128]{1,0:T(8,128)(2,1)}) custom-call(bf16[13824,128]{1,0:T(8,128)(2,1)} %bitcast.13), custom_call_target="tpu_custom_call" | custom-call | tf_op jit(solution)/shard_map/split_bands/pallas_call | solution.py:125
  6.5 0.5 collective-permute-start
  6.9 2.6 %collective-permute-start.1 = (bf16[6912,128]{1,0:T(8,128)(2,1)}, bf16[6912,128]{1,0:T(8,128)(2,1)}, u32[]{:S(2)}, u32[]{:S(2)}) collective-permute-start(bf16[6912,128]{1,0:T(8,128)(2,1)} %get-tuple-element.17.own1), channel_id=1, source_target_pairs={{31,0},{0,1},{1,2},{2,3},{3,4},{4,5},{5,6},{6,7},{7,8},{8,9},{9,10... | collective-permute-start | bytes 5308424 | tf_op jit(solution)/shard_map/ppermute | solution.py:376
  9.5 0.0 copy-done.6
  9.5 0.0 copy-start
  9.5 1.5 copy-done
  11.0 0.0 copy-start.2
  11.0 1.5 copy-done.2
  12.5 9.6 %padded_rows.1.own_u = bf16[2,96,96,128]{3,2,1,0:T(8,128)(2,1)S(1)} custom-call(bf16[6912,128]{1,0:T(8,128)(2,1)S(1)} %copy-done, bf16[6912,128]{1,0:T(8,128)(2,1)S(1)} %copy-done.2, bf16[2,256,256]{2,1,0:T(8,128)(2,1)S(1)} %copy-done.6), custom_call_target="tpu_custom_call" | custom-call | tf_op jit(solution)/shard_map/padded_rows/pallas_call | solution.py:150
  22.1 0.0 copy-start.5
  22.1 2.2 %copy-done.5 = bf16[2,96,96,128]{3,2,1,0:T(8,128)(2,1)} copy-done((bf16[2,96,96,128]{3,2,1,0:T(8,128)(2,1)}, bf16[2,96,96,128]{3,2,1,0:T(8,128)(2,1)S(1)}, u32[]{:S(2)}) %copy-start.5) | copy-done | bytes 4718616
  24.3 9.1 %collective-permute-done.par_ref = bf16[6912,128]{1,0:T(8,128)(2,1)} collective-permute-done((bf16[6912,128]{1,0:T(8,128)(2,1)}, bf16[6912,128]{1,0:T(8,128)(2,1)}, u32[]{:S(2)}, u32[]{:S(2)}) %collective-permute-start) | collective-permute-done | bytes 1769504 | tf_op jit(solution)/shard_map/ppermute | solution.py:376
  33.4 42.2 %pair_terms.2 = (f32[2,6912,128]{2,1,0:T(8,128)}, bf16[6912,128]{1,0:T(8,128)(2,1)}, f32[24,128]{1,0:T(8,128)}) custom-call(bf16[6912,128]{1,0:T(8,128)(2,1)} %get-tuple-element.16.own0, bf16[6912,128]{1,0:T(8,128)(2,1)} %get-tuple-element.17.own1, bf16[2,96,96,128]{3,2,1,0:T(8,128)(2,1)} %copy-done.5, bf16[6912,128]{1,0:T(8,128)(2,1)} %collective-permute-done.par_ref, ...), custom_call_target="tpu_custom_call" | custom-call | flops 20000000000 | bytes 20000000 | tf_op jit(solution)/shard_map/pair_terms/pallas_call | solution.py:282
  75.5 0.0 copy-start.7
  75.5 0.0 copy-start.1
  75.5 0.1 collective-permute-start.2
  75.6 0.0 collective-permute-done.1.par_ref
  75.6 42.2 %pair_terms.3 = (f32[2,6912,128]{2,1,0:T(8,128)}, bf16[6912,128]{1,0:T(8,128)(2,1)}, f32[24,128]{1,0:T(8,128)}) custom-call(bf16[6912,128]{1,0:T(8,128)(2,1)} %get-tuple-element.16.own0, bf16[6912,128]{1,0:T(8,128)(2,1)} %get-tuple-element.17.own1, bf16[2,96,96,128]{3,2,1,0:T(8,128)(2,1)} %copy-done.5, bf16[6912,128]{1,0:T(8,128)(2,1)} %collective-permute-done.1.par_ref, ...), custom_call_target="tpu_custom_call" | custom-call | flops 20000000000 | bytes 20000000 | tf_op jit(solution)/shard_map/pair_terms/pallas_call | solution.py:282
  117.8 2.2 %collective-permute-start.3 = (bf16[6912,128]{1,0:T(8,128)(2,1)}, bf16[6912,128]{1,0:T(8,128)(2,1)S(1)}, u32[]{:S(2)}, u32[]{:S(2)}) collective-permute-start(bf16[6912,128]{1,0:T(8,128)(2,1)} %get-tuple-element.23), channel_id=1, source_target_pairs={{1,0},{2,1},{3,2},{4,3},{5,4},{6,5},{7,6},{8,7},{9,8},{10,9},{11,1... | collective-permute-start | bytes 5308424 | tf_op jit(solution)/shard_map/ppermute | solution.py:376
  120.0 0.0 copy-done.7
  120.0 1.3 add_reduce_fusion
  121.3 0.6 broadcast_in_dim.2
  122.0 0.1 collective-permute-start.4
  122.1 1.2 collective-permute-done.4
  123.2 0.6 broadcast_add_fusion
  123.9 0.1 collective-permute-start.5
  124.0 3.6 %collective-permute-done.5 = f32[8,128]{1,0:T(8,128)S(1)} collective-permute-done((f32[8,128]{1,0:T(8,128)S(1)}, f32[8,128]{1,0:T(8,128)S(1)}, u32[]{:S(2)}, u32[]{:S(2)}) %collective-permute-start.5) | collective-permute-done | bytes 4128 | tf_op jit(solution)/shard_map/ppermute | solution.py:385
  127.6 0.6 fusion
  128.2 0.1 collective-permute-start.6
  128.3 12.2 %collective-permute-done.6 = f32[8,128]{1,0:T(8,128)S(1)} collective-permute-done((f32[8,128]{1,0:T(8,128)S(1)}, f32[8,128]{1,0:T(8,128)S(1)}, u32[]{:S(2)}, u32[]{:S(2)}) %collective-permute-start.6) | collective-permute-done | bytes 4128 | tf_op jit(solution)/shard_map/ppermute | solution.py:385
  140.5 1.5 collective-permute-start.7
  141.9 3.0 %collective-permute-done.7 = f32[8,128]{1,0:T(8,128)S(1)} collective-permute-done((f32[8,128]{1,0:T(8,128)S(1)}, f32[8,128]{1,0:T(8,128)S(1)}, u32[]{:S(2)}, u32[]{:S(2)}) %collective-permute-start.7) | collective-permute-done | bytes 4128 | tf_op jit(solution)/shard_map/ppermute | solution.py:385
  145.0 0.0 collective-permute-start.8
  145.0 3.6 %collective-permute-done.8 = f32[8,128]{1,0:T(8,128)S(1)} collective-permute-done((f32[8,128]{1,0:T(8,128)S(1)}, f32[8,128]{1,0:T(8,128)S(1)}, u32[]{:S(2)}, u32[]{:S(2)}) %collective-permute-start.8) | collective-permute-done | bytes 4128 | tf_op jit(solution)/shard_map/ppermute | solution.py:385
  148.6 0.5 slice.3
  149.8 0.0 collective-permute-done.2.back0
  149.8 0.0 copy-done.1
  149.8 0.0 copy-start.3
  149.8 1.5 copy-done.3
  151.3 0.0 copy-start.4
  151.3 3.0 %copy-done.4 = f32[2,6912,128]{2,1,0:T(8,128)S(1)} copy-done((f32[2,6912,128]{2,1,0:T(8,128)S(1)}, f32[2,6912,128]{2,1,0:T(8,128)}, u32[]{:S(2)}) %copy-start.4) | copy-done | bytes 7077912
  154.3 5.6 %first_sum.1 = (f32[6912,128]{1,0:T(8,128)S(1)}, f32[6912,128]{1,0:T(8,128)S(1)}, f32[2,8,128]{2,1,0:T(8,128)S(1)}) custom-call(bf16[6912,128]{1,0:T(8,128)(2,1)S(1)} %copy-done.1, bf16[6912,128]{1,0:T(8,128)(2,1)S(1)} %copy-done.3, f32[2,6912,128]{2,1,0:T(8,128)S(1)} %copy-done.4, f32[2,6912,128]{2,1,0:T(8,128)} %get-tuple-element.19.second, ...), custom_call_target="tpu_custom_call" | custom-call | tf_op jit(solution)/shard_map/first_sum/pallas_call | solution.py:326
  159.9 0.0 collective-permute-done.3.back1
  159.9 4.1 %last_sum.1 = (f32[13824,128]{1,0:T(8,128)}, f32[2,8,128]{2,1,0:T(8,128)S(1)}) custom-call(bf16[6912,128]{1,0:T(8,128)(2,1)S(1)} %copy-done.1, bf16[6912,128]{1,0:T(8,128)(2,1)S(1)} %copy-done.3, f32[6912,128]{1,0:T(8,128)S(1)} %get-tuple-element.21.exch0, f32[6912,128]{1,0:T(8,128)S(1)} %get-tuple-element.22.part1, ...), custom_call_target="tpu_custom_call" | custom-call | tf_op jit(solution)/shard_map/last_sum/pallas_call | solution.py:356
  163.9 0.1 reduce_sum.28
  164.0 0.1 reduce_sum.27
  164.1 0.7 copy.14
  (4 shorter events, 0.0 us)
Async XLA Ops:
  0.6 8.9 %copy-start.6 = (bf16[2,256,256]{2,1,0:T(8,128)(2,1)S(1)}, bf16[2,256,256]{2,1,0:T(8,128)(2,1)}, u32[]{:S(2)}) copy-start(bf16[2,256,256]{2,1,0:T(8,128)(2,1)} %constant.30.clone.sel) | copy-start | bytes 786436
  6.5 26.9 %collective-permute-start = (bf16[6912,128]{1,0:T(8,128)(2,1)}, bf16[6912,128]{1,0:T(8,128)(2,1)}, u32[]{:S(2)}, u32[]{:S(2)}) collective-permute-start(bf16[6912,128]{1,0:T(8,128)(2,1)} %get-tuple-element.16.own0), channel_id=1, source_target_pairs={{31,0},{0,1},{1,2},{2,3},{3,4},{4,5},{5,6},{6,7},{7,8},{8,9},{9,10... | collective-permute-start | bytes 5308424 | tf_op jit(solution)/shard_map/ppermute | solution.py:376
  6.9 68.7 %collective-permute-start.1 = (bf16[6912,128]{1,0:T(8,128)(2,1)}, bf16[6912,128]{1,0:T(8,128)(2,1)}, u32[]{:S(2)}, u32[]{:S(2)}) collective-permute-start(bf16[6912,128]{1,0:T(8,128)(2,1)} %get-tuple-element.17.own1), channel_id=1, source_target_pairs={{31,0},{0,1},{1,2},{2,3},{3,4},{4,5},{5,6},{6,7},{7,8},{8,9},{9,10... | collective-permute-start | bytes 5308424 | tf_op jit(solution)/shard_map/ppermute | solution.py:376
  9.5 1.5 copy-start
  11.0 1.5 copy-start.2
  22.1 2.2 %copy-start.5 = (bf16[2,96,96,128]{3,2,1,0:T(8,128)(2,1)}, bf16[2,96,96,128]{3,2,1,0:T(8,128)(2,1)S(1)}, u32[]{:S(2)}) copy-start(bf16[2,96,96,128]{3,2,1,0:T(8,128)(2,1)S(1)} %padded_rows.1.own_u) | copy-start | bytes 14155780
  75.5 44.5 %copy-start.7 = (f32[24,128]{1,0:T(8,128)S(1)}, f32[24,128]{1,0:T(8,128)}, u32[]{:S(2)}) copy-start(f32[24,128]{1,0:T(8,128)} %get-tuple-element.27) | copy-start | bytes 36868
  75.5 74.3 %copy-start.1 = (bf16[6912,128]{1,0:T(8,128)(2,1)S(1)}, bf16[6912,128]{1,0:T(8,128)(2,1)}, u32[]{:S(2)}) copy-start(bf16[6912,128]{1,0:T(8,128)(2,1)} %get-tuple-element.16.own0) | copy-start | bytes 5308420
  75.5 74.3 %collective-permute-start.2 = (bf16[6912,128]{1,0:T(8,128)(2,1)}, bf16[6912,128]{1,0:T(8,128)(2,1)}, u32[]{:S(2)}, u32[]{:S(2)}) collective-permute-start(bf16[6912,128]{1,0:T(8,128)(2,1)} %get-tuple-element.20), channel_id=1, source_target_pairs={{1,0},{2,1},{3,2},{4,3},{5,4},{6,5},{7,6},{8,7},{9,8},{10,9},{11,1... | collective-permute-start | bytes 5308424 | tf_op jit(solution)/shard_map/ppermute | solution.py:376
  117.8 42.1 %collective-permute-start.3 = (bf16[6912,128]{1,0:T(8,128)(2,1)}, bf16[6912,128]{1,0:T(8,128)(2,1)S(1)}, u32[]{:S(2)}, u32[]{:S(2)}) collective-permute-start(bf16[6912,128]{1,0:T(8,128)(2,1)} %get-tuple-element.23), channel_id=1, source_target_pairs={{1,0},{2,1},{3,2},{4,3},{5,4},{6,5},{7,6},{8,7},{9,8},{10,9},{11,1... | collective-permute-start | bytes 5308424 | tf_op jit(solution)/shard_map/ppermute | solution.py:376
  122.0 1.2 collective-permute-start.4
  123.9 3.7 %collective-permute-start.5 = (f32[8,128]{1,0:T(8,128)S(1)}, f32[8,128]{1,0:T(8,128)S(1)}, u32[]{:S(2)}, u32[]{:S(2)}) collective-permute-start(f32[8,128]{1,0:T(8,128)S(1)} %broadcast_add_fusion), channel_id=1, source_target_pairs={{4,0},{5,1},{6,2},{7,3},{0,4},{1,5},{2,6},{3,7},{12,8},{13,9},{14,... | collective-permute-start | bytes 12296 | tf_op jit(solution)/shard_map/ppermute | solution.py:385
  128.2 12.3 %collective-permute-start.6 = (f32[8,128]{1,0:T(8,128)S(1)}, f32[8,128]{1,0:T(8,128)S(1)}, u32[]{:S(2)}, u32[]{:S(2)}) collective-permute-start(f32[8,128]{1,0:T(8,128)S(1)} %fusion), channel_id=1, source_target_pairs={{8,0},{9,1},{10,2},{11,3},{12,4},{13,5},{14,6},{15,7},{0,8},{1,9},... | collective-permute-start | bytes 12296 | tf_op jit(solution)/shard_map/ppermute | solution.py:385
  140.5 4.5 %collective-permute-start.7 = (f32[8,128]{1,0:T(8,128)S(1)}, f32[8,128]{1,0:T(8,128)S(1)}, u32[]{:S(2)}, u32[]{:S(2)}) collective-permute-start(f32[8,128]{1,0:T(8,128)S(1)} %add.21), channel_id=1, source_target_pairs={{16,0},{17,1},{18,2},{19,3},{20,4},{21,5},{22,6},{23,7},{24,8},{25... | collective-permute-start | bytes 12296 | tf_op jit(solution)/shard_map/ppermute | solution.py:385
  145.0 3.6 %collective-permute-start.8 = (f32[8,128]{1,0:T(8,128)S(1)}, f32[8,128]{1,0:T(8,128)S(1)}, u32[]{:S(2)}, u32[]{:S(2)}) collective-permute-start(f32[8,128]{1,0:T(8,128)S(1)} %add.22), channel_id=1, source_target_pairs={{2,0},{3,1},{0,2},{1,3},{6,4},{7,5},{4,6},{5,7},{10,8},{11,9},{8,1... | collective-permute-start | bytes 12296 | tf_op jit(solution)/shard_map/ppermute | solution.py:385
  149.8 1.5 copy-start.3
  151.3 3.0 %copy-start.4 = (f32[2,6912,128]{2,1,0:T(8,128)S(1)}, f32[2,6912,128]{2,1,0:T(8,128)}, u32[]{:S(2)}) copy-start(f32[2,6912,128]{2,1,0:T(8,128)} %get-tuple-element.18.first) | copy-start | bytes 21233668

commit v2 on v1

--- a/solution.py
+++ b/solution.py
@@ -1,3 +1,5 @@
+import functools
+
 import jax
 import jax.numpy as jnp
 import ml_dtypes
@@ -41,18 +43,17 @@
     t1[:h] = c[:h]
     t1[h : 2 * h] = -s[:h]
     t2 = np.block([[c, s], [-s, c]])
-    t3 = np.zeros((2, 2, LANES, 4, 2, 64), np.float32)
+    t3 = np.zeros((2, LANES, 4, 64), np.float32)
     back = (G - np.arange(h)) % G
-    for p in range(2):
-        t3[0, p, :G, 0, p, :h] = c[:h].T
-        t3[1, p, :G, 0, p, :h] = s[:h].T
-        t3[0, p, :G, 1, p, :h] = -s[:h].T
-        t3[1, p, :G, 1, p, :h] = c[:h].T
-        t3[0, p, :G, 2, p, :h] = c[back].T
-        t3[1, p, :G, 2, p, :h] = s[back].T
-        t3[0, p, :G, 3, p, :h] = s[back].T
-        t3[1, p, :G, 3, p, :h] = -c[back].T
-    t3 = t3.reshape(4 * LANES, 4 * LANES)
+    t3[0, :G, 0, :h] = c[:h].T
+    t3[1, :G, 0, :h] = s[:h].T
+    t3[0, :G, 1, :h] = -s[:h].T
+    t3[1, :G, 1, :h] = c[:h].T
+    t3[0, :G, 2, :h] = c[back].T
+    t3[1, :G, 2, :h] = s[back].T
+    t3[0, :G, 3, :h] = s[back].T
+    t3[1, :G, 3, :h] = -c[back].T
+    t3 = t3.reshape(2 * LANES, 4 * 64)
     order = np.concatenate([np.arange(G // 2), G - 1 - np.arange(G // 2)])
     a1 = np.block([[c[:, order], -s[:, order]], [s[:, order], c[:, order]]])
     rows = np.arange(G).reshape(QUADS, 4).T.reshape(-1)
@@ -113,24 +114,23 @@
         dst[pl.ds((2 * i + 1) * F_PITCH, PLANE), :] = value[PLANE:]
 
 
-def split_kernel(raw_ref, out0, out1, wide):
+def band_kernel(p, raw_ref, out, wide):
     wide[...] = raw_ref[...].astype(F32)
-    for p, out in enumerate((out0, out1)):
-        out[...] = wide[pl.ds(p, out.shape[0], stride=2), :].astype(BF16)
-
-
-def split_bands(raw, interpret=False):
+    out[...] = wide[pl.ds(p, out.shape[0], stride=2), :].astype(BF16)
+
+
+def take_band(raw, p, interpret=False):
     rows = 1152
-    flat = pl.BlockSpec((rows, LANES), lambda i: (i, 0))
     return pl.pallas_call(
-        split_kernel,
+        functools.partial(band_kernel, p),
         grid=(ROWS // rows,),
-        out_shape=(jax.ShapeDtypeStruct((ROWS, LANES), BF16),) * 2,
+        out_shape=jax.ShapeDtypeStruct((ROWS, LANES), BF16),
         in_specs=[pl.BlockSpec((2 * rows, LANES), lambda i: (i, 0))],
-        out_specs=(flat, flat),
+        out_specs=pl.BlockSpec((rows, LANES), lambda i: (i, 0)),
         scratch_shapes=[pltpu.VMEM((2 * rows, LANES), F32)],
+        compiler_params=pltpu.CompilerParams(vmem_limit_bytes=62 * 1024 * 1024),
         interpret=interpret,
-        name="split_bands",
+        name="take_band",
     )(raw)
 
 
@@ -153,29 +153,49 @@
         in_specs=[vmem] * 3,
         out_specs=vmem,
         scratch_shapes=[pltpu.VMEM((G * F_PITCH, LANES), F32)],
-        compiler_params=pltpu.CompilerParams(vmem_limit_bytes=32 * 1024 * 1024),
+        compiler_params=pltpu.CompilerParams(vmem_limit_bytes=62 * 1024 * 1024),
         interpret=interpret,
         name="padded_rows",
     )(own0, own1, sel)
 
 
 def pairs_kernel(
-    own0, own1, own_u, par_ref, t1, t2, t3, a1, a2, a3, sel, kern,
+    own0, own1, own_u, kern, par_ref, t1, t2, t3, a1, a2, a3, sel,
     own_out, par_out, energy_out,
-    par_f, yw, z, x34, own_f, staged,
+    own_v, own_uv, kern_v, own_ov, par_ov, par_f, par_u, yw, z, x34, own_f, staged, sems,
 ):
+    loads = [
+        pltpu.make_async_copy(own_u, own_uv, sems.at[0]),
+        pltpu.make_async_copy(kern, kern_v, sems.at[1]),
+        pltpu.make_async_copy(own0, own_v.at[0], sems.at[2]),
+        pltpu.make_async_copy(own1, own_v.at[1], sems.at[3]),
+    ]
+    for load in loads:
+        load.start()
+
     widen_planes(par_ref, par_f)
-    half_y = G * Y_PITCH
-
-    @pl.loop(0, QUADS)
+
+    @pl.loop(0, QUADS, unroll=4)
     def _(q):
         rows = [par_f[pl.ds(3 * q + s, G, stride=F_PITCH), :].astype(BF16) for s in range(3)]
         for r, part in enumerate(split_rows(rows, sel)):
-            b = 4 * q + r
-            density = [(own_u[p, b].astype(F32) * part).astype(BF16) for p in range(2)]
-            y = dot(t1[...], lanes(*density))
+            par_u[4 * q + r] = part.astype(BF16)
+
+    half_y = G * Y_PITCH
+    loads[0].wait()
+
+    @pl.loop(0, G // 2, unroll=4)
+    def _(i):
+        density = []
+        for e in range(2):
+            partner = par_u[2 * i + e].astype(F32)
             for p in range(2):
-                yw[pl.ds(p * half_y + b * Y_PITCH, Y_ROWS), :] = y[:, p * LANES : (p + 1) * LANES]
+                density.append((own_uv[p, 2 * i + e].astype(F32) * partner).astype(BF16))
+        out = dot(t1[...], lanes(*density))
+        for e in range(2):
+            for p in range(2):
+                at = pl.ds(p * half_y + (2 * i + e) * Y_PITCH, Y_ROWS)
+                yw[at, :] = out[:, (2 * e + p) * LANES : (2 * e + p + 1) * LANES]
 
     @pl.loop(0, HALF, unroll=7)
     def _(k1):
@@ -184,28 +204,34 @@
 
         out = dot(t2[...], stack(lanes(line(0, 0), line(1, 0)), lanes(line(0, 1), line(1, 1))))
         at = pl.ds(pl.multiple_of(k1 * G, 16), G)
-        x34[at, : 2 * LANES] = out[:G].astype(BF16)
-        x34[at, 2 * LANES :] = out[G:].astype(BF16)
-
-    @pl.loop(0, KPAD // 2)
+        for p in range(2):
+            for part in range(2):
+                left = (2 * p + part) * LANES
+                value = out[part * G : (part + 1) * G, p * LANES : (p + 1) * LANES]
+                x34[at, left : left + LANES] = value.astype(BF16)
+
+    loads[1].wait()
+
+    @pl.loop(0, KPAD // 2, unroll=5)
     def _(m):
         at = pl.ds(pl.multiple_of(m * 2 * G, 16), 2 * G)
-        field = x34[at, :]
-        factor = kern[at, :]
-        for h in range(2):
-            out = dot(field, t3[:, 2 * h * LANES : 2 * (h + 1) * LANES])
-            for e in range(2):
-                spectrum = out[:, e * LANES : (e + 1) * LANES].astype(BF16).astype(F32)
-                value = spectrum * factor
-                for i in range(2):
-                    row = (2 * m + i) * Z_PITCH
-                    z[2 * h + e, pl.ds(row, G), :] = value[i * G : (i + 1) * G]
-
-    @pl.loop(0, G // 2, unroll=2)
-    def _(pair):
+        factor = kern_v[at, :]
+        out = [
+            dot(x34[at, 2 * p * LANES : 2 * (p + 1) * LANES], t3[...]).astype(BF16)
+            for p in range(2)
+        ]
+        for part in range(4):
+            spectrum = lanes(*[o[:, part * 64 : (part + 1) * 64] for o in out]).astype(F32)
+            value = spectrum * factor
+            for i in range(2):
+                row = (2 * m + i) * Z_PITCH
+                z[part, pl.ds(row, G), :] = value[i * G : (i + 1) * G]
+
+    @pl.loop(0, G // 4, unroll=3)
+    def _(four):
         parts = []
-        for e in range(2):
-            k2 = 2 * pair + e
+        for e in range(4):
+            k2 = 4 * four + e
             mirror = Z_PITCH + jnp.where(k2 == 0, 0, G - k2)
             parts.append(
                 stack(
@@ -216,15 +242,15 @@
                 )
             )
         out = dot(a1[...], lanes(*parts))
-        for e in range(2):
-            at = (2 * pair + e) * W_PITCH
+        for e in range(4):
+            at = (4 * four + e) * W_PITCH
             yw[pl.ds(at, 2 * G), :] = out[:, e * LANES : (e + 1) * LANES]
 
-    @pl.loop(0, G // 2, unroll=2)
-    def _(pair):
+    @pl.loop(0, G // 4, unroll=3)
+    def _(four):
         parts = []
-        for e in range(2):
-            x1 = 2 * pair + e
+        for e in range(4):
+            x1 = 4 * four + e
             parts.append(
                 stack(
                     yw[pl.ds(x1, G, stride=W_PITCH), :].astype(BF16),
@@ -238,12 +264,14 @@
                     out[r * QUADS : (r + 1) * QUADS, e * LANES : (e + 1) * LANES],
                     out[G + r * QUADS : G + (r + 1) * QUADS, e * LANES : (e + 1) * LANES],
                 )
-                for e in range(2)
+                for e in range(4)
             ]
-            at = pl.multiple_of((r // 2) * G * QUADS + pair * 2 * QUADS, 16)
+            at = pl.multiple_of((r // 2) * G * QUADS + four * 4 * QUADS, 16)
             left = (r % 2) * 2 * LANES
-            x34[pl.ds(at, 2 * QUADS), left : left + 2 * LANES] = stack(*block).astype(BF16)
-
+            x34[pl.ds(at, 4 * QUADS), left : left + 2 * LANES] = stack(*block).astype(BF16)
+
+    loads[2].wait()
+    loads[3].wait()
     energy_out[...] = jnp.zeros_like(energy_out)
     planes = 8
     block_rows = planes * QUADS
@@ -256,8 +284,7 @@
         high = x34[pl.ds(G * QUADS + at, block_rows), :]
         fields = [low, lanes(low[:, 2 * LANES :], high[:, : 2 * LANES]), high]
         flat = pl.ds(pl.multiple_of(ch * planes * PLANE, 16), planes * PLANE)
-        own_f[0] = own0[flat, :].astype(F32)
-        own_f[1] = own1[flat, :].astype(F32)
+        own_f[...] = own_v[:, flat, :].astype(F32)
         total = jnp.zeros((QUADS, LANES), F32)
         for third in range(3):
             out = dot(fields[third], a3[third]) * scale
@@ -269,16 +296,22 @@
                 sent = jnp.zeros((QUADS, LANES), F32)
                 for p in range(2):
                     potential = out[i * QUADS : (i + 1) * QUADS, p * LANES : (p + 1) * LANES]
-                    own_out[p, there, :] = potential * partner
+                    own_ov[p, there, :] = potential * partner
                     sent = sent + potential * own_f[p, here, :]
                 total = total + sent * partner
                 staged[here, :] = sent
         energy_out[...] += total
-        par_out[flat, :] = staged[...].astype(BF16)
+        par_ov[flat, :] = staged[...].astype(BF16)
+        pltpu.make_async_copy(own_ov.at[:, flat, :], own_out.at[:, flat, :], sems.at[4]).start()
+        pltpu.make_async_copy(par_ov.at[flat, :], par_out.at[flat, :], sems.at[5]).start()
+
+    pltpu.make_async_copy(own_ov, own_out, sems.at[4]).wait()
+    pltpu.make_async_copy(par_ov, par_out, sems.at[5]).wait()
 
 
 def pair_terms(own0, own1, own_u, partner, tables, kern, interpret=False):
     vmem = pl.BlockSpec(memory_space=pltpu.VMEM)
+    hbm = pl.BlockSpec(memory_space=pl.ANY)
     return pl.pallas_call(
         pairs_kernel,
         out_shape=(
@@ -286,15 +319,22 @@
             jax.ShapeDtypeStruct((ROWS, LANES), BF16),
             jax.ShapeDtypeStruct((QUADS, LANES), F32),
         ),
-        in_specs=[vmem] * 12,
-        out_specs=(vmem, vmem, vmem),
+        in_specs=[hbm] * 4 + [vmem] * 8,
+        out_specs=(hbm, hbm, vmem),
         scratch_shapes=[
+            pltpu.VMEM((2, ROWS, LANES), BF16),
+            pltpu.VMEM((2, G, G, LANES), BF16),
+            pltpu.VMEM((KPAD * G, LANES), F32),
+            pltpu.VMEM((2, ROWS, LANES), F32),
+            pltpu.VMEM((ROWS, LANES), BF16),
             pltpu.VMEM((G * F_PITCH, LANES), F32),
+            pltpu.VMEM((G, G, LANES), BF16),
             pltpu.VMEM((2 * G * Y_PITCH, LANES), F32),
             pltpu.VMEM((4, KPAD * Z_PITCH, LANES), F32),
             pltpu.VMEM((KPAD * G, 4 * LANES), BF16),
             pltpu.VMEM((2, 8 * PLANE, LANES), F32),
             pltpu.VMEM((8 * PLANE, LANES), F32),
+            pltpu.SemaphoreType.DMA((6,)),
         ],
         compiler_params=pltpu.CompilerParams(vmem_limit_bytes=62 * 1024 * 1024),
         cost_estimate=pl.CostEstimate(
@@ -302,7 +342,7 @@
         ),
         interpret=interpret,
         name="pair_terms",
-    )(own0, own1, own_u, partner, *tables, kern)
+    )(own0, own1, own_u, kern, partner, *tables)
 
 
 BLOCK = 1152
@@ -333,7 +373,7 @@
         ),
         in_specs=[flat, flat, both, both, flat],
         out_specs=(flat, flat, pl.BlockSpec((2, 8, LANES), lambda i: (0, 0, 0))),
-        compiler_params=pltpu.CompilerParams(vmem_limit_bytes=32 * 1024 * 1024),
+        compiler_params=pltpu.CompilerParams(vmem_limit_bytes=62 * 1024 * 1024),
         interpret=interpret,
         name="first_sum",
     )(*own, first, second, back0)
@@ -365,7 +405,7 @@
             pl.BlockSpec((2 * BLOCK, LANES), lambda i: (i, 0)),
             pl.BlockSpec((2, 8, LANES), lambda i: (0, 0, 0)),
         ),
-        compiler_params=pltpu.CompilerParams(vmem_limit_bytes=32 * 1024 * 1024),
+        compiler_params=pltpu.CompilerParams(vmem_limit_bytes=62 * 1024 * 1024),
         interpret=interpret,
         name="last_sum",
     )(*own, exch0, part1, back1)
@@ -390,7 +430,7 @@
     tables = section_tables()
     kern = screening()
     raw = orbitals.reshape(2, ROWS, LANES).transpose(1, 0, 2).reshape(2 * ROWS, LANES)
-    own = split_bands(raw)
+    own = [take_band(raw, j) for j in range(2)]
     previous = [from_behind(own[j], "band", 1) for j in range(2)]
     own_u = padded_rows(*own, tables[-1])
     first, sent0, energy0 = pair_terms(*own, own_u, previous[0], tables, kern)

time: 166 us -> 137 us (0.83)
  Pallas kernels: 109 us -> 90.9 us
  local copies, waits for them, and re-layouts: 11.4 us -> 4.27 us
  waiting for transfers between devices: 32.7 us -> 28.4 us
    pallas_call x2, Pallas kernels: 84.4 us -> 47.9 us  [pair_terms(): pl.pallas_call(pairs_kernel, out_shape=(jax.ShapeDtypeStruct((2, ROWS, LA...]
    unnamed x17 -> x9, local copies, waits for them, and re-layouts: 10.3 us -> 3.11 us
    pallas_call x1 -> x2, Pallas kernels: 5.82 us -> 10.5 us  [take_band(): pl.pallas_call(functools.partial(band_kernel, p), grid=(ROWS // rows,), o...]
    pallas_call x1, Pallas kernels: 4.05 us -> 8.63 us  [last_sum(): pl.pallas_call(last_sum_kernel, grid=(ROWS // BLOCK,), out_shape=(jax.Sha...]
    pallas_call x1, Pallas kernels: 5.58 us -> 10 us  [first_sum(): pl.pallas_call(first_sum_kernel, grid=(ROWS // BLOCK,), out_shape=(jax.Sh...]
    ppermute x4, waiting for transfers between devices: 9.09 us -> 4.69 us  [from_behind(): lax.ppermute(block, axis, [((i - distance) % size, i) for i in range(size)])]
    pallas_call x1, Pallas kernels: 9.6 us -> 13.8 us  [padded_rows(): pl.pallas_call(rows_kernel, out_shape=jax.ShapeDtypeStruct((2, G, G, LANE...]
  transfers between devices with their start and end apart: 9 -> 9, of which waited for: 6 -> 6; matrix products, arithmetic and copies ran while one was open for 2% -> 3% of each run, Pallas kernels for 60% -> 56%
where the time goes in v2:
time: 137 us
  Pallas kernels  90.9 us (66%)
  waiting for transfers between devices  28.4 us (21%)
  starting transfers between devices  7.13 us (5%)
  local copies, waits for them, and re-layouts  4.27 us (3%)
  other arithmetic  3.52 us (3%)
  between operations  2.54 us (2%)
    pallas_call x2, Pallas kernels, pair_terms(): pl.pallas_call(pairs_kernel, out_shape=(jax.ShapeDtypeStruct((2, ROWS, LA...  47.9 us
    ppermute x5, waiting for transfers between devices, sum_over(): lax.ppermute(value, axis, [(i ^ step, i) for i in range(size)])  23.7 us
    pallas_call x1, Pallas kernels, padded_rows(): pl.pallas_call(rows_kernel, out_shape=jax.ShapeDtypeStruct((2, G, G, LANE...  13.8 us
    pallas_call x2, Pallas kernels, take_band(): pl.pallas_call(functools.partial(band_kernel, p), grid=(ROWS // rows,), o...  10.5 us
    pallas_call x1, Pallas kernels, first_sum(): pl.pallas_call(first_sum_kernel, grid=(ROWS // BLOCK,), out_shape=(jax.Sh...  10 us
    pallas_call x1, Pallas kernels, last_sum(): pl.pallas_call(last_sum_kernel, grid=(ROWS // BLOCK,), out_shape=(jax.Sha...  8.63 us
    ppermute x4, starting transfers between devices, from_behind(): lax.ppermute(block, axis, [((i - distance) % size, i) for i in range(size)])  5.55 us
    ppermute x4, waiting for transfers between devices, from_behind(): lax.ppermute(block, axis, [((i - distance) % size, i) for i in range(size)])  4.69 us
  transfers between devices with their start and end apart: 9, of which 6 were waited for; matrix products, arithmetic and copies ran while one was open for 3% of the time, Pallas kernels for 56%

profile of v2, /device:TPU:0, one launch (start us, length us, event | category | flops | bytes accessed | tf_op | source)
XLA Modules:
  0.0 136.7 jit_solution(2975914250824269005)
XLA Ops:
  0.6 5.2 %take_band.2.own0 = bf16[6912,128]{1,0:T(8,128)(2,1)} custom-call(bf16[13824,128]{1,0:T(8,128)(2,1)} %bitcast.13), custom_call_target="tpu_custom_call" | custom-call | tf_op jit(solution)/shard_map/take_band/pallas_call | solution.py:124
  5.9 0.5 collective-permute-start
  6.3 5.2 %take_band.3.own1 = bf16[6912,128]{1,0:T(8,128)(2,1)} custom-call(bf16[13824,128]{1,0:T(8,128)(2,1)} %bitcast.14), custom_call_target="tpu_custom_call" | custom-call | tf_op jit(solution)/shard_map/take_band/pallas_call | solution.py:124
  11.5 2.6 %collective-permute-start.1 = (bf16[6912,128]{1,0:T(8,128)(2,1)}, bf16[6912,128]{1,0:T(8,128)(2,1)}, u32[]{:S(2)}, u32[]{:S(2)}) collective-permute-start(bf16[6912,128]{1,0:T(8,128)(2,1)} %take_band.3.own1), channel_id=1, source_target_pairs={{31,0},{0,1},{1,2},{2,3},{3,4},{4,5},{5,6},{6,7},{7,8},{8,9},{9,10... | collective-permute-start | bytes 5308424 | tf_op jit(solution)/shard_map/ppermute | solution.py:416
  14.1 13.8 %padded_rows.1.own_u = bf16[2,96,96,128]{3,2,1,0:T(8,128)(2,1)} custom-call(bf16[6912,128]{1,0:T(8,128)(2,1)} %take_band.2.own0, bf16[6912,128]{1,0:T(8,128)(2,1)} %take_band.3.own1, bf16[2,256,256]{2,1,0:T(8,128)(2,1)} %constant.30.clone.sel), custom_call_target="tpu_custom_call" | custom-call | tf_op jit(solution)/shard_map/padded_rows/pallas_call | solution.py:150
  28.0 4.7 %collective-permute-done.par_ref = bf16[6912,128]{1,0:T(8,128)(2,1)S(1)} collective-permute-done((bf16[6912,128]{1,0:T(8,128)(2,1)}, bf16[6912,128]{1,0:T(8,128)(2,1)S(1)}, u32[]{:S(2)}, u32[]{:S(2)}) %collective-permute-start) | collective-permute-done | bytes 1769504 | tf_op jit(solution)/shard_map/ppermute | solution.py:416
  32.6 0.0 copy-start.3
  32.6 1.2 copy-done.3
  33.9 23.9 %pair_terms.2 = (f32[2,6912,128]{2,1,0:T(8,128)}, bf16[6912,128]{1,0:T(8,128)(2,1)}, f32[24,128]{1,0:T(8,128)}) custom-call(bf16[6912,128]{1,0:T(8,128)(2,1)} %take_band.2.own0, bf16[6912,128]{1,0:T(8,128)(2,1)} %take_band.3.own1, bf16[2,96,96,128]{3,2,1,0:T(8,128)(2,1)} %padded_rows.1.own_u, f32[4800,128]{1,0:T(8,128)} %constant.31.clone.kern, ...), custom_call_target="tpu_custom_call" | custom-call | flops 20000000000 | bytes 20000000 | tf_op jit(solution)/shard_map/pair_terms/pallas_call | solution.py:315
  57.8 0.0 copy-start.1
  57.8 0.1 collective-permute-start.2
  57.9 0.0 collective-permute-done.1.par_ref
  57.9 24.0 %pair_terms.3 = (f32[2,6912,128]{2,1,0:T(8,128)}, bf16[6912,128]{1,0:T(8,128)(2,1)}, f32[24,128]{1,0:T(8,128)}) custom-call(bf16[6912,128]{1,0:T(8,128)(2,1)} %take_band.2.own0, bf16[6912,128]{1,0:T(8,128)(2,1)} %take_band.3.own1, bf16[2,96,96,128]{3,2,1,0:T(8,128)(2,1)} %padded_rows.1.own_u, f32[4800,128]{1,0:T(8,128)} %constant.31.clone.kern, ...), custom_call_target="tpu_custom_call" | custom-call | flops 20000000000 | bytes 20000000 | tf_op jit(solution)/shard_map/pair_terms/pallas_call | solution.py:315
  81.9 2.4 %collective-permute-start.3 = (bf16[6912,128]{1,0:T(8,128)(2,1)}, bf16[6912,128]{1,0:T(8,128)(2,1)}, u32[]{:S(2)}, u32[]{:S(2)}) collective-permute-start(bf16[6912,128]{1,0:T(8,128)(2,1)} %get-tuple-element.19), channel_id=1, source_target_pairs={{1,0},{2,1},{3,2},{4,3},{5,4},{6,5},{7,6},{8,7},{9,8},{10,9},{11,1... | collective-permute-start | bytes 5308424 | tf_op jit(solution)/shard_map/ppermute | solution.py:416
  84.3 0.0 copy-done.1
  84.3 1.3 add_reduce_fusion
  85.6 0.6 broadcast_in_dim.2
  86.3 0.1 collective-permute-start.4
  86.4 1.2 collective-permute-done.4
  87.5 0.6 broadcast_add_fusion
  88.2 0.1 collective-permute-start.5
  88.3 3.6 %collective-permute-done.5 = f32[8,128]{1,0:T(8,128)S(1)} collective-permute-done((f32[8,128]{1,0:T(8,128)S(1)}, f32[8,128]{1,0:T(8,128)S(1)}, u32[]{:S(2)}, u32[]{:S(2)}) %collective-permute-start.5) | collective-permute-done | bytes 4128 | tf_op jit(solution)/shard_map/ppermute | solution.py:425
  91.9 0.6 fusion
  92.5 0.1 collective-permute-start.6
  92.6 12.2 %collective-permute-done.6 = f32[8,128]{1,0:T(8,128)S(1)} collective-permute-done((f32[8,128]{1,0:T(8,128)S(1)}, f32[8,128]{1,0:T(8,128)S(1)}, u32[]{:S(2)}, u32[]{:S(2)}) %collective-permute-start.6) | collective-permute-done | bytes 4128 | tf_op jit(solution)/shard_map/ppermute | solution.py:425
  104.8 1.4 %collective-permute-start.7 = (f32[8,128]{1,0:T(8,128)S(1)}, f32[8,128]{1,0:T(8,128)S(1)}, u32[]{:S(2)}, u32[]{:S(2)}) collective-permute-start(f32[8,128]{1,0:T(8,128)S(1)} %add.21), channel_id=1, source_target_pairs={{16,0},{17,1},{18,2},{19,3},{20,4},{21,5},{22,6},{23,7},{24,8},{25... | collective-permute-start | bytes 12296 | tf_op jit(solution)/shard_map/ppermute | solution.py:425
  106.1 3.1 %collective-permute-done.7 = f32[8,128]{1,0:T(8,128)S(1)} collective-permute-done((f32[8,128]{1,0:T(8,128)S(1)}, f32[8,128]{1,0:T(8,128)S(1)}, u32[]{:S(2)}, u32[]{:S(2)}) %collective-permute-start.7) | collective-permute-done | bytes 4128 | tf_op jit(solution)/shard_map/ppermute | solution.py:425
  109.3 0.0 collective-permute-start.8
  109.3 3.6 %collective-permute-done.8 = f32[8,128]{1,0:T(8,128)S(1)} collective-permute-done((f32[8,128]{1,0:T(8,128)S(1)}, f32[8,128]{1,0:T(8,128)S(1)}, u32[]{:S(2)}, u32[]{:S(2)}) %collective-permute-start.8) | collective-permute-done | bytes 4128 | tf_op jit(solution)/shard_map/ppermute | solution.py:425
  112.9 0.5 slice.3
  114.1 0.0 collective-permute-done.2.back0
  114.1 0.0 copy-start
  114.1 1.2 copy-done
  115.3 10.0 %first_sum.1 = (f32[6912,128]{1,0:T(8,128)}, f32[6912,128]{1,0:T(8,128)}, f32[2,8,128]{2,1,0:T(8,128)}) custom-call(bf16[6912,128]{1,0:T(8,128)(2,1)} %take_band.2.own0, bf16[6912,128]{1,0:T(8,128)(2,1)} %take_band.3.own1, f32[2,6912,128]{2,1,0:T(8,128)} %get-tuple-element.14.first, f32[2,6912,128]{2,1,0:T(8,128)} %get-tuple-element.15.second, ...), custom_call_target="tpu_custom_call" | custom-call | tf_op jit(solution)/shard_map/first_sum/pallas_call | solution.py:366
  125.3 0.0 collective-permute-done.3.back1
  125.3 0.0 copy-start.2
  125.4 8.6 %last_sum.1 = (f32[13824,128]{1,0:T(8,128)}, f32[2,8,128]{2,1,0:T(8,128)}) custom-call(bf16[6912,128]{1,0:T(8,128)(2,1)} %take_band.2.own0, bf16[6912,128]{1,0:T(8,128)(2,1)} %take_band.3.own1, f32[6912,128]{1,0:T(8,128)} %get-tuple-element.17.exch0, f32[6912,128]{1,0:T(8,128)} %get-tuple-element.18.part1, bf16[6912,128]{1,0:T(8,128)(2,1)} %collective-permute-done.3.back1), custom_call_target="tpu_custom_call" | custom-call | tf_op jit(solution)/shard_map/last_sum/pallas_call | solution.py:396
  134.0 0.8 reduce_sum.28
  134.8 0.0 copy-done.2
  134.8 0.1 reduce_sum.27
  134.9 0.7 copy.14
  (4 shorter events, 0.0 us)
Async XLA Ops:
  5.9 26.8 %collective-permute-start = (bf16[6912,128]{1,0:T(8,128)(2,1)}, bf16[6912,128]{1,0:T(8,128)(2,1)S(1)}, u32[]{:S(2)}, u32[]{:S(2)}) collective-permute-start(bf16[6912,128]{1,0:T(8,128)(2,1)} %take_band.2.own0), channel_id=1, source_target_pairs={{31,0},{0,1},{1,2},{2,3},{3,4},{4,5},{5,6},{6,7},{7,8},{8,9},{9,10... | collective-permute-start | bytes 5308424 | tf_op jit(solution)/shard_map/ppermute | solution.py:416
  11.5 46.4 %collective-permute-start.1 = (bf16[6912,128]{1,0:T(8,128)(2,1)}, bf16[6912,128]{1,0:T(8,128)(2,1)}, u32[]{:S(2)}, u32[]{:S(2)}) collective-permute-start(bf16[6912,128]{1,0:T(8,128)(2,1)} %take_band.3.own1), channel_id=1, source_target_pairs={{31,0},{0,1},{1,2},{2,3},{3,4},{4,5},{5,6},{6,7},{7,8},{8,9},{9,10... | collective-permute-start | bytes 5308424 | tf_op jit(solution)/shard_map/ppermute | solution.py:416
  32.6 1.2 copy-start.3
  57.8 26.5 %copy-start.1 = (f32[24,128]{1,0:T(8,128)S(1)}, f32[24,128]{1,0:T(8,128)}, u32[]{:S(2)}) copy-start(f32[24,128]{1,0:T(8,128)} %get-tuple-element.23) | copy-start | bytes 36868
  57.8 56.2 %collective-permute-start.2 = (bf16[6912,128]{1,0:T(8,128)(2,1)}, bf16[6912,128]{1,0:T(8,128)(2,1)S(1)}, u32[]{:S(2)}, u32[]{:S(2)}) collective-permute-start(bf16[6912,128]{1,0:T(8,128)(2,1)} %get-tuple-element.16), channel_id=1, source_target_pairs={{1,0},{2,1},{3,2},{4,3},{5,4},{6,5},{7,6},{8,7},{9,8},{10,9},{11,1... | collective-permute-start | bytes 5308424 | tf_op jit(solution)/shard_map/ppermute | solution.py:416
  81.9 43.5 %collective-permute-start.3 = (bf16[6912,128]{1,0:T(8,128)(2,1)}, bf16[6912,128]{1,0:T(8,128)(2,1)}, u32[]{:S(2)}, u32[]{:S(2)}) collective-permute-start(bf16[6912,128]{1,0:T(8,128)(2,1)} %get-tuple-element.19), channel_id=1, source_target_pairs={{1,0},{2,1},{3,2},{4,3},{5,4},{6,5},{7,6},{8,7},{9,8},{10,9},{11,1... | collective-permute-start | bytes 5308424 | tf_op jit(solution)/shard_map/ppermute | solution.py:416
  86.3 1.2 collective-permute-start.4
  88.2 3.7 %collective-permute-start.5 = (f32[8,128]{1,0:T(8,128)S(1)}, f32[8,128]{1,0:T(8,128)S(1)}, u32[]{:S(2)}, u32[]{:S(2)}) collective-permute-start(f32[8,128]{1,0:T(8,128)S(1)} %broadcast_add_fusion), channel_id=1, source_target_pairs={{4,0},{5,1},{6,2},{7,3},{0,4},{1,5},{2,6},{3,7},{12,8},{13,9},{14,... | collective-permute-start | bytes 12296 | tf_op jit(solution)/shard_map/ppermute | solution.py:425
  92.5 12.3 %collective-permute-start.6 = (f32[8,128]{1,0:T(8,128)S(1)}, f32[8,128]{1,0:T(8,128)S(1)}, u32[]{:S(2)}, u32[]{:S(2)}) collective-permute-start(f32[8,128]{1,0:T(8,128)S(1)} %fusion), channel_id=1, source_target_pairs={{8,0},{9,1},{10,2},{11,3},{12,4},{13,5},{14,6},{15,7},{0,8},{1,9},... | collective-permute-start | bytes 12296 | tf_op jit(solution)/shard_map/ppermute | solution.py:425
  104.8 4.5 %collective-permute-start.7 = (f32[8,128]{1,0:T(8,128)S(1)}, f32[8,128]{1,0:T(8,128)S(1)}, u32[]{:S(2)}, u32[]{:S(2)}) collective-permute-start(f32[8,128]{1,0:T(8,128)S(1)} %add.21), channel_id=1, source_target_pairs={{16,0},{17,1},{18,2},{19,3},{20,4},{21,5},{22,6},{23,7},{24,8},{25... | collective-permute-start | bytes 12296 | tf_op jit(solution)/shard_map/ppermute | solution.py:425
  109.3 3.6 %collective-permute-start.8 = (f32[8,128]{1,0:T(8,128)S(1)}, f32[8,128]{1,0:T(8,128)S(1)}, u32[]{:S(2)}, u32[]{:S(2)}) collective-permute-start(f32[8,128]{1,0:T(8,128)S(1)} %add.22), channel_id=1, source_target_pairs={{2,0},{3,1},{0,2},{1,3},{6,4},{7,5},{4,6},{5,7},{10,8},{11,9},{8,1... | collective-permute-start | bytes 12296 | tf_op jit(solution)/shard_map/ppermute | solution.py:425
  114.1 1.2 copy-start
  125.3 9.4 %copy-start.2 = (f32[2,8,128]{2,1,0:T(8,128)S(1)}, f32[2,8,128]{2,1,0:T(8,128)}, u32[]{:S(2)}) copy-start(f32[2,8,128]{2,1,0:T(8,128)} %get-tuple-element.21) | copy-start | bytes 24580

commit v3 on v2

--- a/solution.py
+++ b/solution.py
@@ -22,8 +22,11 @@
 Z_PITCH = G + 1
 W_PITCH = 2 * G + 1
 F_PITCH = PLANE + 1
+PLANES = 16
+PIECES = 3
 WAVE_UNIT = 0.05
 SCREEN_SQ = 0.0121
+VMEM_ALL = pltpu.CompilerParams(vmem_limit_bytes=62 * 1024 * 1024)
 BF16 = jnp.bfloat16
 F32 = jnp.float32
 
@@ -100,49 +103,63 @@
     return jnp.concatenate(parts, axis=0)
 
 
-def split_rows(rows, sel_ref):
-    first = dot(lanes(rows[0], rows[1]), sel_ref[0])
-    second = dot(lanes(rows[1], rows[2]), sel_ref[1])
-    return [first[:, :LANES], first[:, LANES:], second[:, :LANES], second[:, LANES:]]
+def split_rows(src, sel_ref, out, first, count):
+    rows = [
+        [src[pl.ds(3 * (first + i) + s, G, stride=F_PITCH), :].astype(BF16) for s in range(3)]
+        for i in range(count)
+    ]
+    for half in range(2):
+        part = dot(stack(*[lanes(r[half], r[half + 1]) for r in rows]), sel_ref[half])
+        for i in range(count):
+            for e in range(2):
+                value = part[i * G : (i + 1) * G, e * LANES : (e + 1) * LANES]
+                out[4 * (first + i) + 2 * half + e] = value.astype(BF16)
 
 
 def widen_planes(src, dst):
-    @pl.loop(0, G // 2)
+    @pl.loop(0, G // 2, unroll=4)
     def _(i):
         value = src[pl.ds(pl.multiple_of(i * 2 * PLANE, 16), 2 * PLANE), :].astype(F32)
         dst[pl.ds(2 * i * F_PITCH, PLANE), :] = value[:PLANE]
         dst[pl.ds((2 * i + 1) * F_PITCH, PLANE), :] = value[PLANE:]
 
 
-def band_kernel(p, raw_ref, out, wide):
-    wide[...] = raw_ref[...].astype(F32)
-    out[...] = wide[pl.ds(p, out.shape[0], stride=2), :].astype(BF16)
+def band_kernel(raw_ref, pick, out):
+    half = LANES
+    for i in range(raw_ref.shape[0] // (4 * LANES)):
+        top = raw_ref[4 * i * half : (4 * i + 2) * half, :]
+        low = raw_ref[(4 * i + 2) * half : (4 * i + 4) * half, :]
+        rows = dot(pick[...], lanes(top, low)).astype(BF16)
+        out[2 * i * half : (2 * i + 1) * half, :] = rows[:, :half]
+        out[(2 * i + 1) * half : (2 * i + 2) * half, :] = rows[:, half:]
 
 
 def take_band(raw, p, interpret=False):
-    rows = 1152
+    pick = np.zeros((LANES, 2 * LANES), np.float32)
+    pick[np.arange(LANES), 2 * np.arange(LANES) + p] = 1.0
+    rows = 768
     return pl.pallas_call(
-        functools.partial(band_kernel, p),
+        band_kernel,
         grid=(ROWS // rows,),
         out_shape=jax.ShapeDtypeStruct((ROWS, LANES), BF16),
-        in_specs=[pl.BlockSpec((2 * rows, LANES), lambda i: (i, 0))],
+        in_specs=[
+            pl.BlockSpec((2 * rows, LANES), lambda i: (i, 0)),
+            pl.BlockSpec((LANES, 2 * LANES), lambda i: (0, 0)),
+        ],
         out_specs=pl.BlockSpec((rows, LANES), lambda i: (i, 0)),
-        scratch_shapes=[pltpu.VMEM((2 * rows, LANES), F32)],
-        compiler_params=pltpu.CompilerParams(vmem_limit_bytes=62 * 1024 * 1024),
+        compiler_params=VMEM_ALL,
         interpret=interpret,
         name="take_band",
-    )(raw)
+    )(raw, pick.astype(ml_dtypes.bfloat16))
 
 
 def rows_kernel(own0, own1, sel, out, wide):
     for p, own in enumerate((own0, own1)):
         widen_planes(own, wide)
 
-        @pl.loop(0, QUADS)
+        @pl.loop(0, QUADS // 4)
         def _(q):
-            rows = [wide[pl.ds(3 * q + s, G, stride=F_PITCH), :].astype(BF16) for s in range(3)]
-            for r, part in enumerate(split_rows(rows, sel)):
-                out[p, 4 * q + r] = part.astype(BF16)
+            split_rows(wide, sel, out.at[p], 4 * q, 4)
 
 
 def padded_rows(own0, own1, sel, interpret=False):
@@ -153,17 +170,18 @@
         in_specs=[vmem] * 3,
         out_specs=vmem,
         scratch_shapes=[pltpu.VMEM((G * F_PITCH, LANES), F32)],
-        compiler_params=pltpu.CompilerParams(vmem_limit_bytes=62 * 1024 * 1024),
+        compiler_params=VMEM_ALL,
         interpret=interpret,
         name="padded_rows",
     )(own0, own1, sel)
 
 
 def pairs_kernel(
-    own0, own1, own_u, kern, par_ref, t1, t2, t3, a1, a2, a3, sel,
-    own_out, par_out, energy_out,
-    own_v, own_uv, kern_v, own_ov, par_ov, par_f, par_u, yw, z, x34, own_f, staged, sems,
+    pieces, own0, own1, own_u, kern, par_ref, energy_in, t1, t2, t3, a1, a2, a3, sel, own_out, *rest
 ):
+    par_out, energy_out = rest[:pieces], rest[pieces]
+    own_v, own_uv, kern_v, own_ov, par_ov, par_f, par_u, yw, z, x34 = rest[pieces + 1 : pieces + 11]
+    own_f, staged, total_ref, sems = rest[pieces + 11 :]
     loads = [
         pltpu.make_async_copy(own_u, own_uv, sems.at[0]),
         pltpu.make_async_copy(kern, kern_v, sems.at[1]),
@@ -175,11 +193,9 @@
 
     widen_planes(par_ref, par_f)
 
-    @pl.loop(0, QUADS, unroll=4)
+    @pl.loop(0, QUADS // 4)
     def _(q):
-        rows = [par_f[pl.ds(3 * q + s, G, stride=F_PITCH), :].astype(BF16) for s in range(3)]
-        for r, part in enumerate(split_rows(rows, sel)):
-            par_u[4 * q + r] = part.astype(BF16)
+        split_rows(par_f, sel, par_u, 4 * q, 4)
 
     half_y = G * Y_PITCH
     loads[0].wait()
@@ -212,9 +228,11 @@
 
     loads[1].wait()
 
-    @pl.loop(0, KPAD // 2, unroll=5)
+    many = 5
+
+    @pl.loop(0, KPAD // many)
     def _(m):
-        at = pl.ds(pl.multiple_of(m * 2 * G, 16), 2 * G)
+        at = pl.ds(pl.multiple_of(m * many * G, 16), many * G)
         factor = kern_v[at, :]
         out = [
             dot(x34[at, 2 * p * LANES : 2 * (p + 1) * LANES], t3[...]).astype(BF16)
@@ -223,8 +241,8 @@
         for part in range(4):
             spectrum = lanes(*[o[:, part * 64 : (part + 1) * 64] for o in out]).astype(F32)
             value = spectrum * factor
-            for i in range(2):
-                row = (2 * m + i) * Z_PITCH
+            for i in range(many):
+                row = (many * m + i) * Z_PITCH
                 z[part, pl.ds(row, G), :] = value[i * G : (i + 1) * G]
 
     @pl.loop(0, G // 4, unroll=3)
@@ -272,8 +290,8 @@
 
     loads[2].wait()
     loads[3].wait()
-    energy_out[...] = jnp.zeros_like(energy_out)
-    planes = 8
+    total_ref[...] = jnp.zeros_like(total_ref)
+    planes = PLANES
     block_rows = planes * QUADS
     scale = F32(1.0 / NGRID)
 
@@ -300,27 +318,38 @@
                     sent = sent + potential * own_f[p, here, :]
                 total = total + sent * partner
                 staged[here, :] = sent
-        energy_out[...] += total
+        total_ref[...] += total
         par_ov[flat, :] = staged[...].astype(BF16)
         pltpu.make_async_copy(own_ov.at[:, flat, :], own_out.at[:, flat, :], sems.at[4]).start()
-        pltpu.make_async_copy(par_ov.at[flat, :], par_out.at[flat, :], sems.at[5]).start()
-
+        per_piece = G // planes // pieces
+        for i, out in enumerate(par_out):
+
+            @pl.when(ch // per_piece == i)
+            def _():
+                row = pl.multiple_of((ch - i * per_piece) * planes * PLANE, 16)
+                there = out.at[pl.ds(row, planes * PLANE), :]
+                pltpu.make_async_copy(par_ov.at[flat, :], there, sems.at[5 + i]).start()
+
+    energy = jnp.sum(total_ref[...]) * F32(-2.0 / NGRID)
+    energy_out[...] = energy_in[...] + energy
     pltpu.make_async_copy(own_ov, own_out, sems.at[4]).wait()
-    pltpu.make_async_copy(par_ov, par_out, sems.at[5]).wait()
-
-
-def pair_terms(own0, own1, own_u, partner, tables, kern, interpret=False):
+    for i, out in enumerate(par_out):
+        source = par_ov.at[pl.ds(i * out.shape[0], out.shape[0]), :]
+        pltpu.make_async_copy(source, out, sems.at[5 + i]).wait()
+
+
+def pair_terms(own0, own1, own_u, partner, energy, tables, kern, pieces, interpret=False):
     vmem = pl.BlockSpec(memory_space=pltpu.VMEM)
     hbm = pl.BlockSpec(memory_space=pl.ANY)
     return pl.pallas_call(
-        pairs_kernel,
+        functools.partial(pairs_kernel, pieces),
         out_shape=(
             jax.ShapeDtypeStruct((2, ROWS, LANES), F32),
-            jax.ShapeDtypeStruct((ROWS, LANES), BF16),
-            jax.ShapeDtypeStruct((QUADS, LANES), F32),
+            *[jax.ShapeDtypeStruct((ROWS // pieces, LANES), BF16)] * pieces,
+            jax.ShapeDtypeStruct((8, LANES), F32),
         ),
-        in_specs=[hbm] * 4 + [vmem] * 8,
-        out_specs=(hbm, hbm, vmem),
+        in_specs=[hbm] * 4 + [vmem] * 9,
+        out_specs=(hbm, *[hbm] * pieces, vmem),
         scratch_shapes=[
             pltpu.VMEM((2, ROWS, LANES), BF16),
             pltpu.VMEM((2, G, G, LANES), BF16),
@@ -332,20 +361,27 @@
             pltpu.VMEM((2 * G * Y_PITCH, LANES), F32),
             pltpu.VMEM((4, KPAD * Z_PITCH, LANES), F32),
             pltpu.VMEM((KPAD * G, 4 * LANES), BF16),
-            pltpu.VMEM((2, 8 * PLANE, LANES), F32),
-            pltpu.VMEM((8 * PLANE, LANES), F32),
-            pltpu.SemaphoreType.DMA((6,)),
+            pltpu.VMEM((2, PLANES * PLANE, LANES), F32),
+            pltpu.VMEM((PLANES * PLANE, LANES), F32),
+            pltpu.VMEM((QUADS, LANES), F32),
+            pltpu.SemaphoreType.DMA((5 + pieces,)),
         ],
-        compiler_params=pltpu.CompilerParams(vmem_limit_bytes=62 * 1024 * 1024),
+        compiler_params=VMEM_ALL,
         cost_estimate=pl.CostEstimate(
             flops=20_000_000_000, bytes_accessed=20_000_000, transcendentals=0
         ),
         interpret=interpret,
         name="pair_terms",
-    )(own0, own1, own_u, kern, partner, *tables)
-
-
-BLOCK = 1152
+    )(own0, own1, own_u, kern, partner, energy, *tables)
+
+
+BLOCK = 576
+
+
+def add_products(gram_ref, column, own0, own1, exchange):
+    for i, own in enumerate((own0, own1)):
+        product = (own[...].astype(F32) * exchange).reshape(-1, 8, LANES)
+        gram_ref[i, column] += jnp.sum(product, axis=0)
 
 
 def first_sum_kernel(own0, own1, first, second, back0, exch0, part1, gram_ref):
@@ -356,8 +392,7 @@
     exchange = first[0] + second[0] + back0[...].astype(F32)
     exch0[...] = exchange
     part1[...] = first[1] + second[1]
-    for i, own in enumerate((own0, own1)):
-        gram_ref[i] += jnp.sum((own[...].astype(F32) * exchange).reshape(-1, 8, LANES), axis=0)
+    add_products(gram_ref, 0, own0, own1, exchange)
 
 
 def first_sum(own, first, second, back0, interpret=False):
@@ -369,46 +404,70 @@
         out_shape=(
             jax.ShapeDtypeStruct((ROWS, LANES), F32),
             jax.ShapeDtypeStruct((ROWS, LANES), F32),
-            jax.ShapeDtypeStruct((2, 8, LANES), F32),
+            jax.ShapeDtypeStruct((2, 2, 8, LANES), F32),
         ),
         in_specs=[flat, flat, both, both, flat],
-        out_specs=(flat, flat, pl.BlockSpec((2, 8, LANES), lambda i: (0, 0, 0))),
-        compiler_params=pltpu.CompilerParams(vmem_limit_bytes=62 * 1024 * 1024),
+        out_specs=(flat, flat, pl.BlockSpec((2, 2, 8, LANES), lambda i: (0, 0, 0, 0))),
+        compiler_params=VMEM_ALL,
         interpret=interpret,
         name="first_sum",
     )(*own, first, second, back0)
 
 
-def last_sum_kernel(own0, own1, exch0, part1, back1, out_ref, gram_ref):
-    @pl.when(pl.program_id(0) == 0)
+def piece_kernel(piece, own0, own1, exch0, part1, back1, gram_in, *rest):
+    out_ref, gram_out, gram_ref = rest[-3:]
+    step = pl.program_id(0)
+
+    @pl.when(step == 0)
     def _():
-        gram_ref[...] = jnp.zeros_like(gram_ref)
+        gram_ref[...] = gram_in[...]
 
     exchange = part1[...] + back1[...].astype(F32)
     out_ref[pl.ds(0, BLOCK, stride=2), :] = exch0[...]
     out_ref[pl.ds(1, BLOCK, stride=2), :] = exchange
-    for i, own in enumerate((own0, own1)):
-        gram_ref[i] += jnp.sum((own[...].astype(F32) * exchange).reshape(-1, 8, LANES), axis=0)
-
-
-def last_sum(own, exch0, part1, back1, interpret=False):
-    flat = pl.BlockSpec((BLOCK, LANES), lambda i: (i, 0))
+    add_products(gram_ref, 1, own0, own1, exchange)
+
+    @pl.when(step == pl.num_programs(0) - 1)
+    def _():
+        if piece < PIECES - 1:
+            gram_out[...] = gram_ref[...]
+        else:
+            row = lax.broadcasted_iota(jnp.int32, (2, 2), 0)
+            column = lax.broadcasted_iota(jnp.int32, (2, 2), 1)
+            value = jnp.zeros((2, 2), F32)
+            for i in range(2):
+                for j in range(2):
+                    entry = jnp.sum(gram_ref[i, j]) * F32(1.0 / NGRID)
+                    value = jnp.where((row == i) & (column == j), entry, value)
+            gram_out[...] = value
+
+
+def add_piece(piece, own, exch0, part1, back1, gram, out, interpret=False):
+    steps = ROWS // PIECES // BLOCK
+    here = pl.BlockSpec((BLOCK, LANES), lambda i: (piece * steps + i, 0))
+    gram_spec = pl.BlockSpec((2, 2, 8, LANES), lambda i: (0, 0, 0, 0))
+    last = piece == PIECES - 1
+    earlier = [] if out is None else [out]
     return pl.pallas_call(
-        last_sum_kernel,
-        grid=(ROWS // BLOCK,),
+        functools.partial(piece_kernel, piece),
+        grid=(steps,),
         out_shape=(
             jax.ShapeDtypeStruct((2 * ROWS, LANES), F32),
-            jax.ShapeDtypeStruct((2, 8, LANES), F32),
+            jax.ShapeDtypeStruct((2, 2) if last else gram.shape, F32),
         ),
-        in_specs=[flat] * 5,
+        in_specs=[here] * 4
+        + [pl.BlockSpec((BLOCK, LANES), lambda i: (i, 0)), gram_spec]
+        + [pl.BlockSpec(memory_space=pl.ANY)] * len(earlier),
         out_specs=(
-            pl.BlockSpec((2 * BLOCK, LANES), lambda i: (i, 0)),
-            pl.BlockSpec((2, 8, LANES), lambda i: (0, 0, 0)),
+            pl.BlockSpec((2 * BLOCK, LANES), lambda i: (piece * steps + i, 0)),
+            pl.BlockSpec((2, 2), lambda i: (0, 0)) if last else gram_spec,
         ),
-        compiler_params=pltpu.CompilerParams(vmem_limit_bytes=62 * 1024 * 1024),
+        scratch_shapes=[pltpu.VMEM((2, 2, 8, LANES), F32)],
+        input_output_aliases={6: 0} if earlier else {},
+        compiler_params=VMEM_ALL,
         interpret=interpret,
-        name="last_sum",
-    )(*own, exch0, part1, back1)
+        name="add_piece",
+    )(*own, exch0, part1, back1, gram, *earlier)
 
 
 def from_behind(block, axis, distance):
@@ -416,35 +475,53 @@
     return lax.ppermute(block, axis, [((i - distance) % size, i) for i in range(size)])
 
 
-def sum_over(value, axis):
+def exchange_with(value, axis, bits):
     size = lax.axis_size(axis)
-    if size & (size - 1):
-        return lax.psum(value, axis)
-    steps = [1 << bit for bit in range(size.bit_length() - 1)]
-    for step in [s for s in steps if s != 2] + [s for s in steps if s == 2]:
-        value = value + lax.ppermute(value, axis, [(i ^ step, i) for i in range(size)])
-    return value
+    got = {0: value}
+    for flip in sorted({bits[0], bits[-1], sum(bits)}):
+        got[flip] = lax.ppermute(value, axis, [(i ^ flip, i) for i in range(size)])
+    low = got[0] + got[bits[0]]
+    if len(bits) == 1:
+        return low
+    return low + (got[bits[1]] + got[sum(bits)])
+
+
+def after(value, other):
+    return lax.optimization_barrier((value, other))[0]
 
 
 def per_device(orbitals):
     tables = section_tables()
     kern = screening()
+    size = lax.axis_size("band")
     raw = orbitals.reshape(2, ROWS, LANES).transpose(1, 0, 2).reshape(2 * ROWS, LANES)
     own = [take_band(raw, j) for j in range(2)]
     previous = [from_behind(own[j], "band", 1) for j in range(2)]
     own_u = padded_rows(*own, tables[-1])
-    first, sent0, energy0 = pair_terms(*own, own_u, previous[0], tables, kern)
+    energy = jnp.zeros((8, LANES), F32)
+    first, sent0, energy = pair_terms(*own, own_u, previous[0], energy, tables, kern, 1)
     back0 = from_behind(sent0, "band", -1)
-    second, sent1, energy1 = pair_terms(*own, own_u, previous[1], tables, kern)
-    back1 = from_behind(sent1, "band", -1)
-    pair_energy = jnp.sum(energy0 + energy1).reshape(1, 1)
-    total = sum_over(jnp.broadcast_to(pair_energy, (8, LANES)), "band")[0, 0]
-    energy = -2.0 * total / F32(NGRID) / F32(2 * lax.axis_size("band") * orbitals.shape[0])
-    exch0, part1, gram0 = first_sum(own, first, second, back0)
-    exchange, gram1 = last_sum(own, exch0, part1, back1)
-    gram = jnp.stack([jnp.sum(g, axis=(1, 2)) for g in (gram0, gram1)], axis=1) / F32(NGRID)
+    second, *sent1, energy = pair_terms(*own, own_u, previous[1], energy, tables, kern, PIECES)
+    back1 = [from_behind(piece, "band", -1) for piece in sent1]
+    energy = energy * F32(1.0 / (size * orbitals.shape[0] * 2))
+
+    exch0, part1, gram = first_sum(own, first, second, back0)
+    exchange = None
+    if size & (size - 1):
+        energy = lax.psum(energy, "band")
+        groups = []
+    else:
+        bits = [1 << b for b in range(size.bit_length() - 1)]
+        rest = [b for b in bits if b != 2]
+        groups = [rest[i : i + 2] for i in range(0, len(rest), 2)] + [[b] for b in bits if b == 2]
+    for piece in range(PIECES):
+        if groups:
+            energy = exchange_with(after(energy, gram) if piece else energy, "band", groups.pop(0))
+        exchange, gram = add_piece(piece, own, exch0, part1, back1[piece], gram, exchange)
+    for bits in groups:
+        energy = exchange_with(energy, "band", bits)
     exchange = exchange.reshape(ROWS, 2, LANES).transpose(1, 0, 2).reshape(2, NGRID)
-    return exchange, gram, energy
+    return exchange, gram, energy[0, 0]
 
 
 def solution(mesh):

time: 137 us -> 142 us (1.036)
  starting transfers between devices: 7.13 us -> 22.5 us
  waiting for transfers between devices: 28.4 us -> 16.5 us
  Pallas kernels: 90.9 us -> 96.9 us
  other arithmetic: 3.52 us -> 1.39 us
  between operations: 2.54 us -> 0.71 us
    ppermute x5 -> x7, waiting for transfers between devices: 23.7 us -> 7.81 us  [exchange_with(): got[flip] = lax.ppermute(value, axis, [(i ^ flip, i) for i in range(size)])]
    ppermute x5 -> x7, starting transfers between devices: 1.59 us -> 15.4 us  [exchange_with(): got[flip] = lax.ppermute(value, axis, [(i ^ flip, i) for i in range(size)])]
    pallas_call x5 -> x7, Pallas kernels: 67 us -> 76.2 us  [the longest x2 48.7 us: pair_terms(): pl.pallas_call(functools.partial(pairs_kernel, pieces), out_shape=(jax.Sh...]
    pallas_call x1, Pallas kernels: 13.8 us -> 7.91 us  [padded_rows(): pl.pallas_call(rows_kernel, out_shape=jax.ShapeDtypeStruct((2, G, G, LANE...]
    ppermute x4 -> x6, waiting for transfers between devices: 4.69 us -> 8.66 us  [from_behind(): lax.ppermute(block, axis, [((i - distance) % size, i) for i in range(size)])]
    pallas_call x1, Pallas kernels: 10 us -> 12.7 us  [first_sum(): pl.pallas_call(first_sum_kernel, grid=(ROWS // BLOCK,), out_shape=(jax.Sh...]
    reduce_sum x3 -> x0, other arithmetic: 2.2 us -> none  [the longest x1 1.31 us: per_device(): pair_energy = jnp.sum(energy0 + energy1).reshape(1, 1)]
    ppermute x4 -> x6, starting transfers between devices: 5.55 us -> 7.06 us  [from_behind(): lax.ppermute(block, axis, [((i - distance) % size, i) for i in range(size)])]
  transfers between devices with their start and end apart: 9 -> 13, of which waited for: 6 -> 4; matrix products, arithmetic and copies ran while one was open for 3% -> 1% of each run, Pallas kernels for 56% -> 64%
where the time goes in v3:
time: 142 us; the launch traced here: 141 us
  Pallas kernels  96.9 us (68%)
  starting transfers between devices  22.5 us (16%)
  waiting for transfers between devices  16.5 us (12%)
  local copies, waits for them, and re-layouts  3 us (2%)
    pallas_call x2, Pallas kernels, pair_terms(): pl.pallas_call(functools.partial(pairs_kernel, pieces), out_shape=(jax.Sh...  48.7 us
    ppermute x7, starting transfers between devices, exchange_with(): got[flip] = lax.ppermute(value, axis, [(i ^ flip, i) for i in range(size)])  15.4 us
    pallas_call x2, Pallas kernels, take_band(): pl.pallas_call(band_kernel, grid=(ROWS // rows,), out_shape=jax.ShapeDtyp...  14.3 us
    pallas_call x3, Pallas kernels, add_piece(): pl.pallas_call(functools.partial(piece_kernel, piece), grid=(steps,), out...  13.2 us
    pallas_call x1, Pallas kernels, first_sum(): pl.pallas_call(first_sum_kernel, grid=(ROWS // BLOCK,), out_shape=(jax.Sh...  12.7 us
    ppermute x6, waiting for transfers between devices, from_behind(): lax.ppermute(block, axis, [((i - distance) % size, i) for i in range(size)])  8.66 us
    pallas_call x1, Pallas kernels, padded_rows(): pl.pallas_call(rows_kernel, out_shape=jax.ShapeDtypeStruct((2, G, G, LANE...  7.91 us
    ppermute x7, waiting for transfers between devices, exchange_with(): got[flip] = lax.ppermute(value, axis, [(i ^ flip, i) for i in range(size)])  7.81 us
  transfers between devices with their start and end apart: 13, of which 4 were waited for; matrix products, arithmetic and copies ran while one was open for 1% of the time, Pallas kernels for 64%

profile of v3, /device:TPU:0, one launch (start us, length us, event | category | flops | bytes accessed | tf_op | source)
XLA Modules:
  0.0 140.9 jit_solution(570825725144752974)
XLA Ops:
  0.6 7.2 %take_band.2.own0 = bf16[6912,128]{1,0:T(8,128)(2,1)} custom-call(bf16[13824,128]{1,0:T(8,128)(2,1)} %bitcast.12, bf16[128,256]{1,0:T(8,128)(2,1)} %constant.24.clone.pick), custom_call_target="tpu_custom_call" | custom-call | tf_op jit(solution)/shard_map/take_band/pallas_call | solution.py:141
  7.8 0.5 collective-permute-start
  8.3 7.2 %take_band.3.own1 = bf16[6912,128]{1,0:T(8,128)(2,1)} custom-call(bf16[13824,128]{1,0:T(8,128)(2,1)} %bitcast.13, bf16[128,256]{1,0:T(8,128)(2,1)} %constant.25.clone.pick), custom_call_target="tpu_custom_call" | custom-call | tf_op jit(solution)/shard_map/take_band/pallas_call | solution.py:141
  15.4 2.6 %collective-permute-start.1 = (bf16[6912,128]{1,0:T(8,128)(2,1)}, bf16[6912,128]{1,0:T(8,128)(2,1)}, u32[]{:S(2)}, u32[]{:S(2)}) collective-permute-start(bf16[6912,128]{1,0:T(8,128)(2,1)} %take_band.3.own1), channel_id=1, source_target_pairs={{31,0},{0,1},{1,2},{2,3},{3,4},{4,5},{5,6},{6,7},{7,8},{8,9},{9,10... | collective-permute-start | bytes 5308424 | tf_op jit(solution)/shard_map/ppermute | solution.py:475
  18.0 7.9 %padded_rows.1.own_u = bf16[2,96,96,128]{3,2,1,0:T(8,128)(2,1)} custom-call(bf16[6912,128]{1,0:T(8,128)(2,1)} %take_band.2.own0, bf16[6912,128]{1,0:T(8,128)(2,1)} %take_band.3.own1, bf16[2,256,256]{2,1,0:T(8,128)(2,1)} %constant.26.clone.sel), custom_call_target="tpu_custom_call" | custom-call | tf_op jit(solution)/shard_map/padded_rows/pallas_call | solution.py:167
  25.9 8.6 %collective-permute-done.par_ref = bf16[6912,128]{1,0:T(8,128)(2,1)S(1)} collective-permute-done((bf16[6912,128]{1,0:T(8,128)(2,1)}, bf16[6912,128]{1,0:T(8,128)(2,1)S(1)}, u32[]{:S(2)}, u32[]{:S(2)}) %collective-permute-start) | collective-permute-done | bytes 1769504 | tf_op jit(solution)/shard_map/ppermute | solution.py:475
  34.6 0.0 copy-start.1
  34.6 0.6 broadcast_in_dim.3.energy_in
  35.2 0.6 copy-done.1
  35.8 24.3 %pair_terms.2 = (f32[2,6912,128]{2,1,0:T(8,128)}, bf16[6912,128]{1,0:T(8,128)(2,1)}, f32[8,128]{1,0:T(8,128)}) custom-call(bf16[6912,128]{1,0:T(8,128)(2,1)} %take_band.2.own0, bf16[6912,128]{1,0:T(8,128)(2,1)} %take_band.3.own1, bf16[2,96,96,128]{3,2,1,0:T(8,128)(2,1)} %padded_rows.1.own_u, f32[4800,128]{1,0:T(8,128)} %constant.27.clone.kern, ...), custom_call_target="tpu_custom_call" | custom-call | flops 20000000000 | bytes 20000000 | tf_op jit(solution)/shard_map/pair_terms/pallas_call | solution.py:344
  60.1 0.1 collective-permute-start.2
  60.2 0.0 collective-permute-done.1.par_ref
  60.2 24.4 %pair_terms.3 = (f32[2,6912,128]{2,1,0:T(8,128)}, bf16[2304,128]{1,0:T(8,128)(2,1)}, bf16[2304,128]{1,0:T(8,128)(2,1)}, bf16[2304,128]{1,0:T(8,128)(2,1)}, f32[8,128]{1,0:T(8,128)}) custom-call(bf16[6912,128]{1,0:T(8,128)(2,1)} %take_band.2.own0, bf16[6912,128]{1,0:T(8,128)(2,1)} %take_band.3.own1, bf16[2,96,96,128]{3,2,1,0:T(8,128)(2,1)} %padded_rows.1.own_u, ...), custom_call_target="tpu_custom_call" | custom-call | flops 20000000000 | bytes 20000000 | tf_op jit(solution)/shard_map/pair_terms/pallas_call | solution.py:344
  84.6 2.4 %collective-permute-start.5 = (bf16[2304,128]{1,0:T(8,128)(2,1)}, bf16[2304,128]{1,0:T(8,128)(2,1)}, u32[]{:S(2)}, u32[]{:S(2)}) collective-permute-start(bf16[2304,128]{1,0:T(8,128)(2,1)} %get-tuple-element.30), channel_id=1, source_target_pairs={{1,0},{2,1},{3,2},{4,3},{5,4},{6,5},{7,6},{8,7},{9,8},{10,9},{11,1... | collective-permute-start | bytes 1769480 | tf_op jit(solution)/shard_map/ppermute | solution.py:475
  87.0 0.1 collective-permute-start.4
  87.1 1.5 %collective-permute-start.3 = (bf16[2304,128]{1,0:T(8,128)(2,1)}, bf16[2304,128]{1,0:T(8,128)(2,1)}, u32[]{:S(2)}, u32[]{:S(2)}) collective-permute-start(bf16[2304,128]{1,0:T(8,128)(2,1)} %get-tuple-element.28), channel_id=1, source_target_pairs={{1,0},{2,1},{3,2},{4,3},{5,4},{6,5},{7,6},{8,7},{9,8},{10,9},{11,1... | collective-permute-start | bytes 1769480 | tf_op jit(solution)/shard_map/ppermute | solution.py:475
  88.6 0.7 broadcast_multiply_fusion
  89.3 0.0 collective-permute-start.7
  89.3 3.6 %collective-permute-done.7 = f32[8,128]{1,0:T(8,128)S(1)} collective-permute-done((f32[8,128]{1,0:T(8,128)S(1)}, f32[8,128]{1,0:T(8,128)S(1)}, u32[]{:S(2)}, u32[]{:S(2)}) %collective-permute-start.7) | collective-permute-done | bytes 4128 | tf_op jit(solution)/shard_map/ppermute | solution.py:482
  92.9 0.0 collective-permute-start.8
  92.9 3.0 %collective-permute-done.8 = f32[8,128]{1,0:T(8,128)S(1)} collective-permute-done((f32[8,128]{1,0:T(8,128)S(1)}, f32[8,128]{1,0:T(8,128)S(1)}, u32[]{:S(2)}, u32[]{:S(2)}) %collective-permute-start.8) | collective-permute-done | bytes 4128 | tf_op jit(solution)/shard_map/ppermute | solution.py:482
  95.9 0.0 collective-permute-start.6
  95.9 1.2 collective-permute-done.6
  97.1 0.7 add_add_fusion.1
  97.8 0.0 collective-permute-done.2.back0
  97.8 0.0 copy-start
  97.8 1.2 copy-done
  99.0 12.7 %first_sum.1 = (f32[6912,128]{1,0:T(8,128)}, f32[6912,128]{1,0:T(8,128)}, f32[2,2,8,128]{3,2,1,0:T(8,128)}) custom-call(bf16[6912,128]{1,0:T(8,128)(2,1)} %take_band.2.own0, bf16[6912,128]{1,0:T(8,128)(2,1)} %take_band.3.own1, f32[2,6912,128]{2,1,0:T(8,128)} %get-tuple-element.22.first, f32[2,6912,128]{2,1,0:T(8,128)} %get-tuple-element.24.second, ...), custom_call_target="tpu_custom_call" | custom-call | tf_op jit(solution)/shard_map/first_sum/pallas_call | solution.py:401
  111.7 0.0 collective-permute-done.5.back1
  111.7 4.4 %add_piece.3 = (f32[13824,128]{1,0:T(8,128)}, f32[2,2,8,128]{3,2,1,0:T(8,128)}) custom-call(bf16[6912,128]{1,0:T(8,128)(2,1)} %take_band.2.own0, bf16[6912,128]{1,0:T(8,128)(2,1)} %take_band.3.own1, f32[6912,128]{1,0:T(8,128)} %get-tuple-element.26.exch0, f32[6912,128]{1,0:T(8,128)} %get-tuple-element.27.part1, ...), custom_call_target="tpu_custom_call" | custom-call | tf_op jit(solution)/shard_map/add_piece/pallas_call | solution.py:451
  116.1 0.5 collective-permute-start.11
  116.5 0.0 collective-permute-start.10
  116.6 3.9 %collective-permute-start.9 = (f32[8,128]{1,0:T(8,128)S(1)}, f32[8,128]{1,0:T(8,128)S(1)}, u32[]{:S(2)}, u32[]{:S(2)}) collective-permute-start(f32[8,128]{1,0:T(8,128)S(1)} %add_add_fusion.1), channel_id=1, source_target_pairs={{8,0},{9,1},{10,2},{11,3},{12,4},{13,5},{14,6},{15,7},{0,8},{1,9},... | collective-permute-start | bytes 12296 | tf_op jit(solution)/shard_map/ppermute | solution.py:482
  120.5 0.0 collective-permute-done.4.back1
  120.5 4.3 %add_piece.4 = (f32[13824,128]{1,0:T(8,128)}, f32[2,2,8,128]{3,2,1,0:T(8,128)}) custom-call(bf16[6912,128]{1,0:T(8,128)(2,1)} %take_band.2.own0, bf16[6912,128]{1,0:T(8,128)(2,1)} %take_band.3.own1, f32[6912,128]{1,0:T(8,128)} %get-tuple-element.26.exch0, f32[6912,128]{1,0:T(8,128)} %get-tuple-element.27.part1, ...), custom_call_target="tpu_custom_call", output_to_operand_aliasing={{0}: (6, {})} | custom-call | tf_op jit(solution)/shard_map/add_piece/pallas_call | solution.py:451
  124.8 0.0 collective-permute-done.11
  124.8 0.0 collective-permute-done.10
  124.8 0.0 collective-permute-done.9
  124.9 11.0 %collective-permute-start.12 = (f32[8,128]{1,0:T(8,128)S(1)}, f32[8,128]{1,0:T(8,128)S(1)}, u32[]{:S(2)}, u32[]{:S(2)}) collective-permute-start(f32[8,128]{1,0:T(8,128)S(1)} %add_add_fusion), channel_id=1, source_target_pairs={{2,0},{3,1},{0,2},{1,3},{6,4},{7,5},{4,6},{5,7},{10,8},{11,9},{8,1... | collective-permute-start | bytes 12296 | tf_op jit(solution)/shard_map/ppermute | solution.py:482
  135.9 0.0 collective-permute-done.3.back1
  135.9 4.5 %add_piece.5 = (f32[13824,128]{1,0:T(8,128)}, f32[2,2]{1,0:T(2,128)}) custom-call(bf16[6912,128]{1,0:T(8,128)(2,1)} %take_band.2.own0, bf16[6912,128]{1,0:T(8,128)(2,1)} %take_band.3.own1, f32[6912,128]{1,0:T(8,128)} %get-tuple-element.26.exch0, f32[6912,128]{1,0:T(8,128)} %get-tuple-element.27.part1, ...), custom_call_target="tpu_custom_call", output_to_operand_aliasing={{0}: (6, {})} | custom-call | tf_op jit(solution)/shard_map/add_piece/pallas_call | solution.py:451
  140.3 0.0 collective-permute-done.12
  140.4 0.5 slice.3
  (2 shorter events, 0.0 us)
Async XLA Ops:
  7.8 26.8 %collective-permute-start = (bf16[6912,128]{1,0:T(8,128)(2,1)}, bf16[6912,128]{1,0:T(8,128)(2,1)S(1)}, u32[]{:S(2)}, u32[]{:S(2)}) collective-permute-start(bf16[6912,128]{1,0:T(8,128)(2,1)} %take_band.2.own0), channel_id=1, source_target_pairs={{31,0},{0,1},{1,2},{2,3},{3,4},{4,5},{5,6},{6,7},{7,8},{8,9},{9,10... | collective-permute-start | bytes 5308424 | tf_op jit(solution)/shard_map/ppermute | solution.py:475
  15.4 44.8 %collective-permute-start.1 = (bf16[6912,128]{1,0:T(8,128)(2,1)}, bf16[6912,128]{1,0:T(8,128)(2,1)}, u32[]{:S(2)}, u32[]{:S(2)}) collective-permute-start(bf16[6912,128]{1,0:T(8,128)(2,1)} %take_band.3.own1), channel_id=1, source_target_pairs={{31,0},{0,1},{1,2},{2,3},{3,4},{4,5},{5,6},{6,7},{7,8},{8,9},{9,10... | collective-permute-start | bytes 5308424 | tf_op jit(solution)/shard_map/ppermute | solution.py:475
  34.6 1.3 copy-start.1
  60.1 37.6 %collective-permute-start.2 = (bf16[6912,128]{1,0:T(8,128)(2,1)}, bf16[6912,128]{1,0:T(8,128)(2,1)S(1)}, u32[]{:S(2)}, u32[]{:S(2)}) collective-permute-start(bf16[6912,128]{1,0:T(8,128)(2,1)} %get-tuple-element.25), channel_id=1, source_target_pairs={{1,0},{2,1},{3,2},{4,3},{5,4},{6,5},{7,6},{8,7},{9,8},{10,9},{11,1... | collective-permute-start | bytes 5308424 | tf_op jit(solution)/shard_map/ppermute | solution.py:475
  84.6 27.1 %collective-permute-start.5 = (bf16[2304,128]{1,0:T(8,128)(2,1)}, bf16[2304,128]{1,0:T(8,128)(2,1)}, u32[]{:S(2)}, u32[]{:S(2)}) collective-permute-start(bf16[2304,128]{1,0:T(8,128)(2,1)} %get-tuple-element.30), channel_id=1, source_target_pairs={{1,0},{2,1},{3,2},{4,3},{5,4},{6,5},{7,6},{8,7},{9,8},{10,9},{11,1... | collective-permute-start | bytes 1769480 | tf_op jit(solution)/shard_map/ppermute | solution.py:475
  87.0 33.4 %collective-permute-start.4 = (bf16[2304,128]{1,0:T(8,128)(2,1)}, bf16[2304,128]{1,0:T(8,128)(2,1)}, u32[]{:S(2)}, u32[]{:S(2)}) collective-permute-start(bf16[2304,128]{1,0:T(8,128)(2,1)} %get-tuple-element.29), channel_id=1, source_target_pairs={{1,0},{2,1},{3,2},{4,3},{5,4},{6,5},{7,6},{8,7},{9,8},{10,9},{11,1... | collective-permute-start | bytes 1769480 | tf_op jit(solution)/shard_map/ppermute | solution.py:475
  87.1 48.8 %collective-permute-start.3 = (bf16[2304,128]{1,0:T(8,128)(2,1)}, bf16[2304,128]{1,0:T(8,128)(2,1)}, u32[]{:S(2)}, u32[]{:S(2)}) collective-permute-start(bf16[2304,128]{1,0:T(8,128)(2,1)} %get-tuple-element.28), channel_id=1, source_target_pairs={{1,0},{2,1},{3,2},{4,3},{5,4},{6,5},{7,6},{8,7},{9,8},{10,9},{11,1... | collective-permute-start | bytes 1769480 | tf_op jit(solution)/shard_map/ppermute | solution.py:475
  89.3 3.6 %collective-permute-start.7 = (f32[8,128]{1,0:T(8,128)S(1)}, f32[8,128]{1,0:T(8,128)S(1)}, u32[]{:S(2)}, u32[]{:S(2)}) collective-permute-start(f32[8,128]{1,0:T(8,128)S(1)} %broadcast_multiply_fusion), channel_id=1, source_target_pairs={{4,0},{5,1},{6,2},{7,3},{0,4},{1,5},{2,6},{3,7},{12,8},{13,9},{14,... | collective-permute-start | bytes 12296 | tf_op jit(solution)/shard_map/ppermute | solution.py:482
  92.9 3.0 %collective-permute-start.8 = (f32[8,128]{1,0:T(8,128)S(1)}, f32[8,128]{1,0:T(8,128)S(1)}, u32[]{:S(2)}, u32[]{:S(2)}) collective-permute-start(f32[8,128]{1,0:T(8,128)S(1)} %broadcast_multiply_fusion), channel_id=1, source_target_pairs={{5,0},{4,1},{7,2},{6,3},{1,4},{0,5},{3,6},{2,7},{13,8},{12,9},{15,... | collective-permute-start | bytes 12296 | tf_op jit(solution)/shard_map/ppermute | solution.py:482
  95.9 1.2 collective-permute-start.6
  97.8 1.2 copy-start
  116.1 8.7 %collective-permute-start.11 = (f32[8,128]{1,0:T(8,128)S(1)}, f32[8,128]{1,0:T(8,128)S(1)}, u32[]{:S(2)}, u32[]{:S(2)}) collective-permute-start(f32[8,128]{1,0:T(8,128)S(1)} %add_add_fusion.1), channel_id=1, source_target_pairs={{24,0},{25,1},{26,2},{27,3},{28,4},{29,5},{30,6},{31,7},{16,8},{17... | collective-permute-start | bytes 12296 | tf_op jit(solution)/shard_map/ppermute | solution.py:482
  116.5 8.3 %collective-permute-start.10 = (f32[8,128]{1,0:T(8,128)S(1)}, f32[8,128]{1,0:T(8,128)S(1)}, u32[]{:S(2)}, u32[]{:S(2)}) collective-permute-start(f32[8,128]{1,0:T(8,128)S(1)} %add_add_fusion.1), channel_id=1, source_target_pairs={{16,0},{17,1},{18,2},{19,3},{20,4},{21,5},{22,6},{23,7},{24,8},{25... | collective-permute-start | bytes 12296 | tf_op jit(solution)/shard_map/ppermute | solution.py:482
  116.6 8.3 %collective-permute-start.9 = (f32[8,128]{1,0:T(8,128)S(1)}, f32[8,128]{1,0:T(8,128)S(1)}, u32[]{:S(2)}, u32[]{:S(2)}) collective-permute-start(f32[8,128]{1,0:T(8,128)S(1)} %add_add_fusion.1), channel_id=1, source_target_pairs={{8,0},{9,1},{10,2},{11,3},{12,4},{13,5},{14,6},{15,7},{0,8},{1,9},... | collective-permute-start | bytes 12296 | tf_op jit(solution)/shard_map/ppermute | solution.py:482
  124.9 15.5 %collective-permute-start.12 = (f32[8,128]{1,0:T(8,128)S(1)}, f32[8,128]{1,0:T(8,128)S(1)}, u32[]{:S(2)}, u32[]{:S(2)}) collective-permute-start(f32[8,128]{1,0:T(8,128)S(1)} %add_add_fusion), channel_id=1, source_target_pairs={{2,0},{3,1},{0,2},{1,3},{6,4},{7,5},{4,6},{5,7},{10,8},{11,9},{8,1... | collective-permute-start | bytes 12296 | tf_op jit(solution)/shard_map/ppermute | solution.py:482

commit v4 on v3

--- a/solution.py
+++ b/solution.py
@@ -124,29 +124,51 @@
         dst[pl.ds((2 * i + 1) * F_PITCH, PLANE), :] = value[PLANE:]
 
 
-def band_kernel(raw_ref, pick, out):
-    half = LANES
-    for i in range(raw_ref.shape[0] // (4 * LANES)):
-        top = raw_ref[4 * i * half : (4 * i + 2) * half, :]
-        low = raw_ref[(4 * i + 2) * half : (4 * i + 4) * half, :]
-        rows = dot(pick[...], lanes(top, low)).astype(BF16)
-        out[2 * i * half : (2 * i + 1) * half, :] = rows[:, :half]
-        out[(2 * i + 1) * half : (2 * i + 2) * half, :] = rows[:, half:]
+def rows_of(ref, first, count):
+    at = pl.ds(first, count)
+    return ref.at[at, :] if len(ref.shape) == 2 else ref.at[:, at, :]
+
+
+def copy_rows(src, src_row, dst, dst_row, count, sem):
+    return pltpu.make_async_copy(rows_of(src, src_row, count), rows_of(dst, dst_row, count), sem)
+
+
+def band_kernel(raw, pick, out, raw_v, out_v, load_sems, store_sem):
+    chunks = load_sems.shape[0]
+    rows = out.shape[0] // chunks
+    loads = [
+        copy_rows(raw, 2 * c * rows, raw_v, 2 * c * rows, 2 * rows, load_sems.at[c])
+        for c in range(chunks)
+    ]
+    for load in loads:
+        load.start()
+    for c, load in enumerate(loads):
+        load.wait()
+        for row in range(c * rows, (c + 1) * rows, 2 * LANES):
+            top = raw_v[2 * row : 2 * row + 2 * LANES, :]
+            low = raw_v[2 * row + 2 * LANES : 2 * row + 4 * LANES, :]
+            value = dot(pick[...], lanes(top, low)).astype(BF16)
+            out_v[row : row + LANES, :] = value[:, :LANES]
+            out_v[row + LANES : row + 2 * LANES, :] = value[:, LANES:]
+        copy_rows(out_v, c * rows, out, c * rows, rows, store_sem).start()
+    pltpu.make_async_copy(out_v, out, store_sem).wait()
 
 
 def take_band(raw, p, interpret=False):
     pick = np.zeros((LANES, 2 * LANES), np.float32)
     pick[np.arange(LANES), 2 * np.arange(LANES) + p] = 1.0
-    rows = 768
+    hbm = pl.BlockSpec(memory_space=pl.ANY)
     return pl.pallas_call(
         band_kernel,
-        grid=(ROWS // rows,),
         out_shape=jax.ShapeDtypeStruct((ROWS, LANES), BF16),
-        in_specs=[
-            pl.BlockSpec((2 * rows, LANES), lambda i: (i, 0)),
-            pl.BlockSpec((LANES, 2 * LANES), lambda i: (0, 0)),
+        in_specs=[hbm, pl.BlockSpec(memory_space=pltpu.VMEM)],
+        out_specs=hbm,
+        scratch_shapes=[
+            pltpu.VMEM((2 * ROWS, LANES), BF16),
+            pltpu.VMEM((ROWS, LANES), BF16),
+            pltpu.SemaphoreType.DMA((9,)),
+            pltpu.SemaphoreType.DMA,
         ],
-        out_specs=pl.BlockSpec((rows, LANES), lambda i: (i, 0)),
         compiler_params=VMEM_ALL,
         interpret=interpret,
         name="take_band",
@@ -157,7 +179,7 @@
     for p, own in enumerate((own0, own1)):
         widen_planes(own, wide)
 
-        @pl.loop(0, QUADS // 4)
+        @pl.loop(0, QUADS // 4, unroll=2)
         def _(q):
             split_rows(wide, sel, out.at[p], 4 * q, 4)
 
@@ -193,14 +215,14 @@
 
     widen_planes(par_ref, par_f)
 
-    @pl.loop(0, QUADS // 4)
+    @pl.loop(0, QUADS // 4, unroll=2)
     def _(q):
         split_rows(par_f, sel, par_u, 4 * q, 4)
 
     half_y = G * Y_PITCH
     loads[0].wait()
 
-    @pl.loop(0, G // 2, unroll=4)
+    @pl.loop(0, G // 2, unroll=8)
     def _(i):
         density = []
         for e in range(2):
@@ -230,7 +252,7 @@
 
     many = 5
 
-    @pl.loop(0, KPAD // many)
+    @pl.loop(0, KPAD // many, unroll=2)
     def _(m):
         at = pl.ds(pl.multiple_of(m * many * G, 16), many * G)
         factor = kern_v[at, :]
@@ -245,7 +267,7 @@
                 row = (many * m + i) * Z_PITCH
                 z[part, pl.ds(row, G), :] = value[i * G : (i + 1) * G]
 
-    @pl.loop(0, G // 4, unroll=3)
+    @pl.loop(0, G // 4, unroll=6)
     def _(four):
         parts = []
         for e in range(4):
@@ -264,7 +286,7 @@
             at = (4 * four + e) * W_PITCH
             yw[pl.ds(at, 2 * G), :] = out[:, e * LANES : (e + 1) * LANES]
 
-    @pl.loop(0, G // 4, unroll=3)
+    @pl.loop(0, G // 4, unroll=6)
     def _(four):
         parts = []
         for e in range(4):
@@ -295,7 +317,7 @@
     block_rows = planes * QUADS
     scale = F32(1.0 / NGRID)
 
-    @pl.loop(0, G // planes)
+    @pl.loop(0, G // planes, unroll=2)
     def _(ch):
         at = pl.multiple_of(ch * block_rows, 16)
         low = x34[pl.ds(at, block_rows), :]
@@ -375,39 +397,70 @@
     )(own0, own1, own_u, kern, partner, energy, *tables)
 
 
-BLOCK = 576
-
-
-def add_products(gram_ref, column, own0, own1, exchange):
-    for i, own in enumerate((own0, own1)):
-        product = (own[...].astype(F32) * exchange).reshape(-1, 8, LANES)
+def add_products(gram_ref, column, own, exchange):
+    for i in range(2):
+        product = (own[i].astype(F32) * exchange).reshape(-1, 8, LANES)
         gram_ref[i, column] += jnp.sum(product, axis=0)
 
 
-def first_sum_kernel(own0, own1, first, second, back0, exch0, part1, gram_ref):
-    @pl.when(pl.program_id(0) == 0)
-    def _():
-        gram_ref[...] = jnp.zeros_like(gram_ref)
-
-    exchange = first[0] + second[0] + back0[...].astype(F32)
-    exch0[...] = exchange
-    part1[...] = first[1] + second[1]
-    add_products(gram_ref, 0, own0, own1, exchange)
+def first_sum_kernel(
+    own0, own1, first, second, back0, exch0, part1, gram_ref,
+    own_v, first_v, second_v, back_v, exch_v, part_v, load_sems, store_sems,
+):
+    chunks = load_sems.shape[0]
+    rows = ROWS // chunks
+    arrays = [(own0, own_v.at[0]), (own1, own_v.at[1]), (first, first_v), (second, second_v), (back0, back_v)]
+
+    def loads(c):
+        return [
+            copy_rows(src, c * rows, dst, c * rows, rows, load_sems.at[c, i])
+            for i, (src, dst) in enumerate(arrays)
+        ]
+
+    for c in range(chunks):
+        for load in loads(c):
+            load.start()
+    gram_ref[...] = jnp.zeros_like(gram_ref)
+
+    @pl.loop(0, chunks)
+    def _(c):
+        for load in loads(c):
+            load.wait()
+        at = pl.ds(pl.multiple_of(c * rows, 16), rows)
+        exchange = first_v[0, at, :] + second_v[0, at, :] + back_v[at, :].astype(F32)
+        exch_v[at, :] = exchange
+        part_v[at, :] = first_v[1, at, :] + second_v[1, at, :]
+        add_products(gram_ref, 0, [own_v[i, at, :] for i in range(2)], exchange)
+        copy_rows(exch_v, c * rows, exch0, c * rows, rows, store_sems.at[0]).start()
+        copy_rows(part_v, c * rows, part1, c * rows, rows, store_sems.at[1]).start()
+
+    pltpu.make_async_copy(exch_v, exch0, store_sems.at[0]).wait()
+    pltpu.make_async_copy(part_v, part1, store_sems.at[1]).wait()
 
 
 def first_sum(own, first, second, back0, interpret=False):
-    flat = pl.BlockSpec((BLOCK, LANES), lambda i: (i, 0))
-    both = pl.BlockSpec((2, BLOCK, LANES), lambda i: (0, i, 0))
+    hbm = pl.BlockSpec(memory_space=pl.ANY)
+    chunks = 12
+    band = (ROWS, LANES)
     return pl.pallas_call(
         first_sum_kernel,
-        grid=(ROWS // BLOCK,),
         out_shape=(
-            jax.ShapeDtypeStruct((ROWS, LANES), F32),
-            jax.ShapeDtypeStruct((ROWS, LANES), F32),
+            jax.ShapeDtypeStruct(band, F32),
+            jax.ShapeDtypeStruct(band, F32),
             jax.ShapeDtypeStruct((2, 2, 8, LANES), F32),
         ),
-        in_specs=[flat, flat, both, both, flat],
-        out_specs=(flat, flat, pl.BlockSpec((2, 2, 8, LANES), lambda i: (0, 0, 0, 0))),
+        in_specs=[hbm] * 5,
+        out_specs=(hbm, hbm, pl.BlockSpec(memory_space=pltpu.VMEM)),
+        scratch_shapes=[
+            pltpu.VMEM((2, *band), BF16),
+            pltpu.VMEM((2, *band), F32),
+            pltpu.VMEM((2, *band), F32),
+            pltpu.VMEM(band, BF16),
+            pltpu.VMEM(band, F32),
+            pltpu.VMEM(band, F32),
+            pltpu.SemaphoreType.DMA((chunks, 5)),
+            pltpu.SemaphoreType.DMA((2,)),
+        ],
         compiler_params=VMEM_ALL,
         interpret=interpret,
         name="first_sum",
@@ -415,54 +468,76 @@
 
 
 def piece_kernel(piece, own0, own1, exch0, part1, back1, gram_in, *rest):
-    out_ref, gram_out, gram_ref = rest[-3:]
-    step = pl.program_id(0)
-
-    @pl.when(step == 0)
-    def _():
-        gram_ref[...] = gram_in[...]
-
-    exchange = part1[...] + back1[...].astype(F32)
-    out_ref[pl.ds(0, BLOCK, stride=2), :] = exch0[...]
-    out_ref[pl.ds(1, BLOCK, stride=2), :] = exchange
-    add_products(gram_ref, 1, own0, own1, exchange)
-
-    @pl.when(step == pl.num_programs(0) - 1)
-    def _():
-        if piece < PIECES - 1:
-            gram_out[...] = gram_ref[...]
-        else:
-            row = lax.broadcasted_iota(jnp.int32, (2, 2), 0)
-            column = lax.broadcasted_iota(jnp.int32, (2, 2), 1)
-            value = jnp.zeros((2, 2), F32)
-            for i in range(2):
-                for j in range(2):
-                    entry = jnp.sum(gram_ref[i, j]) * F32(1.0 / NGRID)
-                    value = jnp.where((row == i) & (column == j), entry, value)
-            gram_out[...] = value
+    out, gram_out, own_v, exch_v, part_v, back_v, out_v, gram_ref, load_sems, store_sem = rest[-10:]
+    chunks = load_sems.shape[0]
+    size = back1.shape[0]
+    rows = size // chunks
+    base = piece * size
+    arrays = [
+        (own0, own_v.at[0], base), (own1, own_v.at[1], base),
+        (exch0, exch_v, base), (part1, part_v, base), (back1, back_v, 0),
+    ]
+
+    def loads(c):
+        return [
+            copy_rows(src, start + c * rows, dst, c * rows, rows, load_sems.at[c, i])
+            for i, (src, dst, start) in enumerate(arrays)
+        ]
+
+    for c in range(chunks):
+        for load in loads(c):
+            load.start()
+    gram_ref[...] = gram_in[...]
+
+    @pl.loop(0, chunks)
+    def _(c):
+        for load in loads(c):
+            load.wait()
+        at = pl.ds(pl.multiple_of(c * rows, 16), rows)
+        exchange = part_v[at, :] + back_v[at, :].astype(F32)
+        out_v[pl.ds(2 * c * rows, rows, stride=2), :] = exch_v[at, :]
+        out_v[pl.ds(2 * c * rows + 1, rows, stride=2), :] = exchange
+        add_products(gram_ref, 1, [own_v[i, at, :] for i in range(2)], exchange)
+        copy_rows(out_v, 2 * c * rows, out, 2 * (base + c * rows), 2 * rows, store_sem).start()
+
+    if piece < PIECES - 1:
+        gram_out[...] = gram_ref[...]
+    else:
+        row = lax.broadcasted_iota(jnp.int32, (2, 2), 0)
+        column = lax.broadcasted_iota(jnp.int32, (2, 2), 1)
+        value = jnp.zeros((2, 2), F32)
+        for i in range(2):
+            for j in range(2):
+                entry = jnp.sum(gram_ref[i, j]) * F32(1.0 / NGRID)
+                value = jnp.where((row == i) & (column == j), entry, value)
+        gram_out[...] = value
+    copy_rows(out_v, 0, out, 2 * base, 2 * size, store_sem).wait()
 
 
 def add_piece(piece, own, exch0, part1, back1, gram, out, interpret=False):
-    steps = ROWS // PIECES // BLOCK
-    here = pl.BlockSpec((BLOCK, LANES), lambda i: (piece * steps + i, 0))
-    gram_spec = pl.BlockSpec((2, 2, 8, LANES), lambda i: (0, 0, 0, 0))
     last = piece == PIECES - 1
     earlier = [] if out is None else [out]
+    hbm = pl.BlockSpec(memory_space=pl.ANY)
+    vmem = pl.BlockSpec(memory_space=pltpu.VMEM)
+    band = back1.shape
     return pl.pallas_call(
         functools.partial(piece_kernel, piece),
-        grid=(steps,),
         out_shape=(
             jax.ShapeDtypeStruct((2 * ROWS, LANES), F32),
             jax.ShapeDtypeStruct((2, 2) if last else gram.shape, F32),
         ),
-        in_specs=[here] * 4
-        + [pl.BlockSpec((BLOCK, LANES), lambda i: (i, 0)), gram_spec]
-        + [pl.BlockSpec(memory_space=pl.ANY)] * len(earlier),
-        out_specs=(
-            pl.BlockSpec((2 * BLOCK, LANES), lambda i: (piece * steps + i, 0)),
-            pl.BlockSpec((2, 2), lambda i: (0, 0)) if last else gram_spec,
-        ),
-        scratch_shapes=[pltpu.VMEM((2, 2, 8, LANES), F32)],
+        in_specs=[hbm] * 5 + [vmem] + [hbm] * len(earlier),
+        out_specs=(hbm, vmem),
+        scratch_shapes=[
+            pltpu.VMEM((2, *band), BF16),
+            pltpu.VMEM(band, F32),
+            pltpu.VMEM(band, F32),
+            pltpu.VMEM(band, BF16),
+            pltpu.VMEM((2 * band[0], LANES), F32),
+            pltpu.VMEM((2, 2, 8, LANES), F32),
+            pltpu.SemaphoreType.DMA((4, 5)),
+            pltpu.SemaphoreType.DMA,
+        ],
         input_output_aliases={6: 0} if earlier else {},
         compiler_params=VMEM_ALL,
         interpret=interpret,
@@ -475,19 +550,20 @@
     return lax.ppermute(block, axis, [((i - distance) % size, i) for i in range(size)])
 
 
-def exchange_with(value, axis, bits):
+def send_to(value, axis, bits):
     size = lax.axis_size(axis)
-    got = {0: value}
-    for flip in sorted({bits[0], bits[-1], sum(bits)}):
-        got[flip] = lax.ppermute(value, axis, [(i ^ flip, i) for i in range(size)])
-    low = got[0] + got[bits[0]]
-    if len(bits) == 1:
-        return low
-    return low + (got[bits[1]] + got[sum(bits)])
-
-
-def after(value, other):
-    return lax.optimization_barrier((value, other))[0]
+    flips = sorted({bits[0], bits[-1], sum(bits)})
+    return [lax.ppermute(value, axis, [(i ^ flip, i) for i in range(size)]) for flip in flips]
+
+
+def add_up(value, got):
+    if len(got) == 1:
+        return value + got[0]
+    return (value + got[0]) + (got[1] + got[2])
+
+
+def after(values, other):
+    return lax.optimization_barrier((values, other))[0]
 
 
 def per_device(orbitals):
@@ -505,7 +581,6 @@
     back1 = [from_behind(piece, "band", -1) for piece in sent1]
     energy = energy * F32(1.0 / (size * orbitals.shape[0] * 2))
 
-    exch0, part1, gram = first_sum(own, first, second, back0)
     exchange = None
     if size & (size - 1):
         energy = lax.psum(energy, "band")
@@ -514,12 +589,16 @@
         bits = [1 << b for b in range(size.bit_length() - 1)]
         rest = [b for b in bits if b != 2]
         groups = [rest[i : i + 2] for i in range(0, len(rest), 2)] + [[b] for b in bits if b == 2]
+    got = send_to(energy, "band", groups.pop(0)) if groups else None
+    exch0, part1, gram = first_sum(own, first, second, back0)
     for piece in range(PIECES):
-        if groups:
-            energy = exchange_with(after(energy, gram) if piece else energy, "band", groups.pop(0))
+        if got is not None:
+            energy = add_up(energy, after(got, gram))
+            got = send_to(energy, "band", groups.pop(0)) if groups else None
         exchange, gram = add_piece(piece, own, exch0, part1, back1[piece], gram, exchange)
-    for bits in groups:
-        energy = exchange_with(energy, "band", bits)
+    while got is not None:
+        energy = add_up(energy, after(got, gram))
+        got = send_to(energy, "band", groups.pop(0)) if groups else None
     exchange = exchange.reshape(ROWS, 2, LANES).transpose(1, 0, 2).reshape(2, NGRID)
     return exchange, gram, energy[0, 0]
 

time: 142 us -> 117 us (0.82)
  Pallas kernels: 96.9 us -> 82.3 us
  starting transfers between devices: 22.5 us -> 14.4 us
    ppermute x7, starting transfers between devices: 15.4 us -> 7.14 us  [send_to(): lax.ppermute(value, axis, [(i ^ flip, i) for i in range(size)])]
    pallas_call x2, Pallas kernels: 48.7 us -> 41.5 us  [pair_terms(): pl.pallas_call(functools.partial(pairs_kernel, pieces), out_shape=(jax.Sh...]
    pallas_call x6, Pallas kernels: 40.3 us -> 33.8 us  [the longest x3 13.7 us: add_piece(): pl.pallas_call(functools.partial(piece_kernel, piece), out_shape=(jax.Sha...]
    ppermute x7, waiting for transfers between devices: 7.81 us -> 3.05 us  [send_to(): lax.ppermute(value, axis, [(i ^ flip, i) for i in range(size)])]
    ppermute x6, waiting for transfers between devices: 8.66 us -> 12 us  [from_behind(): lax.ppermute(block, axis, [((i - distance) % size, i) for i in range(size)])]
  transfers between devices with their start and end apart: 13 -> 13, of which waited for: 4 -> 2; matrix products, arithmetic and copies ran while one was open for 1% -> 1% of each run, Pallas kernels for 64% -> 67%
where the time goes in v4:
time: 117 us; the launch traced here: 116 us
  Pallas kernels  82.3 us (70%)
  waiting for transfers between devices  15.1 us (13%)
  starting transfers between devices  14.4 us (12%)
  local copies, waits for them, and re-layouts  2.88 us (2%)
    pallas_call x2, Pallas kernels, pair_terms(): pl.pallas_call(functools.partial(pairs_kernel, pieces), out_shape=(jax.Sh...  41.5 us
    pallas_call x3, Pallas kernels, add_piece(): pl.pallas_call(functools.partial(piece_kernel, piece), out_shape=(jax.Sha...  13.7 us
    ppermute x6, waiting for transfers between devices, from_behind(): lax.ppermute(block, axis, [((i - distance) % size, i) for i in range(size)])  12 us
    pallas_call x1, Pallas kernels, first_sum(): pl.pallas_call(first_sum_kernel, out_shape=(jax.ShapeDtypeStruct(band, F3...  10.7 us
    pallas_call x2, Pallas kernels, take_band(): pl.pallas_call(band_kernel, out_shape=jax.ShapeDtypeStruct((ROWS, LANES),...  9.34 us
    ppermute x6, starting transfers between devices, from_behind(): lax.ppermute(block, axis, [((i - distance) % size, i) for i in range(size)])  7.21 us
    ppermute x7, starting transfers between devices, send_to(): lax.ppermute(value, axis, [(i ^ flip, i) for i in range(size)])  7.14 us
    pallas_call x1, Pallas kernels, padded_rows(): pl.pallas_call(rows_kernel, out_shape=jax.ShapeDtypeStruct((2, G, G, LANE...  7 us
  transfers between devices with their start and end apart: 13, of which 2 were waited for; matrix products, arithmetic and copies ran while one was open for 1% of the time, Pallas kernels for 67%

profile of v4, /device:TPU:0, one launch (start us, length us, event | category | flops | bytes accessed | tf_op | source)
XLA Modules:
  0.0 116.1 jit_solution(7799616738671748823)
XLA Ops:
  0.6 4.7 %take_band.2.own0 = bf16[6912,128]{1,0:T(8,128)(2,1)} custom-call(bf16[13824,128]{1,0:T(8,128)(2,1)} %bitcast.12, bf16[128,256]{1,0:T(8,128)(2,1)} %constant.24.clone.pick), custom_call_target="tpu_custom_call" | custom-call | tf_op jit(solution)/shard_map/take_band/pallas_call | solution.py:161
  5.3 0.5 collective-permute-start
  5.8 4.7 %take_band.3.own1 = bf16[6912,128]{1,0:T(8,128)(2,1)} custom-call(bf16[13824,128]{1,0:T(8,128)(2,1)} %bitcast.13, bf16[128,256]{1,0:T(8,128)(2,1)} %constant.25.clone.pick), custom_call_target="tpu_custom_call" | custom-call | tf_op jit(solution)/shard_map/take_band/pallas_call | solution.py:161
  10.5 2.7 %collective-permute-start.1 = (bf16[6912,128]{1,0:T(8,128)(2,1)}, bf16[6912,128]{1,0:T(8,128)(2,1)}, u32[]{:S(2)}, u32[]{:S(2)}) collective-permute-start(bf16[6912,128]{1,0:T(8,128)(2,1)} %take_band.3.own1), channel_id=1, source_target_pairs={{31,0},{0,1},{1,2},{2,3},{3,4},{4,5},{5,6},{6,7},{7,8},{8,9},{9,10... | collective-permute-start | bytes 5308424 | tf_op jit(solution)/shard_map/ppermute | solution.py:550
  13.1 7.0 %padded_rows.1.own_u = bf16[2,96,96,128]{3,2,1,0:T(8,128)(2,1)} custom-call(bf16[6912,128]{1,0:T(8,128)(2,1)} %take_band.2.own0, bf16[6912,128]{1,0:T(8,128)(2,1)} %take_band.3.own1, bf16[2,256,256]{2,1,0:T(8,128)(2,1)} %constant.26.clone.sel), custom_call_target="tpu_custom_call" | custom-call | tf_op jit(solution)/shard_map/padded_rows/pallas_call | solution.py:189
  20.1 12.0 %collective-permute-done.par_ref = bf16[6912,128]{1,0:T(8,128)(2,1)S(1)} collective-permute-done((bf16[6912,128]{1,0:T(8,128)(2,1)}, bf16[6912,128]{1,0:T(8,128)(2,1)S(1)}, u32[]{:S(2)}, u32[]{:S(2)}) %collective-permute-start) | collective-permute-done | bytes 1769504 | tf_op jit(solution)/shard_map/ppermute | solution.py:550
  32.1 0.0 copy-start.2
  32.1 0.6 broadcast_in_dim.3.energy_in
  32.8 0.6 copy-done.2
  33.4 20.7 %pair_terms.2 = (f32[2,6912,128]{2,1,0:T(8,128)}, bf16[6912,128]{1,0:T(8,128)(2,1)}, f32[8,128]{1,0:T(8,128)}) custom-call(bf16[6912,128]{1,0:T(8,128)(2,1)} %take_band.2.own0, bf16[6912,128]{1,0:T(8,128)(2,1)} %take_band.3.own1, bf16[2,96,96,128]{3,2,1,0:T(8,128)(2,1)} %padded_rows.1.own_u, f32[4800,128]{1,0:T(8,128)} %constant.27.clone.kern, ...), custom_call_target="tpu_custom_call" | custom-call | flops 20000000000 | bytes 20000000 | tf_op jit(solution)/shard_map/pair_terms/pallas_call | solution.py:366
  54.1 0.1 collective-permute-start.2
  54.1 0.0 collective-permute-done.1.par_ref
  54.2 20.8 %pair_terms.3 = (f32[2,6912,128]{2,1,0:T(8,128)}, bf16[2304,128]{1,0:T(8,128)(2,1)}, bf16[2304,128]{1,0:T(8,128)(2,1)}, bf16[2304,128]{1,0:T(8,128)(2,1)}, f32[8,128]{1,0:T(8,128)}) custom-call(bf16[6912,128]{1,0:T(8,128)(2,1)} %take_band.2.own0, bf16[6912,128]{1,0:T(8,128)(2,1)} %take_band.3.own1, bf16[2,96,96,128]{3,2,1,0:T(8,128)(2,1)} %padded_rows.1.own_u, ...), custom_call_target="tpu_custom_call" | custom-call | flops 20000000000 | bytes 20000000 | tf_op jit(solution)/shard_map/pair_terms/pallas_call | solution.py:366
  75.0 2.4 %collective-permute-start.5 = (bf16[2304,128]{1,0:T(8,128)(2,1)}, bf16[2304,128]{1,0:T(8,128)(2,1)}, u32[]{:S(2)}, u32[]{:S(2)}) collective-permute-start(bf16[2304,128]{1,0:T(8,128)(2,1)} %get-tuple-element.35), channel_id=1, source_target_pairs={{1,0},{2,1},{3,2},{4,3},{5,4},{6,5},{7,6},{8,7},{9,8},{10,9},{11,1... | collective-permute-start | bytes 1769480 | tf_op jit(solution)/shard_map/ppermute | solution.py:550
  77.4 0.1 collective-permute-start.3
  77.5 1.5 %collective-permute-start.4 = (bf16[2304,128]{1,0:T(8,128)(2,1)}, bf16[2304,128]{1,0:T(8,128)(2,1)}, u32[]{:S(2)}, u32[]{:S(2)}) collective-permute-start(bf16[2304,128]{1,0:T(8,128)(2,1)} %get-tuple-element.34), channel_id=1, source_target_pairs={{1,0},{2,1},{3,2},{4,3},{5,4},{6,5},{7,6},{8,7},{9,8},{10,9},{11,1... | collective-permute-start | bytes 1769480 | tf_op jit(solution)/shard_map/ppermute | solution.py:550
  79.0 0.7 broadcast_multiply_fusion
  79.7 0.0 collective-permute-start.8
  79.7 3.0 %collective-permute-done.8 = f32[8,128]{1,0:T(8,128)S(1)} collective-permute-done((f32[8,128]{1,0:T(8,128)S(1)}, f32[8,128]{1,0:T(8,128)S(1)}, u32[]{:S(2)}, u32[]{:S(2)}) %collective-permute-start.8) | collective-permute-done | bytes 4128 | tf_op jit(solution)/shard_map/ppermute | solution.py:556
  82.7 0.0 collective-permute-start.7
  82.7 0.0 collective-permute-done.2.back0
  82.7 0.0 copy-start
  82.7 0.1 collective-permute-start.6
  82.8 1.1 copy-done
  83.9 0.0 copy-start.1
  83.9 10.7 %first_sum.1 = (f32[6912,128]{1,0:T(8,128)}, f32[6912,128]{1,0:T(8,128)}, f32[2,2,8,128]{3,2,1,0:T(8,128)}) custom-call(bf16[6912,128]{1,0:T(8,128)(2,1)} %take_band.2.own0, bf16[6912,128]{1,0:T(8,128)(2,1)} %take_band.3.own1, f32[2,6912,128]{2,1,0:T(8,128)} %get-tuple-element.27.first, f32[2,6912,128]{2,1,0:T(8,128)} %get-tuple-element.29.second, ...), custom_call_target="tpu_custom_call" | custom-call | tf_op jit(solution)/shard_map/first_sum/pallas_call | solution.py:445
  94.7 0.0 collective-permute-done.7
  94.7 0.0 collective-permute-done.6
  94.7 0.0 copy-done.1
  94.7 2.0 %collective-permute-start.11 = (f32[8,128]{1,0:T(8,128)S(1)}, f32[8,128]{1,0:T(8,128)S(1)}, u32[]{:S(2)}, u32[]{:S(2)}) collective-permute-start(f32[8,128]{1,0:T(8,128)S(1)} %add_add_fusion.1), channel_id=1, source_target_pairs={{24,0},{25,1},{26,2},{27,3},{28,4},{29,5},{30,6},{31,7},{16,8},{17... | collective-permute-start | bytes 12296 | tf_op jit(solution)/shard_map/ppermute | solution.py:556
  96.8 0.0 collective-permute-start.10
  96.8 0.0 collective-permute-done.5.back1
  96.8 2.4 %collective-permute-start.9 = (f32[8,128]{1,0:T(8,128)S(1)}, f32[8,128]{1,0:T(8,128)S(1)}, u32[]{:S(2)}, u32[]{:S(2)}) collective-permute-start(f32[8,128]{1,0:T(8,128)S(1)} %add_add_fusion.1), channel_id=1, source_target_pairs={{8,0},{9,1},{10,2},{11,3},{12,4},{13,5},{14,6},{15,7},{0,8},{1,9},... | collective-permute-start | bytes 12296 | tf_op jit(solution)/shard_map/ppermute | solution.py:556
  99.2 4.6 %add_piece.3 = (f32[13824,128]{1,0:T(8,128)}, f32[2,2,8,128]{3,2,1,0:T(8,128)}) custom-call(bf16[6912,128]{1,0:T(8,128)(2,1)} %take_band.2.own0, bf16[6912,128]{1,0:T(8,128)(2,1)} %take_band.3.own1, f32[6912,128]{1,0:T(8,128)} %get-tuple-element.31.exch0, f32[6912,128]{1,0:T(8,128)} %get-tuple-element.32.part1, ...), custom_call_target="tpu_custom_call" | custom-call | tf_op jit(solution)/shard_map/add_piece/pallas_call | solution.py:523
  103.8 0.0 collective-permute-done.11
  103.8 0.0 collective-permute-done.10
  103.8 0.0 collective-permute-done.9
  103.8 2.6 %collective-permute-start.12 = (f32[8,128]{1,0:T(8,128)S(1)}, f32[8,128]{1,0:T(8,128)S(1)}, u32[]{:S(2)}, u32[]{:S(2)}) collective-permute-start(f32[8,128]{1,0:T(8,128)S(1)} %add_add_fusion), channel_id=1, source_target_pairs={{2,0},{3,1},{0,2},{1,3},{6,4},{7,5},{4,6},{5,7},{10,8},{11,9},{8,1... | collective-permute-start | bytes 12296 | tf_op jit(solution)/shard_map/ppermute | solution.py:556
  106.4 0.0 collective-permute-done.4.back1
  106.4 4.6 %add_piece.4 = (f32[13824,128]{1,0:T(8,128)}, f32[2,2,8,128]{3,2,1,0:T(8,128)}) custom-call(bf16[6912,128]{1,0:T(8,128)(2,1)} %take_band.2.own0, bf16[6912,128]{1,0:T(8,128)(2,1)} %take_band.3.own1, f32[6912,128]{1,0:T(8,128)} %get-tuple-element.31.exch0, f32[6912,128]{1,0:T(8,128)} %get-tuple-element.32.part1, ...), custom_call_target="tpu_custom_call", output_to_operand_aliasing={{0}: (6, {})} | custom-call | tf_op jit(solution)/shard_map/add_piece/pallas_call | solution.py:523
  111.0 0.0 collective-permute-done.3.back1
  111.0 4.5 %add_piece.5 = (f32[13824,128]{1,0:T(8,128)}, f32[2,2]{1,0:T(2,128)}) custom-call(bf16[6912,128]{1,0:T(8,128)(2,1)} %take_band.2.own0, bf16[6912,128]{1,0:T(8,128)(2,1)} %take_band.3.own1, f32[6912,128]{1,0:T(8,128)} %get-tuple-element.31.exch0, f32[6912,128]{1,0:T(8,128)} %get-tuple-element.32.part1, ...), custom_call_target="tpu_custom_call", output_to_operand_aliasing={{0}: (6, {})} | custom-call | tf_op jit(solution)/shard_map/add_piece/pallas_call | solution.py:523
  115.6 0.0 collective-permute-done.12
  115.6 0.5 slice.3
  (3 shorter events, 0.0 us)
Async XLA Ops:
  5.3 26.8 %collective-permute-start = (bf16[6912,128]{1,0:T(8,128)(2,1)}, bf16[6912,128]{1,0:T(8,128)(2,1)S(1)}, u32[]{:S(2)}, u32[]{:S(2)}) collective-permute-start(bf16[6912,128]{1,0:T(8,128)(2,1)} %take_band.2.own0), channel_id=1, source_target_pairs={{31,0},{0,1},{1,2},{2,3},{3,4},{4,5},{5,6},{6,7},{7,8},{8,9},{9,10... | collective-permute-start | bytes 5308424 | tf_op jit(solution)/shard_map/ppermute | solution.py:550
  10.5 43.7 %collective-permute-start.1 = (bf16[6912,128]{1,0:T(8,128)(2,1)}, bf16[6912,128]{1,0:T(8,128)(2,1)}, u32[]{:S(2)}, u32[]{:S(2)}) collective-permute-start(bf16[6912,128]{1,0:T(8,128)(2,1)} %take_band.3.own1), channel_id=1, source_target_pairs={{31,0},{0,1},{1,2},{2,3},{3,4},{4,5},{5,6},{6,7},{7,8},{8,9},{9,10... | collective-permute-start | bytes 5308424 | tf_op jit(solution)/shard_map/ppermute | solution.py:550
  32.1 1.2 %copy-start.2 = (bf16[6912,128]{1,0:T(8,128)(2,1)}, bf16[6912,128]{1,0:T(8,128)(2,1)S(1)}, u32[]{:S(2)}) copy-start(bf16[6912,128]{1,0:T(8,128)(2,1)S(1)} %collective-permute-done.par_ref) | copy-start | bytes 5308420
  54.1 28.6 %collective-permute-start.2 = (bf16[6912,128]{1,0:T(8,128)(2,1)}, bf16[6912,128]{1,0:T(8,128)(2,1)S(1)}, u32[]{:S(2)}, u32[]{:S(2)}) collective-permute-start(bf16[6912,128]{1,0:T(8,128)(2,1)} %get-tuple-element.30), channel_id=1, source_target_pairs={{1,0},{2,1},{3,2},{4,3},{5,4},{6,5},{7,6},{8,7},{9,8},{10,9},{11,1... | collective-permute-start | bytes 5308424 | tf_op jit(solution)/shard_map/ppermute | solution.py:550
  75.0 21.8 %collective-permute-start.5 = (bf16[2304,128]{1,0:T(8,128)(2,1)}, bf16[2304,128]{1,0:T(8,128)(2,1)}, u32[]{:S(2)}, u32[]{:S(2)}) collective-permute-start(bf16[2304,128]{1,0:T(8,128)(2,1)} %get-tuple-element.35), channel_id=1, source_target_pairs={{1,0},{2,1},{3,2},{4,3},{5,4},{6,5},{7,6},{8,7},{9,8},{10,9},{11,1... | collective-permute-start | bytes 1769480 | tf_op jit(solution)/shard_map/ppermute | solution.py:550
  77.4 33.6 %collective-permute-start.3 = (bf16[2304,128]{1,0:T(8,128)(2,1)}, bf16[2304,128]{1,0:T(8,128)(2,1)}, u32[]{:S(2)}, u32[]{:S(2)}) collective-permute-start(bf16[2304,128]{1,0:T(8,128)(2,1)} %get-tuple-element.33), channel_id=1, source_target_pairs={{1,0},{2,1},{3,2},{4,3},{5,4},{6,5},{7,6},{8,7},{9,8},{10,9},{11,1... | collective-permute-start | bytes 1769480 | tf_op jit(solution)/shard_map/ppermute | solution.py:550
  77.5 28.9 %collective-permute-start.4 = (bf16[2304,128]{1,0:T(8,128)(2,1)}, bf16[2304,128]{1,0:T(8,128)(2,1)}, u32[]{:S(2)}, u32[]{:S(2)}) collective-permute-start(bf16[2304,128]{1,0:T(8,128)(2,1)} %get-tuple-element.34), channel_id=1, source_target_pairs={{1,0},{2,1},{3,2},{4,3},{5,4},{6,5},{7,6},{8,7},{9,8},{10,9},{11,1... | collective-permute-start | bytes 1769480 | tf_op jit(solution)/shard_map/ppermute | solution.py:550
  79.7 3.0 %collective-permute-start.8 = (f32[8,128]{1,0:T(8,128)S(1)}, f32[8,128]{1,0:T(8,128)S(1)}, u32[]{:S(2)}, u32[]{:S(2)}) collective-permute-start(f32[8,128]{1,0:T(8,128)S(1)} %broadcast_multiply_fusion), channel_id=1, source_target_pairs={{5,0},{4,1},{7,2},{6,3},{1,4},{0,5},{3,6},{2,7},{13,8},{12,9},{15,... | collective-permute-start | bytes 12296 | tf_op jit(solution)/shard_map/ppermute | solution.py:556
  82.7 12.0 %collective-permute-start.7 = (f32[8,128]{1,0:T(8,128)S(1)}, f32[8,128]{1,0:T(8,128)S(1)}, u32[]{:S(2)}, u32[]{:S(2)}) collective-permute-start(f32[8,128]{1,0:T(8,128)S(1)} %broadcast_multiply_fusion), channel_id=1, source_target_pairs={{4,0},{5,1},{6,2},{7,3},{0,4},{1,5},{2,6},{3,7},{12,8},{13,9},{14,... | collective-permute-start | bytes 12296 | tf_op jit(solution)/shard_map/ppermute | solution.py:556
  82.7 1.2 %copy-start = (bf16[6912,128]{1,0:T(8,128)(2,1)}, bf16[6912,128]{1,0:T(8,128)(2,1)S(1)}, u32[]{:S(2)}) copy-start(bf16[6912,128]{1,0:T(8,128)(2,1)S(1)} %collective-permute-done.2.back0) | copy-start | bytes 5308420
  82.7 12.0 %collective-permute-start.6 = (f32[8,128]{1,0:T(8,128)S(1)}, f32[8,128]{1,0:T(8,128)S(1)}, u32[]{:S(2)}, u32[]{:S(2)}) collective-permute-start(f32[8,128]{1,0:T(8,128)S(1)} %broadcast_multiply_fusion), channel_id=1, source_target_pairs={{1,0},{0,1},{3,2},{2,3},{5,4},{4,5},{7,6},{6,7},{9,8},{8,9},{11,10... | collective-permute-start | bytes 12296 | tf_op jit(solution)/shard_map/ppermute | solution.py:556
  83.9 10.8 %copy-start.1 = (f32[8,128]{1,0:T(8,128)S(1)}, f32[8,128]{1,0:T(8,128)}, u32[]{:S(2)}) copy-start(f32[8,128]{1,0:T(8,128)} %get-tuple-element.43) | copy-start | bytes 12292
  94.7 9.0 %collective-permute-start.11 = (f32[8,128]{1,0:T(8,128)S(1)}, f32[8,128]{1,0:T(8,128)S(1)}, u32[]{:S(2)}, u32[]{:S(2)}) collective-permute-start(f32[8,128]{1,0:T(8,128)S(1)} %add_add_fusion.1), channel_id=1, source_target_pairs={{24,0},{25,1},{26,2},{27,3},{28,4},{29,5},{30,6},{31,7},{16,8},{17... | collective-permute-start | bytes 12296 | tf_op jit(solution)/shard_map/ppermute | solution.py:556
  96.8 7.0 %collective-permute-start.10 = (f32[8,128]{1,0:T(8,128)S(1)}, f32[8,128]{1,0:T(8,128)S(1)}, u32[]{:S(2)}, u32[]{:S(2)}) collective-permute-start(f32[8,128]{1,0:T(8,128)S(1)} %add_add_fusion.1), channel_id=1, source_target_pairs={{16,0},{17,1},{18,2},{19,3},{20,4},{21,5},{22,6},{23,7},{24,8},{25... | collective-permute-start | bytes 12296 | tf_op jit(solution)/shard_map/ppermute | solution.py:556
  96.8 7.0 %collective-permute-start.9 = (f32[8,128]{1,0:T(8,128)S(1)}, f32[8,128]{1,0:T(8,128)S(1)}, u32[]{:S(2)}, u32[]{:S(2)}) collective-permute-start(f32[8,128]{1,0:T(8,128)S(1)} %add_add_fusion.1), channel_id=1, source_target_pairs={{8,0},{9,1},{10,2},{11,3},{12,4},{13,5},{14,6},{15,7},{0,8},{1,9},... | collective-permute-start | bytes 12296 | tf_op jit(solution)/shard_map/ppermute | solution.py:556
  103.8 11.8 %collective-permute-start.12 = (f32[8,128]{1,0:T(8,128)S(1)}, f32[8,128]{1,0:T(8,128)S(1)}, u32[]{:S(2)}, u32[]{:S(2)}) collective-permute-start(f32[8,128]{1,0:T(8,128)S(1)} %add_add_fusion), channel_id=1, source_target_pairs={{2,0},{3,1},{0,2},{1,3},{6,4},{7,5},{4,6},{5,7},{10,8},{11,9},{8,1... | collective-permute-start | bytes 12296 | tf_op jit(solution)/shard_map/ppermute | solution.py:556

commit v5 on v4

v5 whole, which is shorter than its diff:
```python
import functools

import jax
import jax.numpy as jnp
import ml_dtypes
import numpy as np
from jax import lax
from jax.experimental import pallas as pl
from jax.experimental.pallas import tpu as pltpu
from jax.sharding import PartitionSpec as P

G = 96
HALF = G // 2 + 1
NGRID = G * G * G
LANES = 128
ROWS = NGRID // LANES
PLANE = G * G // LANES
QUADS = G // 4
KPAD = HALF + 1
Y_ROWS = 104
Y_PITCH = Y_ROWS + 1
Z_PITCH = G + 1
W_PITCH = 2 * G + 1
F_PITCH = PLANE + 1
PLANES = 16
STEP_ROWS = PLANES * PLANE
STEPS = G // PLANES
PIECES = (3, 2, 1)
HEAD = STEP_ROWS
WAVE_UNIT = 0.05
SCREEN_SQ = 0.0121
MIB = 1024 * 1024
BF16 = jnp.bfloat16
F32 = jnp.float32


def dft_tables():
    n = np.arange(G)
    phases = (n[:, None] * n[None, :]) % G
    angles = phases.astype(np.float32) * np.float32(2.0 * np.pi / G)
    rounded = [f(angles).astype(ml_dtypes.bfloat16).astype(np.float32) for f in (np.cos, np.sin)]
    return rounded[0], rounded[1]


def section_tables():
    c, s = dft_tables()
    h = HALF
    t1 = np.zeros((Y_ROWS, G), np.float32)
    t1[:h] = c[:h]
    t1[h : 2 * h] = -s[:h]
    t2 = np.block([[c, s], [-s, c]])
    t3 = np.zeros((2, LANES, 4, 64), np.float32)
    back = (G - np.arange(h)) % G
    t3[0, :G, 0, :h] = c[:h].T
    t3[1, :G, 0, :h] = s[:h].T
    t3[0, :G, 1, :h] = -s[:h].T
    t3[1, :G, 1, :h] = c[:h].T
    t3[0, :G, 2, :h] = c[back].T
    t3[1, :G, 2, :h] = s[back].T
    t3[0, :G, 3, :h] = s[back].T
    t3[1, :G, 3, :h] = -c[back].T
    t3 = t3.reshape(2 * LANES, 4 * 64)
    order = np.concatenate([np.arange(G // 2), G - 1 - np.arange(G // 2)])
    a1 = np.block([[c[:, order], -s[:, order]], [s[:, order], c[:, order]]])
    rows = np.arange(G).reshape(QUADS, 4).T.reshape(-1)
    a2 = np.block([[c[rows], -s[rows]], [s[rows], c[rows]]])
    weight = np.full((h, 1), 2.0, np.float32)
    weight[0] = weight[h - 1] = 1.0
    a3 = np.zeros((3, 2, 2, 2, 64, 2, LANES), np.float32)
    for third in range(3):
        for lane in range(LANES):
            r, x3 = divmod(third * LANES + lane, G)
            for p in range(2):
                a3[third, r - third, 0, p, :h, p, lane] = weight[:, 0] * c[x3, :h]
                a3[third, r - third, 1, p, :h, p, lane] = -weight[:, 0] * s[x3, :h]
    a3 = a3.reshape(3, 4 * LANES, 2 * LANES)
    sel = np.zeros((2, 2 * LANES, 2 * LANES), np.float32)
    for r in range(4):
        for x in range(G):
            sel[r // 2, r * G + x - (r // 2) * LANES, (r % 2) * LANES + x] = 1.0
    return [t.astype(ml_dtypes.bfloat16) for t in (t1, t2, t3, a1, a2, a3, sel)]


def screening():
    n = np.arange(G)
    m = np.where(n <= G // 2, n, n - G).astype(np.float64)
    sq = m * m
    q2 = WAVE_UNIT * (sq[:HALF, None, None] + sq[None, :, None] + sq[None, None, :HALF])
    safe = np.where(q2 > 0, q2, 1.0)
    kern = 4.0 * np.pi * (1.0 - np.exp(-q2 / (4.0 * SCREEN_SQ))) / safe
    kern = np.where(q2 > 0, kern, np.pi / SCREEN_SQ)
    out = np.zeros((KPAD, G, 2, 64), np.float32)
    out[:HALF, :, :, :HALF] = kern[:, :, None, :]
    return out.reshape(KPAD * G, LANES)


def dot(a, b):
    return jnp.dot(a, b, preferred_element_type=F32)


def lanes(*parts):
    return jnp.concatenate(parts, axis=1)


def stack(*parts):
    return jnp.concatenate(parts, axis=0)


def split_rows(src, sel_ref, out, first, count):
    rows = [
        [src[pl.ds(3 * (first + i) + s, G, stride=F_PITCH), :].astype(BF16) for s in range(3)]
        for i in range(count)
    ]
    for half in range(2):
        part = dot(stack(*[lanes(r[half], r[half + 1]) for r in rows]), sel_ref[half])
        for i in range(count):
            for e in range(2):
                value = part[i * G : (i + 1) * G, e * LANES : (e + 1) * LANES]
                out[4 * (first + i) + 2 * half + e] = value.astype(BF16)


def widen_planes(src, dst, first):
    @pl.loop(0, src.shape[0] // (2 * PLANE), unroll=4)
    def _(i):
        value = src[pl.ds(pl.multiple_of(i * 2 * PLANE, 16), 2 * PLANE), :].astype(F32)
        dst[pl.ds((first + 2 * i) * F_PITCH, PLANE), :] = value[:PLANE]
        dst[pl.ds((first + 2 * i + 1) * F_PITCH, PLANE), :] = value[PLANE:]


def rows_of(ref, first, count):
    at = pl.ds(first, count)
    return ref.at[at, :] if len(ref.shape) == 2 else ref.at[:, at, :]


def copy_rows(src, src_row, dst, dst_row, count, sem):
    return pltpu.make_async_copy(rows_of(src, src_row, count), rows_of(dst, dst_row, count), sem)


def band_kernel(first, chunks, raw, pick, out, raw_v, out_v, load_sems, store_sem):
    rows = out.shape[0] // chunks
    loads = [
        copy_rows(raw, 2 * (first + c * rows), raw_v, 2 * c * rows, 2 * rows, load_sems.at[c])
        for c in range(chunks)
    ]
    for load in loads:
        load.start()
    for c, load in enumerate(loads):
        load.wait()
        for row in range(c * rows, (c + 1) * rows, LANES):
            value = dot(pick[...], raw_v[2 * row : 2 * row + 2 * LANES, :])
            out_v[row : row + LANES, :] = value.astype(BF16)
        copy_rows(out_v, c * rows, out, c * rows, rows, store_sem).start()
    pltpu.make_async_copy(out_v, out, store_sem).wait()


def take_band(raw, p, first, rows, chunks, earlier=None, interpret=False):
    pick = np.zeros((LANES, 2 * LANES), np.float32)
    pick[np.arange(LANES), 2 * np.arange(LANES) + p] = 1.0
    pick = jnp.asarray(pick.astype(ml_dtypes.bfloat16))
    if earlier is not None:
        pick = after(pick, earlier)
    hbm = pl.BlockSpec(memory_space=pl.ANY)
    return pl.pallas_call(
        functools.partial(band_kernel, first, chunks),
        out_shape=jax.ShapeDtypeStruct((rows, LANES), BF16),
        in_specs=[hbm, pl.BlockSpec(memory_space=pltpu.VMEM)],
        out_specs=hbm,
        scratch_shapes=[
            pltpu.VMEM((2 * rows, LANES), BF16),
            pltpu.VMEM((rows, LANES), BF16),
            pltpu.SemaphoreType.DMA((chunks,)),
            pltpu.SemaphoreType.DMA,
        ],
        compiler_params=pltpu.CompilerParams(vmem_limit_bytes=56 * MIB),
        interpret=interpret,
        name="take_band",
    )(raw, pick)


def rows_kernel(head, tail, own1, sel, out, wide):
    for p, parts in enumerate(([head, tail], [own1])):
        first = 0
        for part in parts:
            widen_planes(part, wide, first)
            first += part.shape[0] // PLANE

        @pl.loop(0, QUADS // 4, unroll=2)
        def _(q):
            split_rows(wide, sel, out.at[p], 4 * q, 4)


def padded_rows(own, sel, interpret=False):
    vmem = pl.BlockSpec(memory_space=pltpu.VMEM)
    return pl.pallas_call(
        rows_kernel,
        out_shape=jax.ShapeDtypeStruct((2, G, G, LANES), BF16),
        in_specs=[vmem] * 4,
        out_specs=vmem,
        scratch_shapes=[pltpu.VMEM((G * F_PITCH, LANES), F32)],
        compiler_params=pltpu.CompilerParams(vmem_limit_bytes=63 * MIB),
        interpret=interpret,
        name="padded_rows",
    )(*own, sel)


def pairs_kernel(count, pieces, share, head, tail, own1, own_u, kern, *refs):
    refs = list(refs)
    par_refs, refs = refs[:count], refs[count:]
    earlier = []
    if len(pieces) > 1:
        earlier, refs = refs[:2], refs[2:]
    table_refs, own_out = refs[:7], refs[7]
    par_out, energy_out = refs[8 : 8 + len(pieces)], refs[8 + len(pieces)]
    own_v, own_uv, kern_v, own_ov, par_ov, par_f, par_u, yw, z, x34 = refs[9 + len(pieces) : -13]
    own_f, staged, total_ref = refs[-13:-10]
    tables, (par_sems, table_sems, sems) = refs[-10:-3], refs[-3:]
    t1, t2, t3, a1, a2, a3, sel = tables
    par_v = par_ov
    par_loads = []
    first = 0
    for src in par_refs:
        for row in range(0, src.shape[0], STEP_ROWS):
            sem = par_sems.at[first // STEP_ROWS]
            par_loads.append(copy_rows(src, row, par_v, first, STEP_ROWS, sem))
            first += STEP_ROWS
    for load in par_loads:
        load.start()
    table_loads = [
        pltpu.make_async_copy(src, dst, table_sems.at[i])
        for i, (src, dst) in enumerate(zip(table_refs, tables))
    ]
    for i in (6, 0, 1, 2, 3, 4, 5):
        table_loads[i].start()
    loads = [
        pltpu.make_async_copy(own_u, own_uv, sems.at[0]),
        pltpu.make_async_copy(kern, kern_v, sems.at[1]),
        copy_rows(head, 0, own_v.at[0], 0, HEAD, sems.at[2]),
        copy_rows(tail, 0, own_v.at[0], HEAD, ROWS - HEAD, sems.at[3]),
        copy_rows(own1, 0, own_v.at[1], 0, ROWS, sems.at[4]),
    ]
    if earlier:
        loads.append(pltpu.make_async_copy(earlier[0], own_ov, sems.at[5]))
    for load in loads:
        load.start()

    for i, load in enumerate(par_loads):
        load.wait()
        widen_planes(par_v.at[pl.ds(i * STEP_ROWS, STEP_ROWS), :], par_f, i * PLANES)
    table_loads[6].wait()

    @pl.loop(0, QUADS // 4, unroll=2)
    def _(q):
        split_rows(par_f, sel, par_u, 4 * q, 4)

    half_y = G * Y_PITCH
    loads[0].wait()
    table_loads[0].wait()

    @pl.loop(0, G // 2, unroll=8)
    def _(i):
        density = []
        for e in range(2):
            partner = par_u[2 * i + e].astype(F32)
            for p in range(2):
                density.append((own_uv[p, 2 * i + e].astype(F32) * partner).astype(BF16))
        out = dot(t1[...], lanes(*density))
        for e in range(2):
            for p in range(2):
                at = pl.ds(p * half_y + (2 * i + e) * Y_PITCH, Y_ROWS)
                yw[at, :] = out[:, (2 * e + p) * LANES : (2 * e + p + 1) * LANES]

    table_loads[1].wait()

    @pl.loop(0, HALF, unroll=7)
    def _(k1):
        def line(p, part):
            return yw[pl.ds(p * half_y + part * HALF + k1, G, stride=Y_PITCH), :].astype(BF16)

        out = dot(t2[...], stack(lanes(line(0, 0), line(1, 0)), lanes(line(0, 1), line(1, 1))))
        at = pl.ds(pl.multiple_of(k1 * G, 16), G)
        for p in range(2):
            for part in range(2):
                left = (2 * p + part) * LANES
                value = out[part * G : (part + 1) * G, p * LANES : (p + 1) * LANES]
                x34[at, left : left + LANES] = value.astype(BF16)

    loads[1].wait()
    table_loads[2].wait()

    many = 5

    @pl.loop(0, KPAD // many, unroll=2)
    def _(m):
        at = pl.ds(pl.multiple_of(m * many * G, 16), many * G)
        factor = kern_v[at, :]
        out = [
            dot(x34[at, 2 * p * LANES : 2 * (p + 1) * LANES], t3[...]).astype(BF16)
            for p in range(2)
        ]
        for part in range(4):
            spectrum = lanes(*[o[:, part * 64 : (part + 1) * 64] for o in out]).astype(F32)
            value = spectrum * factor
            for i in range(many):
                row = (many * m + i) * Z_PITCH
                z[part, pl.ds(row, G), :] = value[i * G : (i + 1) * G]

    table_loads[3].wait()

    @pl.loop(0, G // 4, unroll=6)
    def _(four):
        parts = []
        for e in range(4):
            k2 = 4 * four + e
            mirror = Z_PITCH + jnp.where(k2 == 0, 0, G - k2)
            parts.append(
                stack(
                    z[0, pl.ds(k2, G // 2, stride=Z_PITCH), :].astype(BF16),
                    z[2, pl.ds(mirror, G // 2, stride=Z_PITCH), :].astype(BF16),
                    z[1, pl.ds(k2, G // 2, stride=Z_PITCH), :].astype(BF16),
                    z[3, pl.ds(mirror, G // 2, stride=Z_PITCH), :].astype(BF16),
                )
            )
        out = dot(a1[...], lanes(*parts))
        for e in range(4):
            at = (4 * four + e) * W_PITCH
            yw[pl.ds(at, 2 * G), :] = out[:, e * LANES : (e + 1) * LANES]

    table_loads[4].wait()

    @pl.loop(0, G // 4, unroll=6)
    def _(four):
        parts = []
        for e in range(4):
            x1 = 4 * four + e
            parts.append(
                stack(
                    yw[pl.ds(x1, G, stride=W_PITCH), :].astype(BF16),
                    yw[pl.ds(G + x1, G, stride=W_PITCH), :].astype(BF16),
                )
            )
        out = dot(a2[...], lanes(*parts))
        for r in range(4):
            block = [
                lanes(
                    out[r * QUADS : (r + 1) * QUADS, e * LANES : (e + 1) * LANES],
                    out[G + r * QUADS : G + (r + 1) * QUADS, e * LANES : (e + 1) * LANES],
                )
                for e in range(4)
            ]
            at = pl.multiple_of((r // 2) * G * QUADS + four * 4 * QUADS, 16)
            left = (r % 2) * 2 * LANES
            x34[pl.ds(at, 4 * QUADS), left : left + 2 * LANES] = stack(*block).astype(BF16)

    table_loads[5].wait()
    for load in loads[2:]:
        load.wait()
    total_ref[...] = jnp.zeros_like(total_ref)
    block_rows = PLANES * QUADS
    scale = F32(1.0 / NGRID)

    def result(ch):
        at = pl.multiple_of(ch * block_rows, 16)
        low = x34[pl.ds(at, block_rows), :]
        high = x34[pl.ds(G * QUADS + at, block_rows), :]
        fields = [low, lanes(low[:, 2 * LANES :], high[:, : 2 * LANES]), high]
        flat = pl.ds(pl.multiple_of(ch * STEP_ROWS, 16), STEP_ROWS)
        own_f[...] = own_v[:, flat, :].astype(F32)
        total = jnp.zeros((QUADS, LANES), F32)
        for third in range(3):
            out = dot(fields[third], a3[third]) * scale
            for i in range(PLANES):
                plane = ch * PLANES + i
                partner = par_f[pl.ds(plane * F_PITCH + third, QUADS, stride=3), :]
                here = pl.ds(i * PLANE + third, QUADS, stride=3)
                there = pl.ds(plane * PLANE + third, QUADS, stride=3)
                sent = jnp.zeros((QUADS, LANES), F32)
                for p in range(2):
                    potential = out[i * QUADS : (i + 1) * QUADS, p * LANES : (p + 1) * LANES]
                    term = potential * partner
                    own_ov[p, there, :] = own_ov[p, there, :] + term if earlier else term
                    sent = sent + potential * own_f[p, here, :]
                total = total + sent * partner
                staged[here, :] = sent
        total_ref[...] += total
        par_ov[flat, :] = staged[...].astype(BF16)
        row = ch * STEP_ROWS
        copy_rows(own_ov, row, own_out, row, STEP_ROWS, sems.at[6]).start()

    first = 0
    for i, steps in enumerate(pieces):

        @pl.loop(0, steps, unroll=2 if steps % 2 == 0 else steps)
        def _(step):
            ch = first + step
            result(ch)
            source, row = ch * STEP_ROWS, step * STEP_ROWS
            copy_rows(par_ov, source, par_out[i], row, STEP_ROWS, sems.at[7 + i]).start()

        first += steps

    energy = jnp.sum(total_ref[...]) * F32(share)
    if earlier:
        energy_out[...] = earlier[1][...] + energy
    else:
        energy_out[...] = jnp.zeros_like(energy_out) + energy
    pltpu.make_async_copy(own_ov, own_out, sems.at[6]).wait()
    first = 0
    for i, steps in enumerate(pieces):
        rows = steps * STEP_ROWS
        copy_rows(par_ov, first, par_out[i], 0, rows, sems.at[7 + i]).wait()
        first += rows


def pair_terms(own, own_u, partner, earlier, tables, kern, pieces, share, interpret=False):
    vmem = pl.BlockSpec(memory_space=pltpu.VMEM)
    hbm = pl.BlockSpec(memory_space=pl.ANY)
    return pl.pallas_call(
        functools.partial(pairs_kernel, len(partner), pieces, share),
        out_shape=(
            jax.ShapeDtypeStruct((2, ROWS, LANES), F32),
            *[jax.ShapeDtypeStruct((steps * STEP_ROWS, LANES), BF16) for steps in pieces],
            jax.ShapeDtypeStruct((8, LANES), F32),
        ),
        in_specs=[hbm] * (5 + len(partner)) + [hbm, vmem][: len(earlier)] + [hbm] * 7,
        out_specs=(hbm, *[hbm] * len(pieces), vmem),
        scratch_shapes=[
            pltpu.VMEM((2, ROWS, LANES), BF16),
            pltpu.VMEM((2, G, G, LANES), BF16),
            pltpu.VMEM((KPAD * G, LANES), F32),
            pltpu.VMEM((2, ROWS, LANES), F32),
            pltpu.VMEM((ROWS, LANES), BF16),
            pltpu.VMEM((G * F_PITCH, LANES), F32),
            pltpu.VMEM((G, G, LANES), BF16),
            pltpu.VMEM((2 * G * Y_PITCH, LANES), F32),
            pltpu.VMEM((4, KPAD * Z_PITCH, LANES), F32),
            pltpu.VMEM((KPAD * G, 4 * LANES), BF16),
            pltpu.VMEM((2, STEP_ROWS, LANES), F32),
            pltpu.VMEM((STEP_ROWS, LANES), F32),
            pltpu.VMEM((QUADS, LANES), F32),
            *[pltpu.VMEM(table.shape, BF16) for table in tables],
            pltpu.SemaphoreType.DMA((STEPS,)),
            pltpu.SemaphoreType.DMA((len(tables),)),
            pltpu.SemaphoreType.DMA((7 + len(pieces),)),
        ],
        compiler_params=pltpu.CompilerParams(vmem_limit_bytes=56 * MIB),
        cost_estimate=pl.CostEstimate(
            flops=20_000_000_000, bytes_accessed=20_000_000, transcendentals=0
        ),
        interpret=interpret,
        name="pair_terms",
    )(*own, own_u, kern, *partner, *earlier, *tables)


def piece_kernel(first, last, head, tail, own1, terms, back0, back1, *rest):
    gram_in = [] if first == 0 else [rest[0]]
    out, gram_out, own_v, terms_v, back_v, out_v, gram_ref, load_sems, store_sem = rest[-9:]
    size = back1.shape[0]
    rows = size // load_sems.shape[0]

    def loads(c):
        start = first + c * rows
        own0 = (head, start) if start < HEAD else (tail, start - HEAD)
        sources = [
            (*own0, own_v.at[0]), (own1, start, own_v.at[1]), (terms, start, terms_v),
            (back0, start, back_v.at[0]), (back1, c * rows, back_v.at[1]),
        ]
        return [
            copy_rows(src, row, dst, c * rows, rows, load_sems.at[c, i])
            for i, (src, row, dst) in enumerate(sources)
        ]

    chunks = [loads(c) for c in range(load_sems.shape[0])]
    for chunk in chunks:
        for load in chunk:
            load.start()
    gram_ref[...] = gram_in[0][...] if gram_in else jnp.zeros_like(gram_ref)
    for c, chunk in enumerate(chunks):
        for load in chunk:
            load.wait()
        at = pl.ds(c * rows, rows)
        own = [own_v[i, at, :].astype(F32) for i in range(2)]
        for p in range(2):
            exchange = terms_v[p, at, :] + back_v[p, at, :].astype(F32)
            out_v[pl.ds(2 * c * rows + p, rows, stride=2), :] = exchange
            for i in range(2):
                product = (own[i] * exchange).reshape(-1, 8, LANES)
                gram_ref[i, p] += jnp.sum(product, axis=0)
        copy_rows(out_v, 2 * c * rows, out, 2 * (first + c * rows), 2 * rows, store_sem).start()

    if not last:
        gram_out[...] = gram_ref[...]
    else:
        row = lax.broadcasted_iota(jnp.int32, (2, 2), 0)
        column = lax.broadcasted_iota(jnp.int32, (2, 2), 1)
        value = jnp.zeros((2, 2), F32)
        for i in range(2):
            for j in range(2):
                entry = jnp.sum(gram_ref[i, j]) * F32(1.0 / NGRID)
                value = jnp.where((row == i) & (column == j), entry, value)
        gram_out[...] = value
    copy_rows(out_v, 0, out, 2 * first, 2 * size, store_sem).wait()


def add_piece(first, own, terms, back0, back1, earlier, interpret=False):
    hbm = pl.BlockSpec(memory_space=pl.ANY)
    vmem = pl.BlockSpec(memory_space=pltpu.VMEM)
    size = back1.shape[0]
    last = first + size == ROWS
    return pl.pallas_call(
        functools.partial(piece_kernel, first, last),
        out_shape=(
            jax.ShapeDtypeStruct((2 * ROWS, LANES), F32),
            jax.ShapeDtypeStruct((2, 2) if last else (2, 2, 8, LANES), F32),
        ),
        in_specs=[hbm] * 6 + [vmem, hbm][: len(earlier)],
        out_specs=(hbm, vmem),
        scratch_shapes=[
            pltpu.VMEM((2, size, LANES), BF16),
            pltpu.VMEM((2, size, LANES), F32),
            pltpu.VMEM((2, size, LANES), BF16),
            pltpu.VMEM((2 * size, LANES), F32),
            pltpu.VMEM((2, 2, 8, LANES), F32),
            pltpu.SemaphoreType.DMA((2 * size // STEP_ROWS, 5)),
            pltpu.SemaphoreType.DMA,
        ],
        input_output_aliases={7: 0} if earlier else {},
        compiler_params=pltpu.CompilerParams(vmem_limit_bytes=44 * MIB),
        interpret=interpret,
        name="add_piece",
    )(*own, terms, back0, back1, *earlier)


def from_behind(block, axis, distance):
    size = lax.axis_size(axis)
    return lax.ppermute(block, axis, [((i - distance) % size, i) for i in range(size)])


def send_to(value, axis, bits):
    size = lax.axis_size(axis)
    flips = sorted({bits[0], bits[-1], sum(bits)})
    return [lax.ppermute(value, axis, [(i ^ flip, i) for i in range(size)]) for flip in flips]


def add_up(value, got):
    if len(got) == 1:
        return value + got[0]
    return (value + got[0]) + (got[1] + got[2])


def after(values, other):
    return lax.optimization_barrier((values, other))[0]


def per_device(orbitals):
    tables = section_tables()
    kern = screening()
    size = lax.axis_size("band")
    share = -2.0 / (NGRID * 2 * size * orbitals.shape[0])
    raw = orbitals.reshape(2, ROWS, LANES).transpose(1, 0, 2).reshape(2 * ROWS, LANES)
    head = take_band(raw, 0, 0, HEAD, 3)
    tail = take_band(raw, 0, HEAD, ROWS - HEAD, 9, head)
    own = [head, tail, take_band(raw, 1, 0, ROWS, 9, tail)]
    previous = [from_behind(part, "band", 1) for part in own]
    own_u = padded_rows(own, tables[-1])
    terms, back0, energy = pair_terms(
        own, own_u, previous[:2], (), tables, kern, (STEPS,), share
    )
    back0 = from_behind(back0, "band", -1)
    terms, *sent, energy = pair_terms(
        own, own_u, previous[2:], (terms, energy), tables, kern, PIECES, share
    )
    back1 = [from_behind(piece, "band", -1) for piece in sent]

    if size & (size - 1):
        energy = lax.psum(energy, "band")
        groups = []
    else:
        bits = [1 << b for b in range(size.bit_length() - 1)]
        rest = [b for b in bits if b != 2]
        groups = [rest[i : i + 2] for i in range(0, len(rest), 2)]
    for group in groups:
        energy = add_up(energy, send_to(energy, "band", group))
    result = ()
    first = 0
    for i, piece in enumerate(back1):
        if groups and i == len(back1) - 1:
            got = send_to(after(energy, result[1]), "band", [2])
        result = add_piece(first, own, terms, back0, piece, result[::-1])
        first += piece.shape[0]
    exchange, gram = result
    if groups:
        energy = add_up(energy, after(got, gram))
    exchange = exchange.reshape(ROWS, 2, LANES).transpose(1, 0, 2).reshape(2, NGRID)
    return exchange, gram, energy[0, 0]


def solution(mesh):
    return jax.shard_map(
        per_device,
        mesh=mesh,
        in_specs=(P("band", None),),
        out_specs=(P("band", None), P("band", None), P()),
        check_vma=False,
    )
```

time: 117 us -> 132 us (1.13)
  waiting for transfers between devices: 15.1 us -> 31.2 us
  starting transfers between devices: 14.4 us -> 17.5 us
  Pallas kernels: 82.3 us -> 80.5 us
  local copies, waits for them, and re-layouts: 2.88 us -> 1.23 us
    ppermute x7, waiting for transfers between devices: 3.05 us -> 19.4 us  [send_to(): lax.ppermute(value, axis, [(i ^ flip, i) for i in range(size)])]
    ppermute x7, starting transfers between devices: 7.14 us -> 10.2 us  [send_to(): lax.ppermute(value, axis, [(i ^ flip, i) for i in range(size)])]
    pallas_call x8, Pallas kernels: 75.3 us -> 73.6 us  [the longest x2 45.2 us: pair_terms(): pl.pallas_call(functools.partial(pairs_kernel, len(partner), pieces, shar...]
    ppermute x6 -> x7, waiting for transfers between devices: 12 us -> 11.7 us  [from_behind(): lax.ppermute(block, axis, [((i - distance) % size, i) for i in range(size)])]
    ppermute x6 -> x7, starting transfers between devices: 7.21 us -> 7.28 us  [from_behind(): lax.ppermute(block, axis, [((i - distance) % size, i) for i in range(size)])]
  transfers between devices with their start and end apart: 13 -> 14, of which waited for: 2 -> 6; matrix products, arithmetic and copies ran while one was open for 1% -> 1% of each run, Pallas kernels for 67% -> 55%
where the time goes in v5:
time: 132 us
  Pallas kernels  80.5 us (61%)
  waiting for transfers between devices  31.2 us (24%)
  starting transfers between devices  17.5 us (13%)
    pallas_call x2, Pallas kernels, pair_terms(): pl.pallas_call(functools.partial(pairs_kernel, len(partner), pieces, shar...  45.2 us
    ppermute x7, waiting for transfers between devices, send_to(): lax.ppermute(value, axis, [(i ^ flip, i) for i in range(size)])  19.4 us
    pallas_call x3, Pallas kernels, add_piece(): pl.pallas_call(functools.partial(piece_kernel, first, last), out_shape=(j...  15.5 us
    pallas_call x3, Pallas kernels, take_band(): pl.pallas_call(functools.partial(band_kernel, first, chunks), out_shape=j...  12.8 us
    ppermute x7, waiting for transfers between devices, from_behind(): lax.ppermute(block, axis, [((i - distance) % size, i) for i in range(size)])  11.7 us
    ppermute x7, starting transfers between devices, send_to(): lax.ppermute(value, axis, [(i ^ flip, i) for i in range(size)])  10.2 us
    ppermute x7, starting transfers between devices, from_behind(): lax.ppermute(block, axis, [((i - distance) % size, i) for i in range(size)])  7.28 us
    pallas_call x1, Pallas kernels, padded_rows(): pl.pallas_call(rows_kernel, out_shape=jax.ShapeDtypeStruct((2, G, G, LANE...  6.99 us
  transfers between devices with their start and end apart: 14, of which 6 were waited for; matrix products, arithmetic and copies ran while one was open for 1% of the time, Pallas kernels for 55%

profile of v5, /device:TPU:0, one launch (start us, length us, event | category | flops | bytes accessed | tf_op | source)
XLA Modules:
  0.0 132.0 jit_solution(10539386968243318379)
XLA Ops:
  0.6 3.1 %take_band.3.head = bf16[1152,128]{1,0:T(8,128)(2,1)} custom-call(bf16[13824,128]{1,0:T(8,128)(2,1)} %bitcast.11, bf16[128,256]{1,0:T(8,128)(2,1)} %constant.20.clone.pick), custom_call_target="tpu_custom_call" | custom-call | tf_op jit(solution)/shard_map/take_band/pallas_call | solution.py:163
  3.7 0.0 copy-start.2
  3.7 4.9 %take_band.4.tail = bf16[5760,128]{1,0:T(8,128)(2,1)} custom-call(bf16[13824,128]{1,0:T(8,128)(2,1)} %bitcast.12, bf16[128,256]{1,0:T(8,128)(2,1)} %constant.20.clone.pick), custom_call_target="tpu_custom_call" | custom-call | tf_op jit(solution)/shard_map/take_band/pallas_call | solution.py:163
  8.6 0.5 collective-permute-start.2
  9.1 0.0 copy-done.2
  9.1 2.6 %collective-permute-start.1 = (bf16[1152,128]{1,0:T(8,128)(2,1)S(1)}, bf16[1152,128]{1,0:T(8,128)(2,1)S(1)}, u32[]{:S(2)}, u32[]{:S(2)}) collective-permute-start(bf16[1152,128]{1,0:T(8,128)(2,1)S(1)} %copy-done.2), channel_id=1, source_target_pairs={{31,0},{0,1},{1,2},{2,3},{3,4},{4,5},{5,6},{6,7},{7,8},{8,9},{9,10... | collective-permute-start | bytes 884744 | tf_op jit(solution)/shard_map/ppermute | solution.py:535
  11.7 4.9 %take_band.5.own1 = bf16[6912,128]{1,0:T(8,128)(2,1)} custom-call(bf16[13824,128]{1,0:T(8,128)(2,1)} %bitcast.13, bf16[128,256]{1,0:T(8,128)(2,1)} %constant.21.clone.pick), custom_call_target="tpu_custom_call" | custom-call | tf_op jit(solution)/shard_map/take_band/pallas_call | solution.py:163
  16.6 0.1 collective-permute-start
  16.7 7.0 %padded_rows.1.own_u = bf16[2,96,96,128]{3,2,1,0:T(8,128)(2,1)} custom-call(bf16[1152,128]{1,0:T(8,128)(2,1)} %take_band.3.head, bf16[5760,128]{1,0:T(8,128)(2,1)} %take_band.4.tail, bf16[6912,128]{1,0:T(8,128)(2,1)} %take_band.5.own1, bf16[2,256,256]{2,1,0:T(8,128)(2,1)} %constant.22.clone.sel.refs_8_.refs_9_), custom_call_target="tpu_custom_call" | custom-call | tf_op jit(solution)/shard_map/padded_rows/pallas_call | solution.py:194
  23.7 11.7 %collective-permute-done.1.refs_0_ = bf16[1152,128]{1,0:T(8,128)(2,1)S(1)} collective-permute-done((bf16[1152,128]{1,0:T(8,128)(2,1)S(1)}, bf16[1152,128]{1,0:T(8,128)(2,1)S(1)}, u32[]{:S(2)}, u32[]{:S(2)}) %collective-permute-start.1) | collective-permute-done | bytes 294944 | tf_op jit(solution)/shard_map/ppermute | solution.py:535
  35.4 0.0 copy-start.4
  35.4 0.0 collective-permute-done.2.refs_1_
  35.4 0.7 copy-done.4
  36.1 21.9 %pair_terms.2 = (f32[2,6912,128]{2,1,0:T(8,128)}, bf16[6912,128]{1,0:T(8,128)(2,1)}, f32[8,128]{1,0:T(8,128)}) custom-call(bf16[1152,128]{1,0:T(8,128)(2,1)} %take_band.3.head, bf16[5760,128]{1,0:T(8,128)(2,1)} %take_band.4.tail, bf16[6912,128]{1,0:T(8,128)(2,1)} %take_band.5.own1, bf16[2,96,96,128]{3,2,1,0:T(8,128)(2,1)} %padded_rows.1.own_u, ...), custom_call_target="tpu_custom_call" | custom-call | flops 20000000000 | bytes 20000000 | tf_op jit(solution)/shard_map/pair_terms/pallas_call | solution.py:417
  58.1 0.2 collective-permute-start.3
  58.3 0.0 collective-permute-done.refs_0_
  58.3 0.0 copy-start
  58.3 0.0 copy-start.1
  58.3 0.0 copy-start.3
  58.4 23.3 %pair_terms.3 = (f32[2,6912,128]{2,1,0:T(8,128)}, bf16[3456,128]{1,0:T(8,128)(2,1)}, bf16[2304,128]{1,0:T(8,128)(2,1)}, bf16[1152,128]{1,0:T(8,128)(2,1)}, f32[8,128]{1,0:T(8,128)}) custom-call(bf16[1152,128]{1,0:T(8,128)(2,1)} %take_band.3.head, bf16[5760,128]{1,0:T(8,128)(2,1)} %take_band.4.tail, bf16[6912,128]{1,0:T(8,128)(2,1)} %take_band.5.own1, ...), custom_call_target="tpu_custom_call" | custom-call | flops 20000000000 | bytes 20000000 | tf_op jit(solution)/shard_map/pair_terms/pallas_call | solution.py:417
  81.7 2.5 %collective-permute-start.6 = (bf16[3456,128]{1,0:T(8,128)(2,1)}, bf16[3456,128]{1,0:T(8,128)(2,1)S(1)}, u32[]{:S(2)}, u32[]{:S(2)}) collective-permute-start(bf16[3456,128]{1,0:T(8,128)(2,1)} %get-tuple-element.29), channel_id=1, source_target_pairs={{1,0},{2,1},{3,2},{4,3},{5,4},{6,5},{7,6},{8,7},{9,8},{10,9},{11,1... | collective-permute-start | bytes 2654216 | tf_op jit(solution)/shard_map/ppermute | solution.py:535
  84.1 0.1 collective-permute-start.5
  84.2 0.0 collective-permute-start.9
  84.2 2.1 %collective-permute-start.8 = (f32[8,128]{1,0:T(8,128)}, f32[8,128]{1,0:T(8,128)S(1)}, u32[]{:S(2)}, u32[]{:S(2)}) collective-permute-start(f32[8,128]{1,0:T(8,128)} %get-tuple-element.36), channel_id=1, source_target_pairs={{4,0},{5,1},{6,2},{7,3},{0,4},{1,5},{2,6},{3,7},{12,8},{13,9},{14,... | collective-permute-start | bytes 12296 | tf_op jit(solution)/shard_map/ppermute | solution.py:541
  86.3 1.2 collective-permute-done.9
  87.4 0.5 collective-permute-start.7
  87.9 0.2 collective-permute-done.8
  88.1 1.3 collective-permute-start.4
  89.4 0.0 collective-permute-done.7
  89.4 0.7 add_add_fusion.1
  90.1 0.9 collective-permute-start.12
  90.9 14.5 %collective-permute-done.12 = f32[8,128]{1,0:T(8,128)S(1)} collective-permute-done((f32[8,128]{1,0:T(8,128)S(1)}, f32[8,128]{1,0:T(8,128)S(1)}, u32[]{:S(2)}, u32[]{:S(2)}) %collective-permute-start.12) | collective-permute-done | bytes 4128 | tf_op jit(solution)/shard_map/ppermute | solution.py:541
  105.4 2.6 %collective-permute-start.11 = (f32[8,128]{1,0:T(8,128)S(1)}, f32[8,128]{1,0:T(8,128)S(1)}, u32[]{:S(2)}, u32[]{:S(2)}) collective-permute-start(f32[8,128]{1,0:T(8,128)S(1)} %add_add_fusion.1), channel_id=1, source_target_pairs={{16,0},{17,1},{18,2},{19,3},{20,4},{21,5},{22,6},{23,7},{24,8},{25... | collective-permute-start | bytes 12296 | tf_op jit(solution)/shard_map/ppermute | solution.py:541
  108.0 1.9 %collective-permute-done.11 = f32[8,128]{1,0:T(8,128)S(1)} collective-permute-done((f32[8,128]{1,0:T(8,128)S(1)}, f32[8,128]{1,0:T(8,128)S(1)}, u32[]{:S(2)}, u32[]{:S(2)}) %collective-permute-start.11) | collective-permute-done | bytes 4128 | tf_op jit(solution)/shard_map/ppermute | solution.py:541
  110.0 2.6 %collective-permute-start.10 = (f32[8,128]{1,0:T(8,128)S(1)}, f32[8,128]{1,0:T(8,128)S(1)}, u32[]{:S(2)}, u32[]{:S(2)}) collective-permute-start(f32[8,128]{1,0:T(8,128)S(1)} %add_add_fusion.1), channel_id=1, source_target_pairs={{8,0},{9,1},{10,2},{11,3},{12,4},{13,5},{14,6},{15,7},{0,8},{1,9},... | collective-permute-start | bytes 12296 | tf_op jit(solution)/shard_map/ppermute | solution.py:541
  112.6 1.6 %collective-permute-done.10 = f32[8,128]{1,0:T(8,128)S(1)} collective-permute-done((f32[8,128]{1,0:T(8,128)S(1)}, f32[8,128]{1,0:T(8,128)S(1)}, u32[]{:S(2)}, u32[]{:S(2)}) %collective-permute-start.10) | collective-permute-done | bytes 4128 | tf_op jit(solution)/shard_map/ppermute | solution.py:541
  114.2 0.0 collective-permute-done.6.back1
  114.2 0.0 collective-permute-done.3.back0
  114.2 0.0 copy-done
  114.2 0.0 copy-done.1
  114.2 0.0 copy-done.3
  114.2 6.8 %add_piece.3 = (f32[13824,128]{1,0:T(8,128)}, f32[2,2,8,128]{3,2,1,0:T(8,128)S(1)}) custom-call(bf16[1152,128]{1,0:T(8,128)(2,1)S(1)} %copy-done.3, bf16[5760,128]{1,0:T(8,128)(2,1)S(1)} %copy-done.1, bf16[6912,128]{1,0:T(8,128)(2,1)S(1)} %copy-done, f32[2,6912,128]{2,1,0:T(8,128)} %get-tuple-element.25.terms, ...), custom_call_target="tpu_custom_call" | custom-call | tf_op jit(solution)/shard_map/add_piece/pallas_call | solution.py:509
  121.0 0.0 collective-permute-done.5.back1
  121.0 4.9 %add_piece.4 = (f32[13824,128]{1,0:T(8,128)}, f32[2,2,8,128]{3,2,1,0:T(8,128)S(1)}) custom-call(bf16[1152,128]{1,0:T(8,128)(2,1)S(1)} %copy-done.3, bf16[5760,128]{1,0:T(8,128)(2,1)S(1)} %copy-done.1, bf16[6912,128]{1,0:T(8,128)(2,1)S(1)} %copy-done, f32[2,6912,128]{2,1,0:T(8,128)} %get-tuple-element.25.terms, ...), custom_call_target="tpu_custom_call", output_to_operand_aliasing={{0}: (7, {})} | custom-call | tf_op jit(solution)/shard_map/add_piece/pallas_call | solution.py:509
  125.9 1.7 %collective-permute-start.13 = (f32[8,128]{1,0:T(8,128)S(1)}, f32[8,128]{1,0:T(8,128)S(1)}, u32[]{:S(2)}, u32[]{:S(2)}) collective-permute-start(f32[8,128]{1,0:T(8,128)S(1)} %add_add_fusion), channel_id=1, source_target_pairs={{2,0},{3,1},{0,2},{1,3},{6,4},{7,5},{4,6},{5,7},{10,8},{11,9},{8,1... | collective-permute-start | bytes 12296 | tf_op jit(solution)/shard_map/ppermute | solution.py:541
  127.6 0.0 collective-permute-done.4.back1
  127.6 3.8 %add_piece.5 = (f32[13824,128]{1,0:T(8,128)}, f32[2,2]{1,0:T(2,128)}) custom-call(bf16[1152,128]{1,0:T(8,128)(2,1)S(1)} %copy-done.3, bf16[5760,128]{1,0:T(8,128)(2,1)S(1)} %copy-done.1, bf16[6912,128]{1,0:T(8,128)(2,1)S(1)} %copy-done, f32[2,6912,128]{2,1,0:T(8,128)} %get-tuple-element.25.terms, ...), custom_call_target="tpu_custom_call", output_to_operand_aliasing={{0}: (7, {})} | custom-call | tf_op jit(solution)/shard_map/add_piece/pallas_call | solution.py:509
  131.4 0.0 collective-permute-done.13
  131.4 0.5 slice.3
  (2 shorter events, 0.0 us)
Async XLA Ops:
  3.7 5.4 %copy-start.2 = (bf16[1152,128]{1,0:T(8,128)(2,1)S(1)}, bf16[1152,128]{1,0:T(8,128)(2,1)}, u32[]{:S(2)}) copy-start(bf16[1152,128]{1,0:T(8,128)(2,1)} %take_band.3.head) | copy-start | bytes 884740
  8.6 26.8 %collective-permute-start.2 = (bf16[5760,128]{1,0:T(8,128)(2,1)}, bf16[5760,128]{1,0:T(8,128)(2,1)}, u32[]{:S(2)}, u32[]{:S(2)}) collective-permute-start(bf16[5760,128]{1,0:T(8,128)(2,1)} %take_band.4.tail), channel_id=1, source_target_pairs={{31,0},{0,1},{1,2},{2,3},{3,4},{4,5},{5,6},{6,7},{7,8},{8,9},{9,10... | collective-permute-start | bytes 4423688 | tf_op jit(solution)/shard_map/ppermute | solution.py:535
  9.1 26.3 %collective-permute-start.1 = (bf16[1152,128]{1,0:T(8,128)(2,1)S(1)}, bf16[1152,128]{1,0:T(8,128)(2,1)S(1)}, u32[]{:S(2)}, u32[]{:S(2)}) collective-permute-start(bf16[1152,128]{1,0:T(8,128)(2,1)S(1)} %copy-done.2), channel_id=1, source_target_pairs={{31,0},{0,1},{1,2},{2,3},{3,4},{4,5},{5,6},{6,7},{7,8},{8,9},{9,10... | collective-permute-start | bytes 884744 | tf_op jit(solution)/shard_map/ppermute | solution.py:535
  16.6 41.7 %collective-permute-start = (bf16[6912,128]{1,0:T(8,128)(2,1)}, bf16[6912,128]{1,0:T(8,128)(2,1)}, u32[]{:S(2)}, u32[]{:S(2)}) collective-permute-start(bf16[6912,128]{1,0:T(8,128)(2,1)} %take_band.5.own1), channel_id=1, source_target_pairs={{31,0},{0,1},{1,2},{2,3},{3,4},{4,5},{5,6},{6,7},{7,8},{8,9},{9,10... | collective-permute-start | bytes 5308424 | tf_op jit(solution)/shard_map/ppermute | solution.py:535
  35.4 0.7 copy-start.4
  58.1 56.1 %collective-permute-start.3 = (bf16[6912,128]{1,0:T(8,128)(2,1)}, bf16[6912,128]{1,0:T(8,128)(2,1)S(1)}, u32[]{:S(2)}, u32[]{:S(2)}) collective-permute-start(bf16[6912,128]{1,0:T(8,128)(2,1)} %get-tuple-element.26), channel_id=1, source_target_pairs={{1,0},{2,1},{3,2},{4,3},{5,4},{6,5},{7,6},{8,7},{9,8},{10,9},{11,1... | collective-permute-start | bytes 5308424 | tf_op jit(solution)/shard_map/ppermute | solution.py:535
  58.3 55.9 %copy-start = (bf16[6912,128]{1,0:T(8,128)(2,1)S(1)}, bf16[6912,128]{1,0:T(8,128)(2,1)}, u32[]{:S(2)}) copy-start(bf16[6912,128]{1,0:T(8,128)(2,1)} %take_band.5.own1) | copy-start | bytes 5308420
  58.3 55.9 %copy-start.1 = (bf16[5760,128]{1,0:T(8,128)(2,1)S(1)}, bf16[5760,128]{1,0:T(8,128)(2,1)}, u32[]{:S(2)}) copy-start(bf16[5760,128]{1,0:T(8,128)(2,1)} %take_band.4.tail) | copy-start | bytes 4423684
  58.3 55.9 %copy-start.3 = (bf16[1152,128]{1,0:T(8,128)(2,1)S(1)}, bf16[1152,128]{1,0:T(8,128)(2,1)}, u32[]{:S(2)}) copy-start(bf16[1152,128]{1,0:T(8,128)(2,1)} %take_band.3.head) | copy-start | bytes 884740
  81.7 32.5 %collective-permute-start.6 = (bf16[3456,128]{1,0:T(8,128)(2,1)}, bf16[3456,128]{1,0:T(8,128)(2,1)S(1)}, u32[]{:S(2)}, u32[]{:S(2)}) collective-permute-start(bf16[3456,128]{1,0:T(8,128)(2,1)} %get-tuple-element.29), channel_id=1, source_target_pairs={{1,0},{2,1},{3,2},{4,3},{5,4},{6,5},{7,6},{8,7},{9,8},{10,9},{11,1... | collective-permute-start | bytes 2654216 | tf_op jit(solution)/shard_map/ppermute | solution.py:535
  84.1 36.9 %collective-permute-start.5 = (bf16[2304,128]{1,0:T(8,128)(2,1)}, bf16[2304,128]{1,0:T(8,128)(2,1)S(1)}, u32[]{:S(2)}, u32[]{:S(2)}) collective-permute-start(bf16[2304,128]{1,0:T(8,128)(2,1)} %get-tuple-element.28), channel_id=1, source_target_pairs={{1,0},{2,1},{3,2},{4,3},{5,4},{6,5},{7,6},{8,7},{9,8},{10,9},{11,1... | collective-permute-start | bytes 1769480 | tf_op jit(solution)/shard_map/ppermute | solution.py:535
  84.2 3.2 %collective-permute-start.9 = (f32[8,128]{1,0:T(8,128)}, f32[8,128]{1,0:T(8,128)S(1)}, u32[]{:S(2)}, u32[]{:S(2)}) collective-permute-start(f32[8,128]{1,0:T(8,128)} %get-tuple-element.36), channel_id=1, source_target_pairs={{5,0},{4,1},{7,2},{6,3},{1,4},{0,5},{3,6},{2,7},{13,8},{12,9},{15,... | collective-permute-start | bytes 12296 | tf_op jit(solution)/shard_map/ppermute | solution.py:541
  84.2 3.9 %collective-permute-start.8 = (f32[8,128]{1,0:T(8,128)}, f32[8,128]{1,0:T(8,128)S(1)}, u32[]{:S(2)}, u32[]{:S(2)}) collective-permute-start(f32[8,128]{1,0:T(8,128)} %get-tuple-element.36), channel_id=1, source_target_pairs={{4,0},{5,1},{6,2},{7,3},{0,4},{1,5},{2,6},{3,7},{12,8},{13,9},{14,... | collective-permute-start | bytes 12296 | tf_op jit(solution)/shard_map/ppermute | solution.py:541
  87.4 2.0 %collective-permute-start.7 = (f32[8,128]{1,0:T(8,128)}, f32[8,128]{1,0:T(8,128)S(1)}, u32[]{:S(2)}, u32[]{:S(2)}) collective-permute-start(f32[8,128]{1,0:T(8,128)} %get-tuple-element.36), channel_id=1, source_target_pairs={{1,0},{0,1},{3,2},{2,3},{5,4},{4,5},{7,6},{6,7},{9,8},{8,9},{11,10... | collective-permute-start | bytes 12296 | tf_op jit(solution)/shard_map/ppermute | solution.py:541
  88.1 39.5 %collective-permute-start.4 = (bf16[1152,128]{1,0:T(8,128)(2,1)}, bf16[1152,128]{1,0:T(8,128)(2,1)S(1)}, u32[]{:S(2)}, u32[]{:S(2)}) collective-permute-start(bf16[1152,128]{1,0:T(8,128)(2,1)} %get-tuple-element.27), channel_id=1, source_target_pairs={{1,0},{2,1},{3,2},{4,3},{5,4},{6,5},{7,6},{8,7},{9,8},{10,9},{11,1... | collective-permute-start | bytes 884744 | tf_op jit(solution)/shard_map/ppermute | solution.py:535
  90.1 15.4 %collective-permute-start.12 = (f32[8,128]{1,0:T(8,128)S(1)}, f32[8,128]{1,0:T(8,128)S(1)}, u32[]{:S(2)}, u32[]{:S(2)}) collective-permute-start(f32[8,128]{1,0:T(8,128)S(1)} %add_add_fusion.1), channel_id=1, source_target_pairs={{24,0},{25,1},{26,2},{27,3},{28,4},{29,5},{30,6},{31,7},{16,8},{17... | collective-permute-start | bytes 12296 | tf_op jit(solution)/shard_map/ppermute | solution.py:541
  105.4 4.5 %collective-permute-start.11 = (f32[8,128]{1,0:T(8,128)S(1)}, f32[8,128]{1,0:T(8,128)S(1)}, u32[]{:S(2)}, u32[]{:S(2)}) collective-permute-start(f32[8,128]{1,0:T(8,128)S(1)} %add_add_fusion.1), channel_id=1, source_target_pairs={{16,0},{17,1},{18,2},{19,3},{20,4},{21,5},{22,6},{23,7},{24,8},{25... | collective-permute-start | bytes 12296 | tf_op jit(solution)/shard_map/ppermute | solution.py:541
  110.0 4.2 %collective-permute-start.10 = (f32[8,128]{1,0:T(8,128)S(1)}, f32[8,128]{1,0:T(8,128)S(1)}, u32[]{:S(2)}, u32[]{:S(2)}) collective-permute-start(f32[8,128]{1,0:T(8,128)S(1)} %add_add_fusion.1), channel_id=1, source_target_pairs={{8,0},{9,1},{10,2},{11,3},{12,4},{13,5},{14,6},{15,7},{0,8},{1,9},... | collective-permute-start | bytes 12296 | tf_op jit(solution)/shard_map/ppermute | solution.py:541
  125.9 5.5 %collective-permute-start.13 = (f32[8,128]{1,0:T(8,128)S(1)}, f32[8,128]{1,0:T(8,128)S(1)}, u32[]{:S(2)}, u32[]{:S(2)}) collective-permute-start(f32[8,128]{1,0:T(8,128)S(1)} %add_add_fusion), channel_id=1, source_target_pairs={{2,0},{3,1},{0,2},{1,3},{6,4},{7,5},{4,6},{5,7},{10,8},{11,9},{8,1... | collective-permute-start | bytes 12296 | tf_op jit(solution)/shard_map/ppermute | solution.py:541

commit v6 on v5

--- a/solution.py
+++ b/solution.py
@@ -26,7 +26,7 @@
 STEP_ROWS = PLANES * PLANE
 STEPS = G // PLANES
 PIECES = (3, 2, 1)
-HEAD = STEP_ROWS
+RIDER = 16
 WAVE_UNIT = 0.05
 SCREEN_SQ = 0.0121
 MIB = 1024 * 1024
@@ -94,6 +94,10 @@
     return out.reshape(KPAD * G, LANES)
 
 
+def cost(size):
+    return pl.CostEstimate(flops=0, bytes_accessed=size, transcendentals=0)
+
+
 def dot(a, b):
     return jnp.dot(a, b, preferred_element_type=F32)
 
@@ -136,53 +140,52 @@
     return pltpu.make_async_copy(rows_of(src, src_row, count), rows_of(dst, dst_row, count), sem)
 
 
-def band_kernel(first, chunks, raw, pick, out, raw_v, out_v, load_sems, store_sem):
+def band_kernel(p, raw, *refs):
+    out, raw_v, out_v, load_sems, store_sem = refs[-5:]
+    chunks = load_sems.shape[0]
     rows = out.shape[0] // chunks
     loads = [
-        copy_rows(raw, 2 * (first + c * rows), raw_v, 2 * c * rows, 2 * rows, load_sems.at[c])
+        copy_rows(raw, 2 * c * rows, raw_v, 2 * c * rows, 2 * rows, load_sems.at[c])
         for c in range(chunks)
     ]
     for load in loads:
         load.start()
+    shape = (LANES, 2 * LANES)
+    row = lax.broadcasted_iota(jnp.int32, shape, 0)
+    column = lax.broadcasted_iota(jnp.int32, shape, 1)
+    pick = jnp.where(column == 2 * row + p, F32(1.0), F32(0.0)).astype(BF16)
     for c, load in enumerate(loads):
         load.wait()
         for row in range(c * rows, (c + 1) * rows, LANES):
-            value = dot(pick[...], raw_v[2 * row : 2 * row + 2 * LANES, :])
+            value = dot(pick, raw_v[2 * row : 2 * row + 2 * LANES, :])
             out_v[row : row + LANES, :] = value.astype(BF16)
         copy_rows(out_v, c * rows, out, c * rows, rows, store_sem).start()
     pltpu.make_async_copy(out_v, out, store_sem).wait()
 
 
-def take_band(raw, p, first, rows, chunks, earlier=None, interpret=False):
-    pick = np.zeros((LANES, 2 * LANES), np.float32)
-    pick[np.arange(LANES), 2 * np.arange(LANES) + p] = 1.0
-    pick = jnp.asarray(pick.astype(ml_dtypes.bfloat16))
-    if earlier is not None:
-        pick = after(pick, earlier)
+def take_band(raw, p, earlier=(), interpret=False):
     hbm = pl.BlockSpec(memory_space=pl.ANY)
     return pl.pallas_call(
-        functools.partial(band_kernel, first, chunks),
-        out_shape=jax.ShapeDtypeStruct((rows, LANES), BF16),
-        in_specs=[hbm, pl.BlockSpec(memory_space=pltpu.VMEM)],
+        functools.partial(band_kernel, p),
+        out_shape=jax.ShapeDtypeStruct((ROWS, LANES), BF16),
+        in_specs=[hbm] * (1 + len(earlier)),
         out_specs=hbm,
         scratch_shapes=[
-            pltpu.VMEM((2 * rows, LANES), BF16),
-            pltpu.VMEM((rows, LANES), BF16),
-            pltpu.SemaphoreType.DMA((chunks,)),
+            pltpu.VMEM((2 * ROWS, LANES), BF16),
+            pltpu.VMEM((ROWS, LANES), BF16),
+            pltpu.SemaphoreType.DMA((9,)),
             pltpu.SemaphoreType.DMA,
         ],
         compiler_params=pltpu.CompilerParams(vmem_limit_bytes=56 * MIB),
+        cost_estimate=cost(6 * ROWS * LANES),
         interpret=interpret,
         name="take_band",
-    )(raw, pick)
-
-
-def rows_kernel(head, tail, own1, sel, out, wide):
-    for p, parts in enumerate(([head, tail], [own1])):
-        first = 0
-        for part in parts:
-            widen_planes(part, wide, first)
-            first += part.shape[0] // PLANE
+    )(raw, *earlier)
+
+
+def rows_kernel(own0, own1, sel, out, wide):
+    for p, own in enumerate((own0, own1)):
+        widen_planes(own, wide, 0)
 
         @pl.loop(0, QUADS // 4, unroll=2)
         def _(q):
@@ -194,35 +197,32 @@
     return pl.pallas_call(
         rows_kernel,
         out_shape=jax.ShapeDtypeStruct((2, G, G, LANES), BF16),
-        in_specs=[vmem] * 4,
+        in_specs=[vmem] * 3,
         out_specs=vmem,
         scratch_shapes=[pltpu.VMEM((G * F_PITCH, LANES), F32)],
         compiler_params=pltpu.CompilerParams(vmem_limit_bytes=63 * MIB),
+        cost_estimate=cost(16 * NGRID),
         interpret=interpret,
         name="padded_rows",
     )(*own, sel)
 
 
-def pairs_kernel(count, pieces, share, head, tail, own1, own_u, kern, *refs):
-    refs = list(refs)
-    par_refs, refs = refs[:count], refs[count:]
+def pairs_kernel(pieces, share, own0, own1, own_u, kern, par, *refs):
     earlier = []
     if len(pieces) > 1:
         earlier, refs = refs[:2], refs[2:]
     table_refs, own_out = refs[:7], refs[7]
     par_out, energy_out = refs[8 : 8 + len(pieces)], refs[8 + len(pieces)]
-    own_v, own_uv, kern_v, own_ov, par_ov, par_f, par_u, yw, z, x34 = refs[9 + len(pieces) : -13]
-    own_f, staged, total_ref = refs[-13:-10]
+    own_v, own_uv, kern_v, own_ov, par_ov, par_f, par_u, yw, z, x34 = refs[9 + len(pieces) : -16]
+    own_f, staged, total_ref = refs[-16:-13]
+    energy_v, before_v, parts_v = refs[-13:-10]
     tables, (par_sems, table_sems, sems) = refs[-10:-3], refs[-3:]
     t1, t2, t3, a1, a2, a3, sel = tables
     par_v = par_ov
     par_loads = []
-    first = 0
-    for src in par_refs:
-        for row in range(0, src.shape[0], STEP_ROWS):
-            sem = par_sems.at[first // STEP_ROWS]
-            par_loads.append(copy_rows(src, row, par_v, first, STEP_ROWS, sem))
-            first += STEP_ROWS
+    for first in (0, ROWS // 2):
+        sem = par_sems.at[len(par_loads)]
+        par_loads.append(copy_rows(par, first, par_v, first, ROWS // 2, sem))
     for load in par_loads:
         load.start()
     table_loads = [
@@ -234,18 +234,18 @@
     loads = [
         pltpu.make_async_copy(own_u, own_uv, sems.at[0]),
         pltpu.make_async_copy(kern, kern_v, sems.at[1]),
-        copy_rows(head, 0, own_v.at[0], 0, HEAD, sems.at[2]),
-        copy_rows(tail, 0, own_v.at[0], HEAD, ROWS - HEAD, sems.at[3]),
-        copy_rows(own1, 0, own_v.at[1], 0, ROWS, sems.at[4]),
+        copy_rows(own0, 0, own_v.at[0], 0, ROWS, sems.at[2]),
+        copy_rows(own1, 0, own_v.at[1], 0, ROWS, sems.at[3]),
     ]
     if earlier:
         loads.append(pltpu.make_async_copy(earlier[0], own_ov, sems.at[5]))
+        loads.append(pltpu.make_async_copy(earlier[1], before_v, sems.at[8 + len(pieces)]))
     for load in loads:
         load.start()
 
     for i, load in enumerate(par_loads):
         load.wait()
-        widen_planes(par_v.at[pl.ds(i * STEP_ROWS, STEP_ROWS), :], par_f, i * PLANES)
+        widen_planes(par_v.at[pl.ds(i * ROWS // 2, ROWS // 2), :], par_f, i * G // 2)
     table_loads[6].wait()
 
     @pl.loop(0, QUADS // 4, unroll=2)
@@ -398,31 +398,46 @@
 
         first += steps
 
-    energy = jnp.sum(total_ref[...]) * F32(share)
+    energy = jnp.zeros((8, LANES), F32) + jnp.sum(total_ref[...]) * F32(share)
     if earlier:
-        energy_out[...] = earlier[1][...] + energy
-    else:
-        energy_out[...] = jnp.zeros_like(energy_out) + energy
+        energy = energy + before_v[...]
+        row = lax.broadcasted_iota(jnp.int32, (8, LANES), 0)
+        rest, parts = energy, jnp.zeros_like(energy)
+        for i in range(3):
+            part = rest.astype(BF16).astype(F32)
+            parts = jnp.where(row == i, part, parts)
+            rest = rest - part
+        parts_v[...] = stack(parts, jnp.zeros_like(parts)).astype(BF16)
+        rider = copy_rows(parts_v, 0, par_out[0], pieces[0] * STEP_ROWS, RIDER, sems.at[9 + len(pieces)])
+        rider.start()
+    energy_v[...] = energy
+    report = pltpu.make_async_copy(energy_v, energy_out, sems.at[7 + len(pieces)])
+    report.start()
     pltpu.make_async_copy(own_ov, own_out, sems.at[6]).wait()
     first = 0
     for i, steps in enumerate(pieces):
         rows = steps * STEP_ROWS
         copy_rows(par_ov, first, par_out[i], 0, rows, sems.at[7 + i]).wait()
         first += rows
+    report.wait()
+    if earlier:
+        rider.wait()
 
 
 def pair_terms(own, own_u, partner, earlier, tables, kern, pieces, share, interpret=False):
-    vmem = pl.BlockSpec(memory_space=pltpu.VMEM)
     hbm = pl.BlockSpec(memory_space=pl.ANY)
     return pl.pallas_call(
-        functools.partial(pairs_kernel, len(partner), pieces, share),
+        functools.partial(pairs_kernel, pieces, share),
         out_shape=(
             jax.ShapeDtypeStruct((2, ROWS, LANES), F32),
-            *[jax.ShapeDtypeStruct((steps * STEP_ROWS, LANES), BF16) for steps in pieces],
+            *[
+                jax.ShapeDtypeStruct((steps * STEP_ROWS + (RIDER if earlier and i == 0 else 0), LANES), BF16)
+                for i, steps in enumerate(pieces)
+            ],
             jax.ShapeDtypeStruct((8, LANES), F32),
         ),
-        in_specs=[hbm] * (5 + len(partner)) + [hbm, vmem][: len(earlier)] + [hbm] * 7,
-        out_specs=(hbm, *[hbm] * len(pieces), vmem),
+        in_specs=[hbm] * (5 + len(earlier) + len(tables)),
+        out_specs=(hbm,) * (2 + len(pieces)),
         scratch_shapes=[
             pltpu.VMEM((2, ROWS, LANES), BF16),
             pltpu.VMEM((2, G, G, LANES), BF16),
@@ -437,10 +452,13 @@
             pltpu.VMEM((2, STEP_ROWS, LANES), F32),
             pltpu.VMEM((STEP_ROWS, LANES), F32),
             pltpu.VMEM((QUADS, LANES), F32),
+            pltpu.VMEM((8, LANES), F32),
+            pltpu.VMEM((8, LANES), F32),
+            pltpu.VMEM((RIDER, LANES), BF16),
             *[pltpu.VMEM(table.shape, BF16) for table in tables],
-            pltpu.SemaphoreType.DMA((STEPS,)),
+            pltpu.SemaphoreType.DMA((2,)),
             pltpu.SemaphoreType.DMA((len(tables),)),
-            pltpu.SemaphoreType.DMA((7 + len(pieces),)),
+            pltpu.SemaphoreType.DMA((10 + len(pieces),)),
         ],
         compiler_params=pltpu.CompilerParams(vmem_limit_bytes=56 * MIB),
         cost_estimate=pl.CostEstimate(
@@ -448,20 +466,20 @@
         ),
         interpret=interpret,
         name="pair_terms",
-    )(*own, own_u, kern, *partner, *earlier, *tables)
-
-
-def piece_kernel(first, last, head, tail, own1, terms, back0, back1, *rest):
-    gram_in = [] if first == 0 else [rest[0]]
-    out, gram_out, own_v, terms_v, back_v, out_v, gram_ref, load_sems, store_sem = rest[-9:]
-    size = back1.shape[0]
+    )(*own, own_u, kern, partner, *earlier, *tables)
+
+
+def piece_kernel(first, size, own0, own1, terms, back0, back1, *rest):
+    last = first + size == ROWS
+    earlier = rest[: len(rest) - 12]
+    out, gram_out, own_v, terms_v, back_v, out_v, gram_ref, gram_v, value_ref = rest[-12:-3]
+    load_sems, gram_sems, store_sems = rest[-3:]
     rows = size // load_sems.shape[0]
 
     def loads(c):
         start = first + c * rows
-        own0 = (head, start) if start < HEAD else (tail, start - HEAD)
         sources = [
-            (*own0, own_v.at[0]), (own1, start, own_v.at[1]), (terms, start, terms_v),
+            (own0, start, own_v.at[0]), (own1, start, own_v.at[1]), (terms, start, terms_v),
             (back0, start, back_v.at[0]), (back1, c * rows, back_v.at[1]),
         ]
         return [
@@ -473,7 +491,15 @@
     for chunk in chunks:
         for load in chunk:
             load.start()
-    gram_ref[...] = gram_in[0][...] if gram_in else jnp.zeros_like(gram_ref)
+    gram_loads = []
+    if last:
+        gram_loads = [
+            pltpu.make_async_copy(src, gram_v.at[i], gram_sems.at[i])
+            for i, src in enumerate(earlier[:-1])
+        ]
+        for load in gram_loads:
+            load.start()
+    gram_ref[...] = jnp.zeros_like(gram_ref)
     for c, chunk in enumerate(chunks):
         for load in chunk:
             load.wait()
@@ -485,46 +511,57 @@
             for i in range(2):
                 product = (own[i] * exchange).reshape(-1, 8, LANES)
                 gram_ref[i, p] += jnp.sum(product, axis=0)
-        copy_rows(out_v, 2 * c * rows, out, 2 * (first + c * rows), 2 * rows, store_sem).start()
-
-    if not last:
-        gram_out[...] = gram_ref[...]
-    else:
+        copy_rows(out_v, 2 * c * rows, out, 2 * (first + c * rows), 2 * rows, store_sems.at[0]).start()
+
+    result = gram_ref
+    if last:
+        for load in gram_loads:
+            load.wait()
         row = lax.broadcasted_iota(jnp.int32, (2, 2), 0)
         column = lax.broadcasted_iota(jnp.int32, (2, 2), 1)
         value = jnp.zeros((2, 2), F32)
         for i in range(2):
             for j in range(2):
-                entry = jnp.sum(gram_ref[i, j]) * F32(1.0 / NGRID)
-                value = jnp.where((row == i) & (column == j), entry, value)
-        gram_out[...] = value
-    copy_rows(out_v, 0, out, 2 * first, 2 * size, store_sem).wait()
-
-
-def add_piece(first, own, terms, back0, back1, earlier, interpret=False):
+                entry = gram_ref[i, j]
+                for k in range(len(gram_loads)):
+                    entry = entry + gram_v[k, i, j]
+                value = jnp.where((row == i) & (column == j), jnp.sum(entry) * F32(1.0 / NGRID), value)
+        value_ref[...] = value
+        result = value_ref
+    report = pltpu.make_async_copy(result, gram_out, store_sems.at[1])
+    report.start()
+    copy_rows(out_v, 0, out, 2 * first, 2 * size, store_sems.at[0]).wait()
+    report.wait()
+
+
+def add_piece(first, size, own, terms, back0, back1, grams, out, interpret=False):
     hbm = pl.BlockSpec(memory_space=pl.ANY)
-    vmem = pl.BlockSpec(memory_space=pltpu.VMEM)
-    size = back1.shape[0]
     last = first + size == ROWS
+    earlier = [] if out is None else [*(grams if last else []), out]
+    gram_shape = (2, 2, 8, LANES)
     return pl.pallas_call(
-        functools.partial(piece_kernel, first, last),
+        functools.partial(piece_kernel, first, size),
         out_shape=(
             jax.ShapeDtypeStruct((2 * ROWS, LANES), F32),
-            jax.ShapeDtypeStruct((2, 2) if last else (2, 2, 8, LANES), F32),
+            jax.ShapeDtypeStruct((2, 2) if last else gram_shape, F32),
         ),
-        in_specs=[hbm] * 6 + [vmem, hbm][: len(earlier)],
-        out_specs=(hbm, vmem),
+        in_specs=[hbm] * (5 + len(earlier)),
+        out_specs=(hbm, hbm),
         scratch_shapes=[
             pltpu.VMEM((2, size, LANES), BF16),
             pltpu.VMEM((2, size, LANES), F32),
             pltpu.VMEM((2, size, LANES), BF16),
             pltpu.VMEM((2 * size, LANES), F32),
-            pltpu.VMEM((2, 2, 8, LANES), F32),
+            pltpu.VMEM(gram_shape, F32),
+            pltpu.VMEM((len(PIECES), *gram_shape), F32),
+            pltpu.VMEM((2, 2), F32),
             pltpu.SemaphoreType.DMA((2 * size // STEP_ROWS, 5)),
-            pltpu.SemaphoreType.DMA,
+            pltpu.SemaphoreType.DMA((len(PIECES),)),
+            pltpu.SemaphoreType.DMA((2,)),
         ],
-        input_output_aliases={7: 0} if earlier else {},
+        input_output_aliases={4 + len(earlier): 0} if earlier else {},
         compiler_params=pltpu.CompilerParams(vmem_limit_bytes=44 * MIB),
+        cost_estimate=cost(24 * size * LANES),
         interpret=interpret,
         name="add_piece",
     )(*own, terms, back0, back1, *earlier)
@@ -538,7 +575,7 @@
 def send_to(value, axis, bits):
     size = lax.axis_size(axis)
     flips = sorted({bits[0], bits[-1], sum(bits)})
-    return [lax.ppermute(value, axis, [(i ^ flip, i) for i in range(size)]) for flip in flips]
+    return [lax.ppermute(value, axis, [(i ^ flip, i) for i in range(1, size, 2)]) for flip in flips]
 
 
 def add_up(value, got):
@@ -557,39 +594,48 @@
     size = lax.axis_size("band")
     share = -2.0 / (NGRID * 2 * size * orbitals.shape[0])
     raw = orbitals.reshape(2, ROWS, LANES).transpose(1, 0, 2).reshape(2 * ROWS, LANES)
-    head = take_band(raw, 0, 0, HEAD, 3)
-    tail = take_band(raw, 0, HEAD, ROWS - HEAD, 9, head)
-    own = [head, tail, take_band(raw, 1, 0, ROWS, 9, tail)]
+    own = [take_band(raw, 0)]
+    own.append(take_band(raw, 1, own))
     previous = [from_behind(part, "band", 1) for part in own]
     own_u = padded_rows(own, tables[-1])
     terms, back0, energy = pair_terms(
-        own, own_u, previous[:2], (), tables, kern, (STEPS,), share
+        own, own_u, previous[0], (), tables, kern, (STEPS,), share
     )
     back0 = from_behind(back0, "band", -1)
     terms, *sent, energy = pair_terms(
-        own, own_u, previous[2:], (terms, energy), tables, kern, PIECES, share
+        own, own_u, previous[1], (terms, energy), tables, kern, PIECES, share
     )
     back1 = [from_behind(piece, "band", -1) for piece in sent]
 
-    if size & (size - 1):
+    power = size & (size - 1) == 0
+    rounds = []
+    if power:
+        bits = [1 << b for b in range(2, size.bit_length() - 1)] + [2][: size // 4]
+        rounds = [bits[i : i + 2] for i in range(0, len(bits), 2)]
+        energy = energy + jnp.sum(back1[0][-RIDER:, :1].astype(F32))
+    else:
         energy = lax.psum(energy, "band")
-        groups = []
-    else:
-        bits = [1 << b for b in range(size.bit_length() - 1)]
-        rest = [b for b in bits if b != 2]
-        groups = [rest[i : i + 2] for i in range(0, len(rest), 2)]
-    for group in groups:
-        energy = add_up(energy, send_to(energy, "band", group))
-    result = ()
+    exchange, grams = None, []
     first = 0
-    for i, piece in enumerate(back1):
-        if groups and i == len(back1) - 1:
-            got = send_to(after(energy, result[1]), "band", [2])
-        result = add_piece(first, own, terms, back0, piece, result[::-1])
-        first += piece.shape[0]
-    exchange, gram = result
-    if groups:
-        energy = add_up(energy, after(got, gram))
+    for steps, piece in zip(PIECES, back1):
+        sent, got = bool(rounds), None
+        if rounds:
+            got = send_to(energy, "band", rounds.pop(0))
+        elif power and len(grams) == len(PIECES) - 1:
+            total = lax.ppermute(energy, "band", [(i + 1, i) for i in range(0, size, 2)])
+        size_rows = steps * STEP_ROWS
+        exchange, gram = add_piece(first, size_rows, own, terms, back0, piece, grams, exchange)
+        grams.append(gram)
+        first += size_rows
+        if got:
+            energy = add_up(energy, after(got, gram))
+    if power:
+        for bits in rounds:
+            energy = add_up(energy, send_to(energy, "band", bits))
+        if sent:
+            total = lax.ppermute(energy, "band", [(i + 1, i) for i in range(0, size, 2)])
+        odd = lax.axis_index("band") % 2 == 1
+        energy = jnp.where(odd, energy, after(total, gram))
     exchange = exchange.reshape(ROWS, 2, LANES).transpose(1, 0, 2).reshape(2, NGRID)
     return exchange, gram, energy[0, 0]
 

time: 132 us -> 133 us (level)
  the two profiles are of different devices: /device:TPU:0 before, /device:TPU:1 now
where the time goes in v6:
time: 133 us
  Pallas kernels  76.1 us (57%)
  starting transfers between devices  29.9 us (22%)
  waiting for transfers between devices  19 us (14%)
  other arithmetic  3.87 us (3%)
  local copies, waits for them, and re-layouts  3.32 us (2%)
    pallas_call x2, Pallas kernels, pair_terms(): pl.pallas_call(functools.partial(pairs_kernel, pieces, share), out_shape=...  46.1 us
    ppermute x6, waiting for transfers between devices, from_behind(): lax.ppermute(block, axis, [((i - distance) % size, i) for i in range(size)])  19 us
    ppermute x6, starting transfers between devices, send_to(): lax.ppermute(value, axis, [(i ^ flip, i) for i in range(1, size, 2)])  17.9 us
    pallas_call x3, Pallas kernels, add_piece(): pl.pallas_call(functools.partial(piece_kernel, first, size), out_shape=(j...  14.9 us
    ppermute x6, starting transfers between devices, from_behind(): lax.ppermute(block, axis, [((i - distance) % size, i) for i in range(size)])  10.1 us
    pallas_call x2, Pallas kernels, take_band(): pl.pallas_call(functools.partial(band_kernel, p), out_shape=jax.ShapeDtyp...  8.12 us
    pallas_call x1, Pallas kernels, padded_rows(): pl.pallas_call(rows_kernel, out_shape=jax.ShapeDtypeStruct((2, G, G, LANE...  7 us
    unnamed x14, local copies, waits for them, and re-layouts  2.8 us
  transfers between devices with their start and end apart: 13, of which 2 were waited for; matrix products, arithmetic and copies ran while one was open for 2% of the time, Pallas kernels for 54%

profile of v6, /device:TPU:1, one launch (start us, length us, event | category | flops | bytes accessed | tf_op | source)
XLA Modules:
  0.0 133.0 jit_solution(12988917231703418152)
XLA Ops:
  0.6 4.1 %take_band.2.refs_0_.own0 = bf16[6912,128]{1,0:T(8,128)(2,1)} custom-call(bf16[13824,128]{1,0:T(8,128)(2,1)} %bitcast.12), custom_call_target="tpu_custom_call" | custom-call | bytes 5308416 | tf_op jit(solution)/shard_map/take_band/pallas_call | solution.py:168
  4.7 2.7 %collective-permute-start.1 = (bf16[6912,128]{1,0:T(8,128)(2,1)}, bf16[6912,128]{1,0:T(8,128)(2,1)}, u32[]{:S(2)}, u32[]{:S(2)}) collective-permute-start(bf16[6912,128]{1,0:T(8,128)(2,1)} %take_band.2.refs_0_.own0), channel_id=1, source_target_pairs={{31,0},{0,1},{1,2},{2,3},{3,4},{4,5},{5,6},{6,7},{7,8},{8,9},{9,10... | collective-permute-start | bytes 5308424 | tf_op jit(solution)/shard_map/ppermute | solution.py:572
  7.4 4.1 %take_band.3.own1 = bf16[6912,128]{1,0:T(8,128)(2,1)} custom-call(bf16[13824,128]{1,0:T(8,128)(2,1)} %bitcast.13, bf16[6912,128]{1,0:T(8,128)(2,1)} %take_band.2.refs_0_.own0), custom_call_target="tpu_custom_call" | custom-call | bytes 5308416 | tf_op jit(solution)/shard_map/take_band/pallas_call | solution.py:168
  11.4 0.1 collective-permute-start
  11.5 7.0 %padded_rows.1.own_u = bf16[2,96,96,128]{3,2,1,0:T(8,128)(2,1)} custom-call(bf16[6912,128]{1,0:T(8,128)(2,1)} %take_band.2.refs_0_.own0, bf16[6912,128]{1,0:T(8,128)(2,1)} %take_band.3.own1, bf16[2,256,256]{2,1,0:T(8,128)(2,1)} %constant.36.clone.sel.refs_6_.refs_8_), custom_call_target="tpu_custom_call" | custom-call | bytes 14155776 | tf_op jit(solution)/shard_map/padded_rows/pallas_call | solution.py:197
  18.5 8.7 %collective-permute-done.1.par = bf16[6912,128]{1,0:T(8,128)(2,1)} collective-permute-done((bf16[6912,128]{1,0:T(8,128)(2,1)}, bf16[6912,128]{1,0:T(8,128)(2,1)}, u32[]{:S(2)}, u32[]{:S(2)}) %collective-permute-start.1) | collective-permute-done | bytes 1769504 | tf_op jit(solution)/shard_map/ppermute | solution.py:572
  27.1 21.5 %pair_terms.2 = (f32[2,6912,128]{2,1,0:T(8,128)}, bf16[6912,128]{1,0:T(8,128)(2,1)}, f32[8,128]{1,0:T(8,128)}) custom-call(bf16[6912,128]{1,0:T(8,128)(2,1)} %take_band.2.refs_0_.own0, bf16[6912,128]{1,0:T(8,128)(2,1)} %take_band.3.own1, bf16[2,96,96,128]{3,2,1,0:T(8,128)(2,1)} %padded_rows.1.own_u, f32[4800,128]{1,0:T(8,128)} %constant.37.clone.kern, ...), custom_call_target="tpu_custom_call" | custom-call | flops 20000000000 | bytes 20000000 | tf_op jit(solution)/shard_map/pair_terms/pallas_call | solution.py:429
  48.7 4.8 %collective-permute-start.2 = (bf16[6912,128]{1,0:T(8,128)(2,1)}, bf16[6912,128]{1,0:T(8,128)(2,1)S(1)}, u32[]{:S(2)}, u32[]{:S(2)}) collective-permute-start(bf16[6912,128]{1,0:T(8,128)(2,1)} %get-tuple-element.27), channel_id=1, source_target_pairs={{1,0},{2,1},{3,2},{4,3},{5,4},{6,5},{7,6},{8,7},{9,8},{10,9},{11,1... | collective-permute-start | bytes 5308424 | tf_op jit(solution)/shard_map/ppermute | solution.py:572
  53.5 0.0 collective-permute-done.par
  53.5 0.0 copy-start
  53.5 0.0 copy-start.1
  53.5 24.5 %pair_terms.3 = (f32[2,6912,128]{2,1,0:T(8,128)}, bf16[3472,128]{1,0:T(8,128)(2,1)}, bf16[2304,128]{1,0:T(8,128)(2,1)}, bf16[1152,128]{1,0:T(8,128)(2,1)}, f32[8,128]{1,0:T(8,128)}) custom-call(bf16[6912,128]{1,0:T(8,128)(2,1)} %take_band.2.refs_0_.own0, bf16[6912,128]{1,0:T(8,128)(2,1)} %take_band.3.own1, bf16[2,96,96,128]{3,2,1,0:T(8,128)(2,1)} %padded_rows.1.own_u, ...), custom_call_target="tpu_custom_call" | custom-call | flops 20000000000 | bytes 20000000 | tf_op jit(solution)/shard_map/pair_terms/pallas_call | solution.py:429
  78.0 0.1 collective-permute-start.4
  78.1 2.4 %collective-permute-start.5 = (bf16[2304,128]{1,0:T(8,128)(2,1)}, bf16[2304,128]{1,0:T(8,128)(2,1)S(1)}, u32[]{:S(2)}, u32[]{:S(2)}) collective-permute-start(bf16[2304,128]{1,0:T(8,128)(2,1)} %get-tuple-element.31), channel_id=1, source_target_pairs={{1,0},{2,1},{3,2},{4,3},{5,4},{6,5},{7,6},{8,7},{9,8},{10,9},{11,1... | collective-permute-start | bytes 1769480 | tf_op jit(solution)/shard_map/ppermute | solution.py:572
  80.5 10.3 %collective-permute-done.4.back1 = bf16[3472,128]{1,0:T(8,128)(2,1)S(1)} collective-permute-done((bf16[3472,128]{1,0:T(8,128)(2,1)}, bf16[3472,128]{1,0:T(8,128)(2,1)S(1)}, u32[]{:S(2)}, u32[]{:S(2)}) %collective-permute-start.4) | collective-permute-done | bytes 888864 | tf_op jit(solution)/shard_map/ppermute | solution.py:572
  90.8 0.6 convert_reduce_fusion
  91.4 1.3 %broadcast_add_fusion = f32[8,128]{1,0:T(8,128)S(1)} fusion(f32[8,128]{1,0:T(8,128)} %get-tuple-element.37, f32[]{:T(128)} %convert_reduce_fusion), kind=kLoop, calls=%fused_computation.3 | loop fusion | flops 1024 | bytes 8196 | tf_op jit(solution)/shard_map/add | solution.py:615
  92.7 1.9 %collective-permute-start.6 = (f32[8,128]{1,0:T(8,128)S(1)}, f32[8,128]{1,0:T(8,128)S(1)}, u32[]{:S(2)}, u32[]{:S(2)}) collective-permute-start(f32[8,128]{1,0:T(8,128)S(1)} %broadcast_add_fusion), channel_id=1, source_target_pairs={{5,1},{7,3},{1,5},{3,7},{13,9},{15,11},{9,13},{11,15},{21,17},{23,... | collective-permute-start | bytes 12296 | tf_op jit(solution)/shard_map/ppermute | solution.py:578
  94.7 2.1 %collective-permute-start.7 = (f32[8,128]{1,0:T(8,128)S(1)}, f32[8,128]{1,0:T(8,128)S(1)}, u32[]{:S(2)}, u32[]{:S(2)}) collective-permute-start(f32[8,128]{1,0:T(8,128)S(1)} %broadcast_add_fusion), channel_id=1, source_target_pairs={{9,1},{11,3},{13,5},{15,7},{1,9},{3,11},{5,13},{7,15},{25,17},{27,... | collective-permute-start | bytes 12296 | tf_op jit(solution)/shard_map/ppermute | solution.py:578
  96.8 4.3 %collective-permute-start.8 = (f32[8,128]{1,0:T(8,128)S(1)}, f32[8,128]{1,0:T(8,128)S(1)}, u32[]{:S(2)}, u32[]{:S(2)}) collective-permute-start(f32[8,128]{1,0:T(8,128)S(1)} %broadcast_add_fusion), channel_id=1, source_target_pairs={{13,1},{15,3},{9,5},{11,7},{5,9},{7,11},{1,13},{3,15},{29,17},{31,... | collective-permute-start | bytes 12296 | tf_op jit(solution)/shard_map/ppermute | solution.py:578
  101.1 0.0 collective-permute-done.2.back0
  101.1 0.0 copy-start.2
  101.1 0.1 collective-permute-start.3
  101.2 0.0 copy-done
  101.2 0.0 copy-done.1
  101.2 0.0 copy-start.6
  101.2 6.8 %add_piece.3 = (f32[13824,128]{1,0:T(8,128)}, f32[2,2,8,128]{3,2,1,0:T(8,128)S(1)}) custom-call(bf16[6912,128]{1,0:T(8,128)(2,1)S(1)} %copy-done, bf16[6912,128]{1,0:T(8,128)(2,1)S(1)} %copy-done.1, f32[2,6912,128]{2,1,0:T(8,128)} %get-tuple-element.26.terms, bf16[6912,128]{1,0:T(8,128)(2,1)S(1)} %collective-permute-done.2.back0, ...), custom_call_target="tpu_custom_call" | custom-call | bytes 10616832 | tf_op jit(solution)/shard_map/add_piece/pallas_call | solution.py:542
  108.0 0.0 collective-permute-done.6
  108.1 0.0 collective-permute-done.7
  108.1 0.0 collective-permute-done.8
  108.1 0.0 copy-done.6
  108.1 0.7 add_add_fusion.1
  108.7 2.8 %collective-permute-start.10 = (f32[8,128]{1,0:T(8,128)S(1)}, f32[8,128]{1,0:T(8,128)S(1)}, u32[]{:S(2)}, u32[]{:S(2)}) collective-permute-start(f32[8,128]{1,0:T(8,128)S(1)} %add_add_fusion.1), channel_id=1, source_target_pairs={{17,1},{19,3},{21,5},{23,7},{25,9},{27,11},{29,13},{31,15},{1,17},... | collective-permute-start | bytes 12296 | tf_op jit(solution)/shard_map/ppermute | solution.py:578
  111.6 4.5 %collective-permute-start.11 = (f32[8,128]{1,0:T(8,128)S(1)}, f32[8,128]{1,0:T(8,128)S(1)}, u32[]{:S(2)}, u32[]{:S(2)}) collective-permute-start(f32[8,128]{1,0:T(8,128)S(1)} %add_add_fusion.1), channel_id=1, source_target_pairs={{19,1},{17,3},{23,5},{21,7},{27,9},{25,11},{31,13},{29,15},{3,17},... | collective-permute-start | bytes 12296 | tf_op jit(solution)/shard_map/ppermute | solution.py:578
  116.1 2.2 %collective-permute-start.9 = (f32[8,128]{1,0:T(8,128)S(1)}, f32[8,128]{1,0:T(8,128)S(1)}, u32[]{:S(2)}, u32[]{:S(2)}) collective-permute-start(f32[8,128]{1,0:T(8,128)S(1)} %add_add_fusion.1), channel_id=1, source_target_pairs={{3,1},{1,3},{7,5},{5,7},{11,9},{9,11},{15,13},{13,15},{19,17},{17,... | collective-permute-start | bytes 12296 | tf_op jit(solution)/shard_map/ppermute | solution.py:578
  118.3 0.0 collective-permute-done.5.back1
  118.4 0.0 copy-done.2
  118.4 4.9 %add_piece.4 = (f32[13824,128]{1,0:T(8,128)}, f32[2,2,8,128]{3,2,1,0:T(8,128)S(1)}) custom-call(bf16[6912,128]{1,0:T(8,128)(2,1)S(1)} %copy-done, bf16[6912,128]{1,0:T(8,128)(2,1)S(1)} %copy-done.1, f32[2,6912,128]{2,1,0:T(8,128)} %get-tuple-element.26.terms, bf16[6912,128]{1,0:T(8,128)(2,1)S(1)} %collective-permute-done.2.back0, ...), custom_call_target="tpu_custom_call", output_to_operand_aliasing={{0}: (5, {})} | custom-call | bytes 7077888 | tf_op jit(solution)/shard_map/add_piece/pallas_call | solution.py:542
  123.3 0.0 copy-start.4
  123.3 0.6 copy-done.4
  123.9 0.0 collective-permute-done.10
  123.9 0.0 collective-permute-done.11
  123.9 0.0 collective-permute-done.9
  123.9 0.6 add_add_fusion
  124.5 1.9 %collective-permute-start.12 = (f32[8,128]{1,0:T(8,128)}, f32[8,128]{1,0:T(8,128)}, u32[]{:S(2)}, u32[]{:S(2)}) collective-permute-start(f32[8,128]{1,0:T(8,128)} %add_add_fusion), channel_id=1, source_target_pairs={{1,0},{3,2},{5,4},{7,6},{9,8},{11,10},{13,12},{15,14},{17,16},{19,... | collective-permute-start | bytes 12296 | tf_op jit(solution)/shard_map/ppermute | solution.py:625
  126.4 0.0 collective-permute-done.3.back1
  126.4 0.0 copy-start.3
  126.4 1.5 %copy-done.3 = bf16[6912,128]{1,0:T(8,128)(2,1)S(1)} copy-done((bf16[6912,128]{1,0:T(8,128)(2,1)S(1)}, bf16[6912,128]{1,0:T(8,128)(2,1)}, u32[]{:S(2)}) %copy-start.3) | copy-done | bytes 1769496
  127.9 0.0 copy-start.5
  127.9 0.7 copy-done.5
  128.6 3.2 %add_piece.5 = (f32[13824,128]{1,0:T(8,128)}, f32[2,2]{1,0:T(2,128)}) custom-call(bf16[6912,128]{1,0:T(8,128)(2,1)S(1)} %copy-done, bf16[6912,128]{1,0:T(8,128)(2,1)S(1)} %copy-done.1, f32[2,6912,128]{2,1,0:T(8,128)} %get-tuple-element.26.terms, bf16[6912,128]{1,0:T(8,128)(2,1)S(1)} %copy-done.3, ...), custom_call_target="tpu_custom_call", output_to_operand_aliasing={{0}: (7, {})} | custom-call | bytes 3538944 | tf_op jit(solution)/shard_map/add_piece/pallas_call | solution.py:542
  131.8 0.0 collective-permute-done.12
  131.8 0.7 broadcast_select_fusion
  132.5 0.5 slice.7
Async XLA Ops:
  4.7 22.4 %collective-permute-start.1 = (bf16[6912,128]{1,0:T(8,128)(2,1)}, bf16[6912,128]{1,0:T(8,128)(2,1)}, u32[]{:S(2)}, u32[]{:S(2)}) collective-permute-start(bf16[6912,128]{1,0:T(8,128)(2,1)} %take_band.2.refs_0_.own0), channel_id=1, source_target_pairs={{31,0},{0,1},{1,2},{2,3},{3,4},{4,5},{5,6},{6,7},{7,8},{8,9},{9,10... | collective-permute-start | bytes 5308424 | tf_op jit(solution)/shard_map/ppermute | solution.py:572
  11.4 42.1 %collective-permute-start = (bf16[6912,128]{1,0:T(8,128)(2,1)}, bf16[6912,128]{1,0:T(8,128)(2,1)}, u32[]{:S(2)}, u32[]{:S(2)}) collective-permute-start(bf16[6912,128]{1,0:T(8,128)(2,1)} %take_band.3.own1), channel_id=1, source_target_pairs={{31,0},{0,1},{1,2},{2,3},{3,4},{4,5},{5,6},{6,7},{7,8},{8,9},{9,10... | collective-permute-start | bytes 5308424 | tf_op jit(solution)/shard_map/ppermute | solution.py:572
  48.7 52.4 %collective-permute-start.2 = (bf16[6912,128]{1,0:T(8,128)(2,1)}, bf16[6912,128]{1,0:T(8,128)(2,1)S(1)}, u32[]{:S(2)}, u32[]{:S(2)}) collective-permute-start(bf16[6912,128]{1,0:T(8,128)(2,1)} %get-tuple-element.27), channel_id=1, source_target_pairs={{1,0},{2,1},{3,2},{4,3},{5,4},{6,5},{7,6},{8,7},{9,8},{10,9},{11,1... | collective-permute-start | bytes 5308424 | tf_op jit(solution)/shard_map/ppermute | solution.py:572
  53.5 47.7 %copy-start = (bf16[6912,128]{1,0:T(8,128)(2,1)S(1)}, bf16[6912,128]{1,0:T(8,128)(2,1)}, u32[]{:S(2)}) copy-start(bf16[6912,128]{1,0:T(8,128)(2,1)} %take_band.2.refs_0_.own0) | copy-start | bytes 5308420
  53.5 47.7 %copy-start.1 = (bf16[6912,128]{1,0:T(8,128)(2,1)S(1)}, bf16[6912,128]{1,0:T(8,128)(2,1)}, u32[]{:S(2)}) copy-start(bf16[6912,128]{1,0:T(8,128)(2,1)} %take_band.3.own1) | copy-start | bytes 5308420
  78.0 12.8 %collective-permute-start.4 = (bf16[3472,128]{1,0:T(8,128)(2,1)}, bf16[3472,128]{1,0:T(8,128)(2,1)S(1)}, u32[]{:S(2)}, u32[]{:S(2)}) collective-permute-start(bf16[3472,128]{1,0:T(8,128)(2,1)} %get-tuple-element.29), channel_id=1, source_target_pairs={{1,0},{2,1},{3,2},{4,3},{5,4},{6,5},{7,6},{8,7},{9,8},{10,9},{11,1... | collective-permute-start | bytes 2666504 | tf_op jit(solution)/shard_map/ppermute | solution.py:572
  78.1 40.2 %collective-permute-start.5 = (bf16[2304,128]{1,0:T(8,128)(2,1)}, bf16[2304,128]{1,0:T(8,128)(2,1)S(1)}, u32[]{:S(2)}, u32[]{:S(2)}) collective-permute-start(bf16[2304,128]{1,0:T(8,128)(2,1)} %get-tuple-element.31), channel_id=1, source_target_pairs={{1,0},{2,1},{3,2},{4,3},{5,4},{6,5},{7,6},{8,7},{9,8},{10,9},{11,1... | collective-permute-start | bytes 1769480 | tf_op jit(solution)/shard_map/ppermute | solution.py:572
  92.7 15.3 %collective-permute-start.6 = (f32[8,128]{1,0:T(8,128)S(1)}, f32[8,128]{1,0:T(8,128)S(1)}, u32[]{:S(2)}, u32[]{:S(2)}) collective-permute-start(f32[8,128]{1,0:T(8,128)S(1)} %broadcast_add_fusion), channel_id=1, source_target_pairs={{5,1},{7,3},{1,5},{3,7},{13,9},{15,11},{9,13},{11,15},{21,17},{23,... | collective-permute-start | bytes 12296 | tf_op jit(solution)/shard_map/ppermute | solution.py:578
  94.7 13.4 %collective-permute-start.7 = (f32[8,128]{1,0:T(8,128)S(1)}, f32[8,128]{1,0:T(8,128)S(1)}, u32[]{:S(2)}, u32[]{:S(2)}) collective-permute-start(f32[8,128]{1,0:T(8,128)S(1)} %broadcast_add_fusion), channel_id=1, source_target_pairs={{9,1},{11,3},{13,5},{15,7},{1,9},{3,11},{5,13},{7,15},{25,17},{27,... | collective-permute-start | bytes 12296 | tf_op jit(solution)/shard_map/ppermute | solution.py:578
  96.8 11.3 %collective-permute-start.8 = (f32[8,128]{1,0:T(8,128)S(1)}, f32[8,128]{1,0:T(8,128)S(1)}, u32[]{:S(2)}, u32[]{:S(2)}) collective-permute-start(f32[8,128]{1,0:T(8,128)S(1)} %broadcast_add_fusion), channel_id=1, source_target_pairs={{13,1},{15,3},{9,5},{11,7},{5,9},{7,11},{1,13},{3,15},{29,17},{31,... | collective-permute-start | bytes 12296 | tf_op jit(solution)/shard_map/ppermute | solution.py:578
  101.1 17.2 %copy-start.2 = (bf16[6912,128]{1,0:T(8,128)(2,1)}, bf16[6912,128]{1,0:T(8,128)(2,1)S(1)}, u32[]{:S(2)}) copy-start(bf16[6912,128]{1,0:T(8,128)(2,1)S(1)} %collective-permute-done.2.back0) | copy-start | bytes 5308420
  101.1 25.3 %collective-permute-start.3 = (bf16[1152,128]{1,0:T(8,128)(2,1)}, bf16[1152,128]{1,0:T(8,128)(2,1)}, u32[]{:S(2)}, u32[]{:S(2)}) collective-permute-start(bf16[1152,128]{1,0:T(8,128)(2,1)} %get-tuple-element.28), channel_id=1, source_target_pairs={{1,0},{2,1},{3,2},{4,3},{5,4},{6,5},{7,6},{8,7},{9,8},{10,9},{11,1... | collective-permute-start | bytes 884744 | tf_op jit(solution)/shard_map/ppermute | solution.py:572
  101.2 6.8 %copy-start.6 = (f32[8,128]{1,0:T(8,128)S(1)}, f32[8,128]{1,0:T(8,128)}, u32[]{:S(2)}) copy-start(f32[8,128]{1,0:T(8,128)} %get-tuple-element.37) | copy-start | bytes 12292
  108.7 15.2 %collective-permute-start.10 = (f32[8,128]{1,0:T(8,128)S(1)}, f32[8,128]{1,0:T(8,128)S(1)}, u32[]{:S(2)}, u32[]{:S(2)}) collective-permute-start(f32[8,128]{1,0:T(8,128)S(1)} %add_add_fusion.1), channel_id=1, source_target_pairs={{17,1},{19,3},{21,5},{23,7},{25,9},{27,11},{29,13},{31,15},{1,17},... | collective-permute-start | bytes 12296 | tf_op jit(solution)/shard_map/ppermute | solution.py:578
  111.6 12.3 %collective-permute-start.11 = (f32[8,128]{1,0:T(8,128)S(1)}, f32[8,128]{1,0:T(8,128)S(1)}, u32[]{:S(2)}, u32[]{:S(2)}) collective-permute-start(f32[8,128]{1,0:T(8,128)S(1)} %add_add_fusion.1), channel_id=1, source_target_pairs={{19,1},{17,3},{23,5},{21,7},{27,9},{25,11},{31,13},{29,15},{3,17},... | collective-permute-start | bytes 12296 | tf_op jit(solution)/shard_map/ppermute | solution.py:578
  116.1 7.8 %collective-permute-start.9 = (f32[8,128]{1,0:T(8,128)S(1)}, f32[8,128]{1,0:T(8,128)S(1)}, u32[]{:S(2)}, u32[]{:S(2)}) collective-permute-start(f32[8,128]{1,0:T(8,128)S(1)} %add_add_fusion.1), channel_id=1, source_target_pairs={{3,1},{1,3},{7,5},{5,7},{11,9},{9,11},{15,13},{13,15},{19,17},{17,... | collective-permute-start | bytes 12296 | tf_op jit(solution)/shard_map/ppermute | solution.py:578
  123.3 0.6 copy-start.4
  124.5 7.3 %collective-permute-start.12 = (f32[8,128]{1,0:T(8,128)}, f32[8,128]{1,0:T(8,128)}, u32[]{:S(2)}, u32[]{:S(2)}) collective-permute-start(f32[8,128]{1,0:T(8,128)} %add_add_fusion), channel_id=1, source_target_pairs={{1,0},{3,2},{5,4},{7,6},{9,8},{11,10},{13,12},{15,14},{17,16},{19,... | collective-permute-start | bytes 12296 | tf_op jit(solution)/shard_map/ppermute | solution.py:625
  126.4 1.5 %copy-start.3 = (bf16[6912,128]{1,0:T(8,128)(2,1)S(1)}, bf16[6912,128]{1,0:T(8,128)(2,1)}, u32[]{:S(2)}) copy-start(bf16[6912,128]{1,0:T(8,128)(2,1)} %copy-done.2) | copy-start | bytes 5308420
  127.9 0.7 copy-start.5

commit v7 on v6

--- a/solution.py
+++ b/solution.py
@@ -21,12 +21,12 @@
 Y_PITCH = Y_ROWS + 1
 Z_PITCH = G + 1
 W_PITCH = 2 * G + 1
+Z_ROWS = KPAD * Z_PITCH
 F_PITCH = PLANE + 1
 PLANES = 16
 STEP_ROWS = PLANES * PLANE
 STEPS = G // PLANES
 PIECES = (3, 2, 1)
-RIDER = 16
 WAVE_UNIT = 0.05
 SCREEN_SQ = 0.0121
 MIB = 1024 * 1024
@@ -176,7 +176,7 @@
             pltpu.SemaphoreType.DMA((9,)),
             pltpu.SemaphoreType.DMA,
         ],
-        compiler_params=pltpu.CompilerParams(vmem_limit_bytes=56 * MIB),
+        compiler_params=pltpu.CompilerParams(vmem_limit_bytes=63 * MIB),
         cost_estimate=cost(6 * ROWS * LANES),
         interpret=interpret,
         name="take_band",
@@ -213,9 +213,8 @@
         earlier, refs = refs[:2], refs[2:]
     table_refs, own_out = refs[:7], refs[7]
     par_out, energy_out = refs[8 : 8 + len(pieces)], refs[8 + len(pieces)]
-    own_v, own_uv, kern_v, own_ov, par_ov, par_f, par_u, yw, z, x34 = refs[9 + len(pieces) : -16]
-    own_f, staged, total_ref = refs[-16:-13]
-    energy_v, before_v, parts_v = refs[-13:-10]
+    own_v, own_uv, kern_v, own_ov, par_ov, par_f, par_u, yw, z, x34 = refs[9 + len(pieces) : -15]
+    own_f, staged, total_ref, energy_v, before_v = refs[-15:-10]
     tables, (par_sems, table_sems, sems) = refs[-10:-3], refs[-3:]
     t1, t2, t3, a1, a2, a3, sel = tables
     par_v = par_ov
@@ -229,22 +228,23 @@
         pltpu.make_async_copy(src, dst, table_sems.at[i])
         for i, (src, dst) in enumerate(zip(table_refs, tables))
     ]
-    for i in (6, 0, 1, 2, 3, 4, 5):
-        table_loads[i].start()
+    table_loads[6].start()
+    table_loads[0].start()
     loads = [
         pltpu.make_async_copy(own_u, own_uv, sems.at[0]),
         pltpu.make_async_copy(kern, kern_v, sems.at[1]),
         copy_rows(own0, 0, own_v.at[0], 0, ROWS, sems.at[2]),
         copy_rows(own1, 0, own_v.at[1], 0, ROWS, sems.at[3]),
     ]
+    later = []
     if earlier:
-        loads.append(pltpu.make_async_copy(earlier[0], own_ov, sems.at[5]))
+        later = [copy_rows(earlier[0].at[p], 0, z, p * ROWS, ROWS, sems.at[4 + p]) for p in range(2)]
         loads.append(pltpu.make_async_copy(earlier[1], before_v, sems.at[8 + len(pieces)]))
-    for load in loads:
-        load.start()
 
     for i, load in enumerate(par_loads):
         load.wait()
+        for other in ([loads[0]], table_loads[1:5])[i]:
+            other.start()
         widen_planes(par_v.at[pl.ds(i * ROWS // 2, ROWS // 2), :], par_f, i * G // 2)
     table_loads[6].wait()
 
@@ -254,6 +254,9 @@
 
     half_y = G * Y_PITCH
     loads[0].wait()
+    for load in loads[1:]:
+        load.start()
+    table_loads[5].start()
     table_loads[0].wait()
 
     @pl.loop(0, G // 2, unroll=8)
@@ -301,8 +304,8 @@
             spectrum = lanes(*[o[:, part * 64 : (part + 1) * 64] for o in out]).astype(F32)
             value = spectrum * factor
             for i in range(many):
-                row = (many * m + i) * Z_PITCH
-                z[part, pl.ds(row, G), :] = value[i * G : (i + 1) * G]
+                row = part * Z_ROWS + (many * m + i) * Z_PITCH
+                z[pl.ds(row, G), :] = value[i * G : (i + 1) * G]
 
     table_loads[3].wait()
 
@@ -314,10 +317,10 @@
             mirror = Z_PITCH + jnp.where(k2 == 0, 0, G - k2)
             parts.append(
                 stack(
-                    z[0, pl.ds(k2, G // 2, stride=Z_PITCH), :].astype(BF16),
-                    z[2, pl.ds(mirror, G // 2, stride=Z_PITCH), :].astype(BF16),
-                    z[1, pl.ds(k2, G // 2, stride=Z_PITCH), :].astype(BF16),
-                    z[3, pl.ds(mirror, G // 2, stride=Z_PITCH), :].astype(BF16),
+                    z[pl.ds(k2, G // 2, stride=Z_PITCH), :].astype(BF16),
+                    z[pl.ds(2 * Z_ROWS + mirror, G // 2, stride=Z_PITCH), :].astype(BF16),
+                    z[pl.ds(1 * Z_ROWS + k2, G // 2, stride=Z_PITCH), :].astype(BF16),
+                    z[pl.ds(3 * Z_ROWS + mirror, G // 2, stride=Z_PITCH), :].astype(BF16),
                 )
             )
         out = dot(a1[...], lanes(*parts))
@@ -325,6 +328,8 @@
             at = (4 * four + e) * W_PITCH
             yw[pl.ds(at, 2 * G), :] = out[:, e * LANES : (e + 1) * LANES]
 
+    for load in later:
+        load.start()
     table_loads[4].wait()
 
     @pl.loop(0, G // 4, unroll=6)
@@ -352,7 +357,7 @@
             x34[pl.ds(at, 4 * QUADS), left : left + 2 * LANES] = stack(*block).astype(BF16)
 
     table_loads[5].wait()
-    for load in loads[2:]:
+    for load in loads[2:] + later:
         load.wait()
     total_ref[...] = jnp.zeros_like(total_ref)
     block_rows = PLANES * QUADS
@@ -377,7 +382,10 @@
                 for p in range(2):
                     potential = out[i * QUADS : (i + 1) * QUADS, p * LANES : (p + 1) * LANES]
                     term = potential * partner
-                    own_ov[p, there, :] = own_ov[p, there, :] + term if earlier else term
+                    if earlier:
+                        at = p * ROWS + plane * PLANE + third
+                        term = term + z[pl.ds(at, QUADS, stride=3), :]
+                    own_ov[p, there, :] = term
                     sent = sent + potential * own_f[p, here, :]
                 total = total + sent * partner
                 staged[here, :] = sent
@@ -401,15 +409,6 @@
     energy = jnp.zeros((8, LANES), F32) + jnp.sum(total_ref[...]) * F32(share)
     if earlier:
         energy = energy + before_v[...]
-        row = lax.broadcasted_iota(jnp.int32, (8, LANES), 0)
-        rest, parts = energy, jnp.zeros_like(energy)
-        for i in range(3):
-            part = rest.astype(BF16).astype(F32)
-            parts = jnp.where(row == i, part, parts)
-            rest = rest - part
-        parts_v[...] = stack(parts, jnp.zeros_like(parts)).astype(BF16)
-        rider = copy_rows(parts_v, 0, par_out[0], pieces[0] * STEP_ROWS, RIDER, sems.at[9 + len(pieces)])
-        rider.start()
     energy_v[...] = energy
     report = pltpu.make_async_copy(energy_v, energy_out, sems.at[7 + len(pieces)])
     report.start()
@@ -420,8 +419,6 @@
         copy_rows(par_ov, first, par_out[i], 0, rows, sems.at[7 + i]).wait()
         first += rows
     report.wait()
-    if earlier:
-        rider.wait()
 
 
 def pair_terms(own, own_u, partner, earlier, tables, kern, pieces, share, interpret=False):
@@ -430,10 +427,7 @@
         functools.partial(pairs_kernel, pieces, share),
         out_shape=(
             jax.ShapeDtypeStruct((2, ROWS, LANES), F32),
-            *[
-                jax.ShapeDtypeStruct((steps * STEP_ROWS + (RIDER if earlier and i == 0 else 0), LANES), BF16)
-                for i, steps in enumerate(pieces)
-            ],
+            *[jax.ShapeDtypeStruct((steps * STEP_ROWS, LANES), BF16) for steps in pieces],
             jax.ShapeDtypeStruct((8, LANES), F32),
         ),
         in_specs=[hbm] * (5 + len(earlier) + len(tables)),
@@ -447,20 +441,19 @@
             pltpu.VMEM((G * F_PITCH, LANES), F32),
             pltpu.VMEM((G, G, LANES), BF16),
             pltpu.VMEM((2 * G * Y_PITCH, LANES), F32),
-            pltpu.VMEM((4, KPAD * Z_PITCH, LANES), F32),
+            pltpu.VMEM((4 * Z_ROWS, LANES), F32),
             pltpu.VMEM((KPAD * G, 4 * LANES), BF16),
             pltpu.VMEM((2, STEP_ROWS, LANES), F32),
             pltpu.VMEM((STEP_ROWS, LANES), F32),
             pltpu.VMEM((QUADS, LANES), F32),
             pltpu.VMEM((8, LANES), F32),
             pltpu.VMEM((8, LANES), F32),
-            pltpu.VMEM((RIDER, LANES), BF16),
             *[pltpu.VMEM(table.shape, BF16) for table in tables],
             pltpu.SemaphoreType.DMA((2,)),
             pltpu.SemaphoreType.DMA((len(tables),)),
-            pltpu.SemaphoreType.DMA((10 + len(pieces),)),
+            pltpu.SemaphoreType.DMA((9 + len(pieces),)),
         ],
-        compiler_params=pltpu.CompilerParams(vmem_limit_bytes=56 * MIB),
+        compiler_params=pltpu.CompilerParams(vmem_limit_bytes=63 * MIB),
         cost_estimate=pl.CostEstimate(
             flops=20_000_000_000, bytes_accessed=20_000_000, transcendentals=0
         ),
@@ -572,18 +565,6 @@
     return lax.ppermute(block, axis, [((i - distance) % size, i) for i in range(size)])
 
 
-def send_to(value, axis, bits):
-    size = lax.axis_size(axis)
-    flips = sorted({bits[0], bits[-1], sum(bits)})
-    return [lax.ppermute(value, axis, [(i ^ flip, i) for i in range(1, size, 2)]) for flip in flips]
-
-
-def add_up(value, got):
-    if len(got) == 1:
-        return value + got[0]
-    return (value + got[0]) + (got[1] + got[2])
-
-
 def after(values, other):
     return lax.optimization_barrier((values, other))[0]
 
@@ -607,37 +588,18 @@
     )
     back1 = [from_behind(piece, "band", -1) for piece in sent]
 
-    power = size & (size - 1) == 0
-    rounds = []
-    if power:
-        bits = [1 << b for b in range(2, size.bit_length() - 1)] + [2][: size // 4]
-        rounds = [bits[i : i + 2] for i in range(0, len(bits), 2)]
-        energy = energy + jnp.sum(back1[0][-RIDER:, :1].astype(F32))
-    else:
-        energy = lax.psum(energy, "band")
+    energies = lax.all_gather(energy, "band")
+
     exchange, grams = None, []
     first = 0
     for steps, piece in zip(PIECES, back1):
-        sent, got = bool(rounds), None
-        if rounds:
-            got = send_to(energy, "band", rounds.pop(0))
-        elif power and len(grams) == len(PIECES) - 1:
-            total = lax.ppermute(energy, "band", [(i + 1, i) for i in range(0, size, 2)])
-        size_rows = steps * STEP_ROWS
-        exchange, gram = add_piece(first, size_rows, own, terms, back0, piece, grams, exchange)
+        count = steps * STEP_ROWS
+        exchange, gram = add_piece(first, count, own, terms, back0, piece, grams, exchange)
         grams.append(gram)
-        first += size_rows
-        if got:
-            energy = add_up(energy, after(got, gram))
-    if power:
-        for bits in rounds:
-            energy = add_up(energy, send_to(energy, "band", bits))
-        if sent:
-            total = lax.ppermute(energy, "band", [(i + 1, i) for i in range(0, size, 2)])
-        odd = lax.axis_index("band") % 2 == 1
-        energy = jnp.where(odd, energy, after(total, gram))
+        first += count
+    energy = jnp.sum(after(energies, gram)[:, 0, 0])
     exchange = exchange.reshape(ROWS, 2, LANES).transpose(1, 0, 2).reshape(2, NGRID)
-    return exchange, gram, energy[0, 0]
+    return exchange, gram, energy
 
 
 def solution(mesh):

time: 133 us -> 147 us (1.11)
  the two profiles are of different devices: /device:TPU:1 before, /device:TPU:0 now
where the time goes in v7:
time: 147 us
  Pallas kernels  68.9 us (47%)
  blocking collectives  53.8 us (37%)
  waiting for transfers between devices  12.7 us (9%)
  starting transfers between devices  7.38 us (5%)
  local copies, waits for them, and re-layouts  2.95 us (2%)
    all_gather x1, blocking collectives, per_device(): energies = lax.all_gather(energy, 'band')  53.8 us
    pallas_call x2, Pallas kernels, pair_terms(): pl.pallas_call(functools.partial(pairs_kernel, pieces, share), out_shape=...  40.5 us
    pallas_call x3, Pallas kernels, add_piece(): pl.pallas_call(functools.partial(piece_kernel, first, size), out_shape=(j...  13.2 us
    ppermute x6, waiting for transfers between devices, from_behind(): lax.ppermute(block, axis, [((i - distance) % size, i) for i in range(size)])  12.7 us
    pallas_call x2, Pallas kernels, take_band(): pl.pallas_call(functools.partial(band_kernel, p), out_shape=jax.ShapeDtyp...  8.12 us
    ppermute x6, starting transfers between devices, from_behind(): lax.ppermute(block, axis, [((i - distance) % size, i) for i in range(size)])  7.38 us
    pallas_call x1, Pallas kernels, padded_rows(): pl.pallas_call(rows_kernel, out_shape=jax.ShapeDtypeStruct((2, G, G, LANE...  7.01 us
    unnamed x4, local copies, waits for them, and re-layouts  2.95 us
  transfers between devices with their start and end apart: 6, of which 1 were waited for; matrix products, arithmetic and copies ran while one was open for 0% of the time, Pallas kernels for 42%

profile of v7, /device:TPU:0, one launch (start us, length us, event | category | flops | bytes accessed | tf_op | source)
XLA Modules:
  0.0 147.0 jit_solution(7209236969840711383)
XLA Ops:
  0.6 4.1 %take_band.2.refs_0_.own0 = bf16[6912,128]{1,0:T(8,128)(2,1)} custom-call(bf16[13824,128]{1,0:T(8,128)(2,1)} %bitcast.12), custom_call_target="tpu_custom_call" | custom-call | bytes 5308416 | tf_op jit(solution)/shard_map/take_band/pallas_call | solution.py:168
  4.7 0.5 collective-permute-start.1
  5.2 4.1 %take_band.3.own1 = bf16[6912,128]{1,0:T(8,128)(2,1)} custom-call(bf16[13824,128]{1,0:T(8,128)(2,1)} %bitcast.13, bf16[6912,128]{1,0:T(8,128)(2,1)} %take_band.2.refs_0_.own0), custom_call_target="tpu_custom_call" | custom-call | bytes 5308416 | tf_op jit(solution)/shard_map/take_band/pallas_call | solution.py:168
  9.3 2.7 %collective-permute-start = (bf16[6912,128]{1,0:T(8,128)(2,1)}, bf16[6912,128]{1,0:T(8,128)(2,1)}, u32[]{:S(2)}, u32[]{:S(2)}) collective-permute-start(bf16[6912,128]{1,0:T(8,128)(2,1)} %take_band.3.own1), channel_id=1, source_target_pairs={{31,0},{0,1},{1,2},{2,3},{3,4},{4,5},{5,6},{6,7},{7,8},{8,9},{9,10... | collective-permute-start | bytes 5308424 | tf_op jit(solution)/shard_map/ppermute | solution.py:565
  11.9 7.0 %padded_rows.1.own_u = bf16[2,96,96,128]{3,2,1,0:T(8,128)(2,1)} custom-call(bf16[6912,128]{1,0:T(8,128)(2,1)} %take_band.2.refs_0_.own0, bf16[6912,128]{1,0:T(8,128)(2,1)} %take_band.3.own1, bf16[2,256,256]{2,1,0:T(8,128)(2,1)} %constant.18.clone.sel.refs_6_.refs_8_), custom_call_target="tpu_custom_call" | custom-call | bytes 14155776 | tf_op jit(solution)/shard_map/padded_rows/pallas_call | solution.py:197
  18.9 12.7 %collective-permute-done.1.par = bf16[6912,128]{1,0:T(8,128)(2,1)} collective-permute-done((bf16[6912,128]{1,0:T(8,128)(2,1)}, bf16[6912,128]{1,0:T(8,128)(2,1)}, u32[]{:S(2)}, u32[]{:S(2)}) %collective-permute-start.1) | collective-permute-done | bytes 1769504 | tf_op jit(solution)/shard_map/ppermute | solution.py:565
  31.7 19.7 %pair_terms.2 = (f32[2,6912,128]{2,1,0:T(8,128)}, bf16[6912,128]{1,0:T(8,128)(2,1)}, f32[8,128]{1,0:T(8,128)}) custom-call(bf16[6912,128]{1,0:T(8,128)(2,1)} %take_band.2.refs_0_.own0, bf16[6912,128]{1,0:T(8,128)(2,1)} %take_band.3.own1, bf16[2,96,96,128]{3,2,1,0:T(8,128)(2,1)} %padded_rows.1.own_u, f32[4800,128]{1,0:T(8,128)} %constant.19.clone.kern, ...), custom_call_target="tpu_custom_call" | custom-call | flops 20000000000 | bytes 20000000 | tf_op jit(solution)/shard_map/pair_terms/pallas_call | solution.py:426
  51.4 0.2 collective-permute-start.2
  51.6 0.0 collective-permute-done.par
  51.6 20.8 %pair_terms.3 = (f32[2,6912,128]{2,1,0:T(8,128)}, bf16[3456,128]{1,0:T(8,128)(2,1)}, bf16[2304,128]{1,0:T(8,128)(2,1)}, bf16[1152,128]{1,0:T(8,128)(2,1)}, f32[8,128]{1,0:T(8,128)}) custom-call(bf16[6912,128]{1,0:T(8,128)(2,1)} %take_band.2.refs_0_.own0, bf16[6912,128]{1,0:T(8,128)(2,1)} %take_band.3.own1, bf16[2,96,96,128]{3,2,1,0:T(8,128)(2,1)} %padded_rows.1.own_u, ...), custom_call_target="tpu_custom_call" | custom-call | flops 20000000000 | bytes 20000000 | tf_op jit(solution)/shard_map/pair_terms/pallas_call | solution.py:426
  72.5 2.4 %collective-permute-start.4 = (bf16[3456,128]{1,0:T(8,128)(2,1)}, bf16[3456,128]{1,0:T(8,128)(2,1)S(1)}, u32[]{:S(2)}, u32[]{:S(2)}) collective-permute-start(bf16[3456,128]{1,0:T(8,128)(2,1)} %get-tuple-element.23), channel_id=1, source_target_pairs={{1,0},{2,1},{3,2},{4,3},{5,4},{6,5},{7,6},{8,7},{9,8},{10,9},{11,1... | collective-permute-start | bytes 2654216 | tf_op jit(solution)/shard_map/ppermute | solution.py:565
  74.9 0.1 collective-permute-start.5
  74.9 1.5 %collective-permute-start.3 = (bf16[1152,128]{1,0:T(8,128)(2,1)}, bf16[1152,128]{1,0:T(8,128)(2,1)S(1)}, u32[]{:S(2)}, u32[]{:S(2)}) collective-permute-start(bf16[1152,128]{1,0:T(8,128)(2,1)} %get-tuple-element.22), channel_id=1, source_target_pairs={{1,0},{2,1},{3,2},{4,3},{5,4},{6,5},{7,6},{8,7},{9,8},{10,9},{11,1... | collective-permute-start | bytes 884744 | tf_op jit(solution)/shard_map/ppermute | solution.py:565
  76.4 53.8 %all-gather = f32[256,128]{1,0:T(8,128)S(1)} all-gather(f32[8,128]{1,0:T(8,128)} %get-tuple-element.31), channel_id=2, replica_groups=mesh['band'=32] {'band'}, dimensions={0}, use_global_device_ids=true | all-gather | bytes 135168 | tf_op jit(solution)/shard_map/all_gather | solution.py:591
  130.2 0.0 collective-permute-done.4.back1
  130.2 0.0 collective-permute-done.2.back0
  130.2 0.0 copy-start
  130.2 1.5 %copy-done = bf16[6912,128]{1,0:T(8,128)(2,1)S(1)} copy-done((bf16[6912,128]{1,0:T(8,128)(2,1)S(1)}, bf16[6912,128]{1,0:T(8,128)(2,1)}, u32[]{:S(2)}) %copy-start) | copy-done | bytes 1769496
  131.7 0.0 copy-start.1
  131.7 1.5 %copy-done.1 = bf16[6912,128]{1,0:T(8,128)(2,1)S(1)} copy-done((bf16[6912,128]{1,0:T(8,128)(2,1)S(1)}, bf16[6912,128]{1,0:T(8,128)(2,1)}, u32[]{:S(2)}) %copy-start.1) | copy-done | bytes 1769496
  133.1 5.6 %add_piece.3 = (f32[13824,128]{1,0:T(8,128)}, f32[2,2,8,128]{3,2,1,0:T(8,128)S(1)}) custom-call(bf16[6912,128]{1,0:T(8,128)(2,1)S(1)} %copy-done, bf16[6912,128]{1,0:T(8,128)(2,1)S(1)} %copy-done.1, f32[2,6912,128]{2,1,0:T(8,128)} %get-tuple-element.20.terms, bf16[6912,128]{1,0:T(8,128)(2,1)} %collective-permute-done.2.back0, ...), custom_call_target="tpu_custom_call" | custom-call | bytes 10616832 | tf_op jit(solution)/shard_map/add_piece/pallas_call | solution.py:535
  138.8 0.0 collective-permute-done.5.back1
  138.8 4.4 %add_piece.4 = (f32[13824,128]{1,0:T(8,128)}, f32[2,2,8,128]{3,2,1,0:T(8,128)S(1)}) custom-call(bf16[6912,128]{1,0:T(8,128)(2,1)S(1)} %copy-done, bf16[6912,128]{1,0:T(8,128)(2,1)S(1)} %copy-done.1, f32[2,6912,128]{2,1,0:T(8,128)} %get-tuple-element.20.terms, bf16[6912,128]{1,0:T(8,128)(2,1)} %collective-permute-done.2.back0, ...), custom_call_target="tpu_custom_call", output_to_operand_aliasing={{0}: (5, {})} | custom-call | bytes 7077888 | tf_op jit(solution)/shard_map/add_piece/pallas_call | solution.py:535
  143.2 0.0 collective-permute-done.3.back1
  143.2 3.2 %add_piece.5 = (f32[13824,128]{1,0:T(8,128)}, f32[2,2]{1,0:T(2,128)}) custom-call(bf16[6912,128]{1,0:T(8,128)(2,1)S(1)} %copy-done, bf16[6912,128]{1,0:T(8,128)(2,1)S(1)} %copy-done.1, f32[2,6912,128]{2,1,0:T(8,128)} %get-tuple-element.20.terms, bf16[6912,128]{1,0:T(8,128)(2,1)} %collective-permute-done.2.back0, ...), custom_call_target="tpu_custom_call", output_to_operand_aliasing={{0}: (7, {})} | custom-call | bytes 3538944 | tf_op jit(solution)/shard_map/add_piece/pallas_call | solution.py:535
  146.4 0.6 slice_reduce_fusion
Async XLA Ops:
  4.7 26.9 %collective-permute-start.1 = (bf16[6912,128]{1,0:T(8,128)(2,1)}, bf16[6912,128]{1,0:T(8,128)(2,1)}, u32[]{:S(2)}, u32[]{:S(2)}) collective-permute-start(bf16[6912,128]{1,0:T(8,128)(2,1)} %take_band.2.refs_0_.own0), channel_id=1, source_target_pairs={{31,0},{0,1},{1,2},{2,3},{3,4},{4,5},{5,6},{6,7},{7,8},{8,9},{9,10... | collective-permute-start | bytes 5308424 | tf_op jit(solution)/shard_map/ppermute | solution.py:565
  9.3 42.3 %collective-permute-start = (bf16[6912,128]{1,0:T(8,128)(2,1)}, bf16[6912,128]{1,0:T(8,128)(2,1)}, u32[]{:S(2)}, u32[]{:S(2)}) collective-permute-start(bf16[6912,128]{1,0:T(8,128)(2,1)} %take_band.3.own1), channel_id=1, source_target_pairs={{31,0},{0,1},{1,2},{2,3},{3,4},{4,5},{5,6},{6,7},{7,8},{8,9},{9,10... | collective-permute-start | bytes 5308424 | tf_op jit(solution)/shard_map/ppermute | solution.py:565
  51.4 78.8 %collective-permute-start.2 = (bf16[6912,128]{1,0:T(8,128)(2,1)}, bf16[6912,128]{1,0:T(8,128)(2,1)}, u32[]{:S(2)}, u32[]{:S(2)}) collective-permute-start(bf16[6912,128]{1,0:T(8,128)(2,1)} %get-tuple-element.21), channel_id=1, source_target_pairs={{1,0},{2,1},{3,2},{4,3},{5,4},{6,5},{7,6},{8,7},{9,8},{10,9},{11,1... | collective-permute-start | bytes 5308424 | tf_op jit(solution)/shard_map/ppermute | solution.py:565
  72.5 57.7 %collective-permute-start.4 = (bf16[3456,128]{1,0:T(8,128)(2,1)}, bf16[3456,128]{1,0:T(8,128)(2,1)S(1)}, u32[]{:S(2)}, u32[]{:S(2)}) collective-permute-start(bf16[3456,128]{1,0:T(8,128)(2,1)} %get-tuple-element.23), channel_id=1, source_target_pairs={{1,0},{2,1},{3,2},{4,3},{5,4},{6,5},{7,6},{8,7},{9,8},{10,9},{11,1... | collective-permute-start | bytes 2654216 | tf_op jit(solution)/shard_map/ppermute | solution.py:565
  74.9 63.9 %collective-permute-start.5 = (bf16[2304,128]{1,0:T(8,128)(2,1)}, bf16[2304,128]{1,0:T(8,128)(2,1)S(1)}, u32[]{:S(2)}, u32[]{:S(2)}) collective-permute-start(bf16[2304,128]{1,0:T(8,128)(2,1)} %get-tuple-element.25), channel_id=1, source_target_pairs={{1,0},{2,1},{3,2},{4,3},{5,4},{6,5},{7,6},{8,7},{9,8},{10,9},{11,1... | collective-permute-start | bytes 1769480 | tf_op jit(solution)/shard_map/ppermute | solution.py:565
  74.9 68.3 %collective-permute-start.3 = (bf16[1152,128]{1,0:T(8,128)(2,1)}, bf16[1152,128]{1,0:T(8,128)(2,1)S(1)}, u32[]{:S(2)}, u32[]{:S(2)}) collective-permute-start(bf16[1152,128]{1,0:T(8,128)(2,1)} %get-tuple-element.22), channel_id=1, source_target_pairs={{1,0},{2,1},{3,2},{4,3},{5,4},{6,5},{7,6},{8,7},{9,8},{10,9},{11,1... | collective-permute-start | bytes 884744 | tf_op jit(solution)/shard_map/ppermute | solution.py:565
  130.2 1.5 %copy-start = (bf16[6912,128]{1,0:T(8,128)(2,1)S(1)}, bf16[6912,128]{1,0:T(8,128)(2,1)}, u32[]{:S(2)}) copy-start(bf16[6912,128]{1,0:T(8,128)(2,1)} %take_band.2.refs_0_.own0) | copy-start | bytes 5308420
  131.7 1.5 %copy-start.1 = (bf16[6912,128]{1,0:T(8,128)(2,1)S(1)}, bf16[6912,128]{1,0:T(8,128)(2,1)}, u32[]{:S(2)}) copy-start(bf16[6912,128]{1,0:T(8,128)(2,1)} %take_band.3.own1) | copy-start | bytes 5308420

commit v8 on v7

--- a/solution.py
+++ b/solution.py
@@ -26,7 +26,7 @@
 PLANES = 16
 STEP_ROWS = PLANES * PLANE
 STEPS = G // PLANES
-PIECES = (3, 2, 1)
+PIECES = (4, 2)
 WAVE_UNIT = 0.05
 SCREEN_SQ = 0.0121
 MIB = 1024 * 1024
@@ -553,7 +553,7 @@
             pltpu.SemaphoreType.DMA((2,)),
         ],
         input_output_aliases={4 + len(earlier): 0} if earlier else {},
-        compiler_params=pltpu.CompilerParams(vmem_limit_bytes=44 * MIB),
+        compiler_params=pltpu.CompilerParams(vmem_limit_bytes=52 * MIB),
         cost_estimate=cost(24 * size * LANES),
         interpret=interpret,
         name="add_piece",
@@ -563,6 +563,11 @@
 def from_behind(block, axis, distance):
     size = lax.axis_size(axis)
     return lax.ppermute(block, axis, [((i - distance) % size, i) for i in range(size)])
+
+
+def send_to(value, axis, flip):
+    size = lax.axis_size(axis)
+    return lax.ppermute(value, axis, [(i ^ flip, i) for i in range(size)])
 
 
 def after(values, other):
@@ -588,18 +593,28 @@
     )
     back1 = [from_behind(piece, "band", -1) for piece in sent]
 
-    energies = lax.all_gather(energy, "band")
-
-    exchange, grams = None, []
+    steps = []
+    if size & (size - 1):
+        energy = lax.psum(energy, "band")
+    else:
+        steps = [1 << b for b in range(size.bit_length() - 1)]
+        steps = [b for b in steps if b != 2] + [b for b in steps if b == 2]
+    while len(steps) > len(back1):
+        energy = energy + send_to(energy, "band", steps.pop(0))
+    exchange, grams, got = None, [], None
     first = 0
-    for steps, piece in zip(PIECES, back1):
-        count = steps * STEP_ROWS
+    for count, piece in zip(PIECES, back1):
+        count *= STEP_ROWS
+        if steps:
+            got = send_to(energy, "band", steps.pop(0))
         exchange, gram = add_piece(first, count, own, terms, back0, piece, grams, exchange)
+        if got is not None:
+            energy = energy + after(got, gram)
+            got = None
         grams.append(gram)
         first += count
-    energy = jnp.sum(after(energies, gram)[:, 0, 0])
     exchange = exchange.reshape(ROWS, 2, LANES).transpose(1, 0, 2).reshape(2, NGRID)
-    return exchange, gram, energy
+    return exchange, gram, energy[0, 0]
 
 
 def solution(mesh):

time: 147 us -> 107 us (0.73)
  blocking collectives: 53.8 us -> 0 us
  waiting for transfers between devices: 12.7 us -> 32.1 us
  Pallas kernels: 68.9 us -> 65.2 us
  local copies, waits for them, and re-layouts: 2.95 us -> 0.51 us
    all_gather x1 -> x0, blocking collectives: 53.8 us -> none  [per_device(): energies = lax.all_gather(energy, 'band')]
    ppermute x0 -> x5, waiting for transfers between devices: none -> 19.4 us  [send_to(): return lax.ppermute(value, axis, [(i ^ flip, i) for i in range(size)])]
    pallas_call x3 -> x2, Pallas kernels: 13.2 us -> 9.4 us  [add_piece(): pl.pallas_call(functools.partial(piece_kernel, first, size), out_shape=(j...]
    unnamed x4 -> x0, local copies, waits for them, and re-layouts: 2.95 us -> none
    ppermute x0 -> x5, starting transfers between devices: none -> 1.94 us  [send_to(): return lax.ppermute(value, axis, [(i ^ flip, i) for i in range(size)])]
    ppermute x6 -> x5, starting transfers between devices: 7.38 us -> 5.9 us  [from_behind(): lax.ppermute(block, axis, [((i - distance) % size, i) for i in range(size)])]
    ppermute x6 -> x5, waiting for transfers between devices: 12.7 us -> 12.7 us  [from_behind(): lax.ppermute(block, axis, [((i - distance) % size, i) for i in range(size)])]
  transfers between devices with their start and end apart: 6 -> 10, of which waited for: 1 -> 5; matrix products, arithmetic and copies ran while one was open for 0% -> 1% of each run, Pallas kernels for 42% -> 57%
where the time goes in v8:
time: 107 us
  Pallas kernels  65.2 us (61%)
  waiting for transfers between devices  32.1 us (30%)
  starting transfers between devices  7.83 us (7%)
    pallas_call x2, Pallas kernels, pair_terms(): pl.pallas_call(functools.partial(pairs_kernel, pieces, share), out_shape=...  40.7 us
    ppermute x5, waiting for transfers between devices, send_to(): return lax.ppermute(value, axis, [(i ^ flip, i) for i in range(size)])  19.4 us
    ppermute x5, waiting for transfers between devices, from_behind(): lax.ppermute(block, axis, [((i - distance) % size, i) for i in range(size)])  12.7 us
    pallas_call x2, Pallas kernels, add_piece(): pl.pallas_call(functools.partial(piece_kernel, first, size), out_shape=(j...  9.4 us
    pallas_call x2, Pallas kernels, take_band(): pl.pallas_call(functools.partial(band_kernel, p), out_shape=jax.ShapeDtyp...  8.11 us
    pallas_call x1, Pallas kernels, padded_rows(): pl.pallas_call(rows_kernel, out_shape=jax.ShapeDtypeStruct((2, G, G, LANE...  7 us
    ppermute x5, starting transfers between devices, from_behind(): lax.ppermute(block, axis, [((i - distance) % size, i) for i in range(size)])  5.9 us
  transfers between devices with their start and end apart: 10, of which 5 were waited for; matrix products, arithmetic and copies ran while one was open for 1% of the time, Pallas kernels for 57%

profile of v8, /device:TPU:0, one launch (start us, length us, event | category | flops | bytes accessed | tf_op | source)
XLA Modules:
  0.0 107.1 jit_solution(1535856134266188309)
XLA Ops:
  0.6 4.1 %take_band.2.refs_0_.own0 = bf16[6912,128]{1,0:T(8,128)(2,1)} custom-call(bf16[13824,128]{1,0:T(8,128)(2,1)} %bitcast.11), custom_call_target="tpu_custom_call" | custom-call | bytes 5308416 | tf_op jit(solution)/shard_map/take_band/pallas_call | solution.py:168
  4.7 0.5 collective-permute-start.1
  5.2 4.0 %take_band.3.own1 = bf16[6912,128]{1,0:T(8,128)(2,1)} custom-call(bf16[13824,128]{1,0:T(8,128)(2,1)} %bitcast.12, bf16[6912,128]{1,0:T(8,128)(2,1)} %take_band.2.refs_0_.own0), custom_call_target="tpu_custom_call" | custom-call | bytes 5308416 | tf_op jit(solution)/shard_map/take_band/pallas_call | solution.py:168
  9.3 2.7 %collective-permute-start = (bf16[6912,128]{1,0:T(8,128)(2,1)}, bf16[6912,128]{1,0:T(8,128)(2,1)}, u32[]{:S(2)}, u32[]{:S(2)}) collective-permute-start(bf16[6912,128]{1,0:T(8,128)(2,1)} %take_band.3.own1), channel_id=1, source_target_pairs={{31,0},{0,1},{1,2},{2,3},{3,4},{4,5},{5,6},{6,7},{7,8},{8,9},{9,10... | collective-permute-start | bytes 5308424 | tf_op jit(solution)/shard_map/ppermute | solution.py:565
  11.9 7.0 %padded_rows.1.own_u = bf16[2,96,96,128]{3,2,1,0:T(8,128)(2,1)} custom-call(bf16[6912,128]{1,0:T(8,128)(2,1)} %take_band.2.refs_0_.own0, bf16[6912,128]{1,0:T(8,128)(2,1)} %take_band.3.own1, bf16[2,256,256]{2,1,0:T(8,128)(2,1)} %constant.16.clone.sel.refs_6_.refs_8_), custom_call_target="tpu_custom_call" | custom-call | bytes 14155776 | tf_op jit(solution)/shard_map/padded_rows/pallas_call | solution.py:197
  18.9 12.7 %collective-permute-done.1.par = bf16[6912,128]{1,0:T(8,128)(2,1)} collective-permute-done((bf16[6912,128]{1,0:T(8,128)(2,1)}, bf16[6912,128]{1,0:T(8,128)(2,1)}, u32[]{:S(2)}, u32[]{:S(2)}) %collective-permute-start.1) | collective-permute-done | bytes 1769504 | tf_op jit(solution)/shard_map/ppermute | solution.py:565
  31.6 19.7 %pair_terms.2 = (f32[2,6912,128]{2,1,0:T(8,128)}, bf16[6912,128]{1,0:T(8,128)(2,1)}, f32[8,128]{1,0:T(8,128)}) custom-call(bf16[6912,128]{1,0:T(8,128)(2,1)} %take_band.2.refs_0_.own0, bf16[6912,128]{1,0:T(8,128)(2,1)} %take_band.3.own1, bf16[2,96,96,128]{3,2,1,0:T(8,128)(2,1)} %padded_rows.1.own_u, f32[4800,128]{1,0:T(8,128)} %constant.17.clone.kern, ...), custom_call_target="tpu_custom_call" | custom-call | flops 20000000000 | bytes 20000000 | tf_op jit(solution)/shard_map/pair_terms/pallas_call | solution.py:426
  51.4 0.2 collective-permute-start.2
  51.6 0.0 collective-permute-done.par
  51.6 21.0 %pair_terms.3 = (f32[2,6912,128]{2,1,0:T(8,128)}, bf16[4608,128]{1,0:T(8,128)(2,1)}, bf16[2304,128]{1,0:T(8,128)(2,1)}, f32[8,128]{1,0:T(8,128)}) custom-call(bf16[6912,128]{1,0:T(8,128)(2,1)} %take_band.2.refs_0_.own0, bf16[6912,128]{1,0:T(8,128)(2,1)} %take_band.3.own1, bf16[2,96,96,128]{3,2,1,0:T(8,128)(2,1)} %padded_rows.1.own_u, ...), custom_call_target="tpu_custom_call" | custom-call | flops 20000000000 | bytes 20000000 | tf_op jit(solution)/shard_map/pair_terms/pallas_call | solution.py:426
  72.6 2.4 %collective-permute-start.4 = (bf16[4608,128]{1,0:T(8,128)(2,1)}, bf16[4608,128]{1,0:T(8,128)(2,1)S(1)}, u32[]{:S(2)}, u32[]{:S(2)}) collective-permute-start(bf16[4608,128]{1,0:T(8,128)(2,1)} %get-tuple-element.21), channel_id=1, source_target_pairs={{1,0},{2,1},{3,2},{4,3},{5,4},{6,5},{7,6},{8,7},{9,8},{10,9},{11,1... | collective-permute-start | bytes 3538952 | tf_op jit(solution)/shard_map/ppermute | solution.py:565
  75.1 0.1 collective-permute-start.3
  75.2 0.4 collective-permute-start.5
  75.6 1.7 %collective-permute-done.5 = f32[8,128]{1,0:T(8,128)S(1)} collective-permute-done((f32[8,128]{1,0:T(8,128)}, f32[8,128]{1,0:T(8,128)S(1)}, u32[]{:S(2)}, u32[]{:S(2)}) %collective-permute-start.5) | collective-permute-done | bytes 4128 | tf_op jit(solution)/shard_map/ppermute | solution.py:570
  77.3 0.7 add.15
  78.0 0.0 collective-permute-start.6
  78.0 3.6 %collective-permute-done.6 = f32[8,128]{1,0:T(8,128)S(1)} collective-permute-done((f32[8,128]{1,0:T(8,128)S(1)}, f32[8,128]{1,0:T(8,128)S(1)}, u32[]{:S(2)}, u32[]{:S(2)}) %collective-permute-start.6) | collective-permute-done | bytes 4128 | tf_op jit(solution)/shard_map/ppermute | solution.py:570
  81.6 0.0 collective-permute-start.7
  81.6 13.9 %collective-permute-done.7 = f32[8,128]{1,0:T(8,128)S(1)} collective-permute-done((f32[8,128]{1,0:T(8,128)S(1)}, f32[8,128]{1,0:T(8,128)S(1)}, u32[]{:S(2)}, u32[]{:S(2)}) %collective-permute-start.7) | collective-permute-done | bytes 4128 | tf_op jit(solution)/shard_map/ppermute | solution.py:570
  95.5 1.4 %collective-permute-start.8 = (f32[8,128]{1,0:T(8,128)S(1)}, f32[8,128]{1,0:T(8,128)S(1)}, u32[]{:S(2)}, u32[]{:S(2)}) collective-permute-start(f32[8,128]{1,0:T(8,128)S(1)} %add.17), channel_id=1, source_target_pairs={{16,0},{17,1},{18,2},{19,3},{20,4},{21,5},{22,6},{23,7},{24,8},{25... | collective-permute-start | bytes 12296 | tf_op jit(solution)/shard_map/ppermute | solution.py:570
  96.9 0.0 collective-permute-done.4.back1
  97.0 0.0 collective-permute-done.2.back0
  97.0 5.9 %add_piece.2 = (f32[13824,128]{1,0:T(8,128)}, f32[2,2,8,128]{3,2,1,0:T(8,128)S(1)}) custom-call(bf16[6912,128]{1,0:T(8,128)(2,1)} %take_band.2.refs_0_.own0, bf16[6912,128]{1,0:T(8,128)(2,1)} %take_band.3.own1, f32[2,6912,128]{2,1,0:T(8,128)} %get-tuple-element.18.terms, bf16[6912,128]{1,0:T(8,128)(2,1)} %collective-permute-done.2.back0, ...), custom_call_target="tpu_custom_call" | custom-call | bytes 14155776 | tf_op jit(solution)/shard_map/add_piece/pallas_call | solution.py:535
  102.9 0.0 collective-permute-done.8
  102.9 0.1 collective-permute-start.9
  103.0 0.0 collective-permute-done.3.back1
  103.0 3.5 %add_piece.3 = (f32[13824,128]{1,0:T(8,128)}, f32[2,2]{1,0:T(2,128)}) custom-call(bf16[6912,128]{1,0:T(8,128)(2,1)} %take_band.2.refs_0_.own0, bf16[6912,128]{1,0:T(8,128)(2,1)} %take_band.3.own1, f32[2,6912,128]{2,1,0:T(8,128)} %get-tuple-element.18.terms, bf16[6912,128]{1,0:T(8,128)(2,1)} %collective-permute-done.2.back0, ...), custom_call_target="tpu_custom_call", output_to_operand_aliasing={{0}: (6, {})} | custom-call | bytes 7077888 | tf_op jit(solution)/shard_map/add_piece/pallas_call | solution.py:535
  106.5 0.1 collective-permute-done.9
  106.6 0.5 slice.3
  (4 shorter events, 0.0 us)
Async XLA Ops:
  4.7 26.9 %collective-permute-start.1 = (bf16[6912,128]{1,0:T(8,128)(2,1)}, bf16[6912,128]{1,0:T(8,128)(2,1)}, u32[]{:S(2)}, u32[]{:S(2)}) collective-permute-start(bf16[6912,128]{1,0:T(8,128)(2,1)} %take_band.2.refs_0_.own0), channel_id=1, source_target_pairs={{31,0},{0,1},{1,2},{2,3},{3,4},{4,5},{5,6},{6,7},{7,8},{8,9},{9,10... | collective-permute-start | bytes 5308424 | tf_op jit(solution)/shard_map/ppermute | solution.py:565
  9.3 42.4 %collective-permute-start = (bf16[6912,128]{1,0:T(8,128)(2,1)}, bf16[6912,128]{1,0:T(8,128)(2,1)}, u32[]{:S(2)}, u32[]{:S(2)}) collective-permute-start(bf16[6912,128]{1,0:T(8,128)(2,1)} %take_band.3.own1), channel_id=1, source_target_pairs={{31,0},{0,1},{1,2},{2,3},{3,4},{4,5},{5,6},{6,7},{7,8},{8,9},{9,10... | collective-permute-start | bytes 5308424 | tf_op jit(solution)/shard_map/ppermute | solution.py:565
  51.4 45.6 %collective-permute-start.2 = (bf16[6912,128]{1,0:T(8,128)(2,1)}, bf16[6912,128]{1,0:T(8,128)(2,1)}, u32[]{:S(2)}, u32[]{:S(2)}) collective-permute-start(bf16[6912,128]{1,0:T(8,128)(2,1)} %get-tuple-element.19), channel_id=1, source_target_pairs={{1,0},{2,1},{3,2},{4,3},{5,4},{6,5},{7,6},{8,7},{9,8},{10,9},{11,1... | collective-permute-start | bytes 5308424 | tf_op jit(solution)/shard_map/ppermute | solution.py:565
  72.6 24.3 %collective-permute-start.4 = (bf16[4608,128]{1,0:T(8,128)(2,1)}, bf16[4608,128]{1,0:T(8,128)(2,1)S(1)}, u32[]{:S(2)}, u32[]{:S(2)}) collective-permute-start(bf16[4608,128]{1,0:T(8,128)(2,1)} %get-tuple-element.21), channel_id=1, source_target_pairs={{1,0},{2,1},{3,2},{4,3},{5,4},{6,5},{7,6},{8,7},{9,8},{10,9},{11,1... | collective-permute-start | bytes 3538952 | tf_op jit(solution)/shard_map/ppermute | solution.py:565
  75.1 27.9 %collective-permute-start.3 = (bf16[2304,128]{1,0:T(8,128)(2,1)}, bf16[2304,128]{1,0:T(8,128)(2,1)S(1)}, u32[]{:S(2)}, u32[]{:S(2)}) collective-permute-start(bf16[2304,128]{1,0:T(8,128)(2,1)} %get-tuple-element.20), channel_id=1, source_target_pairs={{1,0},{2,1},{3,2},{4,3},{5,4},{6,5},{7,6},{8,7},{9,8},{10,9},{11,1... | collective-permute-start | bytes 1769480 | tf_op jit(solution)/shard_map/ppermute | solution.py:565
  75.2 2.2 %collective-permute-start.5 = (f32[8,128]{1,0:T(8,128)}, f32[8,128]{1,0:T(8,128)S(1)}, u32[]{:S(2)}, u32[]{:S(2)}) collective-permute-start(f32[8,128]{1,0:T(8,128)} %get-tuple-element.26), channel_id=1, source_target_pairs={{1,0},{0,1},{3,2},{2,3},{5,4},{4,5},{7,6},{6,7},{9,8},{8,9},{11,10... | collective-permute-start | bytes 12296 | tf_op jit(solution)/shard_map/ppermute | solution.py:570
  78.0 3.6 %collective-permute-start.6 = (f32[8,128]{1,0:T(8,128)S(1)}, f32[8,128]{1,0:T(8,128)S(1)}, u32[]{:S(2)}, u32[]{:S(2)}) collective-permute-start(f32[8,128]{1,0:T(8,128)S(1)} %add.15), channel_id=1, source_target_pairs={{4,0},{5,1},{6,2},{7,3},{0,4},{1,5},{2,6},{3,7},{12,8},{13,9},{14,... | collective-permute-start | bytes 12296 | tf_op jit(solution)/shard_map/ppermute | solution.py:570
  81.6 13.9 %collective-permute-start.7 = (f32[8,128]{1,0:T(8,128)S(1)}, f32[8,128]{1,0:T(8,128)S(1)}, u32[]{:S(2)}, u32[]{:S(2)}) collective-permute-start(f32[8,128]{1,0:T(8,128)S(1)} %add.16), channel_id=1, source_target_pairs={{8,0},{9,1},{10,2},{11,3},{12,4},{13,5},{14,6},{15,7},{0,8},{1,9},... | collective-permute-start | bytes 12296 | tf_op jit(solution)/shard_map/ppermute | solution.py:570
  95.5 7.4 %collective-permute-start.8 = (f32[8,128]{1,0:T(8,128)S(1)}, f32[8,128]{1,0:T(8,128)S(1)}, u32[]{:S(2)}, u32[]{:S(2)}) collective-permute-start(f32[8,128]{1,0:T(8,128)S(1)} %add.17), channel_id=1, source_target_pairs={{16,0},{17,1},{18,2},{19,3},{20,4},{21,5},{22,6},{23,7},{24,8},{25... | collective-permute-start | bytes 12296 | tf_op jit(solution)/shard_map/ppermute | solution.py:570
  102.9 3.7 %collective-permute-start.9 = (f32[8,128]{1,0:T(8,128)S(1)}, f32[8,128]{1,0:T(8,128)S(1)}, u32[]{:S(2)}, u32[]{:S(2)}) collective-permute-start(f32[8,128]{1,0:T(8,128)S(1)} %add.18), channel_id=1, source_target_pairs={{2,0},{3,1},{0,2},{1,3},{6,4},{7,5},{4,6},{5,7},{10,8},{11,9},{8,1... | collective-permute-start | bytes 12296 | tf_op jit(solution)/shard_map/ppermute | solution.py:570

commit v9 on v8

--- a/solution.py
+++ b/solution.py
@@ -565,11 +565,6 @@
     return lax.ppermute(block, axis, [((i - distance) % size, i) for i in range(size)])
 
 
-def send_to(value, axis, flip):
-    size = lax.axis_size(axis)
-    return lax.ppermute(value, axis, [(i ^ flip, i) for i in range(size)])
-
-
 def after(values, other):
     return lax.optimization_barrier((values, other))[0]
 
@@ -597,20 +592,27 @@
     if size & (size - 1):
         energy = lax.psum(energy, "band")
     else:
-        steps = [1 << b for b in range(size.bit_length() - 1)]
+        energy = energy + lax.ppermute(energy, "band", [(i, i + 1) for i in range(0, size, 2)])
+        steps = [1 << b for b in range(1, size.bit_length() - 1)]
         steps = [b for b in steps if b != 2] + [b for b in steps if b == 2]
-    while len(steps) > len(back1):
-        energy = energy + send_to(energy, "band", steps.pop(0))
-    exchange, grams, got = None, [], None
+        steps = [[(i, i ^ b) for i in range(1, size, 2)] for b in steps]
+    while len(steps) > len(back1) - 1:
+        energy = energy + lax.ppermute(energy, "band", steps.pop(0))
+    exchange, grams = None, []
     first = 0
     for count, piece in zip(PIECES, back1):
         count *= STEP_ROWS
-        if steps:
-            got = send_to(energy, "band", steps.pop(0))
+        got, last = None, piece is back1[-1]
+        if last and size & (size - 1) == 0:
+            got = lax.ppermute(energy, "band", [(i + 1, i) for i in range(0, size, 2)])
+        elif steps:
+            got = lax.ppermute(energy, "band", steps.pop(0))
         exchange, gram = add_piece(first, count, own, terms, back0, piece, grams, exchange)
-        if got is not None:
+        if got is not None and last:
+            odd = lax.axis_index("band") % 2 == 1
+            energy = jnp.where(odd, energy[:1, :1], after(got, gram)[:1, :1])
+        elif got is not None:
             energy = energy + after(got, gram)
-            got = None
         grams.append(gram)
         first += count
     exchange = exchange.reshape(ROWS, 2, LANES).transpose(1, 0, 2).reshape(2, NGRID)

time: 107 us -> 110 us (1.028)
  the two profiles are of different devices: /device:TPU:0 before, /device:TPU:1 now
where the time goes in v9:
time: 110 us; the launch traced here: 109 us
  Pallas kernels  65.2 us (59%)
  starting transfers between devices  20.2 us (18%)
  waiting for transfers between devices  19 us (17%)
  between operations  3.19 us (3%)
    pallas_call x2, Pallas kernels, pair_terms(): pl.pallas_call(functools.partial(pairs_kernel, pieces, share), out_shape=...  40.7 us
    ppermute x5, starting transfers between devices, from_behind(): lax.ppermute(block, axis, [((i - distance) % size, i) for i in range(size)])  10 us
    pallas_call x2, Pallas kernels, add_piece(): pl.pallas_call(functools.partial(piece_kernel, first, size), out_shape=(j...  9.39 us
    ppermute x5, waiting for transfers between devices, from_behind(): lax.ppermute(block, axis, [((i - distance) % size, i) for i in range(size)])  8.65 us
    ppermute x3, waiting for transfers between devices, per_device(): energy = energy + lax.ppermute(energy, 'band', steps.pop(0))  8.38 us
    pallas_call x2, Pallas kernels, take_band(): pl.pallas_call(functools.partial(band_kernel, p), out_shape=jax.ShapeDtyp...  8.13 us
    pallas_call x1, Pallas kernels, padded_rows(): pl.pallas_call(rows_kernel, out_shape=jax.ShapeDtypeStruct((2, G, G, LANE...  7 us
    ppermute x3, starting transfers between devices, per_device(): energy = energy + lax.ppermute(energy, 'band', steps.pop(0))  5.73 us
  transfers between devices with their start and end apart: 11, of which 5 were waited for; matrix products, arithmetic and copies ran while one was open for 1% of the time, Pallas kernels for 56%

profile of v9, /device:TPU:1, one launch (start us, length us, event | category | flops | bytes accessed | tf_op | source)
XLA Modules:
  0.0 109.4 jit_solution(16345157764471320188)
XLA Ops:
  0.6 4.1 %take_band.2.refs_0_.own0 = bf16[6912,128]{1,0:T(8,128)(2,1)} custom-call(bf16[13824,128]{1,0:T(8,128)(2,1)} %bitcast.12), custom_call_target="tpu_custom_call" | custom-call | bytes 5308416 | tf_op jit(solution)/shard_map/take_band/pallas_call | solution.py:168
  4.7 2.7 %collective-permute-start.1 = (bf16[6912,128]{1,0:T(8,128)(2,1)}, bf16[6912,128]{1,0:T(8,128)(2,1)}, u32[]{:S(2)}, u32[]{:S(2)}) collective-permute-start(bf16[6912,128]{1,0:T(8,128)(2,1)} %take_band.2.refs_0_.own0), channel_id=1, source_target_pairs={{31,0},{0,1},{1,2},{2,3},{3,4},{4,5},{5,6},{6,7},{7,8},{8,9},{9,10... | collective-permute-start | bytes 5308424 | tf_op jit(solution)/shard_map/ppermute | solution.py:565
  7.4 4.1 %take_band.3.own1 = bf16[6912,128]{1,0:T(8,128)(2,1)} custom-call(bf16[13824,128]{1,0:T(8,128)(2,1)} %bitcast.13, bf16[6912,128]{1,0:T(8,128)(2,1)} %take_band.2.refs_0_.own0), custom_call_target="tpu_custom_call" | custom-call | bytes 5308416 | tf_op jit(solution)/shard_map/take_band/pallas_call | solution.py:168
  11.4 0.1 collective-permute-start
  11.5 7.0 %padded_rows.1.own_u = bf16[2,96,96,128]{3,2,1,0:T(8,128)(2,1)} custom-call(bf16[6912,128]{1,0:T(8,128)(2,1)} %take_band.2.refs_0_.own0, bf16[6912,128]{1,0:T(8,128)(2,1)} %take_band.3.own1, bf16[2,256,256]{2,1,0:T(8,128)(2,1)} %constant.34.clone.sel.refs_6_.refs_8_), custom_call_target="tpu_custom_call" | custom-call | bytes 14155776 | tf_op jit(solution)/shard_map/padded_rows/pallas_call | solution.py:197
  18.5 8.6 %collective-permute-done.1.par = bf16[6912,128]{1,0:T(8,128)(2,1)} collective-permute-done((bf16[6912,128]{1,0:T(8,128)(2,1)}, bf16[6912,128]{1,0:T(8,128)(2,1)}, u32[]{:S(2)}, u32[]{:S(2)}) %collective-permute-start.1) | collective-permute-done | bytes 1769504 | tf_op jit(solution)/shard_map/ppermute | solution.py:565
  27.1 19.7 %pair_terms.2 = (f32[2,6912,128]{2,1,0:T(8,128)}, bf16[6912,128]{1,0:T(8,128)(2,1)}, f32[8,128]{1,0:T(8,128)}) custom-call(bf16[6912,128]{1,0:T(8,128)(2,1)} %take_band.2.refs_0_.own0, bf16[6912,128]{1,0:T(8,128)(2,1)} %take_band.3.own1, bf16[2,96,96,128]{3,2,1,0:T(8,128)(2,1)} %padded_rows.1.own_u, f32[4800,128]{1,0:T(8,128)} %constant.35.clone.kern, ...), custom_call_target="tpu_custom_call" | custom-call | flops 20000000000 | bytes 20000000 | tf_op jit(solution)/shard_map/pair_terms/pallas_call | solution.py:426
  46.9 4.8 %collective-permute-start.2 = (bf16[6912,128]{1,0:T(8,128)(2,1)}, bf16[6912,128]{1,0:T(8,128)(2,1)}, u32[]{:S(2)}, u32[]{:S(2)}) collective-permute-start(bf16[6912,128]{1,0:T(8,128)(2,1)} %get-tuple-element.19), channel_id=1, source_target_pairs={{1,0},{2,1},{3,2},{4,3},{5,4},{6,5},{7,6},{8,7},{9,8},{10,9},{11,1... | collective-permute-start | bytes 5308424 | tf_op jit(solution)/shard_map/ppermute | solution.py:565
  51.6 0.0 collective-permute-done.par
  51.7 21.0 %pair_terms.3 = (f32[2,6912,128]{2,1,0:T(8,128)}, bf16[4608,128]{1,0:T(8,128)(2,1)}, bf16[2304,128]{1,0:T(8,128)(2,1)}, f32[8,128]{1,0:T(8,128)}) custom-call(bf16[6912,128]{1,0:T(8,128)(2,1)} %take_band.2.refs_0_.own0, bf16[6912,128]{1,0:T(8,128)(2,1)} %take_band.3.own1, bf16[2,96,96,128]{3,2,1,0:T(8,128)(2,1)} %padded_rows.1.own_u, ...), custom_call_target="tpu_custom_call" | custom-call | flops 20000000000 | bytes 20000000 | tf_op jit(solution)/shard_map/pair_terms/pallas_call | solution.py:426
  72.7 0.1 collective-permute-start.4
  72.8 2.4 %collective-permute-start.3 = (bf16[2304,128]{1,0:T(8,128)(2,1)}, bf16[2304,128]{1,0:T(8,128)(2,1)S(1)}, u32[]{:S(2)}, u32[]{:S(2)}) collective-permute-start(bf16[2304,128]{1,0:T(8,128)(2,1)} %get-tuple-element.20), channel_id=1, source_target_pairs={{1,0},{2,1},{3,2},{4,3},{5,4},{6,5},{7,6},{8,7},{9,8},{10,9},{11,1... | collective-permute-start | bytes 1769480 | tf_op jit(solution)/shard_map/ppermute | solution.py:565
  75.2 1.3 %collective-permute-start.5 = (f32[8,128]{1,0:T(8,128)}, f32[8,128]{1,0:T(8,128)S(1)}, u32[]{:S(2)}, u32[]{:S(2)}) collective-permute-start(f32[8,128]{1,0:T(8,128)} %get-tuple-element.26), channel_id=1, source_target_pairs={{0,1},{2,3},{4,5},{6,7},{8,9},{10,11},{12,13},{14,15},{16,17},{18,... | collective-permute-start | bytes 12296 | tf_op jit(solution)/shard_map/ppermute | solution.py:595
  76.4 2.0 %collective-permute-done.5 = f32[8,128]{1,0:T(8,128)S(1)} collective-permute-done((f32[8,128]{1,0:T(8,128)}, f32[8,128]{1,0:T(8,128)S(1)}, u32[]{:S(2)}, u32[]{:S(2)}) %collective-permute-start.5) | collective-permute-done | bytes 4128 | tf_op jit(solution)/shard_map/ppermute | solution.py:595
  78.4 0.7 add.20
  79.1 1.9 %collective-permute-start.6 = (f32[8,128]{1,0:T(8,128)S(1)}, f32[8,128]{1,0:T(8,128)S(1)}, u32[]{:S(2)}, u32[]{:S(2)}) collective-permute-start(f32[8,128]{1,0:T(8,128)S(1)} %add.20), channel_id=1, source_target_pairs={{1,5},{3,7},{5,1},{7,3},{9,13},{11,15},{13,9},{15,11},{17,21},{19,... | collective-permute-start | bytes 12296 | tf_op jit(solution)/shard_map/ppermute | solution.py:600
  81.0 2.4 %collective-permute-done.6 = f32[8,128]{1,0:T(8,128)S(1)} collective-permute-done((f32[8,128]{1,0:T(8,128)S(1)}, f32[8,128]{1,0:T(8,128)S(1)}, u32[]{:S(2)}, u32[]{:S(2)}) %collective-permute-start.6) | collective-permute-done | bytes 4128 | tf_op jit(solution)/shard_map/ppermute | solution.py:600
  83.4 1.9 %collective-permute-start.7 = (f32[8,128]{1,0:T(8,128)S(1)}, f32[8,128]{1,0:T(8,128)S(1)}, u32[]{:S(2)}, u32[]{:S(2)}) collective-permute-start(f32[8,128]{1,0:T(8,128)S(1)} %add.21), channel_id=1, source_target_pairs={{1,9},{3,11},{5,13},{7,15},{9,1},{11,3},{13,5},{15,7},{17,25},{19,... | collective-permute-start | bytes 12296 | tf_op jit(solution)/shard_map/ppermute | solution.py:600
  85.4 2.5 %collective-permute-done.7 = f32[8,128]{1,0:T(8,128)S(1)} collective-permute-done((f32[8,128]{1,0:T(8,128)S(1)}, f32[8,128]{1,0:T(8,128)S(1)}, u32[]{:S(2)}, u32[]{:S(2)}) %collective-permute-start.7) | collective-permute-done | bytes 4128 | tf_op jit(solution)/shard_map/ppermute | solution.py:600
  87.9 1.9 %collective-permute-start.8 = (f32[8,128]{1,0:T(8,128)S(1)}, f32[8,128]{1,0:T(8,128)S(1)}, u32[]{:S(2)}, u32[]{:S(2)}) collective-permute-start(f32[8,128]{1,0:T(8,128)S(1)} %add.22), channel_id=1, source_target_pairs={{1,17},{3,19},{5,21},{7,23},{9,25},{11,27},{13,29},{15,31},{17,1},... | collective-permute-start | bytes 12296 | tf_op jit(solution)/shard_map/ppermute | solution.py:600
  89.8 3.4 %collective-permute-done.8 = f32[8,128]{1,0:T(8,128)S(1)} collective-permute-done((f32[8,128]{1,0:T(8,128)S(1)}, f32[8,128]{1,0:T(8,128)S(1)}, u32[]{:S(2)}, u32[]{:S(2)}) %collective-permute-start.8) | collective-permute-done | bytes 4128 | tf_op jit(solution)/shard_map/ppermute | solution.py:600
  93.2 1.9 %collective-permute-start.9 = (f32[8,128]{1,0:T(8,128)S(1)}, f32[8,128]{1,0:T(8,128)S(1)}, u32[]{:S(2)}, u32[]{:S(2)}) collective-permute-start(f32[8,128]{1,0:T(8,128)S(1)} %add.23), channel_id=1, source_target_pairs={{1,3},{3,1},{5,7},{7,5},{9,11},{11,9},{13,15},{15,13},{17,19},{19,... | collective-permute-start | bytes 12296 | tf_op jit(solution)/shard_map/ppermute | solution.py:609
  95.2 0.0 collective-permute-done.4.back1
  95.2 0.0 collective-permute-done.2.back0
  95.2 5.9 %add_piece.2 = (f32[13824,128]{1,0:T(8,128)}, f32[2,2,8,128]{3,2,1,0:T(8,128)S(1)}) custom-call(bf16[6912,128]{1,0:T(8,128)(2,1)} %take_band.2.refs_0_.own0, bf16[6912,128]{1,0:T(8,128)(2,1)} %take_band.3.own1, f32[2,6912,128]{2,1,0:T(8,128)} %get-tuple-element.18.terms, bf16[6912,128]{1,0:T(8,128)(2,1)} %collective-permute-done.2.back0, ...), custom_call_target="tpu_custom_call" | custom-call | bytes 14155776 | tf_op jit(solution)/shard_map/add_piece/pallas_call | solution.py:535
  101.1 0.0 collective-permute-done.9
  101.2 1.3 %collective-permute-start.10 = (f32[8,128]{1,0:T(8,128)S(1)}, f32[8,128]{1,0:T(8,128)S(1)}, u32[]{:S(2)}, u32[]{:S(2)}) collective-permute-start(f32[8,128]{1,0:T(8,128)S(1)} %add.24), channel_id=1, source_target_pairs={{1,0},{3,2},{5,4},{7,6},{9,8},{11,10},{13,12},{15,14},{17,16},{19,... | collective-permute-start | bytes 12296 | tf_op jit(solution)/shard_map/ppermute | solution.py:607
  102.5 0.5 slice.6
  103.0 0.0 collective-permute-done.3.back1
  103.0 3.4 %add_piece.3 = (f32[13824,128]{1,0:T(8,128)}, f32[2,2]{1,0:T(2,128)}) custom-call(bf16[6912,128]{1,0:T(8,128)(2,1)} %take_band.2.refs_0_.own0, bf16[6912,128]{1,0:T(8,128)(2,1)} %take_band.3.own1, f32[2,6912,128]{2,1,0:T(8,128)} %get-tuple-element.18.terms, bf16[6912,128]{1,0:T(8,128)(2,1)} %collective-permute-done.2.back0, ...), custom_call_target="tpu_custom_call", output_to_operand_aliasing={{0}: (6, {})} | custom-call | bytes 7077888 | tf_op jit(solution)/shard_map/add_piece/pallas_call | solution.py:535
  106.4 0.0 collective-permute-done.10
  106.5 0.5 slice.7
  (4 shorter events, 0.0 us)
Async XLA Ops:
  4.7 22.4 %collective-permute-start.1 = (bf16[6912,128]{1,0:T(8,128)(2,1)}, bf16[6912,128]{1,0:T(8,128)(2,1)}, u32[]{:S(2)}, u32[]{:S(2)}) collective-permute-start(bf16[6912,128]{1,0:T(8,128)(2,1)} %take_band.2.refs_0_.own0), channel_id=1, source_target_pairs={{31,0},{0,1},{1,2},{2,3},{3,4},{4,5},{5,6},{6,7},{7,8},{8,9},{9,10... | collective-permute-start | bytes 5308424 | tf_op jit(solution)/shard_map/ppermute | solution.py:565
  11.4 40.2 %collective-permute-start = (bf16[6912,128]{1,0:T(8,128)(2,1)}, bf16[6912,128]{1,0:T(8,128)(2,1)}, u32[]{:S(2)}, u32[]{:S(2)}) collective-permute-start(bf16[6912,128]{1,0:T(8,128)(2,1)} %take_band.3.own1), channel_id=1, source_target_pairs={{31,0},{0,1},{1,2},{2,3},{3,4},{4,5},{5,6},{6,7},{7,8},{8,9},{9,10... | collective-permute-start | bytes 5308424 | tf_op jit(solution)/shard_map/ppermute | solution.py:565
  46.9 48.3 %collective-permute-start.2 = (bf16[6912,128]{1,0:T(8,128)(2,1)}, bf16[6912,128]{1,0:T(8,128)(2,1)}, u32[]{:S(2)}, u32[]{:S(2)}) collective-permute-start(bf16[6912,128]{1,0:T(8,128)(2,1)} %get-tuple-element.19), channel_id=1, source_target_pairs={{1,0},{2,1},{3,2},{4,3},{5,4},{6,5},{7,6},{8,7},{9,8},{10,9},{11,1... | collective-permute-start | bytes 5308424 | tf_op jit(solution)/shard_map/ppermute | solution.py:565
  72.7 22.5 %collective-permute-start.4 = (bf16[4608,128]{1,0:T(8,128)(2,1)}, bf16[4608,128]{1,0:T(8,128)(2,1)S(1)}, u32[]{:S(2)}, u32[]{:S(2)}) collective-permute-start(bf16[4608,128]{1,0:T(8,128)(2,1)} %get-tuple-element.21), channel_id=1, source_target_pairs={{1,0},{2,1},{3,2},{4,3},{5,4},{6,5},{7,6},{8,7},{9,8},{10,9},{11,1... | collective-permute-start | bytes 3538952 | tf_op jit(solution)/shard_map/ppermute | solution.py:565
  72.8 30.2 %collective-permute-start.3 = (bf16[2304,128]{1,0:T(8,128)(2,1)}, bf16[2304,128]{1,0:T(8,128)(2,1)S(1)}, u32[]{:S(2)}, u32[]{:S(2)}) collective-permute-start(bf16[2304,128]{1,0:T(8,128)(2,1)} %get-tuple-element.20), channel_id=1, source_target_pairs={{1,0},{2,1},{3,2},{4,3},{5,4},{6,5},{7,6},{8,7},{9,8},{10,9},{11,1... | collective-permute-start | bytes 1769480 | tf_op jit(solution)/shard_map/ppermute | solution.py:565
  75.2 3.3 %collective-permute-start.5 = (f32[8,128]{1,0:T(8,128)}, f32[8,128]{1,0:T(8,128)S(1)}, u32[]{:S(2)}, u32[]{:S(2)}) collective-permute-start(f32[8,128]{1,0:T(8,128)} %get-tuple-element.26), channel_id=1, source_target_pairs={{0,1},{2,3},{4,5},{6,7},{8,9},{10,11},{12,13},{14,15},{16,17},{18,... | collective-permute-start | bytes 12296 | tf_op jit(solution)/shard_map/ppermute | solution.py:595
  79.1 4.3 %collective-permute-start.6 = (f32[8,128]{1,0:T(8,128)S(1)}, f32[8,128]{1,0:T(8,128)S(1)}, u32[]{:S(2)}, u32[]{:S(2)}) collective-permute-start(f32[8,128]{1,0:T(8,128)S(1)} %add.20), channel_id=1, source_target_pairs={{1,5},{3,7},{5,1},{7,3},{9,13},{11,15},{13,9},{15,11},{17,21},{19,... | collective-permute-start | bytes 12296 | tf_op jit(solution)/shard_map/ppermute | solution.py:600
  83.4 4.4 %collective-permute-start.7 = (f32[8,128]{1,0:T(8,128)S(1)}, f32[8,128]{1,0:T(8,128)S(1)}, u32[]{:S(2)}, u32[]{:S(2)}) collective-permute-start(f32[8,128]{1,0:T(8,128)S(1)} %add.21), channel_id=1, source_target_pairs={{1,9},{3,11},{5,13},{7,15},{9,1},{11,3},{13,5},{15,7},{17,25},{19,... | collective-permute-start | bytes 12296 | tf_op jit(solution)/shard_map/ppermute | solution.py:600
  87.9 5.3 %collective-permute-start.8 = (f32[8,128]{1,0:T(8,128)S(1)}, f32[8,128]{1,0:T(8,128)S(1)}, u32[]{:S(2)}, u32[]{:S(2)}) collective-permute-start(f32[8,128]{1,0:T(8,128)S(1)} %add.22), channel_id=1, source_target_pairs={{1,17},{3,19},{5,21},{7,23},{9,25},{11,27},{13,29},{15,31},{17,1},... | collective-permute-start | bytes 12296 | tf_op jit(solution)/shard_map/ppermute | solution.py:600
  93.2 7.9 %collective-permute-start.9 = (f32[8,128]{1,0:T(8,128)S(1)}, f32[8,128]{1,0:T(8,128)S(1)}, u32[]{:S(2)}, u32[]{:S(2)}) collective-permute-start(f32[8,128]{1,0:T(8,128)S(1)} %add.23), channel_id=1, source_target_pairs={{1,3},{3,1},{5,7},{7,5},{9,11},{11,9},{13,15},{15,13},{17,19},{19,... | collective-permute-start | bytes 12296 | tf_op jit(solution)/shard_map/ppermute | solution.py:609
  101.2 5.3 %collective-permute-start.10 = (f32[8,128]{1,0:T(8,128)S(1)}, f32[8,128]{1,0:T(8,128)S(1)}, u32[]{:S(2)}, u32[]{:S(2)}) collective-permute-start(f32[8,128]{1,0:T(8,128)S(1)} %add.24), channel_id=1, source_target_pairs={{1,0},{3,2},{5,4},{7,6},{9,8},{11,10},{13,12},{15,14},{17,16},{19,... | collective-permute-start | bytes 12296 | tf_op jit(solution)/shard_map/ppermute | solution.py:607

commit v10 on v9

--- a/solution.py
+++ b/solution.py
@@ -592,10 +592,11 @@
     if size & (size - 1):
         energy = lax.psum(energy, "band")
     else:
-        energy = energy + lax.ppermute(energy, "band", [(i, i + 1) for i in range(0, size, 2)])
+        swap = [(i, i ^ 1) for i in range(size)]
+        energy = energy + lax.ppermute(energy, "band", swap)
         steps = [1 << b for b in range(1, size.bit_length() - 1)]
         steps = [b for b in steps if b != 2] + [b for b in steps if b == 2]
-        steps = [[(i, i ^ b) for i in range(1, size, 2)] for b in steps]
+        steps = [[(i, i ^ b if i % 2 else i) for i in range(size)] for b in steps]
     while len(steps) > len(back1) - 1:
         energy = energy + lax.ppermute(energy, "band", steps.pop(0))
     exchange, grams = None, []
@@ -604,7 +605,7 @@
         count *= STEP_ROWS
         got, last = None, piece is back1[-1]
         if last and size & (size - 1) == 0:
-            got = lax.ppermute(energy, "band", [(i + 1, i) for i in range(0, size, 2)])
+            got = lax.ppermute(energy, "band", swap)
         elif steps:
             got = lax.ppermute(energy, "band", steps.pop(0))
         exchange, gram = add_piece(first, count, own, terms, back0, piece, grams, exchange)

time: 110 us -> 108 us (0.982)
  the two profiles are of different devices: /device:TPU:1 before, /device:TPU:0 now
where the time goes in v10:
time: 108 us; the launch traced here: 107 us
  Pallas kernels  65.2 us (60%)
  waiting for transfers between devices  22.9 us (21%)
  starting transfers between devices  14.1 us (13%)
  between operations  3.21 us (3%)
    pallas_call x2, Pallas kernels, pair_terms(): pl.pallas_call(functools.partial(pairs_kernel, pieces, share), out_shape=...  40.7 us
    ppermute x5, waiting for transfers between devices, from_behind(): lax.ppermute(block, axis, [((i - distance) % size, i) for i in range(size)])  21.2 us
    pallas_call x2, Pallas kernels, add_piece(): pl.pallas_call(functools.partial(piece_kernel, first, size), out_shape=(j...  9.38 us
    pallas_call x2, Pallas kernels, take_band(): pl.pallas_call(functools.partial(band_kernel, p), out_shape=jax.ShapeDtyp...  8.13 us
    pallas_call x1, Pallas kernels, padded_rows(): pl.pallas_call(rows_kernel, out_shape=jax.ShapeDtypeStruct((2, G, G, LANE...  7 us
    ppermute x5, starting transfers between devices, from_behind(): lax.ppermute(block, axis, [((i - distance) % size, i) for i in range(size)])  5.91 us
    ppermute x1, starting transfers between devices, per_device(): got = lax.ppermute(energy, 'band', swap)  5.12 us
  transfers between devices with their start and end apart: 11, of which 3 were waited for; matrix products, arithmetic and copies ran while one was open for 1% of the time, Pallas kernels for 57%

profile of v10, /device:TPU:0, one launch (start us, length us, event | category | flops | bytes accessed | tf_op | source)
XLA Modules:
  0.0 107.2 jit_solution(10290894605311719063)
XLA Ops:
  0.6 4.1 %take_band.2.refs_0_.own0 = bf16[6912,128]{1,0:T(8,128)(2,1)} custom-call(bf16[13824,128]{1,0:T(8,128)(2,1)} %bitcast.12), custom_call_target="tpu_custom_call" | custom-call | bytes 5308416 | tf_op jit(solution)/shard_map/take_band/pallas_call | solution.py:168
  4.7 0.5 collective-permute-start.1
  5.2 4.1 %take_band.3.own1 = bf16[6912,128]{1,0:T(8,128)(2,1)} custom-call(bf16[13824,128]{1,0:T(8,128)(2,1)} %bitcast.13, bf16[6912,128]{1,0:T(8,128)(2,1)} %take_band.2.refs_0_.own0), custom_call_target="tpu_custom_call" | custom-call | bytes 5308416 | tf_op jit(solution)/shard_map/take_band/pallas_call | solution.py:168
  9.3 2.7 %collective-permute-start = (bf16[6912,128]{1,0:T(8,128)(2,1)}, bf16[6912,128]{1,0:T(8,128)(2,1)}, u32[]{:S(2)}, u32[]{:S(2)}) collective-permute-start(bf16[6912,128]{1,0:T(8,128)(2,1)} %take_band.3.own1), channel_id=1, source_target_pairs={{31,0},{0,1},{1,2},{2,3},{3,4},{4,5},{5,6},{6,7},{7,8},{8,9},{9,10... | collective-permute-start | bytes 5308424 | tf_op jit(solution)/shard_map/ppermute | solution.py:565
  11.9 7.0 %padded_rows.1.own_u = bf16[2,96,96,128]{3,2,1,0:T(8,128)(2,1)} custom-call(bf16[6912,128]{1,0:T(8,128)(2,1)} %take_band.2.refs_0_.own0, bf16[6912,128]{1,0:T(8,128)(2,1)} %take_band.3.own1, bf16[2,256,256]{2,1,0:T(8,128)(2,1)} %constant.34.clone.sel.refs_6_.refs_8_), custom_call_target="tpu_custom_call" | custom-call | bytes 14155776 | tf_op jit(solution)/shard_map/padded_rows/pallas_call | solution.py:197
  18.9 12.7 %collective-permute-done.1.par = bf16[6912,128]{1,0:T(8,128)(2,1)} collective-permute-done((bf16[6912,128]{1,0:T(8,128)(2,1)}, bf16[6912,128]{1,0:T(8,128)(2,1)}, u32[]{:S(2)}, u32[]{:S(2)}) %collective-permute-start.1) | collective-permute-done | bytes 1769504 | tf_op jit(solution)/shard_map/ppermute | solution.py:565
  31.6 19.7 %pair_terms.2 = (f32[2,6912,128]{2,1,0:T(8,128)}, bf16[6912,128]{1,0:T(8,128)(2,1)}, f32[8,128]{1,0:T(8,128)}) custom-call(bf16[6912,128]{1,0:T(8,128)(2,1)} %take_band.2.refs_0_.own0, bf16[6912,128]{1,0:T(8,128)(2,1)} %take_band.3.own1, bf16[2,96,96,128]{3,2,1,0:T(8,128)(2,1)} %padded_rows.1.own_u, f32[4800,128]{1,0:T(8,128)} %constant.35.clone.kern, ...), custom_call_target="tpu_custom_call" | custom-call | flops 20000000000 | bytes 20000000 | tf_op jit(solution)/shard_map/pair_terms/pallas_call | solution.py:426
  51.4 0.2 collective-permute-start.2
  51.6 0.0 collective-permute-done.par
  51.6 21.0 %pair_terms.3 = (f32[2,6912,128]{2,1,0:T(8,128)}, bf16[4608,128]{1,0:T(8,128)(2,1)}, bf16[2304,128]{1,0:T(8,128)(2,1)}, f32[8,128]{1,0:T(8,128)}) custom-call(bf16[6912,128]{1,0:T(8,128)(2,1)} %take_band.2.refs_0_.own0, bf16[6912,128]{1,0:T(8,128)(2,1)} %take_band.3.own1, bf16[2,96,96,128]{3,2,1,0:T(8,128)(2,1)} %padded_rows.1.own_u, ...), custom_call_target="tpu_custom_call" | custom-call | flops 20000000000 | bytes 20000000 | tf_op jit(solution)/shard_map/pair_terms/pallas_call | solution.py:426
  72.7 2.4 %collective-permute-start.4 = (bf16[4608,128]{1,0:T(8,128)(2,1)}, bf16[4608,128]{1,0:T(8,128)(2,1)S(1)}, u32[]{:S(2)}, u32[]{:S(2)}) collective-permute-start(bf16[4608,128]{1,0:T(8,128)(2,1)} %get-tuple-element.21), channel_id=1, source_target_pairs={{1,0},{2,1},{3,2},{4,3},{5,4},{6,5},{7,6},{8,7},{9,8},{10,9},{11,1... | collective-permute-start | bytes 3538952 | tf_op jit(solution)/shard_map/ppermute | solution.py:565
  75.1 0.1 collective-permute-start.3
  75.2 0.4 collective-permute-start.5
  75.6 1.7 %collective-permute-done.5 = f32[8,128]{1,0:T(8,128)S(1)} collective-permute-done((f32[8,128]{1,0:T(8,128)}, f32[8,128]{1,0:T(8,128)S(1)}, u32[]{:S(2)}, u32[]{:S(2)}) %collective-permute-start.5) | collective-permute-done | bytes 4128 | tf_op jit(solution)/shard_map/ppermute | solution.py:596
  77.3 0.7 add.20
  78.0 0.6 collective-permute-start.6
  78.7 0.0 collective-permute-done.6
  78.7 0.7 collective-permute-start.7
  79.4 0.0 collective-permute-done.7
  79.4 0.7 collective-permute-start.8
  80.0 0.0 collective-permute-done.8
  80.1 0.7 collective-permute-start.9
  80.7 8.4 %collective-permute-done.4.back1 = bf16[4608,128]{1,0:T(8,128)(2,1)S(1)} collective-permute-done((bf16[4608,128]{1,0:T(8,128)(2,1)}, bf16[4608,128]{1,0:T(8,128)(2,1)S(1)}, u32[]{:S(2)}, u32[]{:S(2)}) %collective-permute-start.4) | collective-permute-done | bytes 1179680 | tf_op jit(solution)/shard_map/ppermute | solution.py:565
  89.2 0.0 collective-permute-done.2.back0
  89.2 5.9 %add_piece.2 = (f32[13824,128]{1,0:T(8,128)}, f32[2,2,8,128]{3,2,1,0:T(8,128)S(1)}) custom-call(bf16[6912,128]{1,0:T(8,128)(2,1)} %take_band.2.refs_0_.own0, bf16[6912,128]{1,0:T(8,128)(2,1)} %take_band.3.own1, f32[2,6912,128]{2,1,0:T(8,128)} %get-tuple-element.18.terms, bf16[6912,128]{1,0:T(8,128)(2,1)} %collective-permute-done.2.back0, ...), custom_call_target="tpu_custom_call" | custom-call | bytes 14155776 | tf_op jit(solution)/shard_map/add_piece/pallas_call | solution.py:535
  95.1 0.0 collective-permute-done.9
  95.2 5.1 %collective-permute-start.10 = (f32[8,128]{1,0:T(8,128)S(1)}, f32[8,128]{1,0:T(8,128)S(1)}, u32[]{:S(2)}, u32[]{:S(2)}) collective-permute-start(f32[8,128]{1,0:T(8,128)S(1)} %add.24), channel_id=1, source_target_pairs={{0,1},{1,0},{2,3},{3,2},{4,5},{5,4},{6,7},{7,6},{8,9},{9,8},{10,11... | collective-permute-start | bytes 12296 | tf_op jit(solution)/shard_map/ppermute | solution.py:608
  100.3 0.5 slice.6
  100.8 0.0 collective-permute-done.3.back1
  100.8 3.4 %add_piece.3 = (f32[13824,128]{1,0:T(8,128)}, f32[2,2]{1,0:T(2,128)}) custom-call(bf16[6912,128]{1,0:T(8,128)(2,1)} %take_band.2.refs_0_.own0, bf16[6912,128]{1,0:T(8,128)(2,1)} %take_band.3.own1, f32[2,6912,128]{2,1,0:T(8,128)} %get-tuple-element.18.terms, bf16[6912,128]{1,0:T(8,128)(2,1)} %collective-permute-done.2.back0, ...), custom_call_target="tpu_custom_call", output_to_operand_aliasing={{0}: (6, {})} | custom-call | bytes 7077888 | tf_op jit(solution)/shard_map/add_piece/pallas_call | solution.py:535
  104.2 0.0 collective-permute-done.10
  104.2 0.5 slice.7
  (4 shorter events, 0.0 us)
Async XLA Ops:
  4.7 26.9 %collective-permute-start.1 = (bf16[6912,128]{1,0:T(8,128)(2,1)}, bf16[6912,128]{1,0:T(8,128)(2,1)}, u32[]{:S(2)}, u32[]{:S(2)}) collective-permute-start(bf16[6912,128]{1,0:T(8,128)(2,1)} %take_band.2.refs_0_.own0), channel_id=1, source_target_pairs={{31,0},{0,1},{1,2},{2,3},{3,4},{4,5},{5,6},{6,7},{7,8},{8,9},{9,10... | collective-permute-start | bytes 5308424 | tf_op jit(solution)/shard_map/ppermute | solution.py:565
  9.3 42.3 %collective-permute-start = (bf16[6912,128]{1,0:T(8,128)(2,1)}, bf16[6912,128]{1,0:T(8,128)(2,1)}, u32[]{:S(2)}, u32[]{:S(2)}) collective-permute-start(bf16[6912,128]{1,0:T(8,128)(2,1)} %take_band.3.own1), channel_id=1, source_target_pairs={{31,0},{0,1},{1,2},{2,3},{3,4},{4,5},{5,6},{6,7},{7,8},{8,9},{9,10... | collective-permute-start | bytes 5308424 | tf_op jit(solution)/shard_map/ppermute | solution.py:565
  51.4 37.8 %collective-permute-start.2 = (bf16[6912,128]{1,0:T(8,128)(2,1)}, bf16[6912,128]{1,0:T(8,128)(2,1)}, u32[]{:S(2)}, u32[]{:S(2)}) collective-permute-start(bf16[6912,128]{1,0:T(8,128)(2,1)} %get-tuple-element.19), channel_id=1, source_target_pairs={{1,0},{2,1},{3,2},{4,3},{5,4},{6,5},{7,6},{8,7},{9,8},{10,9},{11,1... | collective-permute-start | bytes 5308424 | tf_op jit(solution)/shard_map/ppermute | solution.py:565
  72.7 16.5 %collective-permute-start.4 = (bf16[4608,128]{1,0:T(8,128)(2,1)}, bf16[4608,128]{1,0:T(8,128)(2,1)S(1)}, u32[]{:S(2)}, u32[]{:S(2)}) collective-permute-start(bf16[4608,128]{1,0:T(8,128)(2,1)} %get-tuple-element.21), channel_id=1, source_target_pairs={{1,0},{2,1},{3,2},{4,3},{5,4},{6,5},{7,6},{8,7},{9,8},{10,9},{11,1... | collective-permute-start | bytes 3538952 | tf_op jit(solution)/shard_map/ppermute | solution.py:565
  75.1 25.7 %collective-permute-start.3 = (bf16[2304,128]{1,0:T(8,128)(2,1)}, bf16[2304,128]{1,0:T(8,128)(2,1)S(1)}, u32[]{:S(2)}, u32[]{:S(2)}) collective-permute-start(bf16[2304,128]{1,0:T(8,128)(2,1)} %get-tuple-element.20), channel_id=1, source_target_pairs={{1,0},{2,1},{3,2},{4,3},{5,4},{6,5},{7,6},{8,7},{9,8},{10,9},{11,1... | collective-permute-start | bytes 1769480 | tf_op jit(solution)/shard_map/ppermute | solution.py:565
  75.2 2.2 %collective-permute-start.5 = (f32[8,128]{1,0:T(8,128)}, f32[8,128]{1,0:T(8,128)S(1)}, u32[]{:S(2)}, u32[]{:S(2)}) collective-permute-start(f32[8,128]{1,0:T(8,128)} %get-tuple-element.26), channel_id=1, source_target_pairs={{0,1},{1,0},{2,3},{3,2},{4,5},{5,4},{6,7},{7,6},{8,9},{9,8},{10,11... | collective-permute-start | bytes 12296 | tf_op jit(solution)/shard_map/ppermute | solution.py:596
  78.0 0.7 collective-permute-start.6
  78.7 0.7 collective-permute-start.7
  79.4 0.7 collective-permute-start.8
  80.1 15.1 %collective-permute-start.9 = (f32[8,128]{1,0:T(8,128)S(1)}, f32[8,128]{1,0:T(8,128)S(1)}, u32[]{:S(2)}, u32[]{:S(2)}) collective-permute-start(f32[8,128]{1,0:T(8,128)S(1)} %add.23), channel_id=1, source_target_pairs={{0,0},{1,3},{2,2},{3,1},{4,4},{5,7},{6,6},{7,5},{8,8},{9,11},{10,1... | collective-permute-start | bytes 12296 | tf_op jit(solution)/shard_map/ppermute | solution.py:610
  95.2 9.1 %collective-permute-start.10 = (f32[8,128]{1,0:T(8,128)S(1)}, f32[8,128]{1,0:T(8,128)S(1)}, u32[]{:S(2)}, u32[]{:S(2)}) collective-permute-start(f32[8,128]{1,0:T(8,128)S(1)} %add.24), channel_id=1, source_target_pairs={{0,1},{1,0},{2,3},{3,2},{4,5},{5,4},{6,7},{7,6},{8,9},{9,8},{10,11... | collective-permute-start | bytes 12296 | tf_op jit(solution)/shard_map/ppermute | solution.py:608

commit v11 on v10

--- a/solution.py
+++ b/solution.py
@@ -596,7 +596,7 @@
         energy = energy + lax.ppermute(energy, "band", swap)
         steps = [1 << b for b in range(1, size.bit_length() - 1)]
         steps = [b for b in steps if b != 2] + [b for b in steps if b == 2]
-        steps = [[(i, i ^ b if i % 2 else i) for i in range(size)] for b in steps]
+        steps = [[(i, i ^ (b if i % 2 else steps[0])) for i in range(size)] for b in steps]
     while len(steps) > len(back1) - 1:
         energy = energy + lax.ppermute(energy, "band", steps.pop(0))
     exchange, grams = None, []

time: 108 us -> 106 us (0.981)
  the two profiles are of different devices: /device:TPU:0 before, /device:TPU:31 now
where the time goes in v11:
time: 106 us
  Pallas kernels  65.2 us (62%)
  waiting for transfers between devices  22.9 us (22%)
  starting transfers between devices  13.1 us (12%)
  between operations  3.13 us (3%)
  local copies, waits for them, and re-layouts  1.06 us (1%)
    pallas_call x2, Pallas kernels, pair_terms(): pl.pallas_call(functools.partial(pairs_kernel, pieces, share), out_shape=...  40.7 us
    ppermute x5, waiting for transfers between devices, from_behind(): lax.ppermute(block, axis, [((i - distance) % size, i) for i in range(size)])  14.6 us
    pallas_call x2, Pallas kernels, add_piece(): pl.pallas_call(functools.partial(piece_kernel, first, size), out_shape=(j...  9.38 us
    pallas_call x2, Pallas kernels, take_band(): pl.pallas_call(functools.partial(band_kernel, p), out_shape=jax.ShapeDtyp...  8.13 us
    pallas_call x1, Pallas kernels, padded_rows(): pl.pallas_call(rows_kernel, out_shape=jax.ShapeDtypeStruct((2, G, G, LANE...  7 us
    ppermute x3, waiting for transfers between devices, per_device(): energy = energy + lax.ppermute(energy, 'band', steps.pop(0))  6.28 us
    ppermute x5, starting transfers between devices, from_behind(): lax.ppermute(block, axis, [((i - distance) % size, i) for i in range(size)])  5.09 us
    ppermute x1, starting transfers between devices, per_device(): got = lax.ppermute(energy, 'band', swap)  4.85 us
  transfers between devices with their start and end apart: 11, of which 6 were waited for; matrix products, arithmetic and copies ran while one was open for 1% of the time, Pallas kernels for 58%

profile of v11, /device:TPU:31, one launch (start us, length us, event | category | flops | bytes accessed | tf_op | source)
XLA Modules:
  0.0 106.1 jit_solution(16527540100572786223)
XLA Ops:
  0.6 4.1 %take_band.2.refs_0_.own0 = bf16[6912,128]{1,0:T(8,128)(2,1)} custom-call(bf16[13824,128]{1,0:T(8,128)(2,1)} %bitcast.12), custom_call_target="tpu_custom_call" | custom-call | bytes 5308416 | tf_op jit(solution)/shard_map/take_band/pallas_call | solution.py:168
  4.7 0.1 collective-permute-start.1
  4.8 4.1 %take_band.3.own1 = bf16[6912,128]{1,0:T(8,128)(2,1)} custom-call(bf16[13824,128]{1,0:T(8,128)(2,1)} %bitcast.13, bf16[6912,128]{1,0:T(8,128)(2,1)} %take_band.2.refs_0_.own0), custom_call_target="tpu_custom_call" | custom-call | bytes 5308416 | tf_op jit(solution)/shard_map/take_band/pallas_call | solution.py:168
  8.8 0.1 collective-permute-start
  8.9 7.0 %padded_rows.1.own_u = bf16[2,96,96,128]{3,2,1,0:T(8,128)(2,1)} custom-call(bf16[6912,128]{1,0:T(8,128)(2,1)} %take_band.2.refs_0_.own0, bf16[6912,128]{1,0:T(8,128)(2,1)} %take_band.3.own1, bf16[2,256,256]{2,1,0:T(8,128)(2,1)} %constant.34.clone.sel.refs_6_.refs_8_), custom_call_target="tpu_custom_call" | custom-call | bytes 14155776 | tf_op jit(solution)/shard_map/padded_rows/pallas_call | solution.py:197
  15.9 8.6 %collective-permute-done.1.par = bf16[6912,128]{1,0:T(8,128)(2,1)} collective-permute-done((bf16[6912,128]{1,0:T(8,128)(2,1)}, bf16[6912,128]{1,0:T(8,128)(2,1)}, u32[]{:S(2)}, u32[]{:S(2)}) %collective-permute-start.1) | collective-permute-done | bytes 1769504 | tf_op jit(solution)/shard_map/ppermute | solution.py:565
  24.5 19.7 %pair_terms.2 = (f32[2,6912,128]{2,1,0:T(8,128)}, bf16[6912,128]{1,0:T(8,128)(2,1)}, f32[8,128]{1,0:T(8,128)}) custom-call(bf16[6912,128]{1,0:T(8,128)(2,1)} %take_band.2.refs_0_.own0, bf16[6912,128]{1,0:T(8,128)(2,1)} %take_band.3.own1, bf16[2,96,96,128]{3,2,1,0:T(8,128)(2,1)} %padded_rows.1.own_u, f32[4800,128]{1,0:T(8,128)} %constant.35.clone.kern, ...), custom_call_target="tpu_custom_call" | custom-call | flops 20000000000 | bytes 20000000 | tf_op jit(solution)/shard_map/pair_terms/pallas_call | solution.py:426
  44.3 3.4 %collective-permute-start.2 = (bf16[6912,128]{1,0:T(8,128)(2,1)}, bf16[6912,128]{1,0:T(8,128)(2,1)}, u32[]{:S(2)}, u32[]{:S(2)}) collective-permute-start(bf16[6912,128]{1,0:T(8,128)(2,1)} %get-tuple-element.19), channel_id=1, source_target_pairs={{1,0},{2,1},{3,2},{4,3},{5,4},{6,5},{7,6},{8,7},{9,8},{10,9},{11,1... | collective-permute-start | bytes 5308424 | tf_op jit(solution)/shard_map/ppermute | solution.py:565
  47.6 0.0 collective-permute-done.par
  47.6 21.0 %pair_terms.3 = (f32[2,6912,128]{2,1,0:T(8,128)}, bf16[4608,128]{1,0:T(8,128)(2,1)}, bf16[2304,128]{1,0:T(8,128)(2,1)}, f32[8,128]{1,0:T(8,128)}) custom-call(bf16[6912,128]{1,0:T(8,128)(2,1)} %take_band.2.refs_0_.own0, bf16[6912,128]{1,0:T(8,128)(2,1)} %take_band.3.own1, bf16[2,96,96,128]{3,2,1,0:T(8,128)(2,1)} %padded_rows.1.own_u, ...), custom_call_target="tpu_custom_call" | custom-call | flops 20000000000 | bytes 20000000 | tf_op jit(solution)/shard_map/pair_terms/pallas_call | solution.py:426
  68.7 0.1 collective-permute-start.4
  68.8 1.5 %collective-permute-start.3 = (bf16[2304,128]{1,0:T(8,128)(2,1)}, bf16[2304,128]{1,0:T(8,128)(2,1)S(1)}, u32[]{:S(2)}, u32[]{:S(2)}) collective-permute-start(bf16[2304,128]{1,0:T(8,128)(2,1)} %get-tuple-element.20), channel_id=1, source_target_pairs={{1,0},{2,1},{3,2},{4,3},{5,4},{6,5},{7,6},{8,7},{9,8},{10,9},{11,1... | collective-permute-start | bytes 1769480 | tf_op jit(solution)/shard_map/ppermute | solution.py:565
  70.3 0.1 collective-permute-start.5
  70.3 2.0 %collective-permute-done.5 = f32[8,128]{1,0:T(8,128)S(1)} collective-permute-done((f32[8,128]{1,0:T(8,128)}, f32[8,128]{1,0:T(8,128)S(1)}, u32[]{:S(2)}, u32[]{:S(2)}) %collective-permute-start.5) | collective-permute-done | bytes 4128 | tf_op jit(solution)/shard_map/ppermute | solution.py:596
  72.3 0.7 add.20
  73.0 1.0 collective-permute-start.6
  73.9 1.5 %collective-permute-done.6 = f32[8,128]{1,0:T(8,128)S(1)} collective-permute-done((f32[8,128]{1,0:T(8,128)S(1)}, f32[8,128]{1,0:T(8,128)S(1)}, u32[]{:S(2)}, u32[]{:S(2)}) %collective-permute-start.6) | collective-permute-done | bytes 4128 | tf_op jit(solution)/shard_map/ppermute | solution.py:601
  75.4 0.6 collective-permute-start.7
  76.0 1.9 %collective-permute-done.7 = f32[8,128]{1,0:T(8,128)S(1)} collective-permute-done((f32[8,128]{1,0:T(8,128)S(1)}, f32[8,128]{1,0:T(8,128)S(1)}, u32[]{:S(2)}, u32[]{:S(2)}) %collective-permute-start.7) | collective-permute-done | bytes 4128 | tf_op jit(solution)/shard_map/ppermute | solution.py:601
  77.9 0.5 collective-permute-start.8
  78.4 2.9 %collective-permute-done.8 = f32[8,128]{1,0:T(8,128)S(1)} collective-permute-done((f32[8,128]{1,0:T(8,128)S(1)}, f32[8,128]{1,0:T(8,128)S(1)}, u32[]{:S(2)}, u32[]{:S(2)}) %collective-permute-start.8) | collective-permute-done | bytes 4128 | tf_op jit(solution)/shard_map/ppermute | solution.py:601
  81.3 1.1 %collective-permute-start.9 = (f32[8,128]{1,0:T(8,128)S(1)}, f32[8,128]{1,0:T(8,128)S(1)}, u32[]{:S(2)}, u32[]{:S(2)}) collective-permute-start(f32[8,128]{1,0:T(8,128)S(1)} %add.23), channel_id=1, source_target_pairs={{0,4},{1,3},{2,6},{3,1},{4,0},{5,7},{6,2},{7,5},{8,12},{9,11},{10,... | collective-permute-start | bytes 12296 | tf_op jit(solution)/shard_map/ppermute | solution.py:610
  82.4 6.0 %collective-permute-done.4.back1 = bf16[4608,128]{1,0:T(8,128)(2,1)S(1)} collective-permute-done((bf16[4608,128]{1,0:T(8,128)(2,1)}, bf16[4608,128]{1,0:T(8,128)(2,1)S(1)}, u32[]{:S(2)}, u32[]{:S(2)}) %collective-permute-start.4) | collective-permute-done | bytes 1179680 | tf_op jit(solution)/shard_map/ppermute | solution.py:565
  88.4 0.0 collective-permute-done.2.back0
  88.4 5.9 %add_piece.2 = (f32[13824,128]{1,0:T(8,128)}, f32[2,2,8,128]{3,2,1,0:T(8,128)S(1)}) custom-call(bf16[6912,128]{1,0:T(8,128)(2,1)} %take_band.2.refs_0_.own0, bf16[6912,128]{1,0:T(8,128)(2,1)} %take_band.3.own1, f32[2,6912,128]{2,1,0:T(8,128)} %get-tuple-element.18.terms, bf16[6912,128]{1,0:T(8,128)(2,1)} %collective-permute-done.2.back0, ...), custom_call_target="tpu_custom_call" | custom-call | bytes 14155776 | tf_op jit(solution)/shard_map/add_piece/pallas_call | solution.py:535
  94.3 0.0 collective-permute-done.9
  94.4 4.9 %collective-permute-start.10 = (f32[8,128]{1,0:T(8,128)S(1)}, f32[8,128]{1,0:T(8,128)S(1)}, u32[]{:S(2)}, u32[]{:S(2)}) collective-permute-start(f32[8,128]{1,0:T(8,128)S(1)} %add.24), channel_id=1, source_target_pairs={{0,1},{1,0},{2,3},{3,2},{4,5},{5,4},{6,7},{7,6},{8,9},{9,8},{10,11... | collective-permute-start | bytes 12296 | tf_op jit(solution)/shard_map/ppermute | solution.py:608
  99.2 0.5 slice.6
  99.7 0.0 collective-permute-done.3.back1
  99.7 3.4 %add_piece.3 = (f32[13824,128]{1,0:T(8,128)}, f32[2,2]{1,0:T(2,128)}) custom-call(bf16[6912,128]{1,0:T(8,128)(2,1)} %take_band.2.refs_0_.own0, bf16[6912,128]{1,0:T(8,128)(2,1)} %take_band.3.own1, f32[2,6912,128]{2,1,0:T(8,128)} %get-tuple-element.18.terms, bf16[6912,128]{1,0:T(8,128)(2,1)} %collective-permute-done.2.back0, ...), custom_call_target="tpu_custom_call", output_to_operand_aliasing={{0}: (6, {})} | custom-call | bytes 7077888 | tf_op jit(solution)/shard_map/add_piece/pallas_call | solution.py:535
  103.2 0.0 collective-permute-done.10
  103.2 0.5 slice.7
  (4 shorter events, 0.0 us)
Async XLA Ops:
  4.7 19.8 %collective-permute-start.1 = (bf16[6912,128]{1,0:T(8,128)(2,1)}, bf16[6912,128]{1,0:T(8,128)(2,1)}, u32[]{:S(2)}, u32[]{:S(2)}) collective-permute-start(bf16[6912,128]{1,0:T(8,128)(2,1)} %take_band.2.refs_0_.own0), channel_id=1, source_target_pairs={{31,0},{0,1},{1,2},{2,3},{3,4},{4,5},{5,6},{6,7},{7,8},{8,9},{9,10... | collective-permute-start | bytes 5308424 | tf_op jit(solution)/shard_map/ppermute | solution.py:565
  8.8 38.8 %collective-permute-start = (bf16[6912,128]{1,0:T(8,128)(2,1)}, bf16[6912,128]{1,0:T(8,128)(2,1)}, u32[]{:S(2)}, u32[]{:S(2)}) collective-permute-start(bf16[6912,128]{1,0:T(8,128)(2,1)} %take_band.3.own1), channel_id=1, source_target_pairs={{31,0},{0,1},{1,2},{2,3},{3,4},{4,5},{5,6},{6,7},{7,8},{8,9},{9,10... | collective-permute-start | bytes 5308424 | tf_op jit(solution)/shard_map/ppermute | solution.py:565
  44.3 44.1 %collective-permute-start.2 = (bf16[6912,128]{1,0:T(8,128)(2,1)}, bf16[6912,128]{1,0:T(8,128)(2,1)}, u32[]{:S(2)}, u32[]{:S(2)}) collective-permute-start(bf16[6912,128]{1,0:T(8,128)(2,1)} %get-tuple-element.19), channel_id=1, source_target_pairs={{1,0},{2,1},{3,2},{4,3},{5,4},{6,5},{7,6},{8,7},{9,8},{10,9},{11,1... | collective-permute-start | bytes 5308424 | tf_op jit(solution)/shard_map/ppermute | solution.py:565
  68.7 19.7 %collective-permute-start.4 = (bf16[4608,128]{1,0:T(8,128)(2,1)}, bf16[4608,128]{1,0:T(8,128)(2,1)S(1)}, u32[]{:S(2)}, u32[]{:S(2)}) collective-permute-start(bf16[4608,128]{1,0:T(8,128)(2,1)} %get-tuple-element.21), channel_id=1, source_target_pairs={{1,0},{2,1},{3,2},{4,3},{5,4},{6,5},{7,6},{8,7},{9,8},{10,9},{11,1... | collective-permute-start | bytes 3538952 | tf_op jit(solution)/shard_map/ppermute | solution.py:565
  68.8 31.0 %collective-permute-start.3 = (bf16[2304,128]{1,0:T(8,128)(2,1)}, bf16[2304,128]{1,0:T(8,128)(2,1)S(1)}, u32[]{:S(2)}, u32[]{:S(2)}) collective-permute-start(bf16[2304,128]{1,0:T(8,128)(2,1)} %get-tuple-element.20), channel_id=1, source_target_pairs={{1,0},{2,1},{3,2},{4,3},{5,4},{6,5},{7,6},{8,7},{9,8},{10,9},{11,1... | collective-permute-start | bytes 1769480 | tf_op jit(solution)/shard_map/ppermute | solution.py:565
  70.3 2.0 %collective-permute-start.5 = (f32[8,128]{1,0:T(8,128)}, f32[8,128]{1,0:T(8,128)S(1)}, u32[]{:S(2)}, u32[]{:S(2)}) collective-permute-start(f32[8,128]{1,0:T(8,128)} %get-tuple-element.26), channel_id=1, source_target_pairs={{0,1},{1,0},{2,3},{3,2},{4,5},{5,4},{6,7},{7,6},{8,9},{9,8},{10,11... | collective-permute-start | bytes 12296 | tf_op jit(solution)/shard_map/ppermute | solution.py:596
  73.0 2.5 %collective-permute-start.6 = (f32[8,128]{1,0:T(8,128)S(1)}, f32[8,128]{1,0:T(8,128)S(1)}, u32[]{:S(2)}, u32[]{:S(2)}) collective-permute-start(f32[8,128]{1,0:T(8,128)S(1)} %add.20), channel_id=1, source_target_pairs={{0,4},{1,5},{2,6},{3,7},{4,0},{5,1},{6,2},{7,3},{8,12},{9,13},{10,... | collective-permute-start | bytes 12296 | tf_op jit(solution)/shard_map/ppermute | solution.py:601
  75.4 2.5 %collective-permute-start.7 = (f32[8,128]{1,0:T(8,128)S(1)}, f32[8,128]{1,0:T(8,128)S(1)}, u32[]{:S(2)}, u32[]{:S(2)}) collective-permute-start(f32[8,128]{1,0:T(8,128)S(1)} %add.21), channel_id=1, source_target_pairs={{0,4},{1,9},{2,6},{3,11},{4,0},{5,13},{6,2},{7,15},{8,12},{9,1},{1... | collective-permute-start | bytes 12296 | tf_op jit(solution)/shard_map/ppermute | solution.py:601
  77.9 3.4 %collective-permute-start.8 = (f32[8,128]{1,0:T(8,128)S(1)}, f32[8,128]{1,0:T(8,128)S(1)}, u32[]{:S(2)}, u32[]{:S(2)}) collective-permute-start(f32[8,128]{1,0:T(8,128)S(1)} %add.22), channel_id=1, source_target_pairs={{0,4},{1,17},{2,6},{3,19},{4,0},{5,21},{6,2},{7,23},{8,12},{9,25},... | collective-permute-start | bytes 12296 | tf_op jit(solution)/shard_map/ppermute | solution.py:601
  81.3 13.1 %collective-permute-start.9 = (f32[8,128]{1,0:T(8,128)S(1)}, f32[8,128]{1,0:T(8,128)S(1)}, u32[]{:S(2)}, u32[]{:S(2)}) collective-permute-start(f32[8,128]{1,0:T(8,128)S(1)} %add.23), channel_id=1, source_target_pairs={{0,4},{1,3},{2,6},{3,1},{4,0},{5,7},{6,2},{7,5},{8,12},{9,11},{10,... | collective-permute-start | bytes 12296 | tf_op jit(solution)/shard_map/ppermute | solution.py:610
  94.4 8.8 %collective-permute-start.10 = (f32[8,128]{1,0:T(8,128)S(1)}, f32[8,128]{1,0:T(8,128)S(1)}, u32[]{:S(2)}, u32[]{:S(2)}) collective-permute-start(f32[8,128]{1,0:T(8,128)S(1)} %add.24), channel_id=1, source_target_pairs={{0,1},{1,0},{2,3},{3,2},{4,5},{5,4},{6,7},{7,6},{8,9},{9,8},{10,11... | collective-permute-start | bytes 12296 | tf_op jit(solution)/shard_map/ppermute | solution.py:608

commit v12 on v11

--- a/solution.py
+++ b/solution.py
@@ -596,8 +596,8 @@
         energy = energy + lax.ppermute(energy, "band", swap)
         steps = [1 << b for b in range(1, size.bit_length() - 1)]
         steps = [b for b in steps if b != 2] + [b for b in steps if b == 2]
-        steps = [[(i, i ^ (b if i % 2 else steps[0])) for i in range(size)] for b in steps]
-    while len(steps) > len(back1) - 1:
+        steps = [[(i, i ^ b) for i in range(size) if i % 2 or b == 4] for b in steps]
+    while len(steps) > len(back1):
         energy = energy + lax.ppermute(energy, "band", steps.pop(0))
     exchange, grams = None, []
     first = 0
@@ -609,6 +609,9 @@
         elif steps:
             got = lax.ppermute(energy, "band", steps.pop(0))
         exchange, gram = add_piece(first, count, own, terms, back0, piece, grams, exchange)
+        while not last and steps:
+            energy = energy + after(got, gram)
+            got = lax.ppermute(energy, "band", steps.pop(0))
         if got is not None and last:
             odd = lax.axis_index("band") % 2 == 1
             energy = jnp.where(odd, energy[:1, :1], after(got, gram)[:1, :1])

time: 106 us -> 107 us (level)
  the two profiles are of different devices: /device:TPU:31 before, /device:TPU:0 now
where the time goes in v12:
time: 107 us; the launch traced here: 106 us
  Pallas kernels  65.2 us (61%)
  waiting for transfers between devices  24.3 us (23%)
  starting transfers between devices  11.8 us (11%)
  between operations  3.18 us (3%)
    pallas_call x2, Pallas kernels, pair_terms(): pl.pallas_call(functools.partial(pairs_kernel, pieces, share), out_shape=...  40.7 us
    ppermute x5, waiting for transfers between devices, from_behind(): lax.ppermute(block, axis, [((i - distance) % size, i) for i in range(size)])  19 us
    pallas_call x2, Pallas kernels, add_piece(): pl.pallas_call(functools.partial(piece_kernel, first, size), out_shape=(j...  9.38 us
    pallas_call x2, Pallas kernels, take_band(): pl.pallas_call(functools.partial(band_kernel, p), out_shape=jax.ShapeDtyp...  8.13 us
    pallas_call x1, Pallas kernels, padded_rows(): pl.pallas_call(rows_kernel, out_shape=jax.ShapeDtypeStruct((2, G, G, LANE...  7 us
    ppermute x5, starting transfers between devices, from_behind(): lax.ppermute(block, axis, [((i - distance) % size, i) for i in range(size)])  5.91 us
    ppermute x2, waiting for transfers between devices, per_device(): energy = energy + lax.ppermute(energy, 'band', steps.pop(0))  3.61 us
    ppermute x1, starting transfers between devices, per_device(): got = lax.ppermute(energy, 'band', swap)  3.46 us
  transfers between devices with their start and end apart: 11, of which 4 were waited for; matrix products, arithmetic and copies ran while one was open for 1% of the time, Pallas kernels for 58%

profile of v12, /device:TPU:0, one launch (start us, length us, event | category | flops | bytes accessed | tf_op | source)
XLA Modules:
  0.0 106.3 jit_solution(15262217771589590144)
XLA Ops:
  0.6 4.1 %take_band.2.refs_0_.own0 = bf16[6912,128]{1,0:T(8,128)(2,1)} custom-call(bf16[13824,128]{1,0:T(8,128)(2,1)} %bitcast.12), custom_call_target="tpu_custom_call" | custom-call | bytes 5308416 | tf_op jit(solution)/shard_map/take_band/pallas_call | solution.py:168
  4.7 0.5 collective-permute-start.1
  5.2 4.1 %take_band.3.own1 = bf16[6912,128]{1,0:T(8,128)(2,1)} custom-call(bf16[13824,128]{1,0:T(8,128)(2,1)} %bitcast.13, bf16[6912,128]{1,0:T(8,128)(2,1)} %take_band.2.refs_0_.own0), custom_call_target="tpu_custom_call" | custom-call | bytes 5308416 | tf_op jit(solution)/shard_map/take_band/pallas_call | solution.py:168
  9.3 2.7 %collective-permute-start = (bf16[6912,128]{1,0:T(8,128)(2,1)}, bf16[6912,128]{1,0:T(8,128)(2,1)}, u32[]{:S(2)}, u32[]{:S(2)}) collective-permute-start(bf16[6912,128]{1,0:T(8,128)(2,1)} %take_band.3.own1), channel_id=1, source_target_pairs={{31,0},{0,1},{1,2},{2,3},{3,4},{4,5},{5,6},{6,7},{7,8},{8,9},{9,10... | collective-permute-start | bytes 5308424 | tf_op jit(solution)/shard_map/ppermute | solution.py:565
  11.9 7.0 %padded_rows.1.own_u = bf16[2,96,96,128]{3,2,1,0:T(8,128)(2,1)} custom-call(bf16[6912,128]{1,0:T(8,128)(2,1)} %take_band.2.refs_0_.own0, bf16[6912,128]{1,0:T(8,128)(2,1)} %take_band.3.own1, bf16[2,256,256]{2,1,0:T(8,128)(2,1)} %constant.34.clone.sel.refs_6_.refs_8_), custom_call_target="tpu_custom_call" | custom-call | bytes 14155776 | tf_op jit(solution)/shard_map/padded_rows/pallas_call | solution.py:197
  18.9 12.7 %collective-permute-done.1.par = bf16[6912,128]{1,0:T(8,128)(2,1)} collective-permute-done((bf16[6912,128]{1,0:T(8,128)(2,1)}, bf16[6912,128]{1,0:T(8,128)(2,1)}, u32[]{:S(2)}, u32[]{:S(2)}) %collective-permute-start.1) | collective-permute-done | bytes 1769504 | tf_op jit(solution)/shard_map/ppermute | solution.py:565
  31.6 19.7 %pair_terms.2 = (f32[2,6912,128]{2,1,0:T(8,128)}, bf16[6912,128]{1,0:T(8,128)(2,1)}, f32[8,128]{1,0:T(8,128)}) custom-call(bf16[6912,128]{1,0:T(8,128)(2,1)} %take_band.2.refs_0_.own0, bf16[6912,128]{1,0:T(8,128)(2,1)} %take_band.3.own1, bf16[2,96,96,128]{3,2,1,0:T(8,128)(2,1)} %padded_rows.1.own_u, f32[4800,128]{1,0:T(8,128)} %constant.35.clone.kern, ...), custom_call_target="tpu_custom_call" | custom-call | flops 20000000000 | bytes 20000000 | tf_op jit(solution)/shard_map/pair_terms/pallas_call | solution.py:426
  51.4 0.2 collective-permute-start.2
  51.6 0.0 collective-permute-done.par
  51.6 21.0 %pair_terms.3 = (f32[2,6912,128]{2,1,0:T(8,128)}, bf16[4608,128]{1,0:T(8,128)(2,1)}, bf16[2304,128]{1,0:T(8,128)(2,1)}, f32[8,128]{1,0:T(8,128)}) custom-call(bf16[6912,128]{1,0:T(8,128)(2,1)} %take_band.2.refs_0_.own0, bf16[6912,128]{1,0:T(8,128)(2,1)} %take_band.3.own1, bf16[2,96,96,128]{3,2,1,0:T(8,128)(2,1)} %padded_rows.1.own_u, ...), custom_call_target="tpu_custom_call" | custom-call | flops 20000000000 | bytes 20000000 | tf_op jit(solution)/shard_map/pair_terms/pallas_call | solution.py:426
  72.7 2.4 %collective-permute-start.4 = (bf16[4608,128]{1,0:T(8,128)(2,1)}, bf16[4608,128]{1,0:T(8,128)(2,1)S(1)}, u32[]{:S(2)}, u32[]{:S(2)}) collective-permute-start(bf16[4608,128]{1,0:T(8,128)(2,1)} %get-tuple-element.22), channel_id=1, source_target_pairs={{1,0},{2,1},{3,2},{4,3},{5,4},{6,5},{7,6},{8,7},{9,8},{10,9},{11,1... | collective-permute-start | bytes 3538952 | tf_op jit(solution)/shard_map/ppermute | solution.py:565
  75.1 0.1 collective-permute-start.3
  75.2 0.4 collective-permute-start.5
  75.6 1.7 %collective-permute-done.5 = f32[8,128]{1,0:T(8,128)S(1)} collective-permute-done((f32[8,128]{1,0:T(8,128)}, f32[8,128]{1,0:T(8,128)S(1)}, u32[]{:S(2)}, u32[]{:S(2)}) %collective-permute-start.5) | collective-permute-done | bytes 4128 | tf_op jit(solution)/shard_map/ppermute | solution.py:596
  77.3 0.7 add.20
  78.0 0.0 collective-permute-start.6
  78.0 3.6 %collective-permute-done.6 = f32[8,128]{1,0:T(8,128)S(1)} collective-permute-done((f32[8,128]{1,0:T(8,128)S(1)}, f32[8,128]{1,0:T(8,128)S(1)}, u32[]{:S(2)}, u32[]{:S(2)}) %collective-permute-start.6) | collective-permute-done | bytes 4128 | tf_op jit(solution)/shard_map/ppermute | solution.py:601
  81.6 0.7 collective-permute-start.7
  82.3 0.0 collective-permute-done.7
  82.3 0.7 collective-permute-start.8
  83.0 6.3 %collective-permute-done.4.back1 = bf16[4608,128]{1,0:T(8,128)(2,1)S(1)} collective-permute-done((bf16[4608,128]{1,0:T(8,128)(2,1)}, bf16[4608,128]{1,0:T(8,128)(2,1)S(1)}, u32[]{:S(2)}, u32[]{:S(2)}) %collective-permute-start.4) | collective-permute-done | bytes 1179680 | tf_op jit(solution)/shard_map/ppermute | solution.py:565
  89.2 0.0 collective-permute-done.2.back0
  89.2 5.9 %add_piece.2 = (f32[13824,128]{1,0:T(8,128)}, f32[2,2,8,128]{3,2,1,0:T(8,128)S(1)}) custom-call(bf16[6912,128]{1,0:T(8,128)(2,1)} %take_band.2.refs_0_.own0, bf16[6912,128]{1,0:T(8,128)(2,1)} %take_band.3.own1, f32[2,6912,128]{2,1,0:T(8,128)} %get-tuple-element.19.terms, bf16[6912,128]{1,0:T(8,128)(2,1)} %collective-permute-done.2.back0, ...), custom_call_target="tpu_custom_call" | custom-call | bytes 14155776 | tf_op jit(solution)/shard_map/add_piece/pallas_call | solution.py:535
  95.2 0.0 collective-permute-done.8
  95.2 0.7 collective-permute-start.9
  95.9 0.0 collective-permute-done.9
  95.9 3.5 %collective-permute-start.10 = (f32[8,128]{1,0:T(8,128)S(1)}, f32[8,128]{1,0:T(8,128)S(1)}, u32[]{:S(2)}, u32[]{:S(2)}) collective-permute-start(f32[8,128]{1,0:T(8,128)S(1)} %add.24), channel_id=1, source_target_pairs={{0,1},{1,0},{2,3},{3,2},{4,5},{5,4},{6,7},{7,6},{8,9},{9,8},{10,11... | collective-permute-start | bytes 12296 | tf_op jit(solution)/shard_map/ppermute | solution.py:608
  99.4 0.0 collective-permute-done.3.back1
  99.4 3.4 %add_piece.3 = (f32[13824,128]{1,0:T(8,128)}, f32[2,2]{1,0:T(2,128)}) custom-call(bf16[6912,128]{1,0:T(8,128)(2,1)} %take_band.2.refs_0_.own0, bf16[6912,128]{1,0:T(8,128)(2,1)} %take_band.3.own1, f32[2,6912,128]{2,1,0:T(8,128)} %get-tuple-element.19.terms, bf16[6912,128]{1,0:T(8,128)(2,1)} %collective-permute-done.2.back0, ...), custom_call_target="tpu_custom_call", output_to_operand_aliasing={{0}: (6, {})} | custom-call | bytes 7077888 | tf_op jit(solution)/shard_map/add_piece/pallas_call | solution.py:535
  102.8 0.5 slice.6
  103.3 0.0 collective-permute-done.10
  103.3 0.5 slice.7
  (4 shorter events, 0.0 us)
Async XLA Ops:
  4.7 26.9 %collective-permute-start.1 = (bf16[6912,128]{1,0:T(8,128)(2,1)}, bf16[6912,128]{1,0:T(8,128)(2,1)}, u32[]{:S(2)}, u32[]{:S(2)}) collective-permute-start(bf16[6912,128]{1,0:T(8,128)(2,1)} %take_band.2.refs_0_.own0), channel_id=1, source_target_pairs={{31,0},{0,1},{1,2},{2,3},{3,4},{4,5},{5,6},{6,7},{7,8},{8,9},{9,10... | collective-permute-start | bytes 5308424 | tf_op jit(solution)/shard_map/ppermute | solution.py:565
  9.3 42.3 %collective-permute-start = (bf16[6912,128]{1,0:T(8,128)(2,1)}, bf16[6912,128]{1,0:T(8,128)(2,1)}, u32[]{:S(2)}, u32[]{:S(2)}) collective-permute-start(bf16[6912,128]{1,0:T(8,128)(2,1)} %take_band.3.own1), channel_id=1, source_target_pairs={{31,0},{0,1},{1,2},{2,3},{3,4},{4,5},{5,6},{6,7},{7,8},{8,9},{9,10... | collective-permute-start | bytes 5308424 | tf_op jit(solution)/shard_map/ppermute | solution.py:565
  51.4 37.9 %collective-permute-start.2 = (bf16[6912,128]{1,0:T(8,128)(2,1)}, bf16[6912,128]{1,0:T(8,128)(2,1)}, u32[]{:S(2)}, u32[]{:S(2)}) collective-permute-start(bf16[6912,128]{1,0:T(8,128)(2,1)} %get-tuple-element.20), channel_id=1, source_target_pairs={{1,0},{2,1},{3,2},{4,3},{5,4},{6,5},{7,6},{8,7},{9,8},{10,9},{11,1... | collective-permute-start | bytes 5308424 | tf_op jit(solution)/shard_map/ppermute | solution.py:565
  72.7 16.6 %collective-permute-start.4 = (bf16[4608,128]{1,0:T(8,128)(2,1)}, bf16[4608,128]{1,0:T(8,128)(2,1)S(1)}, u32[]{:S(2)}, u32[]{:S(2)}) collective-permute-start(bf16[4608,128]{1,0:T(8,128)(2,1)} %get-tuple-element.22), channel_id=1, source_target_pairs={{1,0},{2,1},{3,2},{4,3},{5,4},{6,5},{7,6},{8,7},{9,8},{10,9},{11,1... | collective-permute-start | bytes 3538952 | tf_op jit(solution)/shard_map/ppermute | solution.py:565
  75.1 24.3 %collective-permute-start.3 = (bf16[2304,128]{1,0:T(8,128)(2,1)}, bf16[2304,128]{1,0:T(8,128)(2,1)S(1)}, u32[]{:S(2)}, u32[]{:S(2)}) collective-permute-start(bf16[2304,128]{1,0:T(8,128)(2,1)} %get-tuple-element.21), channel_id=1, source_target_pairs={{1,0},{2,1},{3,2},{4,3},{5,4},{6,5},{7,6},{8,7},{9,8},{10,9},{11,1... | collective-permute-start | bytes 1769480 | tf_op jit(solution)/shard_map/ppermute | solution.py:565
  75.2 2.2 %collective-permute-start.5 = (f32[8,128]{1,0:T(8,128)}, f32[8,128]{1,0:T(8,128)S(1)}, u32[]{:S(2)}, u32[]{:S(2)}) collective-permute-start(f32[8,128]{1,0:T(8,128)} %get-tuple-element.27), channel_id=1, source_target_pairs={{0,1},{1,0},{2,3},{3,2},{4,5},{5,4},{6,7},{7,6},{8,9},{9,8},{10,11... | collective-permute-start | bytes 12296 | tf_op jit(solution)/shard_map/ppermute | solution.py:596
  78.0 3.6 %collective-permute-start.6 = (f32[8,128]{1,0:T(8,128)S(1)}, f32[8,128]{1,0:T(8,128)S(1)}, u32[]{:S(2)}, u32[]{:S(2)}) collective-permute-start(f32[8,128]{1,0:T(8,128)S(1)} %add.20), channel_id=1, source_target_pairs={{0,4},{1,5},{2,6},{3,7},{4,0},{5,1},{6,2},{7,3},{8,12},{9,13},{10,... | collective-permute-start | bytes 12296 | tf_op jit(solution)/shard_map/ppermute | solution.py:601
  81.6 0.7 collective-permute-start.7
  82.3 12.9 %collective-permute-start.8 = (f32[8,128]{1,0:T(8,128)S(1)}, f32[8,128]{1,0:T(8,128)S(1)}, u32[]{:S(2)}, u32[]{:S(2)}) collective-permute-start(f32[8,128]{1,0:T(8,128)S(1)} %add.22), channel_id=1, source_target_pairs={{1,17},{3,19},{5,21},{7,23},{9,25},{11,27},{13,29},{15,31},{17,1},... | collective-permute-start | bytes 12296 | tf_op jit(solution)/shard_map/ppermute | solution.py:610
  95.2 0.7 collective-permute-start.9
  95.9 7.4 %collective-permute-start.10 = (f32[8,128]{1,0:T(8,128)S(1)}, f32[8,128]{1,0:T(8,128)S(1)}, u32[]{:S(2)}, u32[]{:S(2)}) collective-permute-start(f32[8,128]{1,0:T(8,128)S(1)} %add.24), channel_id=1, source_target_pairs={{0,1},{1,0},{2,3},{3,2},{4,5},{5,4},{6,7},{7,6},{8,9},{9,8},{10,11... | collective-permute-start | bytes 12296 | tf_op jit(solution)/shard_map/ppermute | solution.py:608

commit v13 on v11

--- a/solution.py
+++ b/solution.py
@@ -124,7 +124,7 @@
 
 
 def widen_planes(src, dst, first):
-    @pl.loop(0, src.shape[0] // (2 * PLANE), unroll=4)
+    @pl.loop(0, src.shape[0] // (2 * PLANE), unroll=8)
     def _(i):
         value = src[pl.ds(pl.multiple_of(i * 2 * PLANE, 16), 2 * PLANE), :].astype(F32)
         dst[pl.ds((first + 2 * i) * F_PITCH, PLANE), :] = value[:PLANE]
@@ -248,7 +248,7 @@
         widen_planes(par_v.at[pl.ds(i * ROWS // 2, ROWS // 2), :], par_f, i * G // 2)
     table_loads[6].wait()
 
-    @pl.loop(0, QUADS // 4, unroll=2)
+    @pl.loop(0, QUADS // 4, unroll=3)
     def _(q):
         split_rows(par_f, sel, par_u, 4 * q, 4)
 
@@ -259,7 +259,7 @@
     table_loads[5].start()
     table_loads[0].wait()
 
-    @pl.loop(0, G // 2, unroll=8)
+    @pl.loop(0, G // 2, unroll=16)
     def _(i):
         density = []
         for e in range(2):
@@ -274,25 +274,30 @@
 
     table_loads[1].wait()
 
-    @pl.loop(0, HALF, unroll=7)
-    def _(k1):
-        def line(p, part):
-            return yw[pl.ds(p * half_y + part * HALF + k1, G, stride=Y_PITCH), :].astype(BF16)
-
-        out = dot(t2[...], stack(lanes(line(0, 0), line(1, 0)), lanes(line(0, 1), line(1, 1))))
-        at = pl.ds(pl.multiple_of(k1 * G, 16), G)
-        for p in range(2):
-            for part in range(2):
-                left = (2 * p + part) * LANES
-                value = out[part * G : (part + 1) * G, p * LANES : (p + 1) * LANES]
-                x34[at, left : left + LANES] = value.astype(BF16)
+    @pl.loop(0, KPAD // 2, unroll=5)
+    def _(pair):
+        def line(k1, part):
+            first = part * HALF + k1
+            rows = [yw[pl.ds(p * half_y + first, G, stride=Y_PITCH), :].astype(BF16) for p in range(2)]
+            return lanes(*rows)
+
+        both = [2 * pair, 2 * pair + 1]
+        out = dot(t2[...], lanes(*[stack(line(k1, 0), line(k1, 1)) for k1 in both]))
+        for e, k1 in enumerate(both):
+            at = pl.ds(pl.multiple_of(k1 * G, 16), G)
+            for p in range(2):
+                for part in range(2):
+                    left = (2 * p + part) * LANES
+                    right = (2 * e + p) * LANES
+                    value = out[part * G : (part + 1) * G, right : right + LANES]
+                    x34[at, left : left + LANES] = value.astype(BF16)
 
     loads[1].wait()
     table_loads[2].wait()
 
     many = 5
 
-    @pl.loop(0, KPAD // many, unroll=2)
+    @pl.loop(0, KPAD // many, unroll=5)
     def _(m):
         at = pl.ds(pl.multiple_of(m * many * G, 16), many * G)
         factor = kern_v[at, :]
@@ -309,7 +314,7 @@
 
     table_loads[3].wait()
 
-    @pl.loop(0, G // 4, unroll=6)
+    @pl.loop(0, G // 4, unroll=12)
     def _(four):
         parts = []
         for e in range(4):
@@ -332,7 +337,7 @@
         load.start()
     table_loads[4].wait()
 
-    @pl.loop(0, G // 4, unroll=6)
+    @pl.loop(0, G // 4, unroll=12)
     def _(four):
         parts = []
         for e in range(4):
@@ -596,7 +601,8 @@
         energy = energy + lax.ppermute(energy, "band", swap)
         steps = [1 << b for b in range(1, size.bit_length() - 1)]
         steps = [b for b in steps if b != 2] + [b for b in steps if b == 2]
-        steps = [[(i, i ^ (b if i % 2 else steps[0])) for i in range(size)] for b in steps]
+        aside = [4 if size > 4 else 2, 8 if size > 8 else 2]
+        steps = [[(i, i ^ (b if i % 2 else aside[i // 2 % 2])) for i in range(size)] for b in steps]
     while len(steps) > len(back1) - 1:
         energy = energy + lax.ppermute(energy, "band", steps.pop(0))
     exchange, grams = None, []

time: 106 us -> 98.7 us (0.931)
  the two profiles are of different devices: /device:TPU:31 before, /device:TPU:0 now
where the time goes in v13:
time: 98.7 us; the launch traced here: 98.4 us
  Pallas kernels  61.3 us (62%)
  waiting for transfers between devices  26.2 us (27%)
  starting transfers between devices  6.04 us (6%)
  between operations  3.13 us (3%)
  local copies, waits for them, and re-layouts  1.06 us (1%)
    pallas_call x2, Pallas kernels, pair_terms(): pl.pallas_call(functools.partial(pairs_kernel, pieces, share), out_shape=...  36.9 us
    ppermute x5, waiting for transfers between devices, from_behind(): lax.ppermute(block, axis, [((i - distance) % size, i) for i in range(size)])  13.9 us
    ppermute x3, waiting for transfers between devices, per_device(): energy = energy + lax.ppermute(energy, 'band', steps.pop(0))  10.8 us
    pallas_call x2, Pallas kernels, add_piece(): pl.pallas_call(functools.partial(piece_kernel, first, size), out_shape=(j...  9.39 us
    pallas_call x2, Pallas kernels, take_band(): pl.pallas_call(functools.partial(band_kernel, p), out_shape=jax.ShapeDtyp...  8.13 us
    pallas_call x1, Pallas kernels, padded_rows(): pl.pallas_call(rows_kernel, out_shape=jax.ShapeDtypeStruct((2, G, G, LANE...  6.94 us
    ppermute x5, starting transfers between devices, from_behind(): lax.ppermute(block, axis, [((i - distance) % size, i) for i in range(size)])  5.87 us
  transfers between devices with their start and end apart: 11, of which 6 were waited for; matrix products, arithmetic and copies ran while one was open for 1% of the time, Pallas kernels for 58%

profile of v13, /device:TPU:0, one launch (start us, length us, event | category | flops | bytes accessed | tf_op | source)
XLA Modules:
  0.0 98.4 jit_solution(6432295104987833669)
XLA Ops:
  0.6 4.1 %take_band.2.refs_0_.own0 = bf16[6912,128]{1,0:T(8,128)(2,1)} custom-call(bf16[13824,128]{1,0:T(8,128)(2,1)} %bitcast.12), custom_call_target="tpu_custom_call" | custom-call | bytes 5308416 | tf_op jit(solution)/shard_map/take_band/pallas_call | solution.py:168
  4.7 0.5 collective-permute-start.1
  5.2 4.1 %take_band.3.own1 = bf16[6912,128]{1,0:T(8,128)(2,1)} custom-call(bf16[13824,128]{1,0:T(8,128)(2,1)} %bitcast.13, bf16[6912,128]{1,0:T(8,128)(2,1)} %take_band.2.refs_0_.own0), custom_call_target="tpu_custom_call" | custom-call | bytes 5308416 | tf_op jit(solution)/shard_map/take_band/pallas_call | solution.py:168
  9.3 2.7 %collective-permute-start = (bf16[6912,128]{1,0:T(8,128)(2,1)}, bf16[6912,128]{1,0:T(8,128)(2,1)}, u32[]{:S(2)}, u32[]{:S(2)}) collective-permute-start(bf16[6912,128]{1,0:T(8,128)(2,1)} %take_band.3.own1), channel_id=1, source_target_pairs={{31,0},{0,1},{1,2},{2,3},{3,4},{4,5},{5,6},{6,7},{7,8},{8,9},{9,10... | collective-permute-start | bytes 5308424 | tf_op jit(solution)/shard_map/ppermute | solution.py:570
  11.9 6.9 %padded_rows.1.own_u = bf16[2,96,96,128]{3,2,1,0:T(8,128)(2,1)} custom-call(bf16[6912,128]{1,0:T(8,128)(2,1)} %take_band.2.refs_0_.own0, bf16[6912,128]{1,0:T(8,128)(2,1)} %take_band.3.own1, bf16[2,256,256]{2,1,0:T(8,128)(2,1)} %constant.34.clone.sel.refs_6_.refs_8_), custom_call_target="tpu_custom_call" | custom-call | bytes 14155776 | tf_op jit(solution)/shard_map/padded_rows/pallas_call | solution.py:197
  18.9 12.8 %collective-permute-done.1.par = bf16[6912,128]{1,0:T(8,128)(2,1)} collective-permute-done((bf16[6912,128]{1,0:T(8,128)(2,1)}, bf16[6912,128]{1,0:T(8,128)(2,1)}, u32[]{:S(2)}, u32[]{:S(2)}) %collective-permute-start.1) | collective-permute-done | bytes 1769504 | tf_op jit(solution)/shard_map/ppermute | solution.py:570
  31.6 17.6 %pair_terms.2 = (f32[2,6912,128]{2,1,0:T(8,128)}, bf16[6912,128]{1,0:T(8,128)(2,1)}, f32[8,128]{1,0:T(8,128)}) custom-call(bf16[6912,128]{1,0:T(8,128)(2,1)} %take_band.2.refs_0_.own0, bf16[6912,128]{1,0:T(8,128)(2,1)} %take_band.3.own1, bf16[2,96,96,128]{3,2,1,0:T(8,128)(2,1)} %padded_rows.1.own_u, f32[4800,128]{1,0:T(8,128)} %constant.35.clone.kern, ...), custom_call_target="tpu_custom_call" | custom-call | flops 20000000000 | bytes 20000000 | tf_op jit(solution)/shard_map/pair_terms/pallas_call | solution.py:431
  49.3 0.2 collective-permute-start.2
  49.5 1.1 %collective-permute-done.par = bf16[6912,128]{1,0:T(8,128)(2,1)} collective-permute-done((bf16[6912,128]{1,0:T(8,128)(2,1)}, bf16[6912,128]{1,0:T(8,128)(2,1)}, u32[]{:S(2)}, u32[]{:S(2)}) %collective-permute-start) | collective-permute-done | bytes 1769504 | tf_op jit(solution)/shard_map/ppermute | solution.py:570
  50.6 19.3 %pair_terms.3 = (f32[2,6912,128]{2,1,0:T(8,128)}, bf16[4608,128]{1,0:T(8,128)(2,1)}, bf16[2304,128]{1,0:T(8,128)(2,1)}, f32[8,128]{1,0:T(8,128)}) custom-call(bf16[6912,128]{1,0:T(8,128)(2,1)} %take_band.2.refs_0_.own0, bf16[6912,128]{1,0:T(8,128)(2,1)} %take_band.3.own1, bf16[2,96,96,128]{3,2,1,0:T(8,128)(2,1)} %padded_rows.1.own_u, ...), custom_call_target="tpu_custom_call" | custom-call | flops 20000000000 | bytes 20000000 | tf_op jit(solution)/shard_map/pair_terms/pallas_call | solution.py:431
  69.9 1.4 %collective-permute-start.4 = (bf16[4608,128]{1,0:T(8,128)(2,1)}, bf16[4608,128]{1,0:T(8,128)(2,1)S(1)}, u32[]{:S(2)}, u32[]{:S(2)}) collective-permute-start(bf16[4608,128]{1,0:T(8,128)(2,1)} %get-tuple-element.21), channel_id=1, source_target_pairs={{1,0},{2,1},{3,2},{4,3},{5,4},{6,5},{7,6},{8,7},{9,8},{10,9},{11,1... | collective-permute-start | bytes 3538952 | tf_op jit(solution)/shard_map/ppermute | solution.py:570
  71.3 1.1 %collective-permute-start.3 = (bf16[2304,128]{1,0:T(8,128)(2,1)}, bf16[2304,128]{1,0:T(8,128)(2,1)S(1)}, u32[]{:S(2)}, u32[]{:S(2)}) collective-permute-start(bf16[2304,128]{1,0:T(8,128)(2,1)} %get-tuple-element.20), channel_id=1, source_target_pairs={{1,0},{2,1},{3,2},{4,3},{5,4},{6,5},{7,6},{8,7},{9,8},{10,9},{11,1... | collective-permute-start | bytes 1769480 | tf_op jit(solution)/shard_map/ppermute | solution.py:570
  72.3 0.0 collective-permute-start.5
  72.4 1.5 %collective-permute-done.5 = f32[8,128]{1,0:T(8,128)S(1)} collective-permute-done((f32[8,128]{1,0:T(8,128)}, f32[8,128]{1,0:T(8,128)S(1)}, u32[]{:S(2)}, u32[]{:S(2)}) %collective-permute-start.5) | collective-permute-done | bytes 4128 | tf_op jit(solution)/shard_map/ppermute | solution.py:601
  73.8 0.7 add.20
  74.5 0.0 collective-permute-start.6
  74.5 3.6 %collective-permute-done.6 = f32[8,128]{1,0:T(8,128)S(1)} collective-permute-done((f32[8,128]{1,0:T(8,128)S(1)}, f32[8,128]{1,0:T(8,128)S(1)}, u32[]{:S(2)}, u32[]{:S(2)}) %collective-permute-start.6) | collective-permute-done | bytes 4128 | tf_op jit(solution)/shard_map/ppermute | solution.py:607
  78.1 0.0 collective-permute-start.7
  78.1 3.6 %collective-permute-done.7 = f32[8,128]{1,0:T(8,128)S(1)} collective-permute-done((f32[8,128]{1,0:T(8,128)S(1)}, f32[8,128]{1,0:T(8,128)S(1)}, u32[]{:S(2)}, u32[]{:S(2)}) %collective-permute-start.7) | collective-permute-done | bytes 4128 | tf_op jit(solution)/shard_map/ppermute | solution.py:607
  81.7 0.0 collective-permute-start.8
  81.8 3.6 %collective-permute-done.8 = f32[8,128]{1,0:T(8,128)S(1)} collective-permute-done((f32[8,128]{1,0:T(8,128)S(1)}, f32[8,128]{1,0:T(8,128)S(1)}, u32[]{:S(2)}, u32[]{:S(2)}) %collective-permute-start.8) | collective-permute-done | bytes 4128 | tf_op jit(solution)/shard_map/ppermute | solution.py:607
  85.4 0.0 collective-permute-start.9
  85.4 0.0 collective-permute-done.4.back1
  85.4 0.0 collective-permute-done.2.back0
  85.4 5.9 %add_piece.2 = (f32[13824,128]{1,0:T(8,128)}, f32[2,2,8,128]{3,2,1,0:T(8,128)S(1)}) custom-call(bf16[6912,128]{1,0:T(8,128)(2,1)} %take_band.2.refs_0_.own0, bf16[6912,128]{1,0:T(8,128)(2,1)} %take_band.3.own1, f32[2,6912,128]{2,1,0:T(8,128)} %get-tuple-element.18.terms, bf16[6912,128]{1,0:T(8,128)(2,1)} %collective-permute-done.2.back0, ...), custom_call_target="tpu_custom_call" | custom-call | bytes 14155776 | tf_op jit(solution)/shard_map/add_piece/pallas_call | solution.py:540
  91.3 0.0 collective-permute-done.9
  91.4 0.2 collective-permute-start.10
  91.5 0.5 slice.6
  92.0 0.0 collective-permute-done.3.back1
  92.0 3.4 %add_piece.3 = (f32[13824,128]{1,0:T(8,128)}, f32[2,2]{1,0:T(2,128)}) custom-call(bf16[6912,128]{1,0:T(8,128)(2,1)} %take_band.2.refs_0_.own0, bf16[6912,128]{1,0:T(8,128)(2,1)} %take_band.3.own1, f32[2,6912,128]{2,1,0:T(8,128)} %get-tuple-element.18.terms, bf16[6912,128]{1,0:T(8,128)(2,1)} %collective-permute-done.2.back0, ...), custom_call_target="tpu_custom_call", output_to_operand_aliasing={{0}: (6, {})} | custom-call | bytes 7077888 | tf_op jit(solution)/shard_map/add_piece/pallas_call | solution.py:540
  95.5 0.0 collective-permute-done.10
  95.5 0.5 slice.7
  (4 shorter events, 0.0 us)
Async XLA Ops:
  4.7 26.9 %collective-permute-start.1 = (bf16[6912,128]{1,0:T(8,128)(2,1)}, bf16[6912,128]{1,0:T(8,128)(2,1)}, u32[]{:S(2)}, u32[]{:S(2)}) collective-permute-start(bf16[6912,128]{1,0:T(8,128)(2,1)} %take_band.2.refs_0_.own0), channel_id=1, source_target_pairs={{31,0},{0,1},{1,2},{2,3},{3,4},{4,5},{5,6},{6,7},{7,8},{8,9},{9,10... | collective-permute-start | bytes 5308424 | tf_op jit(solution)/shard_map/ppermute | solution.py:570
  9.3 41.3 %collective-permute-start = (bf16[6912,128]{1,0:T(8,128)(2,1)}, bf16[6912,128]{1,0:T(8,128)(2,1)}, u32[]{:S(2)}, u32[]{:S(2)}) collective-permute-start(bf16[6912,128]{1,0:T(8,128)(2,1)} %take_band.3.own1), channel_id=1, source_target_pairs={{31,0},{0,1},{1,2},{2,3},{3,4},{4,5},{5,6},{6,7},{7,8},{8,9},{9,10... | collective-permute-start | bytes 5308424 | tf_op jit(solution)/shard_map/ppermute | solution.py:570
  49.3 36.1 %collective-permute-start.2 = (bf16[6912,128]{1,0:T(8,128)(2,1)}, bf16[6912,128]{1,0:T(8,128)(2,1)}, u32[]{:S(2)}, u32[]{:S(2)}) collective-permute-start(bf16[6912,128]{1,0:T(8,128)(2,1)} %get-tuple-element.19), channel_id=1, source_target_pairs={{1,0},{2,1},{3,2},{4,3},{5,4},{6,5},{7,6},{8,7},{9,8},{10,9},{11,1... | collective-permute-start | bytes 5308424 | tf_op jit(solution)/shard_map/ppermute | solution.py:570
  69.9 15.5 %collective-permute-start.4 = (bf16[4608,128]{1,0:T(8,128)(2,1)}, bf16[4608,128]{1,0:T(8,128)(2,1)S(1)}, u32[]{:S(2)}, u32[]{:S(2)}) collective-permute-start(bf16[4608,128]{1,0:T(8,128)(2,1)} %get-tuple-element.21), channel_id=1, source_target_pairs={{1,0},{2,1},{3,2},{4,3},{5,4},{6,5},{7,6},{8,7},{9,8},{10,9},{11,1... | collective-permute-start | bytes 3538952 | tf_op jit(solution)/shard_map/ppermute | solution.py:570
  71.3 20.8 %collective-permute-start.3 = (bf16[2304,128]{1,0:T(8,128)(2,1)}, bf16[2304,128]{1,0:T(8,128)(2,1)S(1)}, u32[]{:S(2)}, u32[]{:S(2)}) collective-permute-start(bf16[2304,128]{1,0:T(8,128)(2,1)} %get-tuple-element.20), channel_id=1, source_target_pairs={{1,0},{2,1},{3,2},{4,3},{5,4},{6,5},{7,6},{8,7},{9,8},{10,9},{11,1... | collective-permute-start | bytes 1769480 | tf_op jit(solution)/shard_map/ppermute | solution.py:570
  72.3 1.5 %collective-permute-start.5 = (f32[8,128]{1,0:T(8,128)}, f32[8,128]{1,0:T(8,128)S(1)}, u32[]{:S(2)}, u32[]{:S(2)}) collective-permute-start(f32[8,128]{1,0:T(8,128)} %get-tuple-element.26), channel_id=1, source_target_pairs={{0,1},{1,0},{2,3},{3,2},{4,5},{5,4},{6,7},{7,6},{8,9},{9,8},{10,11... | collective-permute-start | bytes 12296 | tf_op jit(solution)/shard_map/ppermute | solution.py:601
  74.5 3.6 %collective-permute-start.6 = (f32[8,128]{1,0:T(8,128)S(1)}, f32[8,128]{1,0:T(8,128)S(1)}, u32[]{:S(2)}, u32[]{:S(2)}) collective-permute-start(f32[8,128]{1,0:T(8,128)S(1)} %add.20), channel_id=1, source_target_pairs={{0,4},{1,5},{2,10},{3,7},{4,0},{5,1},{6,14},{7,3},{8,12},{9,13},{1... | collective-permute-start | bytes 12296 | tf_op jit(solution)/shard_map/ppermute | solution.py:607
  78.1 3.6 %collective-permute-start.7 = (f32[8,128]{1,0:T(8,128)S(1)}, f32[8,128]{1,0:T(8,128)S(1)}, u32[]{:S(2)}, u32[]{:S(2)}) collective-permute-start(f32[8,128]{1,0:T(8,128)S(1)} %add.21), channel_id=1, source_target_pairs={{0,4},{1,9},{2,10},{3,11},{4,0},{5,13},{6,14},{7,15},{8,12},{9,1},... | collective-permute-start | bytes 12296 | tf_op jit(solution)/shard_map/ppermute | solution.py:607
  81.7 3.6 %collective-permute-start.8 = (f32[8,128]{1,0:T(8,128)S(1)}, f32[8,128]{1,0:T(8,128)S(1)}, u32[]{:S(2)}, u32[]{:S(2)}) collective-permute-start(f32[8,128]{1,0:T(8,128)S(1)} %add.22), channel_id=1, source_target_pairs={{0,4},{1,17},{2,10},{3,19},{4,0},{5,21},{6,14},{7,23},{8,12},{9,25... | collective-permute-start | bytes 12296 | tf_op jit(solution)/shard_map/ppermute | solution.py:607
  85.4 6.0 %collective-permute-start.9 = (f32[8,128]{1,0:T(8,128)S(1)}, f32[8,128]{1,0:T(8,128)S(1)}, u32[]{:S(2)}, u32[]{:S(2)}) collective-permute-start(f32[8,128]{1,0:T(8,128)S(1)} %add.23), channel_id=1, source_target_pairs={{0,4},{1,3},{2,10},{3,1},{4,0},{5,7},{6,14},{7,5},{8,12},{9,11},{1... | collective-permute-start | bytes 12296 | tf_op jit(solution)/shard_map/ppermute | solution.py:616
  91.4 4.1 %collective-permute-start.10 = (f32[8,128]{1,0:T(8,128)S(1)}, f32[8,128]{1,0:T(8,128)S(1)}, u32[]{:S(2)}, u32[]{:S(2)}) collective-permute-start(f32[8,128]{1,0:T(8,128)S(1)} %add.24), channel_id=1, source_target_pairs={{0,1},{1,0},{2,3},{3,2},{4,5},{5,4},{6,7},{7,6},{8,9},{9,8},{10,11... | collective-permute-start | bytes 12296 | tf_op jit(solution)/shard_map/ppermute | solution.py:614

commit v14 on v13

--- a/solution.py
+++ b/solution.py
@@ -156,9 +156,11 @@
     pick = jnp.where(column == 2 * row + p, F32(1.0), F32(0.0)).astype(BF16)
     for c, load in enumerate(loads):
         load.wait()
-        for row in range(c * rows, (c + 1) * rows, LANES):
-            value = dot(pick, raw_v[2 * row : 2 * row + 2 * LANES, :])
-            out_v[row : row + LANES, :] = value.astype(BF16)
+        for row in range(c * rows, (c + 1) * rows, 2 * LANES):
+            blocks = [raw_v[2 * at : 2 * at + 2 * LANES, :] for at in (row, row + LANES)]
+            value = dot(pick, lanes(*blocks)).astype(BF16)
+            out_v[row : row + LANES, :] = value[:, :LANES]
+            out_v[row + LANES : row + 2 * LANES, :] = value[:, LANES:]
         copy_rows(out_v, c * rows, out, c * rows, rows, store_sem).start()
     pltpu.make_async_copy(out_v, out, store_sem).wait()
 
@@ -248,7 +250,7 @@
         widen_planes(par_v.at[pl.ds(i * ROWS // 2, ROWS // 2), :], par_f, i * G // 2)
     table_loads[6].wait()
 
-    @pl.loop(0, QUADS // 4, unroll=3)
+    @pl.loop(0, QUADS // 4, unroll=6)
     def _(q):
         split_rows(par_f, sel, par_u, 4 * q, 4)
 
@@ -259,7 +261,7 @@
     table_loads[5].start()
     table_loads[0].wait()
 
-    @pl.loop(0, G // 2, unroll=16)
+    @pl.loop(0, G // 2, unroll=24)
     def _(i):
         density = []
         for e in range(2):
@@ -274,7 +276,7 @@
 
     table_loads[1].wait()
 
-    @pl.loop(0, KPAD // 2, unroll=5)
+    @pl.loop(0, KPAD // 2, unroll=25)
     def _(pair):
         def line(k1, part):
             first = part * HALF + k1
@@ -297,7 +299,7 @@
 
     many = 5
 
-    @pl.loop(0, KPAD // many, unroll=5)
+    @pl.loop(0, KPAD // many, unroll=10)
     def _(m):
         at = pl.ds(pl.multiple_of(m * many * G, 16), many * G)
         factor = kern_v[at, :]
@@ -314,7 +316,7 @@
 
     table_loads[3].wait()
 
-    @pl.loop(0, G // 4, unroll=12)
+    @pl.loop(0, G // 4, unroll=24)
     def _(four):
         parts = []
         for e in range(4):
@@ -337,7 +339,7 @@
         load.start()
     table_loads[4].wait()
 
-    @pl.loop(0, G // 4, unroll=12)
+    @pl.loop(0, G // 4, unroll=24)
     def _(four):
         parts = []
         for e in range(4):
@@ -402,7 +404,7 @@
     first = 0
     for i, steps in enumerate(pieces):
 
-        @pl.loop(0, steps, unroll=2 if steps % 2 == 0 else steps)
+        @pl.loop(0, steps, unroll=3 if steps % 3 == 0 else 2)
         def _(step):
             ch = first + step
             result(ch)

time: 98.7 us -> 97.1 us (0.984)
  Pallas kernels: 61.3 us -> 57.4 us
  waiting for transfers between devices: 26.2 us -> 28.3 us
    pallas_call x2, Pallas kernels: 36.9 us -> 33.4 us  [pair_terms(): pl.pallas_call(functools.partial(pairs_kernel, pieces, share), out_shape=...]
    ppermute x5, waiting for transfers between devices: 13.9 us -> 15.9 us  [from_behind(): lax.ppermute(block, axis, [((i - distance) % size, i) for i in range(size)])]
  transfers between devices with their start and end apart: 11 -> 11, of which waited for: 6 -> 6; matrix products, arithmetic and copies ran while one was open for 1% -> 1% of each run, Pallas kernels for 58% -> 55%
where the time goes in v14:
time: 97.1 us; the launch traced here: 96.8 us
  Pallas kernels  57.4 us (59%)
  waiting for transfers between devices  28.3 us (29%)
  starting transfers between devices  6.06 us (6%)
  between operations  3.16 us (3%)
  local copies, waits for them, and re-layouts  1.06 us (1%)
    pallas_call x2, Pallas kernels, pair_terms(): pl.pallas_call(functools.partial(pairs_kernel, pieces, share), out_shape=...  33.4 us
    ppermute x5, waiting for transfers between devices, from_behind(): lax.ppermute(block, axis, [((i - distance) % size, i) for i in range(size)])  15.9 us
    ppermute x3, waiting for transfers between devices, per_device(): energy = energy + lax.ppermute(energy, 'band', steps.pop(0))  10.8 us
    pallas_call x2, Pallas kernels, add_piece(): pl.pallas_call(functools.partial(piece_kernel, first, size), out_shape=(j...  9.39 us
    pallas_call x2, Pallas kernels, take_band(): pl.pallas_call(functools.partial(band_kernel, p), out_shape=jax.ShapeDtyp...  7.67 us
    pallas_call x1, Pallas kernels, padded_rows(): pl.pallas_call(rows_kernel, out_shape=jax.ShapeDtypeStruct((2, G, G, LANE...  6.94 us
    ppermute x5, starting transfers between devices, from_behind(): lax.ppermute(block, axis, [((i - distance) % size, i) for i in range(size)])  5.98 us
  transfers between devices with their start and end apart: 11, of which 6 were waited for; matrix products, arithmetic and copies ran while one was open for 1% of the time, Pallas kernels for 55%

profile of v14, /device:TPU:0, one launch (start us, length us, event | category | flops | bytes accessed | tf_op | source)
XLA Modules:
  0.0 96.8 jit_solution(2433958888982021960)
XLA Ops:
  0.6 3.8 %take_band.2.refs_0_.own0 = bf16[6912,128]{1,0:T(8,128)(2,1)} custom-call(bf16[13824,128]{1,0:T(8,128)(2,1)} %bitcast.12), custom_call_target="tpu_custom_call" | custom-call | bytes 5308416 | tf_op jit(solution)/shard_map/take_band/pallas_call | solution.py:170
  4.5 0.5 collective-permute-start.1
  5.0 3.8 %take_band.3.own1 = bf16[6912,128]{1,0:T(8,128)(2,1)} custom-call(bf16[13824,128]{1,0:T(8,128)(2,1)} %bitcast.13, bf16[6912,128]{1,0:T(8,128)(2,1)} %take_band.2.refs_0_.own0), custom_call_target="tpu_custom_call" | custom-call | bytes 5308416 | tf_op jit(solution)/shard_map/take_band/pallas_call | solution.py:170
  8.8 2.8 %collective-permute-start = (bf16[6912,128]{1,0:T(8,128)(2,1)}, bf16[6912,128]{1,0:T(8,128)(2,1)}, u32[]{:S(2)}, u32[]{:S(2)}) collective-permute-start(bf16[6912,128]{1,0:T(8,128)(2,1)} %take_band.3.own1), channel_id=1, source_target_pairs={{31,0},{0,1},{1,2},{2,3},{3,4},{4,5},{5,6},{6,7},{7,8},{8,9},{9,10... | collective-permute-start | bytes 5308424 | tf_op jit(solution)/shard_map/ppermute | solution.py:572
  11.7 6.9 %padded_rows.1.own_u = bf16[2,96,96,128]{3,2,1,0:T(8,128)(2,1)} custom-call(bf16[6912,128]{1,0:T(8,128)(2,1)} %take_band.2.refs_0_.own0, bf16[6912,128]{1,0:T(8,128)(2,1)} %take_band.3.own1, bf16[2,256,256]{2,1,0:T(8,128)(2,1)} %constant.34.clone.sel.refs_6_.refs_8_), custom_call_target="tpu_custom_call" | custom-call | bytes 14155776 | tf_op jit(solution)/shard_map/padded_rows/pallas_call | solution.py:199
  18.6 12.8 %collective-permute-done.1.par = bf16[6912,128]{1,0:T(8,128)(2,1)} collective-permute-done((bf16[6912,128]{1,0:T(8,128)(2,1)}, bf16[6912,128]{1,0:T(8,128)(2,1)}, u32[]{:S(2)}, u32[]{:S(2)}) %collective-permute-start.1) | collective-permute-done | bytes 1769504 | tf_op jit(solution)/shard_map/ppermute | solution.py:572
  31.4 15.7 %pair_terms.2 = (f32[2,6912,128]{2,1,0:T(8,128)}, bf16[6912,128]{1,0:T(8,128)(2,1)}, f32[8,128]{1,0:T(8,128)}) custom-call(bf16[6912,128]{1,0:T(8,128)(2,1)} %take_band.2.refs_0_.own0, bf16[6912,128]{1,0:T(8,128)(2,1)} %take_band.3.own1, bf16[2,96,96,128]{3,2,1,0:T(8,128)(2,1)} %padded_rows.1.own_u, f32[4800,128]{1,0:T(8,128)} %constant.35.clone.kern, ...), custom_call_target="tpu_custom_call" | custom-call | flops 20000000000 | bytes 20000000 | tf_op jit(solution)/shard_map/pair_terms/pallas_call | solution.py:433
  47.1 0.3 collective-permute-start.2
  47.4 3.1 %collective-permute-done.par = bf16[6912,128]{1,0:T(8,128)(2,1)} collective-permute-done((bf16[6912,128]{1,0:T(8,128)(2,1)}, bf16[6912,128]{1,0:T(8,128)(2,1)}, u32[]{:S(2)}, u32[]{:S(2)}) %collective-permute-start) | collective-permute-done | bytes 1769504 | tf_op jit(solution)/shard_map/ppermute | solution.py:572
  50.5 17.8 %pair_terms.3 = (f32[2,6912,128]{2,1,0:T(8,128)}, bf16[4608,128]{1,0:T(8,128)(2,1)}, bf16[2304,128]{1,0:T(8,128)(2,1)}, f32[8,128]{1,0:T(8,128)}) custom-call(bf16[6912,128]{1,0:T(8,128)(2,1)} %take_band.2.refs_0_.own0, bf16[6912,128]{1,0:T(8,128)(2,1)} %take_band.3.own1, bf16[2,96,96,128]{3,2,1,0:T(8,128)(2,1)} %padded_rows.1.own_u, ...), custom_call_target="tpu_custom_call" | custom-call | flops 20000000000 | bytes 20000000 | tf_op jit(solution)/shard_map/pair_terms/pallas_call | solution.py:433
  68.3 0.1 collective-permute-start.4
  68.3 2.3 %collective-permute-start.3 = (bf16[2304,128]{1,0:T(8,128)(2,1)}, bf16[2304,128]{1,0:T(8,128)(2,1)S(1)}, u32[]{:S(2)}, u32[]{:S(2)}) collective-permute-start(bf16[2304,128]{1,0:T(8,128)(2,1)} %get-tuple-element.20), channel_id=1, source_target_pairs={{1,0},{2,1},{3,2},{4,3},{5,4},{6,5},{7,6},{8,7},{9,8},{10,9},{11,1... | collective-permute-start | bytes 1769480 | tf_op jit(solution)/shard_map/ppermute | solution.py:572
  70.6 0.0 collective-permute-start.5
  70.6 1.6 %collective-permute-done.5 = f32[8,128]{1,0:T(8,128)S(1)} collective-permute-done((f32[8,128]{1,0:T(8,128)}, f32[8,128]{1,0:T(8,128)S(1)}, u32[]{:S(2)}, u32[]{:S(2)}) %collective-permute-start.5) | collective-permute-done | bytes 4128 | tf_op jit(solution)/shard_map/ppermute | solution.py:603
  72.2 0.7 add.20
  72.9 0.0 collective-permute-start.6
  72.9 3.6 %collective-permute-done.6 = f32[8,128]{1,0:T(8,128)S(1)} collective-permute-done((f32[8,128]{1,0:T(8,128)S(1)}, f32[8,128]{1,0:T(8,128)S(1)}, u32[]{:S(2)}, u32[]{:S(2)}) %collective-permute-start.6) | collective-permute-done | bytes 4128 | tf_op jit(solution)/shard_map/ppermute | solution.py:609
  76.5 0.0 collective-permute-start.7
  76.5 3.6 %collective-permute-done.7 = f32[8,128]{1,0:T(8,128)S(1)} collective-permute-done((f32[8,128]{1,0:T(8,128)S(1)}, f32[8,128]{1,0:T(8,128)S(1)}, u32[]{:S(2)}, u32[]{:S(2)}) %collective-permute-start.7) | collective-permute-done | bytes 4128 | tf_op jit(solution)/shard_map/ppermute | solution.py:609
  80.1 0.0 collective-permute-start.8
  80.1 3.6 %collective-permute-done.8 = f32[8,128]{1,0:T(8,128)S(1)} collective-permute-done((f32[8,128]{1,0:T(8,128)S(1)}, f32[8,128]{1,0:T(8,128)S(1)}, u32[]{:S(2)}, u32[]{:S(2)}) %collective-permute-start.8) | collective-permute-done | bytes 4128 | tf_op jit(solution)/shard_map/ppermute | solution.py:609
  83.7 0.0 collective-permute-start.9
  83.7 0.0 collective-permute-done.4.back1
  83.8 0.0 collective-permute-done.2.back0
  83.8 5.9 %add_piece.2 = (f32[13824,128]{1,0:T(8,128)}, f32[2,2,8,128]{3,2,1,0:T(8,128)S(1)}) custom-call(bf16[6912,128]{1,0:T(8,128)(2,1)} %take_band.2.refs_0_.own0, bf16[6912,128]{1,0:T(8,128)(2,1)} %take_band.3.own1, f32[2,6912,128]{2,1,0:T(8,128)} %get-tuple-element.18.terms, bf16[6912,128]{1,0:T(8,128)(2,1)} %collective-permute-done.2.back0, ...), custom_call_target="tpu_custom_call" | custom-call | bytes 14155776 | tf_op jit(solution)/shard_map/add_piece/pallas_call | solution.py:542
  89.7 0.0 collective-permute-done.9
  89.7 0.1 collective-permute-start.10
  89.8 0.5 slice.6
  90.3 0.0 collective-permute-done.3.back1
  90.3 3.4 %add_piece.3 = (f32[13824,128]{1,0:T(8,128)}, f32[2,2]{1,0:T(2,128)}) custom-call(bf16[6912,128]{1,0:T(8,128)(2,1)} %take_band.2.refs_0_.own0, bf16[6912,128]{1,0:T(8,128)(2,1)} %take_band.3.own1, f32[2,6912,128]{2,1,0:T(8,128)} %get-tuple-element.18.terms, bf16[6912,128]{1,0:T(8,128)(2,1)} %collective-permute-done.2.back0, ...), custom_call_target="tpu_custom_call", output_to_operand_aliasing={{0}: (6, {})} | custom-call | bytes 7077888 | tf_op jit(solution)/shard_map/add_piece/pallas_call | solution.py:542
  93.8 0.0 collective-permute-done.10
  93.8 0.5 slice.7
  (4 shorter events, 0.0 us)
Async XLA Ops:
  4.5 27.0 %collective-permute-start.1 = (bf16[6912,128]{1,0:T(8,128)(2,1)}, bf16[6912,128]{1,0:T(8,128)(2,1)}, u32[]{:S(2)}, u32[]{:S(2)}) collective-permute-start(bf16[6912,128]{1,0:T(8,128)(2,1)} %take_band.2.refs_0_.own0), channel_id=1, source_target_pairs={{31,0},{0,1},{1,2},{2,3},{3,4},{4,5},{5,6},{6,7},{7,8},{8,9},{9,10... | collective-permute-start | bytes 5308424 | tf_op jit(solution)/shard_map/ppermute | solution.py:572
  8.8 41.7 %collective-permute-start = (bf16[6912,128]{1,0:T(8,128)(2,1)}, bf16[6912,128]{1,0:T(8,128)(2,1)}, u32[]{:S(2)}, u32[]{:S(2)}) collective-permute-start(bf16[6912,128]{1,0:T(8,128)(2,1)} %take_band.3.own1), channel_id=1, source_target_pairs={{31,0},{0,1},{1,2},{2,3},{3,4},{4,5},{5,6},{6,7},{7,8},{8,9},{9,10... | collective-permute-start | bytes 5308424 | tf_op jit(solution)/shard_map/ppermute | solution.py:572
  47.1 36.6 %collective-permute-start.2 = (bf16[6912,128]{1,0:T(8,128)(2,1)}, bf16[6912,128]{1,0:T(8,128)(2,1)}, u32[]{:S(2)}, u32[]{:S(2)}) collective-permute-start(bf16[6912,128]{1,0:T(8,128)(2,1)} %get-tuple-element.19), channel_id=1, source_target_pairs={{1,0},{2,1},{3,2},{4,3},{5,4},{6,5},{7,6},{8,7},{9,8},{10,9},{11,1... | collective-permute-start | bytes 5308424 | tf_op jit(solution)/shard_map/ppermute | solution.py:572
  68.3 15.5 %collective-permute-start.4 = (bf16[4608,128]{1,0:T(8,128)(2,1)}, bf16[4608,128]{1,0:T(8,128)(2,1)S(1)}, u32[]{:S(2)}, u32[]{:S(2)}) collective-permute-start(bf16[4608,128]{1,0:T(8,128)(2,1)} %get-tuple-element.21), channel_id=1, source_target_pairs={{1,0},{2,1},{3,2},{4,3},{5,4},{6,5},{7,6},{8,7},{9,8},{10,9},{11,1... | collective-permute-start | bytes 3538952 | tf_op jit(solution)/shard_map/ppermute | solution.py:572
  68.3 22.0 %collective-permute-start.3 = (bf16[2304,128]{1,0:T(8,128)(2,1)}, bf16[2304,128]{1,0:T(8,128)(2,1)S(1)}, u32[]{:S(2)}, u32[]{:S(2)}) collective-permute-start(bf16[2304,128]{1,0:T(8,128)(2,1)} %get-tuple-element.20), channel_id=1, source_target_pairs={{1,0},{2,1},{3,2},{4,3},{5,4},{6,5},{7,6},{8,7},{9,8},{10,9},{11,1... | collective-permute-start | bytes 1769480 | tf_op jit(solution)/shard_map/ppermute | solution.py:572
  70.6 1.6 %collective-permute-start.5 = (f32[8,128]{1,0:T(8,128)}, f32[8,128]{1,0:T(8,128)S(1)}, u32[]{:S(2)}, u32[]{:S(2)}) collective-permute-start(f32[8,128]{1,0:T(8,128)} %get-tuple-element.26), channel_id=1, source_target_pairs={{0,1},{1,0},{2,3},{3,2},{4,5},{5,4},{6,7},{7,6},{8,9},{9,8},{10,11... | collective-permute-start | bytes 12296 | tf_op jit(solution)/shard_map/ppermute | solution.py:603
  72.9 3.6 %collective-permute-start.6 = (f32[8,128]{1,0:T(8,128)S(1)}, f32[8,128]{1,0:T(8,128)S(1)}, u32[]{:S(2)}, u32[]{:S(2)}) collective-permute-start(f32[8,128]{1,0:T(8,128)S(1)} %add.20), channel_id=1, source_target_pairs={{0,4},{1,5},{2,10},{3,7},{4,0},{5,1},{6,14},{7,3},{8,12},{9,13},{1... | collective-permute-start | bytes 12296 | tf_op jit(solution)/shard_map/ppermute | solution.py:609
  76.5 3.6 %collective-permute-start.7 = (f32[8,128]{1,0:T(8,128)S(1)}, f32[8,128]{1,0:T(8,128)S(1)}, u32[]{:S(2)}, u32[]{:S(2)}) collective-permute-start(f32[8,128]{1,0:T(8,128)S(1)} %add.21), channel_id=1, source_target_pairs={{0,4},{1,9},{2,10},{3,11},{4,0},{5,13},{6,14},{7,15},{8,12},{9,1},... | collective-permute-start | bytes 12296 | tf_op jit(solution)/shard_map/ppermute | solution.py:609
  80.1 3.6 %collective-permute-start.8 = (f32[8,128]{1,0:T(8,128)S(1)}, f32[8,128]{1,0:T(8,128)S(1)}, u32[]{:S(2)}, u32[]{:S(2)}) collective-permute-start(f32[8,128]{1,0:T(8,128)S(1)} %add.22), channel_id=1, source_target_pairs={{0,4},{1,17},{2,10},{3,19},{4,0},{5,21},{6,14},{7,23},{8,12},{9,25... | collective-permute-start | bytes 12296 | tf_op jit(solution)/shard_map/ppermute | solution.py:609
  83.7 6.0 %collective-permute-start.9 = (f32[8,128]{1,0:T(8,128)S(1)}, f32[8,128]{1,0:T(8,128)S(1)}, u32[]{:S(2)}, u32[]{:S(2)}) collective-permute-start(f32[8,128]{1,0:T(8,128)S(1)} %add.23), channel_id=1, source_target_pairs={{0,4},{1,3},{2,10},{3,1},{4,0},{5,7},{6,14},{7,5},{8,12},{9,11},{1... | collective-permute-start | bytes 12296 | tf_op jit(solution)/shard_map/ppermute | solution.py:618
  89.7 4.1 %collective-permute-start.10 = (f32[8,128]{1,0:T(8,128)S(1)}, f32[8,128]{1,0:T(8,128)S(1)}, u32[]{:S(2)}, u32[]{:S(2)}) collective-permute-start(f32[8,128]{1,0:T(8,128)S(1)} %add.24), channel_id=1, source_target_pairs={{0,1},{1,0},{2,3},{3,2},{4,5},{5,4},{6,7},{7,6},{8,9},{9,8},{10,11... | collective-permute-start | bytes 12296 | tf_op jit(solution)/shard_map/ppermute | solution.py:616

commit v15 on v14

--- a/solution.py
+++ b/solution.py
@@ -26,7 +26,7 @@
 PLANES = 16
 STEP_ROWS = PLANES * PLANE
 STEPS = G // PLANES
-PIECES = (4, 2)
+PIECES = (3, 2, 1)
 WAVE_UNIT = 0.05
 SCREEN_SQ = 0.0121
 MIB = 1024 * 1024
@@ -404,7 +404,7 @@
     first = 0
     for i, steps in enumerate(pieces):
 
-        @pl.loop(0, steps, unroll=3 if steps % 3 == 0 else 2)
+        @pl.loop(0, steps, unroll=min(steps, 3))
         def _(step):
             ch = first + step
             result(ch)

time: 97.1 us -> 97.3 us (level)
  waiting for transfers between devices: 28.3 us -> 24.4 us
  starting transfers between devices: 6.06 us -> 8.64 us
  Pallas kernels: 57.4 us -> 59 us
    ppermute x3 -> x2, waiting for transfers between devices: 10.8 us -> 7.21 us  [per_device(): energy = energy + lax.ppermute(energy, 'band', steps.pop(0))]
    ppermute x1 -> x2, starting transfers between devices: 0.01 us -> 2.08 us  [per_device(): got = lax.ppermute(energy, 'band', steps.pop(0))]
    pallas_call x2 -> x3, Pallas kernels: 9.39 us -> 11.2 us  [add_piece(): pl.pallas_call(functools.partial(piece_kernel, first, size), out_shape=(j...]
    ppermute x5 -> x6, starting transfers between devices: 5.98 us -> 6.04 us  [from_behind(): lax.ppermute(block, axis, [((i - distance) % size, i) for i in range(size)])]
    ppermute x5 -> x6, waiting for transfers between devices: 15.9 us -> 15.9 us  [from_behind(): lax.ppermute(block, axis, [((i - distance) % size, i) for i in range(size)])]
  transfers between devices with their start and end apart: 11 -> 12, of which waited for: 6 -> 5; matrix products, arithmetic and copies ran while one was open for 1% -> 1% of each run, Pallas kernels for 55% -> 57%
where the time goes in v15:
time: 97.3 us; the launch traced here: 97 us
  Pallas kernels  59 us (61%)
  waiting for transfers between devices  24.4 us (25%)
  starting transfers between devices  8.64 us (9%)
  between operations  3.19 us (3%)
  local copies, waits for them, and re-layouts  1.05 us (1%)
    pallas_call x2, Pallas kernels, pair_terms(): pl.pallas_call(functools.partial(pairs_kernel, pieces, share), out_shape=...  33.2 us
    ppermute x6, waiting for transfers between devices, from_behind(): lax.ppermute(block, axis, [((i - distance) % size, i) for i in range(size)])  15.9 us
    pallas_call x3, Pallas kernels, add_piece(): pl.pallas_call(functools.partial(piece_kernel, first, size), out_shape=(j...  11.2 us
    pallas_call x2, Pallas kernels, take_band(): pl.pallas_call(functools.partial(band_kernel, p), out_shape=jax.ShapeDtyp...  7.66 us
    ppermute x2, waiting for transfers between devices, per_device(): energy = energy + lax.ppermute(energy, 'band', steps.pop(0))  7.21 us
    pallas_call x1, Pallas kernels, padded_rows(): pl.pallas_call(rows_kernel, out_shape=jax.ShapeDtypeStruct((2, G, G, LANE...  6.95 us
    ppermute x6, starting transfers between devices, from_behind(): lax.ppermute(block, axis, [((i - distance) % size, i) for i in range(size)])  6.04 us
    ppermute x2, starting transfers between devices, per_device(): got = lax.ppermute(energy, 'band', steps.pop(0))  2.08 us
  transfers between devices with their start and end apart: 12, of which 5 were waited for; matrix products, arithmetic and copies ran while one was open for 1% of the time, Pallas kernels for 57%

profile of v15, /device:TPU:0, one launch (start us, length us, event | category | flops | bytes accessed | tf_op | source)
XLA Modules:
  0.0 97.0 jit_solution(15055947864079266028)
XLA Ops:
  0.6 3.8 %take_band.2.refs_0_.own0 = bf16[6912,128]{1,0:T(8,128)(2,1)} custom-call(bf16[13824,128]{1,0:T(8,128)(2,1)} %bitcast.13), custom_call_target="tpu_custom_call" | custom-call | bytes 5308416 | tf_op jit(solution)/shard_map/take_band/pallas_call | solution.py:170
  4.5 0.5 collective-permute-start.1
  5.0 3.8 %take_band.3.own1 = bf16[6912,128]{1,0:T(8,128)(2,1)} custom-call(bf16[13824,128]{1,0:T(8,128)(2,1)} %bitcast.14, bf16[6912,128]{1,0:T(8,128)(2,1)} %take_band.2.refs_0_.own0), custom_call_target="tpu_custom_call" | custom-call | bytes 5308416 | tf_op jit(solution)/shard_map/take_band/pallas_call | solution.py:170
  8.8 2.8 %collective-permute-start = (bf16[6912,128]{1,0:T(8,128)(2,1)}, bf16[6912,128]{1,0:T(8,128)(2,1)}, u32[]{:S(2)}, u32[]{:S(2)}) collective-permute-start(bf16[6912,128]{1,0:T(8,128)(2,1)} %take_band.3.own1), channel_id=1, source_target_pairs={{31,0},{0,1},{1,2},{2,3},{3,4},{4,5},{5,6},{6,7},{7,8},{8,9},{9,10... | collective-permute-start | bytes 5308424 | tf_op jit(solution)/shard_map/ppermute | solution.py:572
  11.6 6.9 %padded_rows.1.own_u = bf16[2,96,96,128]{3,2,1,0:T(8,128)(2,1)} custom-call(bf16[6912,128]{1,0:T(8,128)(2,1)} %take_band.2.refs_0_.own0, bf16[6912,128]{1,0:T(8,128)(2,1)} %take_band.3.own1, bf16[2,256,256]{2,1,0:T(8,128)(2,1)} %constant.34.clone.sel.refs_6_.refs_8_), custom_call_target="tpu_custom_call" | custom-call | bytes 14155776 | tf_op jit(solution)/shard_map/padded_rows/pallas_call | solution.py:199
  18.6 12.8 %collective-permute-done.1.par = bf16[6912,128]{1,0:T(8,128)(2,1)} collective-permute-done((bf16[6912,128]{1,0:T(8,128)(2,1)}, bf16[6912,128]{1,0:T(8,128)(2,1)}, u32[]{:S(2)}, u32[]{:S(2)}) %collective-permute-start.1) | collective-permute-done | bytes 1769504 | tf_op jit(solution)/shard_map/ppermute | solution.py:572
  31.4 15.7 %pair_terms.2 = (f32[2,6912,128]{2,1,0:T(8,128)}, bf16[6912,128]{1,0:T(8,128)(2,1)}, f32[8,128]{1,0:T(8,128)}) custom-call(bf16[6912,128]{1,0:T(8,128)(2,1)} %take_band.2.refs_0_.own0, bf16[6912,128]{1,0:T(8,128)(2,1)} %take_band.3.own1, bf16[2,96,96,128]{3,2,1,0:T(8,128)(2,1)} %padded_rows.1.own_u, f32[4800,128]{1,0:T(8,128)} %constant.35.clone.kern, ...), custom_call_target="tpu_custom_call" | custom-call | flops 20000000000 | bytes 20000000 | tf_op jit(solution)/shard_map/pair_terms/pallas_call | solution.py:433
  47.1 0.3 collective-permute-start.2
  47.4 3.1 %collective-permute-done.par = bf16[6912,128]{1,0:T(8,128)(2,1)} collective-permute-done((bf16[6912,128]{1,0:T(8,128)(2,1)}, bf16[6912,128]{1,0:T(8,128)(2,1)}, u32[]{:S(2)}, u32[]{:S(2)}) %collective-permute-start) | collective-permute-done | bytes 1769504 | tf_op jit(solution)/shard_map/ppermute | solution.py:572
  50.5 17.5 %pair_terms.3 = (f32[2,6912,128]{2,1,0:T(8,128)}, bf16[3456,128]{1,0:T(8,128)(2,1)}, bf16[2304,128]{1,0:T(8,128)(2,1)}, bf16[1152,128]{1,0:T(8,128)(2,1)}, f32[8,128]{1,0:T(8,128)}) custom-call(bf16[6912,128]{1,0:T(8,128)(2,1)} %take_band.2.refs_0_.own0, bf16[6912,128]{1,0:T(8,128)(2,1)} %take_band.3.own1, bf16[2,96,96,128]{3,2,1,0:T(8,128)(2,1)} %padded_rows.1.own_u, ...), custom_call_target="tpu_custom_call" | custom-call | flops 20000000000 | bytes 20000000 | tf_op jit(solution)/shard_map/pair_terms/pallas_call | solution.py:433
  68.0 0.1 collective-permute-start.4
  68.1 2.3 %collective-permute-start.5 = (bf16[2304,128]{1,0:T(8,128)(2,1)}, bf16[2304,128]{1,0:T(8,128)(2,1)S(1)}, u32[]{:S(2)}, u32[]{:S(2)}) collective-permute-start(bf16[2304,128]{1,0:T(8,128)(2,1)} %get-tuple-element.27), channel_id=1, source_target_pairs={{1,0},{2,1},{3,2},{4,3},{5,4},{6,5},{7,6},{8,7},{9,8},{10,9},{11,1... | collective-permute-start | bytes 1769480 | tf_op jit(solution)/shard_map/ppermute | solution.py:572
  70.4 0.1 collective-permute-start.3
  70.5 0.4 collective-permute-start.6
  70.9 1.3 %collective-permute-done.6 = f32[8,128]{1,0:T(8,128)S(1)} collective-permute-done((f32[8,128]{1,0:T(8,128)}, f32[8,128]{1,0:T(8,128)S(1)}, u32[]{:S(2)}, u32[]{:S(2)}) %collective-permute-start.6) | collective-permute-done | bytes 4128 | tf_op jit(solution)/shard_map/ppermute | solution.py:603
  72.2 0.7 add.20
  72.9 0.0 collective-permute-start.7
  72.9 3.6 %collective-permute-done.7 = f32[8,128]{1,0:T(8,128)S(1)} collective-permute-done((f32[8,128]{1,0:T(8,128)S(1)}, f32[8,128]{1,0:T(8,128)S(1)}, u32[]{:S(2)}, u32[]{:S(2)}) %collective-permute-start.7) | collective-permute-done | bytes 4128 | tf_op jit(solution)/shard_map/ppermute | solution.py:609
  76.5 0.0 collective-permute-start.8
  76.5 3.6 %collective-permute-done.8 = f32[8,128]{1,0:T(8,128)S(1)} collective-permute-done((f32[8,128]{1,0:T(8,128)S(1)}, f32[8,128]{1,0:T(8,128)S(1)}, u32[]{:S(2)}, u32[]{:S(2)}) %collective-permute-start.8) | collective-permute-done | bytes 4128 | tf_op jit(solution)/shard_map/ppermute | solution.py:609
  80.1 0.0 collective-permute-start.9
  80.1 0.0 collective-permute-done.4.back1
  80.1 0.0 collective-permute-done.2.back0
  80.1 5.1 %add_piece.3 = (f32[13824,128]{1,0:T(8,128)}, f32[2,2,8,128]{3,2,1,0:T(8,128)S(1)}) custom-call(bf16[6912,128]{1,0:T(8,128)(2,1)} %take_band.2.refs_0_.own0, bf16[6912,128]{1,0:T(8,128)(2,1)} %take_band.3.own1, f32[2,6912,128]{2,1,0:T(8,128)} %get-tuple-element.22.terms, bf16[6912,128]{1,0:T(8,128)(2,1)} %collective-permute-done.2.back0, ...), custom_call_target="tpu_custom_call" | custom-call | bytes 10616832 | tf_op jit(solution)/shard_map/add_piece/pallas_call | solution.py:542
  85.2 0.0 collective-permute-done.9
  85.2 2.1 %collective-permute-start.10 = (f32[8,128]{1,0:T(8,128)S(1)}, f32[8,128]{1,0:T(8,128)S(1)}, u32[]{:S(2)}, u32[]{:S(2)}) collective-permute-start(f32[8,128]{1,0:T(8,128)S(1)} %add.23), channel_id=1, source_target_pairs={{0,4},{1,3},{2,10},{3,1},{4,0},{5,7},{6,14},{7,5},{8,12},{9,11},{1... | collective-permute-start | bytes 12296 | tf_op jit(solution)/shard_map/ppermute | solution.py:618
  87.3 0.0 collective-permute-done.5.back1
  87.3 3.4 %add_piece.4 = (f32[13824,128]{1,0:T(8,128)}, f32[2,2,8,128]{3,2,1,0:T(8,128)S(1)}) custom-call(bf16[6912,128]{1,0:T(8,128)(2,1)} %take_band.2.refs_0_.own0, bf16[6912,128]{1,0:T(8,128)(2,1)} %take_band.3.own1, f32[2,6912,128]{2,1,0:T(8,128)} %get-tuple-element.22.terms, ...), custom_call_target="tpu_custom_call", output_to_operand_aliasing={{0}: (5, {})} | custom-call | bytes 7077888 | tf_op jit(solution)/shard_map/add_piece/pallas_call | solution.py:542
  90.7 0.0 collective-permute-done.10
  90.8 0.1 collective-permute-start.11
  90.9 0.0 collective-permute-done.3.back1
  90.9 2.7 %add_piece.5 = (f32[13824,128]{1,0:T(8,128)}, f32[2,2]{1,0:T(2,128)}) custom-call(bf16[6912,128]{1,0:T(8,128)(2,1)} %take_band.2.refs_0_.own0, bf16[6912,128]{1,0:T(8,128)(2,1)} %take_band.3.own1, f32[2,6912,128]{2,1,0:T(8,128)} %get-tuple-element.22.terms, bf16[6912,128]{1,0:T(8,128)(2,1)} %collective-permute-done.2.back0, ...), custom_call_target="tpu_custom_call", output_to_operand_aliasing={{0}: (7, {})} | custom-call | bytes 3538944 | tf_op jit(solution)/shard_map/add_piece/pallas_call | solution.py:542
  93.5 0.5 slice.6
  94.0 0.0 collective-permute-done.11
  94.0 0.5 slice.7
  (4 shorter events, 0.0 us)
Async XLA Ops:
  4.5 27.0 %collective-permute-start.1 = (bf16[6912,128]{1,0:T(8,128)(2,1)}, bf16[6912,128]{1,0:T(8,128)(2,1)}, u32[]{:S(2)}, u32[]{:S(2)}) collective-permute-start(bf16[6912,128]{1,0:T(8,128)(2,1)} %take_band.2.refs_0_.own0), channel_id=1, source_target_pairs={{31,0},{0,1},{1,2},{2,3},{3,4},{4,5},{5,6},{6,7},{7,8},{8,9},{9,10... | collective-permute-start | bytes 5308424 | tf_op jit(solution)/shard_map/ppermute | solution.py:572
  8.8 41.7 %collective-permute-start = (bf16[6912,128]{1,0:T(8,128)(2,1)}, bf16[6912,128]{1,0:T(8,128)(2,1)}, u32[]{:S(2)}, u32[]{:S(2)}) collective-permute-start(bf16[6912,128]{1,0:T(8,128)(2,1)} %take_band.3.own1), channel_id=1, source_target_pairs={{31,0},{0,1},{1,2},{2,3},{3,4},{4,5},{5,6},{6,7},{7,8},{8,9},{9,10... | collective-permute-start | bytes 5308424 | tf_op jit(solution)/shard_map/ppermute | solution.py:572
  47.1 33.0 %collective-permute-start.2 = (bf16[6912,128]{1,0:T(8,128)(2,1)}, bf16[6912,128]{1,0:T(8,128)(2,1)}, u32[]{:S(2)}, u32[]{:S(2)}) collective-permute-start(bf16[6912,128]{1,0:T(8,128)(2,1)} %get-tuple-element.23), channel_id=1, source_target_pairs={{1,0},{2,1},{3,2},{4,3},{5,4},{6,5},{7,6},{8,7},{9,8},{10,9},{11,1... | collective-permute-start | bytes 5308424 | tf_op jit(solution)/shard_map/ppermute | solution.py:572
  68.0 12.1 %collective-permute-start.4 = (bf16[3456,128]{1,0:T(8,128)(2,1)}, bf16[3456,128]{1,0:T(8,128)(2,1)S(1)}, u32[]{:S(2)}, u32[]{:S(2)}) collective-permute-start(bf16[3456,128]{1,0:T(8,128)(2,1)} %get-tuple-element.25), channel_id=1, source_target_pairs={{1,0},{2,1},{3,2},{4,3},{5,4},{6,5},{7,6},{8,7},{9,8},{10,9},{11,1... | collective-permute-start | bytes 2654216 | tf_op jit(solution)/shard_map/ppermute | solution.py:572
  68.1 19.2 %collective-permute-start.5 = (bf16[2304,128]{1,0:T(8,128)(2,1)}, bf16[2304,128]{1,0:T(8,128)(2,1)S(1)}, u32[]{:S(2)}, u32[]{:S(2)}) collective-permute-start(bf16[2304,128]{1,0:T(8,128)(2,1)} %get-tuple-element.27), channel_id=1, source_target_pairs={{1,0},{2,1},{3,2},{4,3},{5,4},{6,5},{7,6},{8,7},{9,8},{10,9},{11,1... | collective-permute-start | bytes 1769480 | tf_op jit(solution)/shard_map/ppermute | solution.py:572
  70.4 20.5 %collective-permute-start.3 = (bf16[1152,128]{1,0:T(8,128)(2,1)}, bf16[1152,128]{1,0:T(8,128)(2,1)S(1)}, u32[]{:S(2)}, u32[]{:S(2)}) collective-permute-start(bf16[1152,128]{1,0:T(8,128)(2,1)} %get-tuple-element.24), channel_id=1, source_target_pairs={{1,0},{2,1},{3,2},{4,3},{5,4},{6,5},{7,6},{8,7},{9,8},{10,9},{11,1... | collective-permute-start | bytes 884744 | tf_op jit(solution)/shard_map/ppermute | solution.py:572
  70.5 1.7 %collective-permute-start.6 = (f32[8,128]{1,0:T(8,128)}, f32[8,128]{1,0:T(8,128)S(1)}, u32[]{:S(2)}, u32[]{:S(2)}) collective-permute-start(f32[8,128]{1,0:T(8,128)} %get-tuple-element.33), channel_id=1, source_target_pairs={{0,1},{1,0},{2,3},{3,2},{4,5},{5,4},{6,7},{7,6},{8,9},{9,8},{10,11... | collective-permute-start | bytes 12296 | tf_op jit(solution)/shard_map/ppermute | solution.py:603
  72.9 3.6 %collective-permute-start.7 = (f32[8,128]{1,0:T(8,128)S(1)}, f32[8,128]{1,0:T(8,128)S(1)}, u32[]{:S(2)}, u32[]{:S(2)}) collective-permute-start(f32[8,128]{1,0:T(8,128)S(1)} %add.20), channel_id=1, source_target_pairs={{0,4},{1,5},{2,10},{3,7},{4,0},{5,1},{6,14},{7,3},{8,12},{9,13},{1... | collective-permute-start | bytes 12296 | tf_op jit(solution)/shard_map/ppermute | solution.py:609
  76.5 3.6 %collective-permute-start.8 = (f32[8,128]{1,0:T(8,128)S(1)}, f32[8,128]{1,0:T(8,128)S(1)}, u32[]{:S(2)}, u32[]{:S(2)}) collective-permute-start(f32[8,128]{1,0:T(8,128)S(1)} %add.21), channel_id=1, source_target_pairs={{0,4},{1,9},{2,10},{3,11},{4,0},{5,13},{6,14},{7,15},{8,12},{9,1},... | collective-permute-start | bytes 12296 | tf_op jit(solution)/shard_map/ppermute | solution.py:609
  80.1 5.1 %collective-permute-start.9 = (f32[8,128]{1,0:T(8,128)S(1)}, f32[8,128]{1,0:T(8,128)S(1)}, u32[]{:S(2)}, u32[]{:S(2)}) collective-permute-start(f32[8,128]{1,0:T(8,128)S(1)} %add.22), channel_id=1, source_target_pairs={{0,4},{1,17},{2,10},{3,19},{4,0},{5,21},{6,14},{7,23},{8,12},{9,25... | collective-permute-start | bytes 12296 | tf_op jit(solution)/shard_map/ppermute | solution.py:618
  85.2 5.5 %collective-permute-start.10 = (f32[8,128]{1,0:T(8,128)S(1)}, f32[8,128]{1,0:T(8,128)S(1)}, u32[]{:S(2)}, u32[]{:S(2)}) collective-permute-start(f32[8,128]{1,0:T(8,128)S(1)} %add.23), channel_id=1, source_target_pairs={{0,4},{1,3},{2,10},{3,1},{4,0},{5,7},{6,14},{7,5},{8,12},{9,11},{1... | collective-permute-start | bytes 12296 | tf_op jit(solution)/shard_map/ppermute | solution.py:618
  90.8 3.3 %collective-permute-start.11 = (f32[8,128]{1,0:T(8,128)S(1)}, f32[8,128]{1,0:T(8,128)S(1)}, u32[]{:S(2)}, u32[]{:S(2)}) collective-permute-start(f32[8,128]{1,0:T(8,128)S(1)} %add.24), channel_id=1, source_target_pairs={{0,1},{1,0},{2,3},{3,2},{4,5},{5,4},{6,7},{7,6},{8,9},{9,8},{10,11... | collective-permute-start | bytes 12296 | tf_op jit(solution)/shard_map/ppermute | solution.py:616

commit v16 on v15

--- a/solution.py
+++ b/solution.py
@@ -24,7 +24,8 @@
 Z_ROWS = KPAD * Z_PITCH
 F_PITCH = PLANE + 1
 PLANES = 16
-STEP_ROWS = PLANES * PLANE
+STEP_ROWS = PLANES * QUADS
+THIRD = G * QUADS
 STEPS = G // PLANES
 PIECES = (3, 2, 1)
 WAVE_UNIT = 0.05
@@ -132,8 +133,7 @@
 
 
 def rows_of(ref, first, count):
-    at = pl.ds(first, count)
-    return ref.at[at, :] if len(ref.shape) == 2 else ref.at[:, at, :]
+    return ref.at[(slice(None),) * (len(ref.shape) - 2) + (pl.ds(first, count), slice(None))]
 
 
 def copy_rows(src, src_row, dst, dst_row, count, sem):
@@ -185,22 +185,32 @@
     )(raw, *earlier)
 
 
-def rows_kernel(own0, own1, sel, out, wide):
+def rows_kernel(own0, own1, sel, out, thirds, wide):
     for p, own in enumerate((own0, own1)):
         widen_planes(own, wide, 0)
 
         @pl.loop(0, QUADS // 4, unroll=2)
         def _(q):
             split_rows(wide, sel, out.at[p], 4 * q, 4)
+
+        @pl.loop(0, G // 2, unroll=4)
+        def _(i):
+            for s in range(3):
+                rows = [wide[pl.ds((2 * i + e) * F_PITCH + s, QUADS, stride=3), :] for e in range(2)]
+                at = pl.multiple_of(2 * i * QUADS, 16)
+                thirds[p, s, pl.ds(at, 2 * QUADS), :] = stack(*rows).astype(BF16)
 
 
 def padded_rows(own, sel, interpret=False):
     vmem = pl.BlockSpec(memory_space=pltpu.VMEM)
     return pl.pallas_call(
         rows_kernel,
-        out_shape=jax.ShapeDtypeStruct((2, G, G, LANES), BF16),
+        out_shape=(
+            jax.ShapeDtypeStruct((2, G, G, LANES), BF16),
+            jax.ShapeDtypeStruct((2, 3, THIRD, LANES), BF16),
+        ),
         in_specs=[vmem] * 3,
-        out_specs=vmem,
+        out_specs=(vmem, vmem),
         scratch_shapes=[pltpu.VMEM((G * F_PITCH, LANES), F32)],
         compiler_params=pltpu.CompilerParams(vmem_limit_bytes=63 * MIB),
         cost_estimate=cost(16 * NGRID),
@@ -209,17 +219,16 @@
     )(*own, sel)
 
 
-def pairs_kernel(pieces, share, own0, own1, own_u, kern, par, *refs):
+def pairs_kernel(pieces, share, own, own_u, kern, par, *refs):
     earlier = []
     if len(pieces) > 1:
         earlier, refs = refs[:2], refs[2:]
     table_refs, own_out = refs[:7], refs[7]
     par_out, energy_out = refs[8 : 8 + len(pieces)], refs[8 + len(pieces)]
     own_v, own_uv, kern_v, own_ov, par_ov, par_f, par_u, yw, z, x34 = refs[9 + len(pieces) : -15]
-    own_f, staged, total_ref, energy_v, before_v = refs[-15:-10]
-    tables, (par_sems, table_sems, sems) = refs[-10:-3], refs[-3:]
+    par_v, total_ref, energy_v, before_v = refs[-15:-11]
+    tables, (par_sems, table_sems, before_sems, sems) = refs[-11:-4], refs[-4:]
     t1, t2, t3, a1, a2, a3, sel = tables
-    par_v = par_ov
     par_loads = []
     for first in (0, ROWS // 2):
         sem = par_sems.at[len(par_loads)]
@@ -235,13 +244,16 @@
     loads = [
         pltpu.make_async_copy(own_u, own_uv, sems.at[0]),
         pltpu.make_async_copy(kern, kern_v, sems.at[1]),
-        copy_rows(own0, 0, own_v.at[0], 0, ROWS, sems.at[2]),
-        copy_rows(own1, 0, own_v.at[1], 0, ROWS, sems.at[3]),
+        pltpu.make_async_copy(own, own_v, sems.at[2]),
     ]
     later = []
     if earlier:
-        later = [copy_rows(earlier[0].at[p], 0, z, p * ROWS, ROWS, sems.at[4 + p]) for p in range(2)]
-        loads.append(pltpu.make_async_copy(earlier[1], before_v, sems.at[8 + len(pieces)]))
+        later = [
+            copy_rows(earlier[0].at[p, s], 0, z, (3 * p + s) * THIRD, THIRD, before_sems.at[3 * p + s])
+            for p in range(2)
+            for s in range(3)
+        ]
+        loads.append(pltpu.make_async_copy(earlier[1], before_v, sems.at[3]))
 
     for i, load in enumerate(par_loads):
         load.wait()
@@ -367,39 +379,34 @@
     for load in loads[2:] + later:
         load.wait()
     total_ref[...] = jnp.zeros_like(total_ref)
-    block_rows = PLANES * QUADS
     scale = F32(1.0 / NGRID)
 
     def result(ch):
-        at = pl.multiple_of(ch * block_rows, 16)
-        low = x34[pl.ds(at, block_rows), :]
-        high = x34[pl.ds(G * QUADS + at, block_rows), :]
+        at = pl.multiple_of(ch * STEP_ROWS, 16)
+        rows = pl.ds(at, STEP_ROWS)
+        low = x34[rows, :]
+        high = x34[pl.ds(THIRD + at, STEP_ROWS), :]
         fields = [low, lanes(low[:, 2 * LANES :], high[:, : 2 * LANES]), high]
-        flat = pl.ds(pl.multiple_of(ch * STEP_ROWS, 16), STEP_ROWS)
-        own_f[...] = own_v[:, flat, :].astype(F32)
-        total = jnp.zeros((QUADS, LANES), F32)
+        total = jnp.zeros((8, LANES), F32)
         for third in range(3):
             out = dot(fields[third], a3[third]) * scale
-            for i in range(PLANES):
-                plane = ch * PLANES + i
-                partner = par_f[pl.ds(plane * F_PITCH + third, QUADS, stride=3), :]
-                here = pl.ds(i * PLANE + third, QUADS, stride=3)
-                there = pl.ds(plane * PLANE + third, QUADS, stride=3)
-                sent = jnp.zeros((QUADS, LANES), F32)
-                for p in range(2):
-                    potential = out[i * QUADS : (i + 1) * QUADS, p * LANES : (p + 1) * LANES]
-                    term = potential * partner
-                    if earlier:
-                        at = p * ROWS + plane * PLANE + third
-                        term = term + z[pl.ds(at, QUADS, stride=3), :]
-                    own_ov[p, there, :] = term
-                    sent = sent + potential * own_f[p, here, :]
-                total = total + sent * partner
-                staged[here, :] = sent
+            first = ch * PLANES * F_PITCH + third
+            partner = stack(
+                *[par_f[pl.ds(first + i * F_PITCH, QUADS, stride=3), :] for i in range(PLANES)]
+            )
+            sent = None
+            for p in range(2):
+                potential = out[:, p * LANES : (p + 1) * LANES]
+                term = potential * partner
+                if earlier:
+                    term = term + z[pl.ds((3 * p + third) * THIRD + at, STEP_ROWS), :]
+                own_ov[p, third, rows, :] = term
+                part = potential * own_v[p, third, rows, :].astype(F32)
+                sent = part if sent is None else sent + part
+            total = total + jnp.sum((sent * partner).reshape(-1, 8, LANES), axis=0)
+            par_ov[third, rows, :] = sent.astype(BF16)
         total_ref[...] += total
-        par_ov[flat, :] = staged[...].astype(BF16)
-        row = ch * STEP_ROWS
-        copy_rows(own_ov, row, own_out, row, STEP_ROWS, sems.at[6]).start()
+        copy_rows(own_ov, at, own_out, at, STEP_ROWS, sems.at[4]).start()
 
     first = 0
     for i, steps in enumerate(pieces):
@@ -409,7 +416,7 @@
             ch = first + step
             result(ch)
             source, row = ch * STEP_ROWS, step * STEP_ROWS
-            copy_rows(par_ov, source, par_out[i], row, STEP_ROWS, sems.at[7 + i]).start()
+            copy_rows(par_ov, source, par_out[i], row, STEP_ROWS, sems.at[6 + i]).start()
 
         first += steps
 
@@ -417,13 +424,13 @@
     if earlier:
         energy = energy + before_v[...]
     energy_v[...] = energy
-    report = pltpu.make_async_copy(energy_v, energy_out, sems.at[7 + len(pieces)])
+    report = pltpu.make_async_copy(energy_v, energy_out, sems.at[5])
     report.start()
-    pltpu.make_async_copy(own_ov, own_out, sems.at[6]).wait()
+    pltpu.make_async_copy(own_ov, own_out, sems.at[4]).wait()
     first = 0
     for i, steps in enumerate(pieces):
         rows = steps * STEP_ROWS
-        copy_rows(par_ov, first, par_out[i], 0, rows, sems.at[7 + i]).wait()
+        copy_rows(par_ov, first, par_out[i], 0, rows, sems.at[6 + i]).wait()
         first += rows
     report.wait()
 
@@ -433,32 +440,32 @@
     return pl.pallas_call(
         functools.partial(pairs_kernel, pieces, share),
         out_shape=(
-            jax.ShapeDtypeStruct((2, ROWS, LANES), F32),
-            *[jax.ShapeDtypeStruct((steps * STEP_ROWS, LANES), BF16) for steps in pieces],
+            jax.ShapeDtypeStruct((2, 3, THIRD, LANES), F32),
+            *[jax.ShapeDtypeStruct((3, steps * STEP_ROWS, LANES), BF16) for steps in pieces],
             jax.ShapeDtypeStruct((8, LANES), F32),
         ),
-        in_specs=[hbm] * (5 + len(earlier) + len(tables)),
+        in_specs=[hbm] * (4 + len(earlier) + len(tables)),
         out_specs=(hbm,) * (2 + len(pieces)),
         scratch_shapes=[
-            pltpu.VMEM((2, ROWS, LANES), BF16),
+            pltpu.VMEM((2, 3, THIRD, LANES), BF16),
             pltpu.VMEM((2, G, G, LANES), BF16),
             pltpu.VMEM((KPAD * G, LANES), F32),
-            pltpu.VMEM((2, ROWS, LANES), F32),
-            pltpu.VMEM((ROWS, LANES), BF16),
+            pltpu.VMEM((2, 3, THIRD, LANES), F32),
+            pltpu.VMEM((3, THIRD, LANES), BF16),
             pltpu.VMEM((G * F_PITCH, LANES), F32),
             pltpu.VMEM((G, G, LANES), BF16),
             pltpu.VMEM((2 * G * Y_PITCH, LANES), F32),
             pltpu.VMEM((4 * Z_ROWS, LANES), F32),
             pltpu.VMEM((KPAD * G, 4 * LANES), BF16),
-            pltpu.VMEM((2, STEP_ROWS, LANES), F32),
-            pltpu.VMEM((STEP_ROWS, LANES), F32),
-            pltpu.VMEM((QUADS, LANES), F32),
+            pltpu.VMEM((ROWS, LANES), BF16),
+            pltpu.VMEM((8, LANES), F32),
             pltpu.VMEM((8, LANES), F32),
             pltpu.VMEM((8, LANES), F32),
             *[pltpu.VMEM(table.shape, BF16) for table in tables],
             pltpu.SemaphoreType.DMA((2,)),
             pltpu.SemaphoreType.DMA((len(tables),)),
-            pltpu.SemaphoreType.DMA((9 + len(pieces),)),
+            pltpu.SemaphoreType.DMA((6,)),
+            pltpu.SemaphoreType.DMA((6 + len(pieces),)),
         ],
         compiler_params=pltpu.CompilerParams(vmem_limit_bytes=63 * MIB),
         cost_estimate=pl.CostEstimate(
@@ -466,20 +473,21 @@
         ),
         interpret=interpret,
         name="pair_terms",
-    )(*own, own_u, kern, partner, *earlier, *tables)
-
-
-def piece_kernel(first, size, own0, own1, terms, back0, back1, *rest):
-    last = first + size == ROWS
+    )(own, own_u, kern, partner, *earlier, *tables)
+
+
+def piece_kernel(first, size, own, terms, back0, back1, *rest):
+    last = first + size == THIRD
     earlier = rest[: len(rest) - 12]
     out, gram_out, own_v, terms_v, back_v, out_v, gram_ref, gram_v, value_ref = rest[-12:-3]
     load_sems, gram_sems, store_sems = rest[-3:]
     rows = size // load_sems.shape[0]
+    wide = 6 * rows
 
     def loads(c):
         start = first + c * rows
         sources = [
-            (own0, start, own_v.at[0]), (own1, start, own_v.at[1]), (terms, start, terms_v),
+            (own, start, own_v), (terms, start, terms_v),
             (back0, start, back_v.at[0]), (back1, c * rows, back_v.at[1]),
         ]
         return [
@@ -504,14 +512,17 @@
         for load in chunk:
             load.wait()
         at = pl.ds(c * rows, rows)
-        own = [own_v[i, at, :].astype(F32) for i in range(2)]
-        for p in range(2):
-            exchange = terms_v[p, at, :] + back_v[p, at, :].astype(F32)
-            out_v[pl.ds(2 * c * rows + p, rows, stride=2), :] = exchange
-            for i in range(2):
-                product = (own[i] * exchange).reshape(-1, 8, LANES)
-                gram_ref[i, p] += jnp.sum(product, axis=0)
-        copy_rows(out_v, 2 * c * rows, out, 2 * (first + c * rows), 2 * rows, store_sems.at[0]).start()
+        for s in range(3):
+            bands = [own_v[i, s, at, :].astype(F32) for i in range(2)]
+            for p in range(2):
+                exchange = terms_v[p, s, at, :] + back_v[p, s, at, :].astype(F32)
+                for i in range(rows // QUADS):
+                    row = c * wide + 2 * (i * PLANE + s) + p
+                    out_v[pl.ds(row, QUADS, stride=6), :] = exchange[i * QUADS : (i + 1) * QUADS]
+                for i in range(2):
+                    product = (bands[i] * exchange).reshape(-1, 8, LANES)
+                    gram_ref[i, p] += jnp.sum(product, axis=0)
+        copy_rows(out_v, c * wide, out, 6 * first + c * wide, wide, store_sems.at[0]).start()
 
     result = gram_ref
     if last:
@@ -530,13 +541,13 @@
         result = value_ref
     report = pltpu.make_async_copy(result, gram_out, store_sems.at[1])
     report.start()
-    copy_rows(out_v, 0, out, 2 * first, 2 * size, store_sems.at[0]).wait()
+    copy_rows(out_v, 0, out, 6 * first, 6 * size, store_sems.at[0]).wait()
     report.wait()
 
 
 def add_piece(first, size, own, terms, back0, back1, grams, out, interpret=False):
     hbm = pl.BlockSpec(memory_space=pl.ANY)
-    last = first + size == ROWS
+    last = first + size == THIRD
     earlier = [] if out is None else [*(grams if last else []), out]
     gram_shape = (2, 2, 8, LANES)
     return pl.pallas_call(
@@ -545,26 +556,26 @@
             jax.ShapeDtypeStruct((2 * ROWS, LANES), F32),
             jax.ShapeDtypeStruct((2, 2) if last else gram_shape, F32),
         ),
-        in_specs=[hbm] * (5 + len(earlier)),
+        in_specs=[hbm] * (4 + len(earlier)),
         out_specs=(hbm, hbm),
         scratch_shapes=[
-            pltpu.VMEM((2, size, LANES), BF16),
-            pltpu.VMEM((2, size, LANES), F32),
-            pltpu.VMEM((2, size, LANES), BF16),
-            pltpu.VMEM((2 * size, LANES), F32),
+            pltpu.VMEM((2, 3, size, LANES), BF16),
+            pltpu.VMEM((2, 3, size, LANES), F32),
+            pltpu.VMEM((2, 3, size, LANES), BF16),
+            pltpu.VMEM((6 * size, LANES), F32),
             pltpu.VMEM(gram_shape, F32),
             pltpu.VMEM((len(PIECES), *gram_shape), F32),
             pltpu.VMEM((2, 2), F32),
-            pltpu.SemaphoreType.DMA((2 * size // STEP_ROWS, 5)),
+            pltpu.SemaphoreType.DMA((2 * size // STEP_ROWS, 4)),
             pltpu.SemaphoreType.DMA((len(PIECES),)),
             pltpu.SemaphoreType.DMA((2,)),
         ],
-        input_output_aliases={4 + len(earlier): 0} if earlier else {},
+        input_output_aliases={3 + len(earlier): 0} if earlier else {},
         compiler_params=pltpu.CompilerParams(vmem_limit_bytes=52 * MIB),
-        cost_estimate=cost(24 * size * LANES),
+        cost_estimate=cost(72 * size * LANES),
         interpret=interpret,
         name="add_piece",
-    )(*own, terms, back0, back1, *earlier)
+    )(own, terms, back0, back1, *earlier)
 
 
 def from_behind(block, axis, distance):
@@ -585,13 +596,13 @@
     own = [take_band(raw, 0)]
     own.append(take_band(raw, 1, own))
     previous = [from_behind(part, "band", 1) for part in own]
-    own_u = padded_rows(own, tables[-1])
+    own_u, thirds = padded_rows(own, tables[-1])
     terms, back0, energy = pair_terms(
-        own, own_u, previous[0], (), tables, kern, (STEPS,), share
+        thirds, own_u, previous[0], (), tables, kern, (STEPS,), share
     )
     back0 = from_behind(back0, "band", -1)
     terms, *sent, energy = pair_terms(
-        own, own_u, previous[1], (terms, energy), tables, kern, PIECES, share
+        thirds, own_u, previous[1], (terms, energy), tables, kern, PIECES, share
     )
     back1 = [from_behind(piece, "band", -1) for piece in sent]
 
@@ -616,7 +627,7 @@
             got = lax.ppermute(energy, "band", swap)
         elif steps:
             got = lax.ppermute(energy, "band", steps.pop(0))
-        exchange, gram = add_piece(first, count, own, terms, back0, piece, grams, exchange)
+        exchange, gram = add_piece(first, count, thirds, terms, back0, piece, grams, exchange)
         if got is not None and last:
             odd = lax.axis_index("band") % 2 == 1
             energy = jnp.where(odd, energy[:1, :1], after(got, gram)[:1, :1])

time: 97.3 us -> 96.1 us (0.988)
  waiting for transfers between devices: 24.4 us -> 23.2 us
    pallas_call x1, Pallas kernels: 6.95 us -> 8.58 us  [padded_rows(): pl.pallas_call(rows_kernel, out_shape=(jax.ShapeDtypeStruct((2, G, G, LAN...]
    ppermute x6, waiting for transfers between devices: 15.9 us -> 14.7 us  [from_behind(): lax.ppermute(block, axis, [((i - distance) % size, i) for i in range(size)])]
    pallas_call x2, Pallas kernels: 33.2 us -> 32.2 us  [pair_terms(): pl.pallas_call(functools.partial(pairs_kernel, pieces, share), out_shape=...]
  transfers between devices with their start and end apart: 12 -> 12, of which waited for: 5 -> 5; matrix products, arithmetic and copies ran while one was open for 1% -> 1% of each run, Pallas kernels for 57% -> 58%
where the time goes in v16:
time: 96.1 us; the launch traced here: 95.8 us
  Pallas kernels  59.1 us (61%)
  waiting for transfers between devices  23.2 us (24%)
  starting transfers between devices  8.69 us (9%)
  between operations  3.1 us (3%)
  local copies, waits for them, and re-layouts  0.99 us (1%)
    pallas_call x2, Pallas kernels, pair_terms(): pl.pallas_call(functools.partial(pairs_kernel, pieces, share), out_shape=...  32.2 us
    ppermute x6, waiting for transfers between devices, from_behind(): lax.ppermute(block, axis, [((i - distance) % size, i) for i in range(size)])  14.7 us
    pallas_call x3, Pallas kernels, add_piece(): pl.pallas_call(functools.partial(piece_kernel, first, size), out_shape=(j...  10.7 us
    pallas_call x1, Pallas kernels, padded_rows(): pl.pallas_call(rows_kernel, out_shape=(jax.ShapeDtypeStruct((2, G, G, LAN...  8.58 us
    pallas_call x2, Pallas kernels, take_band(): pl.pallas_call(functools.partial(band_kernel, p), out_shape=jax.ShapeDtyp...  7.66 us
    ppermute x2, waiting for transfers between devices, per_device(): energy = energy + lax.ppermute(energy, 'band', steps.pop(0))  7.21 us
    ppermute x6, starting transfers between devices, from_behind(): lax.ppermute(block, axis, [((i - distance) % size, i) for i in range(size)])  6.09 us
    ppermute x2, starting transfers between devices, per_device(): got = lax.ppermute(energy, 'band', steps.pop(0))  2.08 us
  transfers between devices with their start and end apart: 12, of which 5 were waited for; matrix products, arithmetic and copies ran while one was open for 1% of the time, Pallas kernels for 58%

profile of v16, /device:TPU:0, one launch (start us, length us, event | category | flops | bytes accessed | tf_op | source)
XLA Modules:
  0.0 95.8 jit_solution(11845239243961056470)
XLA Ops:
  0.6 3.8 %take_band.2.refs_0_.own0 = bf16[6912,128]{1,0:T(8,128)(2,1)} custom-call(bf16[13824,128]{1,0:T(8,128)(2,1)} %bitcast.13), custom_call_target="tpu_custom_call" | custom-call | bytes 5308416 | tf_op jit(solution)/shard_map/take_band/pallas_call | solution.py:170
  4.5 0.5 collective-permute-start.1
  5.0 3.8 %take_band.3.own1 = bf16[6912,128]{1,0:T(8,128)(2,1)} custom-call(bf16[13824,128]{1,0:T(8,128)(2,1)} %bitcast.14, bf16[6912,128]{1,0:T(8,128)(2,1)} %take_band.2.refs_0_.own0), custom_call_target="tpu_custom_call" | custom-call | bytes 5308416 | tf_op jit(solution)/shard_map/take_band/pallas_call | solution.py:170
  8.8 2.8 %collective-permute-start = (bf16[6912,128]{1,0:T(8,128)(2,1)}, bf16[6912,128]{1,0:T(8,128)(2,1)}, u32[]{:S(2)}, u32[]{:S(2)}) collective-permute-start(bf16[6912,128]{1,0:T(8,128)(2,1)} %take_band.3.own1), channel_id=1, source_target_pairs={{31,0},{0,1},{1,2},{2,3},{3,4},{4,5},{5,6},{6,7},{7,8},{8,9},{9,10... | collective-permute-start | bytes 5308424 | tf_op jit(solution)/shard_map/ppermute | solution.py:583
  11.7 8.6 %padded_rows.1 = (bf16[2,96,96,128]{3,2,1,0:T(8,128)(2,1)}, bf16[2,3,2304,128]{3,2,1,0:T(8,128)(2,1)}) custom-call(bf16[6912,128]{1,0:T(8,128)(2,1)} %take_band.2.refs_0_.own0, bf16[6912,128]{1,0:T(8,128)(2,1)} %take_band.3.own1, bf16[2,256,256]{2,1,0:T(8,128)(2,1)} %constant.34.clone.sel.refs_6_.refs_8_), custom_call_target="tpu_custom_call" | custom-call | bytes 14155776 | tf_op jit(solution)/shard_map/padded_rows/pallas_call | solution.py:206
  20.2 11.2 %collective-permute-done.1.par = bf16[6912,128]{1,0:T(8,128)(2,1)} collective-permute-done((bf16[6912,128]{1,0:T(8,128)(2,1)}, bf16[6912,128]{1,0:T(8,128)(2,1)}, u32[]{:S(2)}, u32[]{:S(2)}) %collective-permute-start.1) | collective-permute-done | bytes 1769504 | tf_op jit(solution)/shard_map/ppermute | solution.py:583
  31.4 15.3 %pair_terms.2 = (f32[2,3,2304,128]{3,2,1,0:T(8,128)}, bf16[3,2304,128]{2,1,0:T(8,128)(2,1)}, f32[8,128]{1,0:T(8,128)}) custom-call(bf16[2,3,2304,128]{3,2,1,0:T(8,128)(2,1)} %get-tuple-element.22.own, bf16[2,96,96,128]{3,2,1,0:T(8,128)(2,1)} %get-tuple-element.23.own_u, f32[4800,128]{1,0:T(8,128)} %constant.35.clone.kern, ...), custom_call_target="tpu_custom_call" | custom-call | flops 20000000000 | bytes 20000000 | tf_op jit(solution)/shard_map/pair_terms/pallas_call | solution.py:440
  46.7 0.3 collective-permute-start.2
  47.0 3.5 %collective-permute-done.par = bf16[6912,128]{1,0:T(8,128)(2,1)} collective-permute-done((bf16[6912,128]{1,0:T(8,128)(2,1)}, bf16[6912,128]{1,0:T(8,128)(2,1)}, u32[]{:S(2)}, u32[]{:S(2)}) %collective-permute-start) | collective-permute-done | bytes 1769504 | tf_op jit(solution)/shard_map/ppermute | solution.py:583
  50.5 16.9 %pair_terms.3 = (f32[2,3,2304,128]{3,2,1,0:T(8,128)}, bf16[3,1152,128]{2,1,0:T(8,128)(2,1)}, bf16[3,768,128]{2,1,0:T(8,128)(2,1)}, bf16[3,384,128]{2,1,0:T(8,128)(2,1)}, f32[8,128]{1,0:T(8,128)}) custom-call(bf16[2,3,2304,128]{3,2,1,0:T(8,128)(2,1)} %get-tuple-element.22.own, bf16[2,96,96,128]{3,2,1,0:T(8,128)(2,1)} %get-tuple-element.23.own_u, ...), custom_call_target="tpu_custom_call" | custom-call | flops 20000000000 | bytes 20000000 | tf_op jit(solution)/shard_map/pair_terms/pallas_call | solution.py:440
  67.4 0.1 collective-permute-start.4
  67.4 2.3 %collective-permute-start.5 = (bf16[3,768,128]{2,1,0:T(8,128)(2,1)}, bf16[3,768,128]{2,1,0:T(8,128)(2,1)S(1)}, u32[]{:S(2)}, u32[]{:S(2)}) collective-permute-start(bf16[3,768,128]{2,1,0:T(8,128)(2,1)} %get-tuple-element.31), channel_id=1, source_target_pairs={{1,0},{2,1},{3,2},{4,3},{5,4},{6,5},{7,6},{8,7},{9,8},{10,9},{11,1... | collective-permute-start | bytes 1769480 | tf_op jit(solution)/shard_map/ppermute | solution.py:583
  69.8 0.1 collective-permute-start.3
  69.8 0.4 collective-permute-start.6
  70.3 1.3 %collective-permute-done.6 = f32[8,128]{1,0:T(8,128)S(1)} collective-permute-done((f32[8,128]{1,0:T(8,128)}, f32[8,128]{1,0:T(8,128)S(1)}, u32[]{:S(2)}, u32[]{:S(2)}) %collective-permute-start.6) | collective-permute-done | bytes 4128 | tf_op jit(solution)/shard_map/ppermute | solution.py:614
  71.6 0.7 add.20
  72.3 0.0 collective-permute-start.7
  72.3 3.6 %collective-permute-done.7 = f32[8,128]{1,0:T(8,128)S(1)} collective-permute-done((f32[8,128]{1,0:T(8,128)S(1)}, f32[8,128]{1,0:T(8,128)S(1)}, u32[]{:S(2)}, u32[]{:S(2)}) %collective-permute-start.7) | collective-permute-done | bytes 4128 | tf_op jit(solution)/shard_map/ppermute | solution.py:620
  75.9 0.0 collective-permute-start.8
  75.9 3.6 %collective-permute-done.8 = f32[8,128]{1,0:T(8,128)S(1)} collective-permute-done((f32[8,128]{1,0:T(8,128)S(1)}, f32[8,128]{1,0:T(8,128)S(1)}, u32[]{:S(2)}, u32[]{:S(2)}) %collective-permute-start.8) | collective-permute-done | bytes 4128 | tf_op jit(solution)/shard_map/ppermute | solution.py:620
  79.5 0.0 collective-permute-start.9
  79.5 0.0 collective-permute-done.4.back1
  79.5 0.0 collective-permute-done.2.back0
  79.5 4.9 %add_piece.3 = (f32[13824,128]{1,0:T(8,128)}, f32[2,2,8,128]{3,2,1,0:T(8,128)S(1)}) custom-call(bf16[2,3,2304,128]{3,2,1,0:T(8,128)(2,1)} %get-tuple-element.22.own, f32[2,3,2304,128]{3,2,1,0:T(8,128)} %get-tuple-element.26.terms, bf16[3,2304,128]{2,1,0:T(8,128)(2,1)} %collective-permute-done.2.back0, bf16[3,1152,128]{2,1,0:T(8,128)(2,1)S(1)} %collective-permute-done.4.back1), custom_call_target="tpu_custom_call" | custom-call | bytes 10616832 | tf_op jit(solution)/shard_map/add_piece/pallas_call | solution.py:553
  84.4 0.0 collective-permute-done.9
  84.4 2.1 %collective-permute-start.10 = (f32[8,128]{1,0:T(8,128)S(1)}, f32[8,128]{1,0:T(8,128)S(1)}, u32[]{:S(2)}, u32[]{:S(2)}) collective-permute-start(f32[8,128]{1,0:T(8,128)S(1)} %add.23), channel_id=1, source_target_pairs={{0,4},{1,3},{2,10},{3,1},{4,0},{5,7},{6,14},{7,5},{8,12},{9,11},{1... | collective-permute-start | bytes 12296 | tf_op jit(solution)/shard_map/ppermute | solution.py:629
  86.5 0.0 collective-permute-done.5.back1
  86.5 3.3 %add_piece.4 = (f32[13824,128]{1,0:T(8,128)}, f32[2,2,8,128]{3,2,1,0:T(8,128)S(1)}) custom-call(bf16[2,3,2304,128]{3,2,1,0:T(8,128)(2,1)} %get-tuple-element.22.own, f32[2,3,2304,128]{3,2,1,0:T(8,128)} %get-tuple-element.26.terms, bf16[3,2304,128]{2,1,0:T(8,128)(2,1)} %collective-permute-done.2.back0, ...), custom_call_target="tpu_custom_call", output_to_operand_aliasing={{0}: (4, {})} | custom-call | bytes 7077888 | tf_op jit(solution)/shard_map/add_piece/pallas_call | solution.py:553
  89.8 0.0 collective-permute-done.10
  89.8 0.1 collective-permute-start.11
  89.9 0.0 collective-permute-done.3.back1
  89.9 2.6 %add_piece.5 = (f32[13824,128]{1,0:T(8,128)}, f32[2,2]{1,0:T(2,128)}) custom-call(bf16[2,3,2304,128]{3,2,1,0:T(8,128)(2,1)} %get-tuple-element.22.own, f32[2,3,2304,128]{3,2,1,0:T(8,128)} %get-tuple-element.26.terms, bf16[3,2304,128]{2,1,0:T(8,128)(2,1)} %collective-permute-done.2.back0, ...), custom_call_target="tpu_custom_call", output_to_operand_aliasing={{0}: (6, {})} | custom-call | bytes 3538944 | tf_op jit(solution)/shard_map/add_piece/pallas_call | solution.py:553
  92.5 0.5 slice.6
  93.0 0.0 collective-permute-done.11
  93.0 0.5 slice.7
  (4 shorter events, 0.0 us)
Async XLA Ops:
  4.5 27.0 %collective-permute-start.1 = (bf16[6912,128]{1,0:T(8,128)(2,1)}, bf16[6912,128]{1,0:T(8,128)(2,1)}, u32[]{:S(2)}, u32[]{:S(2)}) collective-permute-start(bf16[6912,128]{1,0:T(8,128)(2,1)} %take_band.2.refs_0_.own0), channel_id=1, source_target_pairs={{31,0},{0,1},{1,2},{2,3},{3,4},{4,5},{5,6},{6,7},{7,8},{8,9},{9,10... | collective-permute-start | bytes 5308424 | tf_op jit(solution)/shard_map/ppermute | solution.py:583
  8.8 41.7 %collective-permute-start = (bf16[6912,128]{1,0:T(8,128)(2,1)}, bf16[6912,128]{1,0:T(8,128)(2,1)}, u32[]{:S(2)}, u32[]{:S(2)}) collective-permute-start(bf16[6912,128]{1,0:T(8,128)(2,1)} %take_band.3.own1), channel_id=1, source_target_pairs={{31,0},{0,1},{1,2},{2,3},{3,4},{4,5},{5,6},{6,7},{7,8},{8,9},{9,10... | collective-permute-start | bytes 5308424 | tf_op jit(solution)/shard_map/ppermute | solution.py:583
  46.7 32.8 %collective-permute-start.2 = (bf16[3,2304,128]{2,1,0:T(8,128)(2,1)}, bf16[3,2304,128]{2,1,0:T(8,128)(2,1)}, u32[]{:S(2)}, u32[]{:S(2)}) collective-permute-start(bf16[3,2304,128]{2,1,0:T(8,128)(2,1)} %get-tuple-element.27), channel_id=1, source_target_pairs={{1,0},{2,1},{3,2},{4,3},{5,4},{6,5},{7,6},{8,7},{9,8},{10,9},{11,1... | collective-permute-start | bytes 5308424 | tf_op jit(solution)/shard_map/ppermute | solution.py:583
  67.4 12.1 %collective-permute-start.4 = (bf16[3,1152,128]{2,1,0:T(8,128)(2,1)}, bf16[3,1152,128]{2,1,0:T(8,128)(2,1)S(1)}, u32[]{:S(2)}, u32[]{:S(2)}) collective-permute-start(bf16[3,1152,128]{2,1,0:T(8,128)(2,1)} %get-tuple-element.29), channel_id=1, source_target_pairs={{1,0},{2,1},{3,2},{4,3},{5,4},{6,5},{7,6},{8,7},{9,8},{10,9},{11,1... | collective-permute-start | bytes 2654216 | tf_op jit(solution)/shard_map/ppermute | solution.py:583
  67.4 19.0 %collective-permute-start.5 = (bf16[3,768,128]{2,1,0:T(8,128)(2,1)}, bf16[3,768,128]{2,1,0:T(8,128)(2,1)S(1)}, u32[]{:S(2)}, u32[]{:S(2)}) collective-permute-start(bf16[3,768,128]{2,1,0:T(8,128)(2,1)} %get-tuple-element.31), channel_id=1, source_target_pairs={{1,0},{2,1},{3,2},{4,3},{5,4},{6,5},{7,6},{8,7},{9,8},{10,9},{11,1... | collective-permute-start | bytes 1769480 | tf_op jit(solution)/shard_map/ppermute | solution.py:583
  69.8 20.1 %collective-permute-start.3 = (bf16[3,384,128]{2,1,0:T(8,128)(2,1)}, bf16[3,384,128]{2,1,0:T(8,128)(2,1)S(1)}, u32[]{:S(2)}, u32[]{:S(2)}) collective-permute-start(bf16[3,384,128]{2,1,0:T(8,128)(2,1)} %get-tuple-element.28), channel_id=1, source_target_pairs={{1,0},{2,1},{3,2},{4,3},{5,4},{6,5},{7,6},{8,7},{9,8},{10,9},{11,1... | collective-permute-start | bytes 884744 | tf_op jit(solution)/shard_map/ppermute | solution.py:583
  69.8 1.7 %collective-permute-start.6 = (f32[8,128]{1,0:T(8,128)}, f32[8,128]{1,0:T(8,128)S(1)}, u32[]{:S(2)}, u32[]{:S(2)}) collective-permute-start(f32[8,128]{1,0:T(8,128)} %get-tuple-element.37), channel_id=1, source_target_pairs={{0,1},{1,0},{2,3},{3,2},{4,5},{5,4},{6,7},{7,6},{8,9},{9,8},{10,11... | collective-permute-start | bytes 12296 | tf_op jit(solution)/shard_map/ppermute | solution.py:614
  72.3 3.6 %collective-permute-start.7 = (f32[8,128]{1,0:T(8,128)S(1)}, f32[8,128]{1,0:T(8,128)S(1)}, u32[]{:S(2)}, u32[]{:S(2)}) collective-permute-start(f32[8,128]{1,0:T(8,128)S(1)} %add.20), channel_id=1, source_target_pairs={{0,4},{1,5},{2,10},{3,7},{4,0},{5,1},{6,14},{7,3},{8,12},{9,13},{1... | collective-permute-start | bytes 12296 | tf_op jit(solution)/shard_map/ppermute | solution.py:620
  75.9 3.6 %collective-permute-start.8 = (f32[8,128]{1,0:T(8,128)S(1)}, f32[8,128]{1,0:T(8,128)S(1)}, u32[]{:S(2)}, u32[]{:S(2)}) collective-permute-start(f32[8,128]{1,0:T(8,128)S(1)} %add.21), channel_id=1, source_target_pairs={{0,4},{1,9},{2,10},{3,11},{4,0},{5,13},{6,14},{7,15},{8,12},{9,1},... | collective-permute-start | bytes 12296 | tf_op jit(solution)/shard_map/ppermute | solution.py:620
  79.5 4.9 %collective-permute-start.9 = (f32[8,128]{1,0:T(8,128)S(1)}, f32[8,128]{1,0:T(8,128)S(1)}, u32[]{:S(2)}, u32[]{:S(2)}) collective-permute-start(f32[8,128]{1,0:T(8,128)S(1)} %add.22), channel_id=1, source_target_pairs={{0,4},{1,17},{2,10},{3,19},{4,0},{5,21},{6,14},{7,23},{8,12},{9,25... | collective-permute-start | bytes 12296 | tf_op jit(solution)/shard_map/ppermute | solution.py:629
  84.4 5.4 %collective-permute-start.10 = (f32[8,128]{1,0:T(8,128)S(1)}, f32[8,128]{1,0:T(8,128)S(1)}, u32[]{:S(2)}, u32[]{:S(2)}) collective-permute-start(f32[8,128]{1,0:T(8,128)S(1)} %add.23), channel_id=1, source_target_pairs={{0,4},{1,3},{2,10},{3,1},{4,0},{5,7},{6,14},{7,5},{8,12},{9,11},{1... | collective-permute-start | bytes 12296 | tf_op jit(solution)/shard_map/ppermute | solution.py:629
  89.8 3.2 %collective-permute-start.11 = (f32[8,128]{1,0:T(8,128)S(1)}, f32[8,128]{1,0:T(8,128)S(1)}, u32[]{:S(2)}, u32[]{:S(2)}) collective-permute-start(f32[8,128]{1,0:T(8,128)S(1)} %add.24), channel_id=1, source_target_pairs={{0,1},{1,0},{2,3},{3,2},{4,5},{5,4},{6,7},{7,6},{8,9},{9,8},{10,11... | collective-permute-start | bytes 12296 | tf_op jit(solution)/shard_map/ppermute | solution.py:627

commit v17 on v16

--- a/solution.py
+++ b/solution.py
@@ -27,7 +27,7 @@
 STEP_ROWS = PLANES * QUADS
 THIRD = G * QUADS
 STEPS = G // PLANES
-PIECES = (3, 2, 1)
+PIECES = (2, 2, 1, 1)
 WAVE_UNIT = 0.05
 SCREEN_SQ = 0.0121
 MIB = 1024 * 1024
@@ -248,10 +248,14 @@
     ]
     later = []
     if earlier:
+        group = 2 * STEP_ROWS
         later = [
-            copy_rows(earlier[0].at[p, s], 0, z, (3 * p + s) * THIRD, THIRD, before_sems.at[3 * p + s])
-            for p in range(2)
-            for s in range(3)
+            [
+                copy_rows(earlier[0].at[p, s], row, z, (3 * p + s) * THIRD + row, group, before_sems.at[g, 3 * p + s])
+                for p in range(2)
+                for s in range(3)
+            ]
+            for g, row in enumerate(range(0, THIRD, group))
         ]
         loads.append(pltpu.make_async_copy(earlier[1], before_v, sems.at[3]))
 
@@ -347,7 +351,7 @@
             at = (4 * four + e) * W_PITCH
             yw[pl.ds(at, 2 * G), :] = out[:, e * LANES : (e + 1) * LANES]
 
-    for load in later:
+    for load in sum(later, []):
         load.start()
     table_loads[4].wait()
 
@@ -376,13 +380,13 @@
             x34[pl.ds(at, 4 * QUADS), left : left + 2 * LANES] = stack(*block).astype(BF16)
 
     table_loads[5].wait()
-    for load in loads[2:] + later:
+    for load in loads[2:]:
         load.wait()
     total_ref[...] = jnp.zeros_like(total_ref)
     scale = F32(1.0 / NGRID)
 
     def result(ch):
-        at = pl.multiple_of(ch * STEP_ROWS, 16)
+        at = ch * STEP_ROWS
         rows = pl.ds(at, STEP_ROWS)
         low = x34[rows, :]
         high = x34[pl.ds(THIRD + at, STEP_ROWS), :]
@@ -408,19 +412,17 @@
         total_ref[...] += total
         copy_rows(own_ov, at, own_out, at, STEP_ROWS, sems.at[4]).start()
 
-    first = 0
+    ch = 0
     for i, steps in enumerate(pieces):
-
-        @pl.loop(0, steps, unroll=min(steps, 3))
-        def _(step):
-            ch = first + step
+        for step in range(steps):
+            for load in later[ch // 2] if earlier and ch % 2 == 0 else ():
+                load.wait()
             result(ch)
             source, row = ch * STEP_ROWS, step * STEP_ROWS
             copy_rows(par_ov, source, par_out[i], row, STEP_ROWS, sems.at[6 + i]).start()
-
-        first += steps
-
-    energy = jnp.zeros((8, LANES), F32) + jnp.sum(total_ref[...]) * F32(share)
+            ch += 1
+
+    energy = jnp.zeros((1, 1), F32) + jnp.sum(total_ref[...]) * F32(share)
     if earlier:
         energy = energy + before_v[...]
     energy_v[...] = energy
@@ -442,7 +444,7 @@
         out_shape=(
             jax.ShapeDtypeStruct((2, 3, THIRD, LANES), F32),
             *[jax.ShapeDtypeStruct((3, steps * STEP_ROWS, LANES), BF16) for steps in pieces],
-            jax.ShapeDtypeStruct((8, LANES), F32),
+            jax.ShapeDtypeStruct((1, 1), F32),
         ),
         in_specs=[hbm] * (4 + len(earlier) + len(tables)),
         out_specs=(hbm,) * (2 + len(pieces)),
@@ -459,12 +461,12 @@
             pltpu.VMEM((KPAD * G, 4 * LANES), BF16),
             pltpu.VMEM((ROWS, LANES), BF16),
             pltpu.VMEM((8, LANES), F32),
-            pltpu.VMEM((8, LANES), F32),
-            pltpu.VMEM((8, LANES), F32),
+            pltpu.VMEM((1, 1), F32),
+            pltpu.VMEM((1, 1), F32),
             *[pltpu.VMEM(table.shape, BF16) for table in tables],
             pltpu.SemaphoreType.DMA((2,)),
             pltpu.SemaphoreType.DMA((len(tables),)),
-            pltpu.SemaphoreType.DMA((6,)),
+            pltpu.SemaphoreType.DMA((3, 6)),
             pltpu.SemaphoreType.DMA((6 + len(pieces),)),
         ],
         compiler_params=pltpu.CompilerParams(vmem_limit_bytes=63 * MIB),
@@ -476,7 +478,7 @@
     )(own, own_u, kern, partner, *earlier, *tables)
 
 
-def piece_kernel(first, size, own, terms, back0, back1, *rest):
+def piece_kernel(first, size, own, terms, back0, back1, _, *rest):
     last = first + size == THIRD
     earlier = rest[: len(rest) - 12]
     out, gram_out, own_v, terms_v, back_v, out_v, gram_ref, gram_v, value_ref = rest[-12:-3]
@@ -545,7 +547,7 @@
     report.wait()
 
 
-def add_piece(first, size, own, terms, back0, back1, grams, out, interpret=False):
+def add_piece(first, size, own, terms, back0, back1, energy, grams, out, interpret=False):
     hbm = pl.BlockSpec(memory_space=pl.ANY)
     last = first + size == THIRD
     earlier = [] if out is None else [*(grams if last else []), out]
@@ -556,7 +558,7 @@
             jax.ShapeDtypeStruct((2 * ROWS, LANES), F32),
             jax.ShapeDtypeStruct((2, 2) if last else gram_shape, F32),
         ),
-        in_specs=[hbm] * (4 + len(earlier)),
+        in_specs=[hbm] * (5 + len(earlier)),
         out_specs=(hbm, hbm),
         scratch_shapes=[
             pltpu.VMEM((2, 3, size, LANES), BF16),
@@ -570,12 +572,12 @@
             pltpu.SemaphoreType.DMA((len(PIECES),)),
             pltpu.SemaphoreType.DMA((2,)),
         ],
-        input_output_aliases={3 + len(earlier): 0} if earlier else {},
+        input_output_aliases={4 + len(earlier): 0} if earlier else {},
         compiler_params=pltpu.CompilerParams(vmem_limit_bytes=52 * MIB),
         cost_estimate=cost(72 * size * LANES),
         interpret=interpret,
         name="add_piece",
-    )(own, terms, back0, back1, *earlier)
+    )(own, terms, back0, back1, energy, *earlier)
 
 
 def from_behind(block, axis, distance):
@@ -627,10 +629,12 @@
             got = lax.ppermute(energy, "band", swap)
         elif steps:
             got = lax.ppermute(energy, "band", steps.pop(0))
-        exchange, gram = add_piece(first, count, thirds, terms, back0, piece, grams, exchange)
+        exchange, gram = add_piece(
+            first, count, thirds, terms, back0, piece, energy, grams, exchange
+        )
         if got is not None and last:
             odd = lax.axis_index("band") % 2 == 1
-            energy = jnp.where(odd, energy[:1, :1], after(got, gram)[:1, :1])
+            energy = jnp.where(odd, energy, after(got, gram))
         elif got is not None:
             energy = energy + after(got, gram)
         grams.append(gram)

time: 96.1 us -> 100 us (1.041)
  starting transfers between devices: 8.69 us -> 15.8 us
  waiting for transfers between devices: 23.2 us -> 18 us
  between operations: 3.1 us -> 6.29 us
    ppermute x2 -> x1, waiting for transfers between devices: 7.21 us -> 2.19 us  [per_device(): energy = energy + lax.ppermute(energy, 'band', steps.pop(0))]
    ppermute x2 -> x3, starting transfers between devices: 2.08 us -> 6.12 us  [per_device(): got = lax.ppermute(energy, 'band', steps.pop(0))]
    ppermute x2 -> x1, starting transfers between devices: 0.01 us -> 1.37 us  [per_device(): energy = energy + lax.ppermute(energy, 'band', steps.pop(0))]
    pallas_call x3 -> x4, Pallas kernels: 10.7 us -> 11.7 us  [add_piece(): pl.pallas_call(functools.partial(piece_kernel, first, size), out_shape=(j...]
    ppermute x6 -> x7, starting transfers between devices: 6.09 us -> 7.01 us  [from_behind(): lax.ppermute(block, axis, [((i - distance) % size, i) for i in range(size)])]
    ppermute x6 -> x7, waiting for transfers between devices: 14.7 us -> 14.5 us  [from_behind(): lax.ppermute(block, axis, [((i - distance) % size, i) for i in range(size)])]
  transfers between devices with their start and end apart: 12 -> 13, of which waited for: 5 -> 4; matrix products, arithmetic and copies ran while one was open for 1% -> 0% of each run, Pallas kernels for 58% -> 56%
where the time goes in v17:
time: 100 us
  Pallas kernels  60 us (60%)
  waiting for transfers between devices  18 us (18%)
  starting transfers between devices  15.8 us (16%)
  between operations  6.29 us (6%)
    pallas_call x2, Pallas kernels, pair_terms(): pl.pallas_call(functools.partial(pairs_kernel, pieces, share), out_shape=...  32 us
    ppermute x7, waiting for transfers between devices, from_behind(): lax.ppermute(block, axis, [((i - distance) % size, i) for i in range(size)])  14.5 us
    pallas_call x4, Pallas kernels, add_piece(): pl.pallas_call(functools.partial(piece_kernel, first, size), out_shape=(j...  11.7 us
    pallas_call x1, Pallas kernels, padded_rows(): pl.pallas_call(rows_kernel, out_shape=(jax.ShapeDtypeStruct((2, G, G, LAN...  8.57 us
    pallas_call x2, Pallas kernels, take_band(): pl.pallas_call(functools.partial(band_kernel, p), out_shape=jax.ShapeDtyp...  7.67 us
    ppermute x7, starting transfers between devices, from_behind(): lax.ppermute(block, axis, [((i - distance) % size, i) for i in range(size)])  7.01 us
    ppermute x3, starting transfers between devices, per_device(): got = lax.ppermute(energy, 'band', steps.pop(0))  6.12 us
    ppermute x1, waiting for transfers between devices, per_device(): energy = energy + lax.ppermute(energy, 'band', steps.pop(0))  2.19 us
  transfers between devices with their start and end apart: 13, of which 4 were waited for; matrix products, arithmetic and copies ran while one was open for 0% of the time, Pallas kernels for 56%

profile of v17, /device:TPU:0, one launch (start us, length us, event | category | flops | bytes accessed | tf_op | source)
XLA Modules:
  0.0 100.0 jit_solution(2861408924810873793)
XLA Ops:
  0.6 3.8 %take_band.2.refs_0_.own0 = bf16[6912,128]{1,0:T(8,128)(2,1)} custom-call(bf16[13824,128]{1,0:T(8,128)(2,1)} %bitcast.13), custom_call_target="tpu_custom_call" | custom-call | bytes 5308416 | tf_op jit(solution)/shard_map/take_band/pallas_call | solution.py:170
  4.5 0.5 collective-permute-start.1
  5.0 3.8 %take_band.3.own1 = bf16[6912,128]{1,0:T(8,128)(2,1)} custom-call(bf16[13824,128]{1,0:T(8,128)(2,1)} %bitcast.14, bf16[6912,128]{1,0:T(8,128)(2,1)} %take_band.2.refs_0_.own0), custom_call_target="tpu_custom_call" | custom-call | bytes 5308416 | tf_op jit(solution)/shard_map/take_band/pallas_call | solution.py:170
  8.8 2.8 %collective-permute-start = (bf16[6912,128]{1,0:T(8,128)(2,1)}, bf16[6912,128]{1,0:T(8,128)(2,1)}, u32[]{:S(2)}, u32[]{:S(2)}) collective-permute-start(bf16[6912,128]{1,0:T(8,128)(2,1)} %take_band.3.own1), channel_id=1, source_target_pairs={{31,0},{0,1},{1,2},{2,3},{3,4},{4,5},{5,6},{6,7},{7,8},{8,9},{9,10... | collective-permute-start | bytes 5308424 | tf_op jit(solution)/shard_map/ppermute | solution.py:585
  11.7 8.6 %padded_rows.1 = (bf16[2,96,96,128]{3,2,1,0:T(8,128)(2,1)}, bf16[2,3,2304,128]{3,2,1,0:T(8,128)(2,1)}) custom-call(bf16[6912,128]{1,0:T(8,128)(2,1)} %take_band.2.refs_0_.own0, bf16[6912,128]{1,0:T(8,128)(2,1)} %take_band.3.own1, bf16[2,256,256]{2,1,0:T(8,128)(2,1)} %constant.34.clone.sel.refs_6_.refs_8_), custom_call_target="tpu_custom_call" | custom-call | bytes 14155776 | tf_op jit(solution)/shard_map/padded_rows/pallas_call | solution.py:206
  20.2 11.2 %collective-permute-done.1.par = bf16[6912,128]{1,0:T(8,128)(2,1)} collective-permute-done((bf16[6912,128]{1,0:T(8,128)(2,1)}, bf16[6912,128]{1,0:T(8,128)(2,1)}, u32[]{:S(2)}, u32[]{:S(2)}) %collective-permute-start.1) | collective-permute-done | bytes 1769504 | tf_op jit(solution)/shard_map/ppermute | solution.py:585
  31.4 15.5 %pair_terms.2 = (f32[2,3,2304,128]{3,2,1,0:T(8,128)}, bf16[3,2304,128]{2,1,0:T(8,128)(2,1)}, f32[1,1]{1,0:T(1,128)}) custom-call(bf16[2,3,2304,128]{3,2,1,0:T(8,128)(2,1)} %get-tuple-element.26.own, bf16[2,96,96,128]{3,2,1,0:T(8,128)(2,1)} %get-tuple-element.27.own_u, f32[4800,128]{1,0:T(8,128)} %constant.35.clone.kern, ...), custom_call_target="tpu_custom_call" | custom-call | flops 20000000000 | bytes 20000000 | tf_op jit(solution)/shard_map/pair_terms/pallas_call | solution.py:442
  46.9 0.3 collective-permute-start.2
  47.2 3.3 %collective-permute-done.par = bf16[6912,128]{1,0:T(8,128)(2,1)} collective-permute-done((bf16[6912,128]{1,0:T(8,128)(2,1)}, bf16[6912,128]{1,0:T(8,128)(2,1)}, u32[]{:S(2)}, u32[]{:S(2)}) %collective-permute-start) | collective-permute-done | bytes 1769504 | tf_op jit(solution)/shard_map/ppermute | solution.py:585
  50.5 16.5 %pair_terms.3 = (f32[2,3,2304,128]{3,2,1,0:T(8,128)}, bf16[3,768,128]{2,1,0:T(8,128)(2,1)}, bf16[3,768,128]{2,1,0:T(8,128)(2,1)}, bf16[3,384,128]{2,1,0:T(8,128)...) custom-call(bf16[2,3,2304,128]{3,2,1,0:T(8,128)(2,1)} %get-tuple-element.26.own, ...), custom_call_target="tpu_custom_call" | custom-call | flops 20000000000 | bytes 20000000 | tf_op jit(solution)/shard_map/pair_terms/pallas_call | solution.py:442
  67.0 0.1 collective-permute-start.7
  67.0 2.3 %collective-permute-start.9 = (bf16[3,768,128]{2,1,0:T(8,128)(2,1)}, bf16[3,768,128]{2,1,0:T(8,128)(2,1)S(1)}, u32[]{:S(2)}, u32[]{:S(2)}) collective-permute-start(bf16[3,768,128]{2,1,0:T(8,128)(2,1)} %get-tuple-element.37), channel_id=1, source_target_pairs={{1,0},{2,1},{3,2},{4,3},{5,4},{6,5},{7,6},{8,7},{9,8},{10,9},{11,1... | collective-permute-start | bytes 1769480 | tf_op jit(solution)/shard_map/ppermute | solution.py:585
  69.3 0.1 collective-permute-start.11
  69.4 0.4 collective-permute-start.4
  69.8 1.3 %collective-permute-done.4 = f32[1,1]{1,0:T(1,128)} collective-permute-done((f32[1,1]{1,0:T(1,128)}, f32[1,1]{1,0:T(1,128)}, u32[]{:S(2)}, u32[]{:S(2)}) %collective-permute-start.4) | collective-permute-done | bytes 36 | tf_op jit(solution)/shard_map/ppermute | solution.py:616
  72.3 1.4 %collective-permute-start.5 = (f32[1,1]{1,0:T(1,128)}, f32[1,1]{1,0:T(1,128)}, u32[]{:S(2)}, u32[]{:S(2)}) collective-permute-start(f32[1,1]{1,0:T(1,128)} %add.19), channel_id=1, source_target_pairs={{0,4},{1,5},{2,10},{3,7},{4,0},{5,1},{6,14},{7,3},{8,12},{9,13},{1... | collective-permute-start | bytes 20 | tf_op jit(solution)/shard_map/ppermute | solution.py:622
  73.7 2.2 %collective-permute-done.5 = f32[1,1]{1,0:T(1,128)} collective-permute-done((f32[1,1]{1,0:T(1,128)}, f32[1,1]{1,0:T(1,128)}, u32[]{:S(2)}, u32[]{:S(2)}) %collective-permute-start.5) | collective-permute-done | bytes 36 | tf_op jit(solution)/shard_map/ppermute | solution.py:622
  75.9 1.0 collective-permute-start.3
  77.6 0.0 collective-permute-done.7.back1
  77.6 1.4 %collective-permute-start.6 = (f32[1,1]{1,0:T(1,128)}, f32[1,1]{1,0:T(1,128)}, u32[]{:S(2)}, u32[]{:S(2)}) collective-permute-start(f32[1,1]{1,0:T(1,128)} %add.20._), channel_id=1, source_target_pairs={{0,4},{1,9},{2,10},{3,11},{4,0},{5,13},{6,14},{7,15},{8,12},{9,1},... | collective-permute-start | bytes 20 | tf_op jit(solution)/shard_map/ppermute | solution.py:631
  78.9 0.0 collective-permute-done.2.back0
  78.9 3.3 %add_piece.4 = (f32[13824,128]{1,0:T(8,128)}, f32[2,2,8,128]{3,2,1,0:T(8,128)S(1)}) custom-call(bf16[2,3,2304,128]{3,2,1,0:T(8,128)(2,1)} %get-tuple-element.26.own, f32[2,3,2304,128]{3,2,1,0:T(8,128)} %get-tuple-element.30.terms, bf16[3,2304,128]{2,1,0:T(8,128)(2,1)} %collective-permute-done.2.back0, bf16[3,768,128]{2,1,0:T(8,128)(2,1)S(1)} %collective-permute-done.7.back1, ...), custom_call_target="tpu_custom_call" | custom-call | bytes 7077888 | tf_op jit(solution)/shard_map/add_piece/pallas_call | solution.py:555
  82.3 0.0 collective-permute-done.6
  82.9 3.4 %collective-permute-start.8 = (f32[1,1]{1,0:T(1,128)}, f32[1,1]{1,0:T(1,128)}, u32[]{:S(2)}, u32[]{:S(2)}) collective-permute-start(f32[1,1]{1,0:T(1,128)} %add.21._), channel_id=1, source_target_pairs={{0,4},{1,17},{2,10},{3,19},{4,0},{5,21},{6,14},{7,23},{8,12},{9,25... | collective-permute-start | bytes 20 | tf_op jit(solution)/shard_map/ppermute | solution.py:631
  86.3 0.0 collective-permute-done.9.back1
  86.3 3.3 %add_piece.5 = (f32[13824,128]{1,0:T(8,128)}, f32[2,2,8,128]{3,2,1,0:T(8,128)S(1)}) custom-call(bf16[2,3,2304,128]{3,2,1,0:T(8,128)(2,1)} %get-tuple-element.26.own, f32[2,3,2304,128]{3,2,1,0:T(8,128)} %get-tuple-element.30.terms, bf16[3,2304,128]{2,1,0:T(8,128)(2,1)} %collective-permute-done.2.back0, ...), custom_call_target="tpu_custom_call", output_to_operand_aliasing={{0}: (5, {})} | custom-call | bytes 7077888 | tf_op jit(solution)/shard_map/add_piece/pallas_call | solution.py:555
  89.6 0.0 collective-permute-done.8
  90.2 1.4 %collective-permute-start.10 = (f32[1,1]{1,0:T(1,128)}, f32[1,1]{1,0:T(1,128)}, u32[]{:S(2)}, u32[]{:S(2)}) collective-permute-start(f32[1,1]{1,0:T(1,128)} %add.22._), channel_id=1, source_target_pairs={{0,4},{1,3},{2,10},{3,1},{4,0},{5,7},{6,14},{7,5},{8,12},{9,11},{1... | collective-permute-start | bytes 20 | tf_op jit(solution)/shard_map/ppermute | solution.py:631
  91.6 0.0 collective-permute-done.11.back1
  91.6 2.6 %add_piece.6 = (f32[13824,128]{1,0:T(8,128)}, f32[2,2,8,128]{3,2,1,0:T(8,128)S(1)}) custom-call(bf16[2,3,2304,128]{3,2,1,0:T(8,128)(2,1)} %get-tuple-element.26.own, f32[2,3,2304,128]{3,2,1,0:T(8,128)} %get-tuple-element.30.terms, bf16[3,2304,128]{2,1,0:T(8,128)(2,1)} %collective-permute-done.2.back0, ...), custom_call_target="tpu_custom_call", output_to_operand_aliasing={{0}: (5, {})} | custom-call | bytes 3538944 | tf_op jit(solution)/shard_map/add_piece/pallas_call | solution.py:555
  94.2 0.0 collective-permute-done.10
  94.8 0.9 collective-permute-start.12
  95.7 0.0 collective-permute-done.3.back1
  95.7 2.6 %add_piece.7 = (f32[13824,128]{1,0:T(8,128)}, f32[2,2]{1,0:T(2,128)}) custom-call(bf16[2,3,2304,128]{3,2,1,0:T(8,128)(2,1)} %get-tuple-element.26.own, f32[2,3,2304,128]{3,2,1,0:T(8,128)} %get-tuple-element.30.terms, bf16[3,2304,128]{2,1,0:T(8,128)(2,1)} %collective-permute-done.2.back0, ...), custom_call_target="tpu_custom_call", output_to_operand_aliasing={{0}: (8, {})} | custom-call | bytes 3538944 | tf_op jit(solution)/shard_map/add_piece/pallas_call | solution.py:555
  98.3 0.0 collective-permute-done.12
Async XLA Ops:
  4.5 27.0 %collective-permute-start.1 = (bf16[6912,128]{1,0:T(8,128)(2,1)}, bf16[6912,128]{1,0:T(8,128)(2,1)}, u32[]{:S(2)}, u32[]{:S(2)}) collective-permute-start(bf16[6912,128]{1,0:T(8,128)(2,1)} %take_band.2.refs_0_.own0), channel_id=1, source_target_pairs={{31,0},{0,1},{1,2},{2,3},{3,4},{4,5},{5,6},{6,7},{7,8},{8,9},{9,10... | collective-permute-start | bytes 5308424 | tf_op jit(solution)/shard_map/ppermute | solution.py:585
  8.8 41.7 %collective-permute-start = (bf16[6912,128]{1,0:T(8,128)(2,1)}, bf16[6912,128]{1,0:T(8,128)(2,1)}, u32[]{:S(2)}, u32[]{:S(2)}) collective-permute-start(bf16[6912,128]{1,0:T(8,128)(2,1)} %take_band.3.own1), channel_id=1, source_target_pairs={{31,0},{0,1},{1,2},{2,3},{3,4},{4,5},{5,6},{6,7},{7,8},{8,9},{9,10... | collective-permute-start | bytes 5308424 | tf_op jit(solution)/shard_map/ppermute | solution.py:585
  46.9 32.0 %collective-permute-start.2 = (bf16[3,2304,128]{2,1,0:T(8,128)(2,1)}, bf16[3,2304,128]{2,1,0:T(8,128)(2,1)}, u32[]{:S(2)}, u32[]{:S(2)}) collective-permute-start(bf16[3,2304,128]{2,1,0:T(8,128)(2,1)} %get-tuple-element.31), channel_id=1, source_target_pairs={{1,0},{2,1},{3,2},{4,3},{5,4},{6,5},{7,6},{8,7},{9,8},{10,9},{11,1... | collective-permute-start | bytes 5308424 | tf_op jit(solution)/shard_map/ppermute | solution.py:585
  67.0 10.6 %collective-permute-start.7 = (bf16[3,768,128]{2,1,0:T(8,128)(2,1)}, bf16[3,768,128]{2,1,0:T(8,128)(2,1)S(1)}, u32[]{:S(2)}, u32[]{:S(2)}) collective-permute-start(bf16[3,768,128]{2,1,0:T(8,128)(2,1)} %get-tuple-element.34), channel_id=1, source_target_pairs={{1,0},{2,1},{3,2},{4,3},{5,4},{6,5},{7,6},{8,7},{9,8},{10,9},{11,1... | collective-permute-start | bytes 1769480 | tf_op jit(solution)/shard_map/ppermute | solution.py:585
  67.0 19.3 %collective-permute-start.9 = (bf16[3,768,128]{2,1,0:T(8,128)(2,1)}, bf16[3,768,128]{2,1,0:T(8,128)(2,1)S(1)}, u32[]{:S(2)}, u32[]{:S(2)}) collective-permute-start(bf16[3,768,128]{2,1,0:T(8,128)(2,1)} %get-tuple-element.37), channel_id=1, source_target_pairs={{1,0},{2,1},{3,2},{4,3},{5,4},{6,5},{7,6},{8,7},{9,8},{10,9},{11,1... | collective-permute-start | bytes 1769480 | tf_op jit(solution)/shard_map/ppermute | solution.py:585
  69.3 22.3 %collective-permute-start.11 = (bf16[3,384,128]{2,1,0:T(8,128)(2,1)}, bf16[3,384,128]{2,1,0:T(8,128)(2,1)S(1)}, u32[]{:S(2)}, u32[]{:S(2)}) collective-permute-start(bf16[3,384,128]{2,1,0:T(8,128)(2,1)} %get-tuple-element.41), channel_id=1, source_target_pairs={{1,0},{2,1},{3,2},{4,3},{5,4},{6,5},{7,6},{8,7},{9,8},{10,9},{11,1... | collective-permute-start | bytes 884744 | tf_op jit(solution)/shard_map/ppermute | solution.py:585
  69.4 1.7 %collective-permute-start.4 = (f32[1,1]{1,0:T(1,128)}, f32[1,1]{1,0:T(1,128)}, u32[]{:S(2)}, u32[]{:S(2)}) collective-permute-start(f32[1,1]{1,0:T(1,128)} %get-tuple-element.33), channel_id=1, source_target_pairs={{0,1},{1,0},{2,3},{3,2},{4,5},{5,4},{6,7},{7,6},{8,9},{9,8},{10,11... | collective-permute-start | bytes 20 | tf_op jit(solution)/shard_map/ppermute | solution.py:616
  72.3 3.6 %collective-permute-start.5 = (f32[1,1]{1,0:T(1,128)}, f32[1,1]{1,0:T(1,128)}, u32[]{:S(2)}, u32[]{:S(2)}) collective-permute-start(f32[1,1]{1,0:T(1,128)} %add.19), channel_id=1, source_target_pairs={{0,4},{1,5},{2,10},{3,7},{4,0},{5,1},{6,14},{7,3},{8,12},{9,13},{1... | collective-permute-start | bytes 20 | tf_op jit(solution)/shard_map/ppermute | solution.py:622
  75.9 19.8 %collective-permute-start.3 = (bf16[3,384,128]{2,1,0:T(8,128)(2,1)}, bf16[3,384,128]{2,1,0:T(8,128)(2,1)S(1)}, u32[]{:S(2)}, u32[]{:S(2)}) collective-permute-start(bf16[3,384,128]{2,1,0:T(8,128)(2,1)} %get-tuple-element.32), channel_id=1, source_target_pairs={{1,0},{2,1},{3,2},{4,3},{5,4},{6,5},{7,6},{8,7},{9,8},{10,9},{11,1... | collective-permute-start | bytes 884744 | tf_op jit(solution)/shard_map/ppermute | solution.py:585
  77.6 4.7 %collective-permute-start.6 = (f32[1,1]{1,0:T(1,128)}, f32[1,1]{1,0:T(1,128)}, u32[]{:S(2)}, u32[]{:S(2)}) collective-permute-start(f32[1,1]{1,0:T(1,128)} %add.20._), channel_id=1, source_target_pairs={{0,4},{1,9},{2,10},{3,11},{4,0},{5,13},{6,14},{7,15},{8,12},{9,1},... | collective-permute-start | bytes 20 | tf_op jit(solution)/shard_map/ppermute | solution.py:631
  82.9 6.7 %collective-permute-start.8 = (f32[1,1]{1,0:T(1,128)}, f32[1,1]{1,0:T(1,128)}, u32[]{:S(2)}, u32[]{:S(2)}) collective-permute-start(f32[1,1]{1,0:T(1,128)} %add.21._), channel_id=1, source_target_pairs={{0,4},{1,17},{2,10},{3,19},{4,0},{5,21},{6,14},{7,23},{8,12},{9,25... | collective-permute-start | bytes 20 | tf_op jit(solution)/shard_map/ppermute | solution.py:631
  90.2 4.0 %collective-permute-start.10 = (f32[1,1]{1,0:T(1,128)}, f32[1,1]{1,0:T(1,128)}, u32[]{:S(2)}, u32[]{:S(2)}) collective-permute-start(f32[1,1]{1,0:T(1,128)} %add.22._), channel_id=1, source_target_pairs={{0,4},{1,3},{2,10},{3,1},{4,0},{5,7},{6,14},{7,5},{8,12},{9,11},{1... | collective-permute-start | bytes 20 | tf_op jit(solution)/shard_map/ppermute | solution.py:631
  94.8 3.5 %collective-permute-start.12 = (f32[1,1]{1,0:T(1,128)}, f32[1,1]{1,0:T(1,128)}, u32[]{:S(2)}, u32[]{:S(2)}) collective-permute-start(f32[1,1]{1,0:T(1,128)} %add.23._), channel_id=1, source_target_pairs={{0,1},{1,0},{2,3},{3,2},{4,5},{5,4},{6,7},{7,6},{8,9},{9,8},{10,11... | collective-permute-start | bytes 20 | tf_op jit(solution)/shard_map/ppermute | solution.py:629

commit v18 on v17

--- a/solution.py
+++ b/solution.py
@@ -27,7 +27,7 @@
 STEP_ROWS = PLANES * QUADS
 THIRD = G * QUADS
 STEPS = G // PLANES
-PIECES = (2, 2, 1, 1)
+PIECES = (3, 2, 1)
 WAVE_UNIT = 0.05
 SCREEN_SQ = 0.0121
 MIB = 1024 * 1024
@@ -422,7 +422,7 @@
             copy_rows(par_ov, source, par_out[i], row, STEP_ROWS, sems.at[6 + i]).start()
             ch += 1
 
-    energy = jnp.zeros((1, 1), F32) + jnp.sum(total_ref[...]) * F32(share)
+    energy = jnp.zeros((8, LANES), F32) + jnp.sum(total_ref[...]) * F32(share)
     if earlier:
         energy = energy + before_v[...]
     energy_v[...] = energy
@@ -444,7 +444,7 @@
         out_shape=(
             jax.ShapeDtypeStruct((2, 3, THIRD, LANES), F32),
             *[jax.ShapeDtypeStruct((3, steps * STEP_ROWS, LANES), BF16) for steps in pieces],
-            jax.ShapeDtypeStruct((1, 1), F32),
+            jax.ShapeDtypeStruct((8, LANES), F32),
         ),
         in_specs=[hbm] * (4 + len(earlier) + len(tables)),
         out_specs=(hbm,) * (2 + len(pieces)),
@@ -461,8 +461,8 @@
             pltpu.VMEM((KPAD * G, 4 * LANES), BF16),
             pltpu.VMEM((ROWS, LANES), BF16),
             pltpu.VMEM((8, LANES), F32),
-            pltpu.VMEM((1, 1), F32),
-            pltpu.VMEM((1, 1), F32),
+            pltpu.VMEM((8, LANES), F32),
+            pltpu.VMEM((8, LANES), F32),
             *[pltpu.VMEM(table.shape, BF16) for table in tables],
             pltpu.SemaphoreType.DMA((2,)),
             pltpu.SemaphoreType.DMA((len(tables),)),
@@ -478,7 +478,7 @@
     )(own, own_u, kern, partner, *earlier, *tables)
 
 
-def piece_kernel(first, size, own, terms, back0, back1, _, *rest):
+def piece_kernel(first, size, own, terms, back0, back1, *rest):
     last = first + size == THIRD
     earlier = rest[: len(rest) - 12]
     out, gram_out, own_v, terms_v, back_v, out_v, gram_ref, gram_v, value_ref = rest[-12:-3]
@@ -505,7 +505,7 @@
     if last:
         gram_loads = [
             pltpu.make_async_copy(src, gram_v.at[i], gram_sems.at[i])
-            for i, src in enumerate(earlier[:-1])
+            for i, src in enumerate(earlier[1:-1])
         ]
         for load in gram_loads:
             load.start()
@@ -550,7 +550,7 @@
 def add_piece(first, size, own, terms, back0, back1, energy, grams, out, interpret=False):
     hbm = pl.BlockSpec(memory_space=pl.ANY)
     last = first + size == THIRD
-    earlier = [] if out is None else [*(grams if last else []), out]
+    earlier = [] if out is None else [*([energy, *grams] if last else []), out]
     gram_shape = (2, 2, 8, LANES)
     return pl.pallas_call(
         functools.partial(piece_kernel, first, size),
@@ -558,7 +558,7 @@
             jax.ShapeDtypeStruct((2 * ROWS, LANES), F32),
             jax.ShapeDtypeStruct((2, 2) if last else gram_shape, F32),
         ),
-        in_specs=[hbm] * (5 + len(earlier)),
+        in_specs=[hbm] * (4 + len(earlier)),
         out_specs=(hbm, hbm),
         scratch_shapes=[
             pltpu.VMEM((2, 3, size, LANES), BF16),
@@ -572,12 +572,12 @@
             pltpu.SemaphoreType.DMA((len(PIECES),)),
             pltpu.SemaphoreType.DMA((2,)),
         ],
-        input_output_aliases={4 + len(earlier): 0} if earlier else {},
+        input_output_aliases={3 + len(earlier): 0} if earlier else {},
         compiler_params=pltpu.CompilerParams(vmem_limit_bytes=52 * MIB),
         cost_estimate=cost(72 * size * LANES),
         interpret=interpret,
         name="add_piece",
-    )(own, terms, back0, back1, energy, *earlier)
+    )(own, terms, back0, back1, *earlier)
 
 
 def from_behind(block, axis, distance):
@@ -627,6 +627,7 @@
         got, last = None, piece is back1[-1]
         if last and size & (size - 1) == 0:
             got = lax.ppermute(energy, "band", swap)
+            energy = energy[:1, :1]
         elif steps:
             got = lax.ppermute(energy, "band", steps.pop(0))
         exchange, gram = add_piece(
@@ -634,7 +635,7 @@
         )
         if got is not None and last:
             odd = lax.axis_index("band") % 2 == 1
-            energy = jnp.where(odd, energy, after(got, gram))
+            energy = jnp.where(odd, energy, after(got, gram)[:1, :1])
         elif got is not None:
             energy = energy + after(got, gram)
         grams.append(gram)

time: 100 us -> 95.5 us (0.955)
  starting transfers between devices: 15.8 us -> 8.64 us
  waiting for transfers between devices: 18 us -> 23 us
  between operations: 6.29 us -> 3.1 us
  Pallas kernels: 60 us -> 58.8 us
    ppermute x1 -> x2, waiting for transfers between devices: 2.19 us -> 7.21 us  [per_device(): energy = energy + lax.ppermute(energy, 'band', steps.pop(0))]
    ppermute x3 -> x2, starting transfers between devices: 6.12 us -> 2.08 us  [per_device(): got = lax.ppermute(energy, 'band', steps.pop(0))]
    ppermute x1 -> x2, starting transfers between devices: 1.37 us -> 0.01 us  [per_device(): energy = energy + lax.ppermute(energy, 'band', steps.pop(0))]
    ppermute x7 -> x6, starting transfers between devices: 7.01 us -> 6.04 us  [from_behind(): lax.ppermute(block, axis, [((i - distance) % size, i) for i in range(size)])]
    pallas_call x4 -> x3, Pallas kernels: 11.7 us -> 11.4 us  [add_piece(): pl.pallas_call(functools.partial(piece_kernel, first, size), out_shape=(j...]
    ppermute x7 -> x6, waiting for transfers between devices: 14.5 us -> 14.5 us  [from_behind(): lax.ppermute(block, axis, [((i - distance) % size, i) for i in range(size)])]
  transfers between devices with their start and end apart: 13 -> 12, of which waited for: 4 -> 5; matrix products, arithmetic and copies ran while one was open for 0% -> 1% of each run, Pallas kernels for 56% -> 58%
where the time goes in v18:
time: 95.5 us; the launch traced here: 95.2 us
  Pallas kernels  58.8 us (62%)
  waiting for transfers between devices  23 us (24%)
  starting transfers between devices  8.64 us (9%)
  between operations  3.1 us (3%)
  local copies, waits for them, and re-layouts  0.99 us (1%)
    pallas_call x2, Pallas kernels, pair_terms(): pl.pallas_call(functools.partial(pairs_kernel, pieces, share), out_shape=...  31.2 us
    ppermute x6, waiting for transfers between devices, from_behind(): lax.ppermute(block, axis, [((i - distance) % size, i) for i in range(size)])  14.5 us
    pallas_call x3, Pallas kernels, add_piece(): pl.pallas_call(functools.partial(piece_kernel, first, size), out_shape=(j...  11.4 us
    pallas_call x1, Pallas kernels, padded_rows(): pl.pallas_call(rows_kernel, out_shape=(jax.ShapeDtypeStruct((2, G, G, LAN...  8.58 us
    pallas_call x2, Pallas kernels, take_band(): pl.pallas_call(functools.partial(band_kernel, p), out_shape=jax.ShapeDtyp...  7.66 us
    ppermute x2, waiting for transfers between devices, per_device(): energy = energy + lax.ppermute(energy, 'band', steps.pop(0))  7.21 us
    ppermute x6, starting transfers between devices, from_behind(): lax.ppermute(block, axis, [((i - distance) % size, i) for i in range(size)])  6.04 us
    ppermute x2, starting transfers between devices, per_device(): got = lax.ppermute(energy, 'band', steps.pop(0))  2.08 us
  transfers between devices with their start and end apart: 12, of which 5 were waited for; matrix products, arithmetic and copies ran while one was open for 1% of the time, Pallas kernels for 58%

profile of v18, /device:TPU:0, one launch (start us, length us, event | category | flops | bytes accessed | tf_op | source)
XLA Modules:
  0.0 95.2 jit_solution(13563540090702995556)
XLA Ops:
  0.6 3.8 %take_band.2.refs_0_.own0 = bf16[6912,128]{1,0:T(8,128)(2,1)} custom-call(bf16[13824,128]{1,0:T(8,128)(2,1)} %bitcast.13), custom_call_target="tpu_custom_call" | custom-call | bytes 5308416 | tf_op jit(solution)/shard_map/take_band/pallas_call | solution.py:170
  4.5 0.5 collective-permute-start.1
  5.0 3.8 %take_band.3.own1 = bf16[6912,128]{1,0:T(8,128)(2,1)} custom-call(bf16[13824,128]{1,0:T(8,128)(2,1)} %bitcast.14, bf16[6912,128]{1,0:T(8,128)(2,1)} %take_band.2.refs_0_.own0), custom_call_target="tpu_custom_call" | custom-call | bytes 5308416 | tf_op jit(solution)/shard_map/take_band/pallas_call | solution.py:170
  8.8 2.8 %collective-permute-start = (bf16[6912,128]{1,0:T(8,128)(2,1)}, bf16[6912,128]{1,0:T(8,128)(2,1)}, u32[]{:S(2)}, u32[]{:S(2)}) collective-permute-start(bf16[6912,128]{1,0:T(8,128)(2,1)} %take_band.3.own1), channel_id=1, source_target_pairs={{31,0},{0,1},{1,2},{2,3},{3,4},{4,5},{5,6},{6,7},{7,8},{8,9},{9,10... | collective-permute-start | bytes 5308424 | tf_op jit(solution)/shard_map/ppermute | solution.py:585
  11.7 8.6 %padded_rows.1 = (bf16[2,96,96,128]{3,2,1,0:T(8,128)(2,1)}, bf16[2,3,2304,128]{3,2,1,0:T(8,128)(2,1)}) custom-call(bf16[6912,128]{1,0:T(8,128)(2,1)} %take_band.2.refs_0_.own0, bf16[6912,128]{1,0:T(8,128)(2,1)} %take_band.3.own1, bf16[2,256,256]{2,1,0:T(8,128)(2,1)} %constant.34.clone.sel.refs_6_.refs_8_), custom_call_target="tpu_custom_call" | custom-call | bytes 14155776 | tf_op jit(solution)/shard_map/padded_rows/pallas_call | solution.py:206
  20.2 11.2 %collective-permute-done.1.par = bf16[6912,128]{1,0:T(8,128)(2,1)} collective-permute-done((bf16[6912,128]{1,0:T(8,128)(2,1)}, bf16[6912,128]{1,0:T(8,128)(2,1)}, u32[]{:S(2)}, u32[]{:S(2)}) %collective-permute-start.1) | collective-permute-done | bytes 1769504 | tf_op jit(solution)/shard_map/ppermute | solution.py:585
  31.4 15.5 %pair_terms.2 = (f32[2,3,2304,128]{3,2,1,0:T(8,128)}, bf16[3,2304,128]{2,1,0:T(8,128)(2,1)}, f32[8,128]{1,0:T(8,128)}) custom-call(bf16[2,3,2304,128]{3,2,1,0:T(8,128)(2,1)} %get-tuple-element.22.own, bf16[2,96,96,128]{3,2,1,0:T(8,128)(2,1)} %get-tuple-element.23.own_u, f32[4800,128]{1,0:T(8,128)} %constant.35.clone.kern, ...), custom_call_target="tpu_custom_call" | custom-call | flops 20000000000 | bytes 20000000 | tf_op jit(solution)/shard_map/pair_terms/pallas_call | solution.py:442
  46.9 0.3 collective-permute-start.2
  47.2 3.3 %collective-permute-done.par = bf16[6912,128]{1,0:T(8,128)(2,1)} collective-permute-done((bf16[6912,128]{1,0:T(8,128)(2,1)}, bf16[6912,128]{1,0:T(8,128)(2,1)}, u32[]{:S(2)}, u32[]{:S(2)}) %collective-permute-start) | collective-permute-done | bytes 1769504 | tf_op jit(solution)/shard_map/ppermute | solution.py:585
  50.5 15.7 %pair_terms.3 = (f32[2,3,2304,128]{3,2,1,0:T(8,128)}, bf16[3,1152,128]{2,1,0:T(8,128)(2,1)}, bf16[3,768,128]{2,1,0:T(8,128)(2,1)}, bf16[3,384,128]{2,1,0:T(8,128)(2,1)}, f32[8,128]{1,0:T(8,128)}) custom-call(bf16[2,3,2304,128]{3,2,1,0:T(8,128)(2,1)} %get-tuple-element.22.own, bf16[2,96,96,128]{3,2,1,0:T(8,128)(2,1)} %get-tuple-element.23.own_u, ...), custom_call_target="tpu_custom_call" | custom-call | flops 20000000000 | bytes 20000000 | tf_op jit(solution)/shard_map/pair_terms/pallas_call | solution.py:442
  66.2 0.1 collective-permute-start.8
  66.3 2.3 %collective-permute-start.10 = (bf16[3,768,128]{2,1,0:T(8,128)(2,1)}, bf16[3,768,128]{2,1,0:T(8,128)(2,1)S(1)}, u32[]{:S(2)}, u32[]{:S(2)}) collective-permute-start(bf16[3,768,128]{2,1,0:T(8,128)(2,1)} %get-tuple-element.33), channel_id=1, source_target_pairs={{1,0},{2,1},{3,2},{4,3},{5,4},{6,5},{7,6},{8,7},{9,8},{10,9},{11,1... | collective-permute-start | bytes 1769480 | tf_op jit(solution)/shard_map/ppermute | solution.py:585
  68.6 0.1 collective-permute-start.3
  68.6 0.4 collective-permute-start.4
  69.1 1.3 %collective-permute-done.4 = f32[8,128]{1,0:T(8,128)S(1)} collective-permute-done((f32[8,128]{1,0:T(8,128)}, f32[8,128]{1,0:T(8,128)S(1)}, u32[]{:S(2)}, u32[]{:S(2)}) %collective-permute-start.4) | collective-permute-done | bytes 4128 | tf_op jit(solution)/shard_map/ppermute | solution.py:616
  70.4 0.7 add.19
  71.0 0.0 collective-permute-start.5
  71.0 3.6 %collective-permute-done.5 = f32[8,128]{1,0:T(8,128)S(1)} collective-permute-done((f32[8,128]{1,0:T(8,128)S(1)}, f32[8,128]{1,0:T(8,128)S(1)}, u32[]{:S(2)}, u32[]{:S(2)}) %collective-permute-start.5) | collective-permute-done | bytes 4128 | tf_op jit(solution)/shard_map/ppermute | solution.py:622
  74.7 0.0 collective-permute-start.6
  74.7 3.6 %collective-permute-done.6 = f32[8,128]{1,0:T(8,128)S(1)} collective-permute-done((f32[8,128]{1,0:T(8,128)S(1)}, f32[8,128]{1,0:T(8,128)S(1)}, u32[]{:S(2)}, u32[]{:S(2)}) %collective-permute-start.6) | collective-permute-done | bytes 4128 | tf_op jit(solution)/shard_map/ppermute | solution.py:622
  78.3 0.0 collective-permute-start.7
  78.3 0.0 collective-permute-done.8.back1
  78.3 0.0 collective-permute-done.2.back0
  78.3 4.9 %add_piece.3 = (f32[13824,128]{1,0:T(8,128)}, f32[2,2,8,128]{3,2,1,0:T(8,128)S(1)}) custom-call(bf16[2,3,2304,128]{3,2,1,0:T(8,128)(2,1)} %get-tuple-element.22.own, f32[2,3,2304,128]{3,2,1,0:T(8,128)} %get-tuple-element.26.terms, bf16[3,2304,128]{2,1,0:T(8,128)(2,1)} %collective-permute-done.2.back0, bf16[3,1152,128]{2,1,0:T(8,128)(2,1)S(1)} %collective-permute-done.8.back1), custom_call_target="tpu_custom_call" | custom-call | bytes 10616832 | tf_op jit(solution)/shard_map/add_piece/pallas_call | solution.py:555
  83.1 0.0 collective-permute-done.7
  83.2 2.1 %collective-permute-start.9 = (f32[8,128]{1,0:T(8,128)S(1)}, f32[8,128]{1,0:T(8,128)S(1)}, u32[]{:S(2)}, u32[]{:S(2)}) collective-permute-start(f32[8,128]{1,0:T(8,128)S(1)} %add.22), channel_id=1, source_target_pairs={{0,4},{1,3},{2,10},{3,1},{4,0},{5,7},{6,14},{7,5},{8,12},{9,11},{1... | collective-permute-start | bytes 12296 | tf_op jit(solution)/shard_map/ppermute | solution.py:632
  85.2 0.0 collective-permute-done.10.back1
  85.3 3.3 %add_piece.4 = (f32[13824,128]{1,0:T(8,128)}, f32[2,2,8,128]{3,2,1,0:T(8,128)S(1)}) custom-call(bf16[2,3,2304,128]{3,2,1,0:T(8,128)(2,1)} %get-tuple-element.22.own, f32[2,3,2304,128]{3,2,1,0:T(8,128)} %get-tuple-element.26.terms, bf16[3,2304,128]{2,1,0:T(8,128)(2,1)} %collective-permute-done.2.back0, ...), custom_call_target="tpu_custom_call", output_to_operand_aliasing={{0}: (4, {})} | custom-call | bytes 7077888 | tf_op jit(solution)/shard_map/add_piece/pallas_call | solution.py:555
  88.5 0.0 collective-permute-done.9
  88.6 0.1 collective-permute-start.11
  88.7 0.5 slice.6.rest_0_
  89.2 0.0 collective-permute-done.3.back1
  89.2 3.2 %add_piece.5 = (f32[13824,128]{1,0:T(8,128)}, f32[2,2]{1,0:T(2,128)}) custom-call(bf16[2,3,2304,128]{3,2,1,0:T(8,128)(2,1)} %get-tuple-element.22.own, f32[2,3,2304,128]{3,2,1,0:T(8,128)} %get-tuple-element.26.terms, bf16[3,2304,128]{2,1,0:T(8,128)(2,1)} %collective-permute-done.2.back0, ...), custom_call_target="tpu_custom_call", output_to_operand_aliasing={{0}: (7, {})} | custom-call | bytes 3538944 | tf_op jit(solution)/shard_map/add_piece/pallas_call | solution.py:555
  92.4 0.0 collective-permute-done.11
  92.4 0.5 slice.7
  (4 shorter events, 0.0 us)
Async XLA Ops:
  4.5 27.0 %collective-permute-start.1 = (bf16[6912,128]{1,0:T(8,128)(2,1)}, bf16[6912,128]{1,0:T(8,128)(2,1)}, u32[]{:S(2)}, u32[]{:S(2)}) collective-permute-start(bf16[6912,128]{1,0:T(8,128)(2,1)} %take_band.2.refs_0_.own0), channel_id=1, source_target_pairs={{31,0},{0,1},{1,2},{2,3},{3,4},{4,5},{5,6},{6,7},{7,8},{8,9},{9,10... | collective-permute-start | bytes 5308424 | tf_op jit(solution)/shard_map/ppermute | solution.py:585
  8.8 41.7 %collective-permute-start = (bf16[6912,128]{1,0:T(8,128)(2,1)}, bf16[6912,128]{1,0:T(8,128)(2,1)}, u32[]{:S(2)}, u32[]{:S(2)}) collective-permute-start(bf16[6912,128]{1,0:T(8,128)(2,1)} %take_band.3.own1), channel_id=1, source_target_pairs={{31,0},{0,1},{1,2},{2,3},{3,4},{4,5},{5,6},{6,7},{7,8},{8,9},{9,10... | collective-permute-start | bytes 5308424 | tf_op jit(solution)/shard_map/ppermute | solution.py:585
  46.9 31.4 %collective-permute-start.2 = (bf16[3,2304,128]{2,1,0:T(8,128)(2,1)}, bf16[3,2304,128]{2,1,0:T(8,128)(2,1)}, u32[]{:S(2)}, u32[]{:S(2)}) collective-permute-start(bf16[3,2304,128]{2,1,0:T(8,128)(2,1)} %get-tuple-element.27), channel_id=1, source_target_pairs={{1,0},{2,1},{3,2},{4,3},{5,4},{6,5},{7,6},{8,7},{9,8},{10,9},{11,1... | collective-permute-start | bytes 5308424 | tf_op jit(solution)/shard_map/ppermute | solution.py:585
  66.2 12.1 %collective-permute-start.8 = (bf16[3,1152,128]{2,1,0:T(8,128)(2,1)}, bf16[3,1152,128]{2,1,0:T(8,128)(2,1)S(1)}, u32[]{:S(2)}, u32[]{:S(2)}) collective-permute-start(bf16[3,1152,128]{2,1,0:T(8,128)(2,1)} %get-tuple-element.30), channel_id=1, source_target_pairs={{1,0},{2,1},{3,2},{4,3},{5,4},{6,5},{7,6},{8,7},{9,8},{10,9},{11,1... | collective-permute-start | bytes 2654216 | tf_op jit(solution)/shard_map/ppermute | solution.py:585
  66.3 19.0 %collective-permute-start.10 = (bf16[3,768,128]{2,1,0:T(8,128)(2,1)}, bf16[3,768,128]{2,1,0:T(8,128)(2,1)S(1)}, u32[]{:S(2)}, u32[]{:S(2)}) collective-permute-start(bf16[3,768,128]{2,1,0:T(8,128)(2,1)} %get-tuple-element.33), channel_id=1, source_target_pairs={{1,0},{2,1},{3,2},{4,3},{5,4},{6,5},{7,6},{8,7},{9,8},{10,9},{11,1... | collective-permute-start | bytes 1769480 | tf_op jit(solution)/shard_map/ppermute | solution.py:585
  68.6 20.6 %collective-permute-start.3 = (bf16[3,384,128]{2,1,0:T(8,128)(2,1)}, bf16[3,384,128]{2,1,0:T(8,128)(2,1)S(1)}, u32[]{:S(2)}, u32[]{:S(2)}) collective-permute-start(bf16[3,384,128]{2,1,0:T(8,128)(2,1)} %get-tuple-element.28), channel_id=1, source_target_pairs={{1,0},{2,1},{3,2},{4,3},{5,4},{6,5},{7,6},{8,7},{9,8},{10,9},{11,1... | collective-permute-start | bytes 884744 | tf_op jit(solution)/shard_map/ppermute | solution.py:585
  68.6 1.7 %collective-permute-start.4 = (f32[8,128]{1,0:T(8,128)}, f32[8,128]{1,0:T(8,128)S(1)}, u32[]{:S(2)}, u32[]{:S(2)}) collective-permute-start(f32[8,128]{1,0:T(8,128)} %get-tuple-element.29), channel_id=1, source_target_pairs={{0,1},{1,0},{2,3},{3,2},{4,5},{5,4},{6,7},{7,6},{8,9},{9,8},{10,11... | collective-permute-start | bytes 12296 | tf_op jit(solution)/shard_map/ppermute | solution.py:616
  71.0 3.6 %collective-permute-start.5 = (f32[8,128]{1,0:T(8,128)S(1)}, f32[8,128]{1,0:T(8,128)S(1)}, u32[]{:S(2)}, u32[]{:S(2)}) collective-permute-start(f32[8,128]{1,0:T(8,128)S(1)} %add.19), channel_id=1, source_target_pairs={{0,4},{1,5},{2,10},{3,7},{4,0},{5,1},{6,14},{7,3},{8,12},{9,13},{1... | collective-permute-start | bytes 12296 | tf_op jit(solution)/shard_map/ppermute | solution.py:622
  74.7 3.6 %collective-permute-start.6 = (f32[8,128]{1,0:T(8,128)S(1)}, f32[8,128]{1,0:T(8,128)S(1)}, u32[]{:S(2)}, u32[]{:S(2)}) collective-permute-start(f32[8,128]{1,0:T(8,128)S(1)} %add.20), channel_id=1, source_target_pairs={{0,4},{1,9},{2,10},{3,11},{4,0},{5,13},{6,14},{7,15},{8,12},{9,1},... | collective-permute-start | bytes 12296 | tf_op jit(solution)/shard_map/ppermute | solution.py:622
  78.3 4.9 %collective-permute-start.7 = (f32[8,128]{1,0:T(8,128)S(1)}, f32[8,128]{1,0:T(8,128)S(1)}, u32[]{:S(2)}, u32[]{:S(2)}) collective-permute-start(f32[8,128]{1,0:T(8,128)S(1)} %add.21), channel_id=1, source_target_pairs={{0,4},{1,17},{2,10},{3,19},{4,0},{5,21},{6,14},{7,23},{8,12},{9,25... | collective-permute-start | bytes 12296 | tf_op jit(solution)/shard_map/ppermute | solution.py:632
  83.2 5.4 %collective-permute-start.9 = (f32[8,128]{1,0:T(8,128)S(1)}, f32[8,128]{1,0:T(8,128)S(1)}, u32[]{:S(2)}, u32[]{:S(2)}) collective-permute-start(f32[8,128]{1,0:T(8,128)S(1)} %add.22), channel_id=1, source_target_pairs={{0,4},{1,3},{2,10},{3,1},{4,0},{5,7},{6,14},{7,5},{8,12},{9,11},{1... | collective-permute-start | bytes 12296 | tf_op jit(solution)/shard_map/ppermute | solution.py:632
  88.6 3.8 %collective-permute-start.11 = (f32[8,128]{1,0:T(8,128)S(1)}, f32[8,128]{1,0:T(8,128)S(1)}, u32[]{:S(2)}, u32[]{:S(2)}) collective-permute-start(f32[8,128]{1,0:T(8,128)S(1)} %add.23), channel_id=1, source_target_pairs={{0,1},{1,0},{2,3},{3,2},{4,5},{5,4},{6,7},{7,6},{8,9},{9,8},{10,11... | collective-permute-start | bytes 12296 | tf_op jit(solution)/shard_map/ppermute | solution.py:629

commit v19 on v18

--- a/solution.py
+++ b/solution.py
@@ -585,6 +585,20 @@
     return lax.ppermute(block, axis, [((i - distance) % size, i) for i in range(size)])
 
 
+def send_among_odd(value, axis, bits):
+    size = lax.axis_size(axis)
+    aside = [4 if size > 4 else 2, 8 if size > 8 else 2]
+    flips = sorted({bits[0], bits[-1], sum(bits)})
+    routes = [[(i, i ^ (f if i % 2 else aside[i // 2 % 2])) for i in range(size)] for f in flips]
+    return [lax.ppermute(value, axis, route) for route in routes]
+
+
+def add_up(value, got):
+    if len(got) == 1:
+        return value + got[0]
+    return (value + got[0]) + (got[1] + got[2])
+
+
 def after(values, other):
     return lax.optimization_barrier((values, other))[0]
 
@@ -614,12 +628,11 @@
     else:
         swap = [(i, i ^ 1) for i in range(size)]
         energy = energy + lax.ppermute(energy, "band", swap)
-        steps = [1 << b for b in range(1, size.bit_length() - 1)]
-        steps = [b for b in steps if b != 2] + [b for b in steps if b == 2]
-        aside = [4 if size > 4 else 2, 8 if size > 8 else 2]
-        steps = [[(i, i ^ (b if i % 2 else aside[i // 2 % 2])) for i in range(size)] for b in steps]
+        bits = [1 << b for b in range(2, size.bit_length() - 1)]
+        steps = [bits[:1]] + [bits[i : i + 2] for i in range(1, len(bits), 2)]
+        steps = [group for group in steps + [[2][: size // 4]] if group]
     while len(steps) > len(back1) - 1:
-        energy = energy + lax.ppermute(energy, "band", steps.pop(0))
+        energy = add_up(energy, send_among_odd(energy, "band", steps.pop(0)))
     exchange, grams = None, []
     first = 0
     for count, piece in zip(PIECES, back1):
@@ -629,7 +642,7 @@
             got = lax.ppermute(energy, "band", swap)
             energy = energy[:1, :1]
         elif steps:
-            got = lax.ppermute(energy, "band", steps.pop(0))
+            got = send_among_odd(energy, "band", steps.pop(0))
         exchange, gram = add_piece(
             first, count, thirds, terms, back0, piece, energy, grams, exchange
         )
@@ -637,7 +650,7 @@
             odd = lax.axis_index("band") % 2 == 1
             energy = jnp.where(odd, energy, after(got, gram)[:1, :1])
         elif got is not None:
-            energy = energy + after(got, gram)
+            energy = add_up(energy, after(got, gram))
         grams.append(gram)
         first += count
     exchange = exchange.reshape(ROWS, 2, LANES).transpose(1, 0, 2).reshape(2, NGRID)

time: 95.5 us -> 97.2 us (1.018)
  starting transfers between devices: 8.64 us -> 11 us
    ppermute x4 -> x5, waiting for transfers between devices: 7.21 us -> 3.89 us  [send_among_odd(): return [lax.ppermute(value, axis, route) for route in routes]]
    ppermute x6, waiting for transfers between devices: 14.5 us -> 17 us  [from_behind(): lax.ppermute(block, axis, [((i - distance) % size, i) for i in range(size)])]
    ppermute x1, starting transfers between devices: 0.07 us -> 2.35 us  [per_device(): got = lax.ppermute(energy, 'band', swap)]
    ppermute x4 -> x5, starting transfers between devices: 2.08 us -> 2.13 us  [send_among_odd(): return [lax.ppermute(value, axis, route) for route in routes]]
  transfers between devices with their start and end apart: 12 -> 13, of which waited for: 5 -> 6; matrix products, arithmetic and copies ran while one was open for 1% -> 1% of each run, Pallas kernels for 58% -> 57%
where the time goes in v19:
time: 97.2 us; the launch traced here: 96.9 us
  Pallas kernels  58.8 us (60%)
  waiting for transfers between devices  22.2 us (23%)
  starting transfers between devices  11 us (11%)
  between operations  3.21 us (3%)
  local copies, waits for them, and re-layouts  1.1 us (1%)
    pallas_call x2, Pallas kernels, pair_terms(): pl.pallas_call(functools.partial(pairs_kernel, pieces, share), out_shape=...  31.2 us
    ppermute x6, waiting for transfers between devices, from_behind(): lax.ppermute(block, axis, [((i - distance) % size, i) for i in range(size)])  17 us
    pallas_call x3, Pallas kernels, add_piece(): pl.pallas_call(functools.partial(piece_kernel, first, size), out_shape=(j...  11.4 us
    pallas_call x1, Pallas kernels, padded_rows(): pl.pallas_call(rows_kernel, out_shape=(jax.ShapeDtypeStruct((2, G, G, LAN...  8.58 us
    pallas_call x2, Pallas kernels, take_band(): pl.pallas_call(functools.partial(band_kernel, p), out_shape=jax.ShapeDtyp...  7.67 us
    ppermute x6, starting transfers between devices, from_behind(): lax.ppermute(block, axis, [((i - distance) % size, i) for i in range(size)])  6.04 us
    ppermute x5, waiting for transfers between devices, send_among_odd(): return [lax.ppermute(value, axis, route) for route in routes]  3.89 us
    ppermute x1, starting transfers between devices, per_device(): got = lax.ppermute(energy, 'band', swap)  2.35 us
  transfers between devices with their start and end apart: 13, of which 6 were waited for; matrix products, arithmetic and copies ran while one was open for 1% of the time, Pallas kernels for 57%

profile of v19, /device:TPU:0, one launch (start us, length us, event | category | flops | bytes accessed | tf_op | source)
XLA Modules:
  0.0 96.9 jit_solution(14781719066715904904)
XLA Ops:
  0.6 3.8 %take_band.2.refs_0_.own0 = bf16[6912,128]{1,0:T(8,128)(2,1)} custom-call(bf16[13824,128]{1,0:T(8,128)(2,1)} %bitcast.13), custom_call_target="tpu_custom_call" | custom-call | bytes 5308416 | tf_op jit(solution)/shard_map/take_band/pallas_call | solution.py:170
  4.5 0.5 collective-permute-start.1
  5.0 3.8 %take_band.3.own1 = bf16[6912,128]{1,0:T(8,128)(2,1)} custom-call(bf16[13824,128]{1,0:T(8,128)(2,1)} %bitcast.14, bf16[6912,128]{1,0:T(8,128)(2,1)} %take_band.2.refs_0_.own0), custom_call_target="tpu_custom_call" | custom-call | bytes 5308416 | tf_op jit(solution)/shard_map/take_band/pallas_call | solution.py:170
  8.8 2.8 %collective-permute-start = (bf16[6912,128]{1,0:T(8,128)(2,1)}, bf16[6912,128]{1,0:T(8,128)(2,1)}, u32[]{:S(2)}, u32[]{:S(2)}) collective-permute-start(bf16[6912,128]{1,0:T(8,128)(2,1)} %take_band.3.own1), channel_id=1, source_target_pairs={{31,0},{0,1},{1,2},{2,3},{3,4},{4,5},{5,6},{6,7},{7,8},{8,9},{9,10... | collective-permute-start | bytes 5308424 | tf_op jit(solution)/shard_map/ppermute | solution.py:585
  11.7 8.6 %padded_rows.1 = (bf16[2,96,96,128]{3,2,1,0:T(8,128)(2,1)}, bf16[2,3,2304,128]{3,2,1,0:T(8,128)(2,1)}) custom-call(bf16[6912,128]{1,0:T(8,128)(2,1)} %take_band.2.refs_0_.own0, bf16[6912,128]{1,0:T(8,128)(2,1)} %take_band.3.own1, bf16[2,256,256]{2,1,0:T(8,128)(2,1)} %constant.34.clone.sel.refs_6_.refs_8_), custom_call_target="tpu_custom_call" | custom-call | bytes 14155776 | tf_op jit(solution)/shard_map/padded_rows/pallas_call | solution.py:206
  20.2 11.2 %collective-permute-done.1.par = bf16[6912,128]{1,0:T(8,128)(2,1)} collective-permute-done((bf16[6912,128]{1,0:T(8,128)(2,1)}, bf16[6912,128]{1,0:T(8,128)(2,1)}, u32[]{:S(2)}, u32[]{:S(2)}) %collective-permute-start.1) | collective-permute-done | bytes 1769504 | tf_op jit(solution)/shard_map/ppermute | solution.py:585
  31.4 15.5 %pair_terms.2 = (f32[2,3,2304,128]{3,2,1,0:T(8,128)}, bf16[3,2304,128]{2,1,0:T(8,128)(2,1)}, f32[8,128]{1,0:T(8,128)}) custom-call(bf16[2,3,2304,128]{3,2,1,0:T(8,128)(2,1)} %get-tuple-element.24.own, bf16[2,96,96,128]{3,2,1,0:T(8,128)(2,1)} %get-tuple-element.25.own_u, f32[4800,128]{1,0:T(8,128)} %constant.35.clone.kern, ...), custom_call_target="tpu_custom_call" | custom-call | flops 20000000000 | bytes 20000000 | tf_op jit(solution)/shard_map/pair_terms/pallas_call | solution.py:442
  46.9 0.3 collective-permute-start.2
  47.2 3.3 %collective-permute-done.par = bf16[6912,128]{1,0:T(8,128)(2,1)} collective-permute-done((bf16[6912,128]{1,0:T(8,128)(2,1)}, bf16[6912,128]{1,0:T(8,128)(2,1)}, u32[]{:S(2)}, u32[]{:S(2)}) %collective-permute-start) | collective-permute-done | bytes 1769504 | tf_op jit(solution)/shard_map/ppermute | solution.py:585
  50.5 15.7 %pair_terms.3 = (f32[2,3,2304,128]{3,2,1,0:T(8,128)}, bf16[3,1152,128]{2,1,0:T(8,128)(2,1)}, bf16[3,768,128]{2,1,0:T(8,128)(2,1)}, bf16[3,384,128]{2,1,0:T(8,128)(2,1)}, f32[8,128]{1,0:T(8,128)}) custom-call(bf16[2,3,2304,128]{3,2,1,0:T(8,128)(2,1)} %get-tuple-element.24.own, bf16[2,96,96,128]{3,2,1,0:T(8,128)(2,1)} %get-tuple-element.25.own_u, ...), custom_call_target="tpu_custom_call" | custom-call | flops 20000000000 | bytes 20000000 | tf_op jit(solution)/shard_map/pair_terms/pallas_call | solution.py:442
  66.2 0.1 collective-permute-start.9
  66.3 2.3 %collective-permute-start.11 = (bf16[3,768,128]{2,1,0:T(8,128)(2,1)}, bf16[3,768,128]{2,1,0:T(8,128)(2,1)S(1)}, u32[]{:S(2)}, u32[]{:S(2)}) collective-permute-start(bf16[3,768,128]{2,1,0:T(8,128)(2,1)} %get-tuple-element.37), channel_id=1, source_target_pairs={{1,0},{2,1},{3,2},{4,3},{5,4},{6,5},{7,6},{8,7},{9,8},{10,9},{11,1... | collective-permute-start | bytes 1769480 | tf_op jit(solution)/shard_map/ppermute | solution.py:585
  68.5 0.1 collective-permute-start.3
  68.6 0.4 collective-permute-start.4
  69.1 1.3 %collective-permute-done.4 = f32[8,128]{1,0:T(8,128)S(1)} collective-permute-done((f32[8,128]{1,0:T(8,128)}, f32[8,128]{1,0:T(8,128)S(1)}, u32[]{:S(2)}, u32[]{:S(2)}) %collective-permute-start.4) | collective-permute-done | bytes 4128 | tf_op jit(solution)/shard_map/ppermute | solution.py:630
  70.3 0.7 add.22
  71.0 0.0 collective-permute-start.5
  71.0 3.6 %collective-permute-done.5 = f32[8,128]{1,0:T(8,128)S(1)} collective-permute-done((f32[8,128]{1,0:T(8,128)S(1)}, f32[8,128]{1,0:T(8,128)S(1)}, u32[]{:S(2)}, u32[]{:S(2)}) %collective-permute-start.5) | collective-permute-done | bytes 4128 | tf_op jit(solution)/shard_map/ppermute | solution.py:593
  74.6 0.0 collective-permute-start.6
  74.6 2.5 %collective-permute-done.9.back1 = bf16[3,1152,128]{2,1,0:T(8,128)(2,1)S(1)} collective-permute-done((bf16[3,1152,128]{2,1,0:T(8,128)(2,1)}, bf16[3,1152,128]{2,1,0:T(8,128)(2,1)S(1)}, u32[]{:S(2)}, u32[]{:S(2)}) %collective-permute-start.9) | collective-permute-done | bytes 884768 | tf_op jit(solution)/shard_map/ppermute | solution.py:585
  77.2 0.0 collective-permute-start.7
  77.2 0.0 collective-permute-done.2.back0
  77.2 2.0 %collective-permute-start.8 = (f32[8,128]{1,0:T(8,128)S(1)}, f32[8,128]{1,0:T(8,128)S(1)}, u32[]{:S(2)}, u32[]{:S(2)}) collective-permute-start(f32[8,128]{1,0:T(8,128)S(1)} %add.23), channel_id=1, source_target_pairs={{0,4},{1,25},{2,10},{3,27},{4,0},{5,29},{6,14},{7,31},{8,12},{9,17... | collective-permute-start | bytes 12296 | tf_op jit(solution)/shard_map/ppermute | solution.py:593
  79.2 4.9 %add_piece.3 = (f32[13824,128]{1,0:T(8,128)}, f32[2,2,8,128]{3,2,1,0:T(8,128)S(1)}) custom-call(bf16[2,3,2304,128]{3,2,1,0:T(8,128)(2,1)} %get-tuple-element.24.own, f32[2,3,2304,128]{3,2,1,0:T(8,128)} %get-tuple-element.28.terms, bf16[3,2304,128]{2,1,0:T(8,128)(2,1)} %collective-permute-done.2.back0, bf16[3,1152,128]{2,1,0:T(8,128)(2,1)S(1)} %collective-permute-done.9.back1), custom_call_target="tpu_custom_call" | custom-call | bytes 10616832 | tf_op jit(solution)/shard_map/add_piece/pallas_call | solution.py:555
  84.1 0.0 collective-permute-done.6
  84.1 0.0 collective-permute-done.7
  84.1 0.0 collective-permute-done.8
  84.1 0.1 collective-permute-start.10
  84.2 0.0 collective-permute-done.11.back1
  84.2 3.3 %add_piece.4 = (f32[13824,128]{1,0:T(8,128)}, f32[2,2,8,128]{3,2,1,0:T(8,128)S(1)}) custom-call(bf16[2,3,2304,128]{3,2,1,0:T(8,128)(2,1)} %get-tuple-element.24.own, f32[2,3,2304,128]{3,2,1,0:T(8,128)} %get-tuple-element.28.terms, bf16[3,2304,128]{2,1,0:T(8,128)(2,1)} %collective-permute-done.2.back0, ...), custom_call_target="tpu_custom_call", output_to_operand_aliasing={{0}: (4, {})} | custom-call | bytes 7077888 | tf_op jit(solution)/shard_map/add_piece/pallas_call | solution.py:555
  87.5 0.3 collective-permute-done.10
  87.8 2.3 %collective-permute-start.12 = (f32[8,128]{1,0:T(8,128)S(1)}, f32[8,128]{1,0:T(8,128)S(1)}, u32[]{:S(2)}, u32[]{:S(2)}) collective-permute-start(f32[8,128]{1,0:T(8,128)S(1)} %add.27), channel_id=1, source_target_pairs={{0,1},{1,0},{2,3},{3,2},{4,5},{5,4},{6,7},{7,6},{8,9},{9,8},{10,11... | collective-permute-start | bytes 12296 | tf_op jit(solution)/shard_map/ppermute | solution.py:642
  90.1 0.5 slice.6.rest_0_
  90.6 0.0 collective-permute-done.3.back1
  90.6 3.2 %add_piece.5 = (f32[13824,128]{1,0:T(8,128)}, f32[2,2]{1,0:T(2,128)}) custom-call(bf16[2,3,2304,128]{3,2,1,0:T(8,128)(2,1)} %get-tuple-element.24.own, f32[2,3,2304,128]{3,2,1,0:T(8,128)} %get-tuple-element.28.terms, bf16[3,2304,128]{2,1,0:T(8,128)(2,1)} %collective-permute-done.2.back0, ...), custom_call_target="tpu_custom_call", output_to_operand_aliasing={{0}: (7, {})} | custom-call | bytes 3538944 | tf_op jit(solution)/shard_map/add_piece/pallas_call | solution.py:555
  93.9 0.0 collective-permute-done.12
  93.9 0.6 slice.7
  (3 shorter events, 0.0 us)
Async XLA Ops:
  4.5 27.0 %collective-permute-start.1 = (bf16[6912,128]{1,0:T(8,128)(2,1)}, bf16[6912,128]{1,0:T(8,128)(2,1)}, u32[]{:S(2)}, u32[]{:S(2)}) collective-permute-start(bf16[6912,128]{1,0:T(8,128)(2,1)} %take_band.2.refs_0_.own0), channel_id=1, source_target_pairs={{31,0},{0,1},{1,2},{2,3},{3,4},{4,5},{5,6},{6,7},{7,8},{8,9},{9,10... | collective-permute-start | bytes 5308424 | tf_op jit(solution)/shard_map/ppermute | solution.py:585
  8.8 41.7 %collective-permute-start = (bf16[6912,128]{1,0:T(8,128)(2,1)}, bf16[6912,128]{1,0:T(8,128)(2,1)}, u32[]{:S(2)}, u32[]{:S(2)}) collective-permute-start(bf16[6912,128]{1,0:T(8,128)(2,1)} %take_band.3.own1), channel_id=1, source_target_pairs={{31,0},{0,1},{1,2},{2,3},{3,4},{4,5},{5,6},{6,7},{7,8},{8,9},{9,10... | collective-permute-start | bytes 5308424 | tf_op jit(solution)/shard_map/ppermute | solution.py:585
  46.9 30.3 %collective-permute-start.2 = (bf16[3,2304,128]{2,1,0:T(8,128)(2,1)}, bf16[3,2304,128]{2,1,0:T(8,128)(2,1)}, u32[]{:S(2)}, u32[]{:S(2)}) collective-permute-start(bf16[3,2304,128]{2,1,0:T(8,128)(2,1)} %get-tuple-element.29), channel_id=1, source_target_pairs={{1,0},{2,1},{3,2},{4,3},{5,4},{6,5},{7,6},{8,7},{9,8},{10,9},{11,1... | collective-permute-start | bytes 5308424 | tf_op jit(solution)/shard_map/ppermute | solution.py:585
  66.2 11.0 %collective-permute-start.9 = (bf16[3,1152,128]{2,1,0:T(8,128)(2,1)}, bf16[3,1152,128]{2,1,0:T(8,128)(2,1)S(1)}, u32[]{:S(2)}, u32[]{:S(2)}) collective-permute-start(bf16[3,1152,128]{2,1,0:T(8,128)(2,1)} %get-tuple-element.32), channel_id=1, source_target_pairs={{1,0},{2,1},{3,2},{4,3},{5,4},{6,5},{7,6},{8,7},{9,8},{10,9},{11,1... | collective-permute-start | bytes 2654216 | tf_op jit(solution)/shard_map/ppermute | solution.py:585
  66.3 18.0 %collective-permute-start.11 = (bf16[3,768,128]{2,1,0:T(8,128)(2,1)}, bf16[3,768,128]{2,1,0:T(8,128)(2,1)S(1)}, u32[]{:S(2)}, u32[]{:S(2)}) collective-permute-start(bf16[3,768,128]{2,1,0:T(8,128)(2,1)} %get-tuple-element.37), channel_id=1, source_target_pairs={{1,0},{2,1},{3,2},{4,3},{5,4},{6,5},{7,6},{8,7},{9,8},{10,9},{11,1... | collective-permute-start | bytes 1769480 | tf_op jit(solution)/shard_map/ppermute | solution.py:585
  68.5 22.1 %collective-permute-start.3 = (bf16[3,384,128]{2,1,0:T(8,128)(2,1)}, bf16[3,384,128]{2,1,0:T(8,128)(2,1)S(1)}, u32[]{:S(2)}, u32[]{:S(2)}) collective-permute-start(bf16[3,384,128]{2,1,0:T(8,128)(2,1)} %get-tuple-element.30), channel_id=1, source_target_pairs={{1,0},{2,1},{3,2},{4,3},{5,4},{6,5},{7,6},{8,7},{9,8},{10,9},{11,1... | collective-permute-start | bytes 884744 | tf_op jit(solution)/shard_map/ppermute | solution.py:585
  68.6 1.7 %collective-permute-start.4 = (f32[8,128]{1,0:T(8,128)}, f32[8,128]{1,0:T(8,128)S(1)}, u32[]{:S(2)}, u32[]{:S(2)}) collective-permute-start(f32[8,128]{1,0:T(8,128)} %get-tuple-element.31), channel_id=1, source_target_pairs={{0,1},{1,0},{2,3},{3,2},{4,5},{5,4},{6,7},{7,6},{8,9},{9,8},{10,11... | collective-permute-start | bytes 12296 | tf_op jit(solution)/shard_map/ppermute | solution.py:630
  71.0 3.6 %collective-permute-start.5 = (f32[8,128]{1,0:T(8,128)S(1)}, f32[8,128]{1,0:T(8,128)S(1)}, u32[]{:S(2)}, u32[]{:S(2)}) collective-permute-start(f32[8,128]{1,0:T(8,128)S(1)} %add.22), channel_id=1, source_target_pairs={{0,4},{1,5},{2,10},{3,7},{4,0},{5,1},{6,14},{7,3},{8,12},{9,13},{1... | collective-permute-start | bytes 12296 | tf_op jit(solution)/shard_map/ppermute | solution.py:593
  74.6 9.4 %collective-permute-start.6 = (f32[8,128]{1,0:T(8,128)S(1)}, f32[8,128]{1,0:T(8,128)S(1)}, u32[]{:S(2)}, u32[]{:S(2)}) collective-permute-start(f32[8,128]{1,0:T(8,128)S(1)} %add.23), channel_id=1, source_target_pairs={{0,4},{1,9},{2,10},{3,11},{4,0},{5,13},{6,14},{7,15},{8,12},{9,1},... | collective-permute-start | bytes 12296 | tf_op jit(solution)/shard_map/ppermute | solution.py:593
  77.2 6.9 %collective-permute-start.7 = (f32[8,128]{1,0:T(8,128)S(1)}, f32[8,128]{1,0:T(8,128)S(1)}, u32[]{:S(2)}, u32[]{:S(2)}) collective-permute-start(f32[8,128]{1,0:T(8,128)S(1)} %add.23), channel_id=1, source_target_pairs={{0,4},{1,17},{2,10},{3,19},{4,0},{5,21},{6,14},{7,23},{8,12},{9,25... | collective-permute-start | bytes 12296 | tf_op jit(solution)/shard_map/ppermute | solution.py:593
  77.2 6.9 %collective-permute-start.8 = (f32[8,128]{1,0:T(8,128)S(1)}, f32[8,128]{1,0:T(8,128)S(1)}, u32[]{:S(2)}, u32[]{:S(2)}) collective-permute-start(f32[8,128]{1,0:T(8,128)S(1)} %add.23), channel_id=1, source_target_pairs={{0,4},{1,25},{2,10},{3,27},{4,0},{5,29},{6,14},{7,31},{8,12},{9,17... | collective-permute-start | bytes 12296 | tf_op jit(solution)/shard_map/ppermute | solution.py:593
  84.1 3.7 %collective-permute-start.10 = (f32[8,128]{1,0:T(8,128)S(1)}, f32[8,128]{1,0:T(8,128)S(1)}, u32[]{:S(2)}, u32[]{:S(2)}) collective-permute-start(f32[8,128]{1,0:T(8,128)S(1)} %add_add_fusion), channel_id=1, source_target_pairs={{0,4},{1,3},{2,10},{3,1},{4,0},{5,7},{6,14},{7,5},{8,12},{9,11},{1... | collective-permute-start | bytes 12296 | tf_op jit(solution)/shard_map/ppermute | solution.py:593
  87.8 6.1 %collective-permute-start.12 = (f32[8,128]{1,0:T(8,128)S(1)}, f32[8,128]{1,0:T(8,128)S(1)}, u32[]{:S(2)}, u32[]{:S(2)}) collective-permute-start(f32[8,128]{1,0:T(8,128)S(1)} %add.27), channel_id=1, source_target_pairs={{0,1},{1,0},{2,3},{3,2},{4,5},{5,4},{6,7},{7,6},{8,9},{9,8},{10,11... | collective-permute-start | bytes 12296 | tf_op jit(solution)/shard_map/ppermute | solution.py:642

commit v20 on v18

--- a/solution.py
+++ b/solution.py
@@ -242,10 +242,13 @@
     table_loads[6].start()
     table_loads[0].start()
     loads = [
-        pltpu.make_async_copy(own_u, own_uv, sems.at[0]),
+        pltpu.make_async_copy(own_u.at[:, : G // 2], own_uv.at[:, : G // 2], sems.at[0]),
         pltpu.make_async_copy(kern, kern_v, sems.at[1]),
         pltpu.make_async_copy(own, own_v, sems.at[2]),
     ]
+    rest_u = pltpu.make_async_copy(
+        own_u.at[:, G // 2 :], own_uv.at[:, G // 2 :], sems.at[6 + len(pieces)]
+    )
     later = []
     if earlier:
         group = 2 * STEP_ROWS
@@ -261,7 +264,7 @@
 
     for i, load in enumerate(par_loads):
         load.wait()
-        for other in ([loads[0]], table_loads[1:5])[i]:
+        for other in ([loads[0]], [rest_u, *table_loads[1:5]])[i]:
             other.start()
         widen_planes(par_v.at[pl.ds(i * ROWS // 2, ROWS // 2), :], par_f, i * G // 2)
     table_loads[6].wait()
@@ -271,24 +274,29 @@
         split_rows(par_f, sel, par_u, 4 * q, 4)
 
     half_y = G * Y_PITCH
-    loads[0].wait()
-    for load in loads[1:]:
-        load.start()
-    table_loads[5].start()
-    table_loads[0].wait()
-
-    @pl.loop(0, G // 2, unroll=24)
-    def _(i):
-        density = []
-        for e in range(2):
-            partner = par_u[2 * i + e].astype(F32)
-            for p in range(2):
-                density.append((own_uv[p, 2 * i + e].astype(F32) * partner).astype(BF16))
-        out = dot(t1[...], lanes(*density))
-        for e in range(2):
-            for p in range(2):
-                at = pl.ds(p * half_y + (2 * i + e) * Y_PITCH, Y_ROWS)
-                yw[at, :] = out[:, (2 * e + p) * LANES : (2 * e + p + 1) * LANES]
+    for half in range(2):
+        if half == 0:
+            loads[0].wait()
+            table_loads[0].wait()
+        else:
+            rest_u.wait()
+            for load in loads[1:]:
+                load.start()
+            table_loads[5].start()
+
+        @pl.loop(0, G // 4, unroll=G // 4)
+        def _(i):
+            b = half * G // 2 + 2 * i
+            density = []
+            for e in range(2):
+                partner = par_u[b + e].astype(F32)
+                for p in range(2):
+                    density.append((own_uv[p, b + e].astype(F32) * partner).astype(BF16))
+            out = dot(t1[...], lanes(*density))
+            for e in range(2):
+                for p in range(2):
+                    at = pl.ds(p * half_y + (b + e) * Y_PITCH, Y_ROWS)
+                    yw[at, :] = out[:, (2 * e + p) * LANES : (2 * e + p + 1) * LANES]
 
     table_loads[1].wait()
 
@@ -467,7 +475,7 @@
             pltpu.SemaphoreType.DMA((2,)),
             pltpu.SemaphoreType.DMA((len(tables),)),
             pltpu.SemaphoreType.DMA((3, 6)),
-            pltpu.SemaphoreType.DMA((6 + len(pieces),)),
+            pltpu.SemaphoreType.DMA((7 + len(pieces),)),
         ],
         compiler_params=pltpu.CompilerParams(vmem_limit_bytes=63 * MIB),
         cost_estimate=pl.CostEstimate(
@@ -505,7 +513,7 @@
     if last:
         gram_loads = [
             pltpu.make_async_copy(src, gram_v.at[i], gram_sems.at[i])
-            for i, src in enumerate(earlier[1:-1])
+            for i, src in enumerate(earlier[:-1])
         ]
         for load in gram_loads:
             load.start()
@@ -547,10 +555,10 @@
     report.wait()
 
 
-def add_piece(first, size, own, terms, back0, back1, energy, grams, out, interpret=False):
+def add_piece(first, size, own, terms, back0, back1, grams, out, interpret=False):
     hbm = pl.BlockSpec(memory_space=pl.ANY)
     last = first + size == THIRD
-    earlier = [] if out is None else [*([energy, *grams] if last else []), out]
+    earlier = [] if out is None else [*(grams if last else []), out]
     gram_shape = (2, 2, 8, LANES)
     return pl.pallas_call(
         functools.partial(piece_kernel, first, size),
@@ -627,15 +635,12 @@
         got, last = None, piece is back1[-1]
         if last and size & (size - 1) == 0:
             got = lax.ppermute(energy, "band", swap)
-            energy = energy[:1, :1]
         elif steps:
             got = lax.ppermute(energy, "band", steps.pop(0))
-        exchange, gram = add_piece(
-            first, count, thirds, terms, back0, piece, energy, grams, exchange
-        )
+        exchange, gram = add_piece(first, count, thirds, terms, back0, piece, grams, exchange)
         if got is not None and last:
             odd = lax.axis_index("band") % 2 == 1
-            energy = jnp.where(odd, energy, after(got, gram)[:1, :1])
+            energy = jnp.where(odd, energy[:1, :1], after(got, gram)[:1, :1])
         elif got is not None:
             energy = energy + after(got, gram)
         grams.append(gram)

time: 95.5 us -> 94.7 us (level)
  Pallas kernels: 58.8 us -> 56.8 us
    pallas_call x2, Pallas kernels: 31.2 us -> 29.9 us  [pair_terms(): pl.pallas_call(functools.partial(pairs_kernel, pieces, share), out_shape=...]
  transfers between devices with their start and end apart: 12 -> 12, of which waited for: 5 -> 5; matrix products, arithmetic and copies ran while one was open for 1% -> 1% of each run, Pallas kernels for 58% -> 56%
where the time goes in v20:
time: 94.7 us; the launch traced here: 94.4 us
  Pallas kernels  56.8 us (60%)
  waiting for transfers between devices  23.6 us (25%)
  starting transfers between devices  9.13 us (10%)
  between operations  3.1 us (3%)
  local copies, waits for them, and re-layouts  0.99 us (1%)
    pallas_call x2, Pallas kernels, pair_terms(): pl.pallas_call(functools.partial(pairs_kernel, pieces, share), out_shape=...  29.9 us
    ppermute x6, waiting for transfers between devices, from_behind(): lax.ppermute(block, axis, [((i - distance) % size, i) for i in range(size)])  15.1 us
    pallas_call x3, Pallas kernels, add_piece(): pl.pallas_call(functools.partial(piece_kernel, first, size), out_shape=(j...  10.7 us
    pallas_call x1, Pallas kernels, padded_rows(): pl.pallas_call(rows_kernel, out_shape=(jax.ShapeDtypeStruct((2, G, G, LAN...  8.58 us
    pallas_call x2, Pallas kernels, take_band(): pl.pallas_call(functools.partial(band_kernel, p), out_shape=jax.ShapeDtyp...  7.66 us
    ppermute x2, waiting for transfers between devices, per_device(): energy = energy + lax.ppermute(energy, 'band', steps.pop(0))  7.21 us
    ppermute x6, starting transfers between devices, from_behind(): lax.ppermute(block, axis, [((i - distance) % size, i) for i in range(size)])  6.53 us
    ppermute x2, starting transfers between devices, per_device(): got = lax.ppermute(energy, 'band', steps.pop(0))  2.08 us
  transfers between devices with their start and end apart: 12, of which 5 were waited for; matrix products, arithmetic and copies ran while one was open for 1% of the time, Pallas kernels for 56%

profile of v20, /device:TPU:0, one launch (start us, length us, event | category | flops | bytes accessed | tf_op | source)
XLA Modules:
  0.0 94.4 jit_solution(14689394736465029139)
XLA Ops:
  0.6 3.8 %take_band.2.refs_0_.own0 = bf16[6912,128]{1,0:T(8,128)(2,1)} custom-call(bf16[13824,128]{1,0:T(8,128)(2,1)} %bitcast.13), custom_call_target="tpu_custom_call" | custom-call | bytes 5308416 | tf_op jit(solution)/shard_map/take_band/pallas_call | solution.py:170
  4.5 0.5 collective-permute-start.1
  5.0 3.8 %take_band.3.own1 = bf16[6912,128]{1,0:T(8,128)(2,1)} custom-call(bf16[13824,128]{1,0:T(8,128)(2,1)} %bitcast.14, bf16[6912,128]{1,0:T(8,128)(2,1)} %take_band.2.refs_0_.own0), custom_call_target="tpu_custom_call" | custom-call | bytes 5308416 | tf_op jit(solution)/shard_map/take_band/pallas_call | solution.py:170
  8.8 2.8 %collective-permute-start = (bf16[6912,128]{1,0:T(8,128)(2,1)}, bf16[6912,128]{1,0:T(8,128)(2,1)}, u32[]{:S(2)}, u32[]{:S(2)}) collective-permute-start(bf16[6912,128]{1,0:T(8,128)(2,1)} %take_band.3.own1), channel_id=1, source_target_pairs={{31,0},{0,1},{1,2},{2,3},{3,4},{4,5},{5,6},{6,7},{7,8},{8,9},{9,10... | collective-permute-start | bytes 5308424 | tf_op jit(solution)/shard_map/ppermute | solution.py:593
  11.7 8.6 %padded_rows.1 = (bf16[2,96,96,128]{3,2,1,0:T(8,128)(2,1)}, bf16[2,3,2304,128]{3,2,1,0:T(8,128)(2,1)}) custom-call(bf16[6912,128]{1,0:T(8,128)(2,1)} %take_band.2.refs_0_.own0, bf16[6912,128]{1,0:T(8,128)(2,1)} %take_band.3.own1, bf16[2,256,256]{2,1,0:T(8,128)(2,1)} %constant.34.clone.sel.refs_6_.refs_8_), custom_call_target="tpu_custom_call" | custom-call | bytes 14155776 | tf_op jit(solution)/shard_map/padded_rows/pallas_call | solution.py:206
  20.2 11.2 %collective-permute-done.1.par = bf16[6912,128]{1,0:T(8,128)(2,1)} collective-permute-done((bf16[6912,128]{1,0:T(8,128)(2,1)}, bf16[6912,128]{1,0:T(8,128)(2,1)}, u32[]{:S(2)}, u32[]{:S(2)}) %collective-permute-start.1) | collective-permute-done | bytes 1769504 | tf_op jit(solution)/shard_map/ppermute | solution.py:593
  31.4 14.8 %pair_terms.2 = (f32[2,3,2304,128]{3,2,1,0:T(8,128)}, bf16[3,2304,128]{2,1,0:T(8,128)(2,1)}, f32[8,128]{1,0:T(8,128)}) custom-call(bf16[2,3,2304,128]{3,2,1,0:T(8,128)(2,1)} %get-tuple-element.22.own, bf16[2,96,96,128]{3,2,1,0:T(8,128)(2,1)} %get-tuple-element.23.own_u, f32[4800,128]{1,0:T(8,128)} %constant.35.clone.kern, ...), custom_call_target="tpu_custom_call" | custom-call | flops 20000000000 | bytes 20000000 | tf_op jit(solution)/shard_map/pair_terms/pallas_call | solution.py:450
  46.3 0.3 collective-permute-start.2
  46.5 3.9 %collective-permute-done.par = bf16[6912,128]{1,0:T(8,128)(2,1)} collective-permute-done((bf16[6912,128]{1,0:T(8,128)(2,1)}, bf16[6912,128]{1,0:T(8,128)(2,1)}, u32[]{:S(2)}, u32[]{:S(2)}) %collective-permute-start) | collective-permute-done | bytes 1769504 | tf_op jit(solution)/shard_map/ppermute | solution.py:593
  50.5 15.1 %pair_terms.3 = (f32[2,3,2304,128]{3,2,1,0:T(8,128)}, bf16[3,1152,128]{2,1,0:T(8,128)(2,1)}, bf16[3,768,128]{2,1,0:T(8,128)(2,1)}, bf16[3,384,128]{2,1,0:T(8,128)(2,1)}, f32[8,128]{1,0:T(8,128)}) custom-call(bf16[2,3,2304,128]{3,2,1,0:T(8,128)(2,1)} %get-tuple-element.22.own, bf16[2,96,96,128]{3,2,1,0:T(8,128)(2,1)} %get-tuple-element.23.own_u, ...), custom_call_target="tpu_custom_call" | custom-call | flops 20000000000 | bytes 20000000 | tf_op jit(solution)/shard_map/pair_terms/pallas_call | solution.py:450
  65.5 0.1 collective-permute-start.4
  65.6 2.8 %collective-permute-start.5 = (bf16[3,768,128]{2,1,0:T(8,128)(2,1)}, bf16[3,768,128]{2,1,0:T(8,128)(2,1)S(1)}, u32[]{:S(2)}, u32[]{:S(2)}) collective-permute-start(bf16[3,768,128]{2,1,0:T(8,128)(2,1)} %get-tuple-element.31), channel_id=1, source_target_pairs={{1,0},{2,1},{3,2},{4,3},{5,4},{6,5},{7,6},{8,7},{9,8},{10,9},{11,1... | collective-permute-start | bytes 1769480 | tf_op jit(solution)/shard_map/ppermute | solution.py:593
  68.4 0.1 collective-permute-start.3
  68.5 0.4 collective-permute-start.6
  68.9 1.3 %collective-permute-done.6 = f32[8,128]{1,0:T(8,128)S(1)} collective-permute-done((f32[8,128]{1,0:T(8,128)}, f32[8,128]{1,0:T(8,128)S(1)}, u32[]{:S(2)}, u32[]{:S(2)}) %collective-permute-start.6) | collective-permute-done | bytes 4128 | tf_op jit(solution)/shard_map/ppermute | solution.py:624
  70.2 0.7 add.20
  70.9 0.0 collective-permute-start.7
  70.9 3.6 %collective-permute-done.7 = f32[8,128]{1,0:T(8,128)S(1)} collective-permute-done((f32[8,128]{1,0:T(8,128)S(1)}, f32[8,128]{1,0:T(8,128)S(1)}, u32[]{:S(2)}, u32[]{:S(2)}) %collective-permute-start.7) | collective-permute-done | bytes 4128 | tf_op jit(solution)/shard_map/ppermute | solution.py:630
  74.5 0.0 collective-permute-start.8
  74.5 3.6 %collective-permute-done.8 = f32[8,128]{1,0:T(8,128)S(1)} collective-permute-done((f32[8,128]{1,0:T(8,128)S(1)}, f32[8,128]{1,0:T(8,128)S(1)}, u32[]{:S(2)}, u32[]{:S(2)}) %collective-permute-start.8) | collective-permute-done | bytes 4128 | tf_op jit(solution)/shard_map/ppermute | solution.py:630
  78.1 0.0 collective-permute-start.9
  78.1 0.0 collective-permute-done.4.back1
  78.1 0.0 collective-permute-done.2.back0
  78.1 4.9 %add_piece.3 = (f32[13824,128]{1,0:T(8,128)}, f32[2,2,8,128]{3,2,1,0:T(8,128)S(1)}) custom-call(bf16[2,3,2304,128]{3,2,1,0:T(8,128)(2,1)} %get-tuple-element.22.own, f32[2,3,2304,128]{3,2,1,0:T(8,128)} %get-tuple-element.26.terms, bf16[3,2304,128]{2,1,0:T(8,128)(2,1)} %collective-permute-done.2.back0, bf16[3,1152,128]{2,1,0:T(8,128)(2,1)S(1)} %collective-permute-done.4.back1), custom_call_target="tpu_custom_call" | custom-call | bytes 10616832 | tf_op jit(solution)/shard_map/add_piece/pallas_call | solution.py:563
  83.0 0.0 collective-permute-done.9
  83.0 2.1 %collective-permute-start.10 = (f32[8,128]{1,0:T(8,128)S(1)}, f32[8,128]{1,0:T(8,128)S(1)}, u32[]{:S(2)}, u32[]{:S(2)}) collective-permute-start(f32[8,128]{1,0:T(8,128)S(1)} %add.23), channel_id=1, source_target_pairs={{0,4},{1,3},{2,10},{3,1},{4,0},{5,7},{6,14},{7,5},{8,12},{9,11},{1... | collective-permute-start | bytes 12296 | tf_op jit(solution)/shard_map/ppermute | solution.py:639
  85.1 0.0 collective-permute-done.5.back1
  85.1 3.3 %add_piece.4 = (f32[13824,128]{1,0:T(8,128)}, f32[2,2,8,128]{3,2,1,0:T(8,128)S(1)}) custom-call(bf16[2,3,2304,128]{3,2,1,0:T(8,128)(2,1)} %get-tuple-element.22.own, f32[2,3,2304,128]{3,2,1,0:T(8,128)} %get-tuple-element.26.terms, bf16[3,2304,128]{2,1,0:T(8,128)(2,1)} %collective-permute-done.2.back0, ...), custom_call_target="tpu_custom_call", output_to_operand_aliasing={{0}: (4, {})} | custom-call | bytes 7077888 | tf_op jit(solution)/shard_map/add_piece/pallas_call | solution.py:563
  88.4 0.0 collective-permute-done.10
  88.4 0.1 collective-permute-start.11
  88.5 0.0 collective-permute-done.3.back1
  88.5 2.6 %add_piece.5 = (f32[13824,128]{1,0:T(8,128)}, f32[2,2]{1,0:T(2,128)}) custom-call(bf16[2,3,2304,128]{3,2,1,0:T(8,128)(2,1)} %get-tuple-element.22.own, f32[2,3,2304,128]{3,2,1,0:T(8,128)} %get-tuple-element.26.terms, bf16[3,2304,128]{2,1,0:T(8,128)(2,1)} %collective-permute-done.2.back0, ...), custom_call_target="tpu_custom_call", output_to_operand_aliasing={{0}: (6, {})} | custom-call | bytes 3538944 | tf_op jit(solution)/shard_map/add_piece/pallas_call | solution.py:563
  91.1 0.5 slice.6
  91.6 0.0 collective-permute-done.11
  91.6 0.5 slice.7
  (4 shorter events, 0.0 us)
Async XLA Ops:
  4.5 27.0 %collective-permute-start.1 = (bf16[6912,128]{1,0:T(8,128)(2,1)}, bf16[6912,128]{1,0:T(8,128)(2,1)}, u32[]{:S(2)}, u32[]{:S(2)}) collective-permute-start(bf16[6912,128]{1,0:T(8,128)(2,1)} %take_band.2.refs_0_.own0), channel_id=1, source_target_pairs={{31,0},{0,1},{1,2},{2,3},{3,4},{4,5},{5,6},{6,7},{7,8},{8,9},{9,10... | collective-permute-start | bytes 5308424 | tf_op jit(solution)/shard_map/ppermute | solution.py:593
  8.8 41.7 %collective-permute-start = (bf16[6912,128]{1,0:T(8,128)(2,1)}, bf16[6912,128]{1,0:T(8,128)(2,1)}, u32[]{:S(2)}, u32[]{:S(2)}) collective-permute-start(bf16[6912,128]{1,0:T(8,128)(2,1)} %take_band.3.own1), channel_id=1, source_target_pairs={{31,0},{0,1},{1,2},{2,3},{3,4},{4,5},{5,6},{6,7},{7,8},{8,9},{9,10... | collective-permute-start | bytes 5308424 | tf_op jit(solution)/shard_map/ppermute | solution.py:593
  46.3 31.9 %collective-permute-start.2 = (bf16[3,2304,128]{2,1,0:T(8,128)(2,1)}, bf16[3,2304,128]{2,1,0:T(8,128)(2,1)}, u32[]{:S(2)}, u32[]{:S(2)}) collective-permute-start(bf16[3,2304,128]{2,1,0:T(8,128)(2,1)} %get-tuple-element.27), channel_id=1, source_target_pairs={{1,0},{2,1},{3,2},{4,3},{5,4},{6,5},{7,6},{8,7},{9,8},{10,9},{11,1... | collective-permute-start | bytes 5308424 | tf_op jit(solution)/shard_map/ppermute | solution.py:593
  65.5 12.6 %collective-permute-start.4 = (bf16[3,1152,128]{2,1,0:T(8,128)(2,1)}, bf16[3,1152,128]{2,1,0:T(8,128)(2,1)S(1)}, u32[]{:S(2)}, u32[]{:S(2)}) collective-permute-start(bf16[3,1152,128]{2,1,0:T(8,128)(2,1)} %get-tuple-element.29), channel_id=1, source_target_pairs={{1,0},{2,1},{3,2},{4,3},{5,4},{6,5},{7,6},{8,7},{9,8},{10,9},{11,1... | collective-permute-start | bytes 2654216 | tf_op jit(solution)/shard_map/ppermute | solution.py:593
  65.6 19.5 %collective-permute-start.5 = (bf16[3,768,128]{2,1,0:T(8,128)(2,1)}, bf16[3,768,128]{2,1,0:T(8,128)(2,1)S(1)}, u32[]{:S(2)}, u32[]{:S(2)}) collective-permute-start(bf16[3,768,128]{2,1,0:T(8,128)(2,1)} %get-tuple-element.31), channel_id=1, source_target_pairs={{1,0},{2,1},{3,2},{4,3},{5,4},{6,5},{7,6},{8,7},{9,8},{10,9},{11,1... | collective-permute-start | bytes 1769480 | tf_op jit(solution)/shard_map/ppermute | solution.py:593
  68.4 20.1 %collective-permute-start.3 = (bf16[3,384,128]{2,1,0:T(8,128)(2,1)}, bf16[3,384,128]{2,1,0:T(8,128)(2,1)S(1)}, u32[]{:S(2)}, u32[]{:S(2)}) collective-permute-start(bf16[3,384,128]{2,1,0:T(8,128)(2,1)} %get-tuple-element.28), channel_id=1, source_target_pairs={{1,0},{2,1},{3,2},{4,3},{5,4},{6,5},{7,6},{8,7},{9,8},{10,9},{11,1... | collective-permute-start | bytes 884744 | tf_op jit(solution)/shard_map/ppermute | solution.py:593
  68.5 1.7 %collective-permute-start.6 = (f32[8,128]{1,0:T(8,128)}, f32[8,128]{1,0:T(8,128)S(1)}, u32[]{:S(2)}, u32[]{:S(2)}) collective-permute-start(f32[8,128]{1,0:T(8,128)} %get-tuple-element.37), channel_id=1, source_target_pairs={{0,1},{1,0},{2,3},{3,2},{4,5},{5,4},{6,7},{7,6},{8,9},{9,8},{10,11... | collective-permute-start | bytes 12296 | tf_op jit(solution)/shard_map/ppermute | solution.py:624
  70.9 3.6 %collective-permute-start.7 = (f32[8,128]{1,0:T(8,128)S(1)}, f32[8,128]{1,0:T(8,128)S(1)}, u32[]{:S(2)}, u32[]{:S(2)}) collective-permute-start(f32[8,128]{1,0:T(8,128)S(1)} %add.20), channel_id=1, source_target_pairs={{0,4},{1,5},{2,10},{3,7},{4,0},{5,1},{6,14},{7,3},{8,12},{9,13},{1... | collective-permute-start | bytes 12296 | tf_op jit(solution)/shard_map/ppermute | solution.py:630
  74.5 3.6 %collective-permute-start.8 = (f32[8,128]{1,0:T(8,128)S(1)}, f32[8,128]{1,0:T(8,128)S(1)}, u32[]{:S(2)}, u32[]{:S(2)}) collective-permute-start(f32[8,128]{1,0:T(8,128)S(1)} %add.21), channel_id=1, source_target_pairs={{0,4},{1,9},{2,10},{3,11},{4,0},{5,13},{6,14},{7,15},{8,12},{9,1},... | collective-permute-start | bytes 12296 | tf_op jit(solution)/shard_map/ppermute | solution.py:630
  78.1 4.9 %collective-permute-start.9 = (f32[8,128]{1,0:T(8,128)S(1)}, f32[8,128]{1,0:T(8,128)S(1)}, u32[]{:S(2)}, u32[]{:S(2)}) collective-permute-start(f32[8,128]{1,0:T(8,128)S(1)} %add.22), channel_id=1, source_target_pairs={{0,4},{1,17},{2,10},{3,19},{4,0},{5,21},{6,14},{7,23},{8,12},{9,25... | collective-permute-start | bytes 12296 | tf_op jit(solution)/shard_map/ppermute | solution.py:639
  83.0 5.4 %collective-permute-start.10 = (f32[8,128]{1,0:T(8,128)S(1)}, f32[8,128]{1,0:T(8,128)S(1)}, u32[]{:S(2)}, u32[]{:S(2)}) collective-permute-start(f32[8,128]{1,0:T(8,128)S(1)} %add.23), channel_id=1, source_target_pairs={{0,4},{1,3},{2,10},{3,1},{4,0},{5,7},{6,14},{7,5},{8,12},{9,11},{1... | collective-permute-start | bytes 12296 | tf_op jit(solution)/shard_map/ppermute | solution.py:639
  88.4 3.2 %collective-permute-start.11 = (f32[8,128]{1,0:T(8,128)S(1)}, f32[8,128]{1,0:T(8,128)S(1)}, u32[]{:S(2)}, u32[]{:S(2)}) collective-permute-start(f32[8,128]{1,0:T(8,128)S(1)} %add.24), channel_id=1, source_target_pairs={{0,1},{1,0},{2,3},{3,2},{4,5},{5,4},{6,7},{7,6},{8,9},{9,8},{10,11... | collective-permute-start | bytes 12296 | tf_op jit(solution)/shard_map/ppermute | solution.py:637
